TPU v7x, 32 devices: a whole 2x2x4 slice. The times are simulated.
32 devices in a mesh: shot: 2 (over core), gx: 8 (over z, y), gy: 2 (over x).
Axes of the slice: x: 2, y: 2, z: 4, core: 2. Of those that a mesh axis runs over, the one named last changes fastest.
Arguments:
- source_now: float32 [2, 256, 256, 128], P('shot', 'gx', 'gy'), may hold values from -6 to 6
- source_before: float32 [2, 256, 256, 128], P('shot', 'gx', 'gy'), may hold values from -6 to 6
- receiver_now: float32 [2, 256, 256, 128], P('shot', 'gx', 'gy'), may hold values from -6 to 6
- receiver_before: float32 [2, 256, 256, 128], P('shot', 'gx', 'gy'), may hold values from -6 to 6
- courant: float32 [256, 256, 128], P('gx', 'gy'), may hold values from 0.02 to 0.18
Outputs:
- offset_gathers: float32 [65, 64, 64, 128], P(None, 'gx', 'gy', 'shot')
All inputs are finite; a program needn't handle non-finite values.
Results may differ from a plain program's by a relative error of at most 0.000096.
Values sent between devices are 32-bit elements; how exact they have to be, the bound alone decides.
No kernel may reach another device: no remote copies, remote signals or barrier semaphores. Data moves between devices by JAX's collectives and lax.ppermute only.
A program may use at most 192 MiB of HBM per device.

v0:
```python
import jax
import jax.numpy as jnp
from jax import lax
from jax.sharding import PartitionSpec as P

HALF = 32
SUB = 2


STENCIL_WEIGHTS = (-205.0 / 72.0, 8.0 / 5.0, -1.0 / 5.0, 8.0 / 315.0, -1.0 / 560.0)


def extended(array, sides, width):
    for axis, dim in sides:
        size, length = (lax.axis_size(axis), array.shape[dim])
        up = [(i, (i + 1) % size) for i in range(size - 1)]
        down = [(j, i) for i, j in up]
        last = lax.slice_in_dim(array, length - width, length, axis=dim)
        leading = lax.slice_in_dim(array, 0, width, axis=dim)
        before = lax.ppermute(last, axis, up)
        after = lax.ppermute(leading, axis, down)
        array = jnp.concatenate([before, array, after], axis=dim)
    return array


def stencil_sum(padded, field):
    size_x, size_y, size_z = (field.shape[1], field.shape[2], field.shape[3])
    result = 3.0 * STENCIL_WEIGHTS[0] * field
    for distance in range(1, 5):
        weight = STENCIL_WEIGHTS[distance]
        along_x = (
            padded[:, 4 + distance : 4 + distance + size_x, 4 : 4 + size_y, 4 : 4 + size_z]
            + padded[:, 4 - distance : 4 - distance + size_x, 4 : 4 + size_y, 4 : 4 + size_z]
        )
        along_y = (
            padded[:, 4 : 4 + size_x, 4 + distance : 4 + distance + size_y, 4 : 4 + size_z]
            + padded[:, 4 : 4 + size_x, 4 - distance : 4 - distance + size_y, 4 : 4 + size_z]
        )
        along_z = (
            padded[:, 4 : 4 + size_x, 4 : 4 + size_y, 4 + distance : 4 + distance + size_z]
            + padded[:, 4 : 4 + size_x, 4 : 4 + size_y, 4 - distance : 4 - distance + size_z]
        )
        result = result + weight * (along_x + along_y + along_z)
    return result


def correlate(padded, shot_count):
    row_count = padded.shape[1] - 2 * HALF
    sample_rows = jnp.arange(row_count // 4, dtype=jnp.int32) * 4
    offsets = jnp.arange(2 * HALF + 1, dtype=jnp.int32)
    source_index = sample_rows[None, :] + 2 * HALF - offsets[:, None]
    receiver_index = sample_rows[None, :] + offsets[:, None]
    source_rows = jnp.take(padded[:shot_count], source_index, axis=1)
    receiver_rows = jnp.take(padded[shot_count:], receiver_index, axis=1)
    return jnp.sum(source_rows * receiver_rows, axis=0)


def on_device(source_now, source_before, receiver_now, receiver_before, courant):
    shot_count = source_now.shape[0]
    fields = jnp.concatenate([source_now, receiver_now], axis=0)
    before = jnp.concatenate([source_before, receiver_before], axis=0)

    def image_step(current):
        source_part = current[:shot_count, :, ::4, :]
        receiver_part = current[shot_count:, :, ::4, :]
        count = source_part.shape[0]
        decimated = jnp.concatenate([source_part, receiver_part], axis=0)
        padded = extended(decimated, (("gx", 1),), HALF)
        return correlate(padded, count)

    image_sum = image_step(fields)
    for repeat in range(SUB):
        advance_padded = extended(fields, (("gx", 1), ("gy", 2)), 4)
        advance_padded = jnp.pad(advance_padded, ((0, 0), (0, 0), (0, 0), (4, 4)))
        advanced = 2.0 * fields - before + courant[None] * stencil_sum(advance_padded, fields)
        before = fields
        fields = advanced
    image_sum = image_sum + image_step(fields)
    summed = lax.psum_scatter(image_sum, "shot", scatter_dimension=3, tiled=True)
    return summed


def solution(mesh):
    in_specs = (
        P("shot", "gx", "gy", None),
        P("shot", "gx", "gy", None),
        P("shot", "gx", "gy", None),
        P("shot", "gx", "gy", None),
        P("gx", "gy", None),
    )
    out_specs = P(None, "gx", "gy", "shot")
    return jax.shard_map(
        on_device, mesh=mesh, in_specs=in_specs, out_specs=out_specs, check_vma=False
    )
```

profile of v0, /device:TPU:0, one launch (start us, length us, event | category | flops | bytes accessed | tf_op | source)
XLA Modules:
  0.0 417.8 jit_solution(2193294838663399703)
XLA Ops:
  10.3 5.5 %collective-permute-start.3 = (f32[2,4,128,128]{3,2,1,0:T(8,128)S(1)}, f32[2,4,128,128]{3,2,1,0:T(8,128)S(1)}, u32[]{:S(2)}, u32[]{:S(2)}) collective-permute-start(f32[2,4,128,128]{3,2,1,0:T(8,128)S(1)} %get-tuple-element.17), channel_id=1, source_target_pairs={{0,2},{2,4},{4,6},{6,8},{8,10},{10,12},{12,14},{1,3},{3,5},{5,7},{... | collective-permute-start | bytes 1572872 | tf_op jit(solution)/shard_map/ppermute | solution.py:20
  15.9 10.0 %collective-permute-done.2 = f32[2,4,128,128]{3,2,1,0:T(8,128)S(1)} collective-permute-done((f32[2,4,128,128]{3,2,1,0:T(8,128)S(1)}, f32[2,4,128,128]{3,2,1,0:T(8,128)S(1)}, u32[]{:S(2)}, u32[]{:S(2)}) %collective-permute-start.2) | collective-permute-done | bytes 524320 | tf_op jit(solution)/shard_map/ppermute | solution.py:21
  25.8 11.4 %collective-permute-done.3 = f32[2,4,128,128]{3,2,1,0:T(8,128)S(1)} collective-permute-done((f32[2,4,128,128]{3,2,1,0:T(8,128)S(1)}, f32[2,4,128,128]{3,2,1,0:T(8,128)S(1)}, u32[]{:S(2)}, u32[]{:S(2)}) %collective-permute-start.3) | collective-permute-done | bytes 524320 | tf_op jit(solution)/shard_map/ppermute | solution.py:20
  39.3 4.6 %collective-permute-start.5 = (f32[2,40,4,128]{3,2,1,0:T(4,128)}, f32[2,40,4,128]{3,2,1,0:T(4,128)S(1)}, u32[]{:S(2)}, u32[]{:S(2)}) collective-permute-start(f32[2,40,4,128]{3,2,1,0:T(4,128)} %get-tuple-element.12), channel_id=1, source_target_pairs={{0,1},{2,3},{4,5},{6,7},{8,9},{10,11},{12,13},{14,15},{16,17},{18,... | collective-permute-start | bytes 491528 | tf_op jit(solution)/shard_map/ppermute | solution.py:20
  50.6 7.9 %pad_maximum_fusion = (f32[2,40,132,128]{3,2,1,0:T(8,128)}, f32[2,40,132,128]{3,2,1,0:T(8,128)}) fusion(f32[2,40,4,128]{3,2,1,0:T(4,128)S(1)} %collective-permute-done.4, f32[2,4,128,128]{3,2,1,0:T(8,128)S(1)} %collective-permute-done.2, f32[2,32,128,128]{3,2,1,0:T(8,128)} %copy-done, f32[2,4,128,128]{3,2,1,0:T(8,128)S(1)} %collective-permute-done.3, ...), kind=kLoop, calls=%fused_computation.31 | loop fusion | flops 8110080 | bytes 16384000 | tf_op jit(solution)/shard_map/concatenate | solution.py:22
  58.5 11.1 %select_maximum_fusion.4 = f32[2,40,136,136]{3,2,1,0:T(8,128)} fusion(f32[2,40,4,128]{3,2,1,0:T(4,128)S(1)} %collective-permute-done.4, f32[2,40,4,128]{3,2,1,0:T(4,128)S(1)} %collective-permute-done.5, f32[2,4,128,128]{3,2,1,0:T(8,128)S(1)} %collective-permute-done.2, f32[2,32,128,128]{3,2,1,0:T(8,128)S(1)} %copy-done.1, ...), kind=kLoop, calls=%fused_computation.10 | loop fusion | flops 17756160 | bytes 11489280 | tf_op jit(solution)/shard_map/concatenate | solution.py:22
  69.5 51.4 %fusion.35 = f32[2,32,128,128]{3,2,1,0:T(8,128)} fusion(f32[2,32,128,128]{3,2,1,0:T(8,128)} %copy-done, f32[2,4,128,128]{3,2,1,0:T(8,128)S(1)} %collective-permute-done.3, f32[2,4,128,128]{3,2,1,0:T(8,128)S(1)} %collective-permute-done.2, f32[2,40,136,136]{3,2,1,0:T(8,128)} %select_maximum_fusion.4, f32[2,40,132,128]{3,2,1,0:T(8,128)} %get-tuple-element.11, ...), kind=kLoop, calls=%fused_computation.79 | loop fusion | flops 44040192 | bytes 82837504 | tf_op jit(solution)/shard_map/add | solution.py:75
  124.5 5.0 %collective-permute-start.7 = (f32[2,4,128,128]{3,2,1,0:T(8,128)}, f32[2,4,128,128]{3,2,1,0:T(8,128)S(1)}, u32[]{:S(2)}, u32[]{:S(2)}) collective-permute-start(f32[2,4,128,128]{3,2,1,0:T(8,128)} %get-tuple-element.15), channel_id=1, source_target_pairs={{0,2},{2,4},{4,6},{6,8},{8,10},{10,12},{12,14},{1,3},{3,5},{5,7},{... | collective-permute-start | bytes 1572872 | tf_op jit(solution)/shard_map/ppermute | solution.py:20
  131.9 5.8 %collective-permute-start = (f32[2,32,32,128]{3,2,1,0:T(8,128)}, f32[2,32,32,128]{3,2,1,0:T(8,128)}, u32[]{:S(2)}, u32[]{:S(2)}) collective-permute-start(f32[2,32,32,128]{3,2,1,0:T(8,128)} %pad_maximum_fusion.8), channel_id=1, source_target_pairs={{0,2},{2,4},{4,6},{6,8},{8,10},{10,12},{12,14},{1,3},{3,5},{5,7},{... | collective-permute-start | bytes 3145736 | tf_op jit(solution)/shard_map/ppermute | solution.py:20
  139.4 34.1 %collective-permute-done.7 = f32[2,4,128,128]{3,2,1,0:T(8,128)S(1)} collective-permute-done((f32[2,4,128,128]{3,2,1,0:T(8,128)}, f32[2,4,128,128]{3,2,1,0:T(8,128)S(1)}, u32[]{:S(2)}, u32[]{:S(2)}) %collective-permute-start.7) | collective-permute-done | bytes 524320 | tf_op jit(solution)/shard_map/ppermute | solution.py:20
  176.5 4.7 %collective-permute-start.9 = (f32[2,40,4,128]{3,2,1,0:T(4,128)}, f32[2,40,4,128]{3,2,1,0:T(4,128)S(1)}, u32[]{:S(2)}, u32[]{:S(2)}) collective-permute-start(f32[2,40,4,128]{3,2,1,0:T(4,128)} %get-tuple-element.8), channel_id=1, source_target_pairs={{0,1},{2,3},{4,5},{6,7},{8,9},{10,11},{12,13},{14,15},{16,17},{18,... | collective-permute-start | bytes 491528 | tf_op jit(solution)/shard_map/ppermute | solution.py:20
  184.7 7.9 %pad_maximum_fusion.1 = (f32[2,40,132,128]{3,2,1,0:T(8,128)}, f32[2,40,132,128]{3,2,1,0:T(8,128)}) fusion(f32[2,40,4,128]{3,2,1,0:T(4,128)S(1)} %collective-permute-done.8, f32[2,4,128,128]{3,2,1,0:T(8,128)S(1)} %collective-permute-done.6, f32[2,32,128,128]{3,2,1,0:T(8,128)} %fusion.35, f32[2,4,128,128]{3,2,1,0:T(8,128)S(1)} %collective-permute-done.7, ...), kind=kLoop, calls=%fused_computation.33 | loop fusion | flops 8110080 | bytes 16384000 | tf_op jit(solution)/shard_map/concatenate | solution.py:22
  192.6 11.0 %select_maximum_fusion = f32[2,40,136,136]{3,2,1,0:T(8,128)} fusion(f32[2,40,4,128]{3,2,1,0:T(4,128)S(1)} %collective-permute-done.8, f32[2,40,4,128]{3,2,1,0:T(4,128)S(1)} %collective-permute-done.9, f32[2,4,128,128]{3,2,1,0:T(8,128)S(1)} %collective-permute-done.6, f32[2,32,128,128]{3,2,1,0:T(8,128)S(1)} %copy-done.2, ...), kind=kLoop, calls=%fused_computation.6 | loop fusion | flops 17756160 | bytes 11489280 | tf_op jit(solution)/shard_map/concatenate | solution.py:22
  203.6 69.8 %fusion.11 = f32[2,32,128,128]{3,2,1,0:T(8,128)} fusion(f32[2,32,128,128]{3,2,1,0:T(8,128)} %fusion.35, f32[2,4,128,128]{3,2,1,0:T(8,128)S(1)} %collective-permute-done.7, f32[2,4,128,128]{3,2,1,0:T(8,128)S(1)} %collective-permute-done.6, f32[2,40,136,136]{3,2,1,0:T(8,128)} %select_maximum_fusion, f32[2,40,132,128]{3,2,1,0:T(8,128)} %get-tuple-element.7, ...), kind=kLoop, calls=%fused_computation.55 | loop fusion | flops 42991616 | bytes 82837504 | tf_op jit(solution)/shard_map/add | solution.py:75
  281.3 5.3 %collective-permute-start.10 = (f32[2,32,32,128]{3,2,1,0:T(8,128)}, f32[2,32,32,128]{3,2,1,0:T(8,128)}, u32[]{:S(2)}, u32[]{:S(2)}) collective-permute-start(f32[2,32,32,128]{3,2,1,0:T(8,128)} %pad_maximum_fusion.9), channel_id=1, source_target_pairs={{0,2},{2,4},{4,6},{6,8},{8,10},{10,12},{12,14},{1,3},{3,5},{5,7},{... | collective-permute-start | bytes 3145736 | tf_op jit(solution)/shard_map/ppermute | solution.py:20
  290.8 4.5 %gather_fusion = f32[520,32,128]{2,1,0:T(8,128)} fusion(f32[96,32,128]{2,1,0:T(8,128)S(1)} %get-tuple-element.18, s32[1024]{0:T(1024)S(1)} %get-tuple-element.23), kind=kCustom, calls=%fused_computation.clone | custom fusion | bytes 17041440 | tf_op jit(solution)/shard_map/jit(_take)/gather | solution.py:53
  295.2 4.5 %gather_fusion.1 = f32[520,32,128]{2,1,0:T(8,128)} fusion(f32[96,32,128]{2,1,0:T(8,128)S(1)} %get-tuple-element.19, s32[1024]{0:T(1024)S(1)} %get-tuple-element.22), kind=kCustom, calls=%fused_computation.1.clone | custom fusion | bytes 17041440 | tf_op jit(solution)/shard_map/jit(_take)/gather | solution.py:54
  299.7 30.0 %collective-permute-done.10 = f32[2,32,32,128]{3,2,1,0:T(8,128)} collective-permute-done((f32[2,32,32,128]{3,2,1,0:T(8,128)}, f32[2,32,32,128]{3,2,1,0:T(8,128)}, u32[]{:S(2)}, u32[]{:S(2)}) %collective-permute-start.10) | collective-permute-done | bytes 1048608 | tf_op jit(solution)/shard_map/ppermute | solution.py:20
  331.9 4.5 %gather_fusion.2 = f32[520,32,128]{2,1,0:T(8,128)} fusion(f32[96,32,128]{2,1,0:T(8,128)S(1)} %get-tuple-element.20, s32[1024]{0:T(1024)S(1)} %get-tuple-element.23), kind=kCustom, calls=%fused_computation.2.clone | custom fusion | bytes 17041440 | tf_op jit(solution)/shard_map/jit(_take)/gather | solution.py:53
  336.4 4.5 %gather_fusion.3 = f32[520,32,128]{2,1,0:T(8,128)} fusion(f32[96,32,128]{2,1,0:T(8,128)S(1)} %get-tuple-element.21, s32[1024]{0:T(1024)S(1)} %get-tuple-element.22), kind=kCustom, calls=%fused_computation.3.clone | custom fusion | bytes 17041440 | tf_op jit(solution)/shard_map/jit(_take)/gather | solution.py:54
  340.9 15.4 %fusion.2 = f32[65,8,32,128]{3,2,1,0:T(8,128)} fusion(f32[1,65,8,32,128]{4,3,2,1,0:T(8,128)} %bitcast.17, f32[1,65,8,32,128]{4,3,2,1,0:T(8,128)} %bitcast.16, f32[1,65,8,32,128]{4,3,2,1,0:T(8,128)} %bitcast.15, f32[1,65,8,32,128]{4,3,2,1,0:T(8,128)} %bitcast.14, pred[65,8]{1,0:T(8,128)(4,1)S(1)} %copy.11, pred[65,8]{1,0:T(8,128)(4,1)S(1)} %copy.9), kind=kLoop, calls=%fused_computation.17 | loop fusion | flops 14909440 | bytes 42599440 | tf_op jit(solution)/shard_map/add | solution.py:78
  356.2 14.6 %copy.17 = f32[65,8,32,128]{0,2,1,3:T(8,128)} copy(f32[65,8,32,128]{3,2,1,0:T(8,128)} %fusion.2) | data formatting | bytes 17039360 | tf_op jit(solution)/shard_map/add | solution.py:78
  370.8 28.6 %reduce-scatter.2.cloned.1.call-done = f32[65,8,32,64]{0,2,1,3:T(8,128)} async-done(((f32[65,8,32,128]{0,2,1,3:T(8,128)}), f32[65,8,32,64]{0,2,1,3:T(8,128)}) %reduce-scatter.2.cloned.1.call-update) | async-done | bytes 4259856 | tf_op jit(solution)/shard_map/reduce_scatter | solution.py:79
  399.5 11.5 %copy.18 = f32[65,8,32,64]{0,3,2,1:T(8,128)} copy(f32[65,8,32,64]{0,2,1,3:T(8,128)} %reduce-scatter.2.cloned.1.call-done) | data formatting | bytes 8519680 | tf_op jit(solution)/shard_map/reduce_scatter | solution.py:79
  (67 shorter events, 40.8 us)
Async XLA Ops:
  6.5 2.2 copy-start.10
  6.5 392.9 %reduce-scatter.2.cloned.1.call-start = ((), (), s32[]{:S(2)}) async-start(), calls=%async_computation.1 | async-start | bytes 25165824 | tf_op jit(solution)/shard_map/reduce_scatter | solution.py:79
  9.0 28.3 %copy-start = (f32[2,32,128,128]{3,2,1,0:T(8,128)}, f32[2,32,128,128]{3,2,1,0:T(8,128)S(1)}, u32[]{:S(2)}) copy-start(f32[2,32,128,128]{3,2,1,0:T(8,128)S(1)} %constant_dynamic-update-slice_fusion) | copy-start | bytes 12582916
  9.0 16.8 %collective-permute-start.2 = (f32[2,4,128,128]{3,2,1,0:T(8,128)S(1)}, f32[2,4,128,128]{3,2,1,0:T(8,128)S(1)}, u32[]{:S(2)}, u32[]{:S(2)}) collective-permute-start(f32[2,4,128,128]{3,2,1,0:T(8,128)S(1)} %get-tuple-element.16), channel_id=1, source_target_pairs={{2,0},{4,2},{6,4},{8,6},{10,8},{12,10},{14,12},{3,1},{5,3},{7,5},{... | collective-permute-start | bytes 1572872 | tf_op jit(solution)/shard_map/ppermute | solution.py:21
  10.3 26.9 %collective-permute-start.3 = (f32[2,4,128,128]{3,2,1,0:T(8,128)S(1)}, f32[2,4,128,128]{3,2,1,0:T(8,128)S(1)}, u32[]{:S(2)}, u32[]{:S(2)}) collective-permute-start(f32[2,4,128,128]{3,2,1,0:T(8,128)S(1)} %get-tuple-element.17), channel_id=1, source_target_pairs={{0,2},{2,4},{4,6},{6,8},{8,10},{10,12},{12,14},{1,3},{3,5},{5,7},{... | collective-permute-start | bytes 1572872 | tf_op jit(solution)/shard_map/ppermute | solution.py:20
  38.0 12.6 %collective-permute-start.4 = (f32[2,40,4,128]{3,2,1,0:T(4,128)}, f32[2,40,4,128]{3,2,1,0:T(4,128)S(1)}, u32[]{:S(2)}, u32[]{:S(2)}) collective-permute-start(f32[2,40,4,128]{3,2,1,0:T(4,128)} %get-tuple-element.13), channel_id=1, source_target_pairs={{1,0},{3,2},{5,4},{7,6},{9,8},{11,10},{13,12},{15,14},{17,16},{19,... | collective-permute-start | bytes 491528 | tf_op jit(solution)/shard_map/ppermute | solution.py:21
  39.3 11.3 %collective-permute-start.5 = (f32[2,40,4,128]{3,2,1,0:T(4,128)}, f32[2,40,4,128]{3,2,1,0:T(4,128)S(1)}, u32[]{:S(2)}, u32[]{:S(2)}) collective-permute-start(f32[2,40,4,128]{3,2,1,0:T(4,128)} %get-tuple-element.12), channel_id=1, source_target_pairs={{0,1},{2,3},{4,5},{6,7},{8,9},{10,11},{12,13},{14,15},{16,17},{18,... | collective-permute-start | bytes 491528 | tf_op jit(solution)/shard_map/ppermute | solution.py:20
  50.6 7.9 %copy-start.1 = (f32[2,32,128,128]{3,2,1,0:T(8,128)S(1)}, f32[2,32,128,128]{3,2,1,0:T(8,128)}, u32[]{:S(2)}) copy-start(f32[2,32,128,128]{3,2,1,0:T(8,128)} %copy-done) | copy-start | bytes 12582916
  58.5 11.1 %copy-start.3 = (f32[32,128,128]{2,1,0:T(8,128)S(1)}, f32[32,128,128]{2,1,0:T(8,128)}, u32[]{:S(2)}) copy-start(f32[32,128,128]{2,1,0:T(8,128)} %param.11) | copy-start | bytes 6291460
  123.2 16.1 %collective-permute-start.6 = (f32[2,4,128,128]{3,2,1,0:T(8,128)}, f32[2,4,128,128]{3,2,1,0:T(8,128)S(1)}, u32[]{:S(2)}, u32[]{:S(2)}) collective-permute-start(f32[2,4,128,128]{3,2,1,0:T(8,128)} %get-tuple-element.14), channel_id=1, source_target_pairs={{2,0},{4,2},{6,4},{8,6},{10,8},{12,10},{14,12},{3,1},{5,3},{7,5},{... | collective-permute-start | bytes 1572872 | tf_op jit(solution)/shard_map/ppermute | solution.py:21
  124.5 48.9 %collective-permute-start.7 = (f32[2,4,128,128]{3,2,1,0:T(8,128)}, f32[2,4,128,128]{3,2,1,0:T(8,128)S(1)}, u32[]{:S(2)}, u32[]{:S(2)}) collective-permute-start(f32[2,4,128,128]{3,2,1,0:T(8,128)} %get-tuple-element.15), channel_id=1, source_target_pairs={{0,2},{2,4},{4,6},{6,8},{8,10},{10,12},{12,14},{1,3},{3,5},{5,7},{... | collective-permute-start | bytes 1572872 | tf_op jit(solution)/shard_map/ppermute | solution.py:20
  131.9 156.7 %collective-permute-start = (f32[2,32,32,128]{3,2,1,0:T(8,128)}, f32[2,32,32,128]{3,2,1,0:T(8,128)}, u32[]{:S(2)}, u32[]{:S(2)}) collective-permute-start(f32[2,32,32,128]{3,2,1,0:T(8,128)} %pad_maximum_fusion.8), channel_id=1, source_target_pairs={{0,2},{2,4},{4,6},{6,8},{8,10},{10,12},{12,14},{1,3},{3,5},{5,7},{... | collective-permute-start | bytes 3145736 | tf_op jit(solution)/shard_map/ppermute | solution.py:20
  137.6 150.9 %collective-permute-start.1 = (f32[2,32,32,128]{3,2,1,0:T(8,128)}, f32[2,32,32,128]{3,2,1,0:T(8,128)}, u32[]{:S(2)}, u32[]{:S(2)}) collective-permute-start(f32[2,32,32,128]{3,2,1,0:T(8,128)} %pad_maximum_fusion.8), channel_id=1, source_target_pairs={{2,0},{4,2},{6,4},{8,6},{10,8},{12,10},{14,12},{3,1},{5,3},{7,5},{... | collective-permute-start | bytes 3145736 | tf_op jit(solution)/shard_map/ppermute | solution.py:21
  175.3 8.1 %collective-permute-start.8 = (f32[2,40,4,128]{3,2,1,0:T(4,128)}, f32[2,40,4,128]{3,2,1,0:T(4,128)S(1)}, u32[]{:S(2)}, u32[]{:S(2)}) collective-permute-start(f32[2,40,4,128]{3,2,1,0:T(4,128)} %get-tuple-element.9), channel_id=1, source_target_pairs={{1,0},{3,2},{5,4},{7,6},{9,8},{11,10},{13,12},{15,14},{17,16},{19,... | collective-permute-start | bytes 491528 | tf_op jit(solution)/shard_map/ppermute | solution.py:21
  176.5 8.1 %collective-permute-start.9 = (f32[2,40,4,128]{3,2,1,0:T(4,128)}, f32[2,40,4,128]{3,2,1,0:T(4,128)S(1)}, u32[]{:S(2)}, u32[]{:S(2)}) collective-permute-start(f32[2,40,4,128]{3,2,1,0:T(4,128)} %get-tuple-element.8), channel_id=1, source_target_pairs={{0,1},{2,3},{4,5},{6,7},{8,9},{10,11},{12,13},{14,15},{16,17},{18,... | collective-permute-start | bytes 491528 | tf_op jit(solution)/shard_map/ppermute | solution.py:20
  181.6 11.0 %copy-start.2 = (f32[2,32,128,128]{3,2,1,0:T(8,128)S(1)}, f32[2,32,128,128]{3,2,1,0:T(8,128)}, u32[]{:S(2)}) copy-start(f32[2,32,128,128]{3,2,1,0:T(8,128)} %fusion.35) | copy-start | bytes 12582916
  273.4 15.2 %copy-start.4 = (f32[1,32,32,128]{3,2,1,0:T(8,128)S(1)}, f32[1,32,32,128]{3,2,1,0:T(8,128)}, u32[]{:S(2)}) copy-start(f32[1,32,32,128]{3,2,1,0:T(8,128)} %slice.272) | copy-start | bytes 1572868
  273.4 15.2 %copy-start.5 = (f32[1,32,32,128]{3,2,1,0:T(8,128)S(1)}, f32[1,32,32,128]{3,2,1,0:T(8,128)}, u32[]{:S(2)}) copy-start(f32[1,32,32,128]{3,2,1,0:T(8,128)} %slice.273) | copy-start | bytes 1572868
  276.8 11.8 %copy-start.6 = (f32[1,32,32,128]{3,2,1,0:T(8,128)}, f32[1,32,32,128]{3,2,1,0:T(8,128)S(1)}, u32[]{:S(2)}) copy-start(f32[1,32,32,128]{3,2,1,0:T(8,128)S(1)} %slice.332) | copy-start | bytes 1572868
  280.2 8.3 %copy-start.8 = (f32[1,32,32,128]{3,2,1,0:T(8,128)}, f32[1,32,32,128]{3,2,1,0:T(8,128)S(1)}, u32[]{:S(2)}) copy-start(f32[1,32,32,128]{3,2,1,0:T(8,128)S(1)} %slice.333) | copy-start | bytes 1572868
  281.3 48.4 %collective-permute-start.10 = (f32[2,32,32,128]{3,2,1,0:T(8,128)}, f32[2,32,32,128]{3,2,1,0:T(8,128)}, u32[]{:S(2)}, u32[]{:S(2)}) collective-permute-start(f32[2,32,32,128]{3,2,1,0:T(8,128)} %pad_maximum_fusion.9), channel_id=1, source_target_pairs={{0,2},{2,4},{4,6},{6,8},{8,10},{10,12},{12,14},{1,3},{3,5},{5,7},{... | collective-permute-start | bytes 3145736 | tf_op jit(solution)/shard_map/ppermute | solution.py:20
  286.6 43.1 %collective-permute-start.11 = (f32[2,32,32,128]{3,2,1,0:T(8,128)}, f32[2,32,32,128]{3,2,1,0:T(8,128)}, u32[]{:S(2)}, u32[]{:S(2)}) collective-permute-start(f32[2,32,32,128]{3,2,1,0:T(8,128)} %pad_maximum_fusion.9), channel_id=1, source_target_pairs={{2,0},{4,2},{6,4},{8,6},{10,8},{12,10},{14,12},{3,1},{5,3},{7,5},{... | collective-permute-start | bytes 3145736 | tf_op jit(solution)/shard_map/ppermute | solution.py:21
  295.2 34.5 %copy-start.7 = (f32[1,32,32,128]{3,2,1,0:T(8,128)S(1)}, f32[1,32,32,128]{3,2,1,0:T(8,128)}, u32[]{:S(2)}) copy-start(f32[1,32,32,128]{3,2,1,0:T(8,128)} %copy-done.6) | copy-start | bytes 1572868
  295.2 34.5 %copy-start.9 = (f32[1,32,32,128]{3,2,1,0:T(8,128)S(1)}, f32[1,32,32,128]{3,2,1,0:T(8,128)}, u32[]{:S(2)}) copy-start(f32[1,32,32,128]{3,2,1,0:T(8,128)} %copy-done.8) | copy-start | bytes 1572868
Sparse Core Ops, SparseCore 0:
  371.0 28.4 reduce-scatter.1
where the time goes:
time: 419 us; the launch traced here: 418 us
  other arithmetic  184 us (44%)
  waiting for transfers between devices  117 us (28%)
  local copies, waits for them, and re-layouts  63.6 us (15%)
  starting transfers between devices  38.8 us (9%)
  between operations  13.7 us (3%)
    add x2, other arithmetic, on_device(): 2.0 * fields - before + courant[None] * stencil_sum(advance_padded, fields)  121 us
    ppermute x6, waiting for transfers between devices, extended(): before = lax.ppermute(last, axis, up)  76.7 us
    concatenate x8, other arithmetic, extended(): array = jnp.concatenate([before, array, after], axis=dim)  44.2 us
    ppermute x6, starting transfers between devices, extended(): before = lax.ppermute(last, axis, up)  30.9 us
    reduce_scatter x1, waiting for transfers between devices, on_device(): lax.psum_scatter(image_sum, 'shot', scatter_dimension=3, tiled=True)  28.6 us
    add x1, other arithmetic, on_device(): image_sum = image_sum + image_step(fields)  15.4 us
    add x1, local copies, waits for them, and re-layouts, on_device(): image_sum = image_sum + image_step(fields)  14.6 us
    ppermute x6, waiting for transfers between devices, extended(): after = lax.ppermute(leading, axis, down)  11.9 us
  transfers between devices with their start and end apart: 13, of which 8 were waited for; matrix products, arithmetic and copies ran while one was open for 29% of the time, Pallas kernels for 0%

commit v1 on v0

v1 whole, which is shorter than its diff:
```python
import functools

import jax
import jax.numpy as jnp
from jax import lax
from jax.experimental import pallas as pl
from jax.experimental.pallas import tpu as pltpu
from jax.sharding import PartitionSpec as P

HALF = 32
REACH = 4
KEEP_EVERY = 4
OFFSETS = 2 * HALF + 1
OFFSETS_PER_STEP = 5
WEIGHTS = (-205.0 / 72.0, 8.0 / 5.0, -1.0 / 5.0, 8.0 / 315.0, -1.0 / 560.0)
PAD = 8
F32 = jnp.float32
HBM = pl.BlockSpec(memory_space=pl.ANY)
VMEM = pl.BlockSpec(memory_space=pltpu.VMEM)
SMEM = pl.BlockSpec(memory_space=pltpu.SMEM)


def params(mib):
    return pltpu.CompilerParams(vmem_limit_bytes=mib * 2**20)


def cost(flops, nbytes):
    return pl.CostEstimate(flops=flops, bytes_accessed=nbytes, transcendentals=0)


def run_copies(copies):
    for copy in copies:
        copy.start()
    for copy in copies:
        copy.wait()


def edge_kernel(source, receiver, up, down, sems):
    rows = source.shape[1]
    copies = []
    for field, ref in enumerate((source, receiver)):
        for out, start in ((up, rows - REACH), (down, 0)):
            copies.append(
                pltpu.make_async_copy(
                    ref.at[0, pl.ds(start, REACH)], out.at[field], sems.at[len(copies)]
                )
            )
    run_copies(copies)


def edges(source, receiver):
    _, _, size_y, size_z = source.shape
    shape = jax.ShapeDtypeStruct((2, REACH, size_y, size_z), F32)
    return pl.pallas_call(
        edge_kernel,
        out_shape=(shape, shape),
        in_specs=[HBM, HBM],
        out_specs=(HBM, HBM),
        scratch_shapes=[pltpu.SemaphoreType.DMA((4,))],
        cost_estimate=cost(0, 2 * 2**20),
        name="edges",
    )(source, receiver)


def z_halves(lines):
    count, size_z = lines.shape
    top, bottom = lines[: count // 2], lines[count // 2 :]
    low = lax.broadcasted_iota(jnp.int32, top.shape, 1) < size_z // 2
    first = jnp.where(low, top, pltpu.roll(bottom, size_z // 2, 1))
    second = jnp.where(low, pltpu.roll(top, size_z // 2, 1), bottom)
    return first, second


def pack_kernel(place, source, receiver, keep, give, side):
    shot, gy = place[0], place[1]
    rows, size_y, size_z = source.shape[1:]
    lines = size_y // KEEP_EVERY
    for row in range(rows):
        parts = []
        for field, ref in enumerate((source, receiver)):
            first, second = z_halves(ref[0, row, pl.ds(0, lines, stride=KEEP_EVERY), :])
            keep[field, row] = jnp.where(shot == 0, first, second)
            give[field, row] = jnp.where(shot == 0, second, first)
            low = ref[0, row, 0:REACH, :]
            high = ref[0, row, size_y - REACH : size_y, :]
            parts.append(jnp.where(gy == 0, high, low))
        side[row] = jnp.concatenate(parts, axis=0)


def pack(place, source, receiver):
    _, rows, size_y, size_z = source.shape
    lines = size_y // KEEP_EVERY // 2
    step = 4
    half = jax.ShapeDtypeStruct((2, rows, lines, size_z), F32)
    half_spec = pl.BlockSpec((2, step, lines, size_z), lambda i: (0, i, 0, 0))
    field_spec = pl.BlockSpec((1, step, size_y, size_z), lambda i: (0, i, 0, 0))
    return pl.pallas_call(
        pack_kernel,
        grid=(rows // step,),
        out_shape=(half, half, jax.ShapeDtypeStruct((rows, 2 * REACH, size_z), F32)),
        in_specs=[SMEM, field_spec, field_spec],
        out_specs=(
            half_spec,
            half_spec,
            pl.BlockSpec((step, 2 * REACH, size_z), lambda i: (i, 0, 0)),
        ),
        cost_estimate=cost(2**20, 7 * 2**20),
        name="pack",
    )(place, source, receiver)


def z_weights(size_z):
    z = lax.broadcasted_iota(jnp.int32, (8, size_z), 1)
    return [
        (jnp.where(z >= d, WEIGHTS[d], 0.0), jnp.where(z < size_z - d, WEIGHTS[d], 0.0))
        for d in range(1, REACH + 1)
    ]


def z_terms(center, masks):
    size_z = center.shape[1]
    total = None
    for d, (below, above) in enumerate(masks, start=1):
        term = below * pltpu.roll(center, d, 1) + above * pltpu.roll(center, size_z - d, 1)
        total = term if total is None else total + term
    return total


def step_kernel(
    place, source, receiver, source_before, receiver_before, courant, left, right, side,
    partial, kept_courant, up, down, side_out, now, before, scale, after, sems,
):
    gy = place[1]
    rows, size_y, size_z = courant.shape
    lines = size_y // KEEP_EVERY
    copies = []

    def copy(src, dst):
        copies.append(pltpu.make_async_copy(src, dst, sems.at[len(copies)]))

    middle = pl.ds(PAD, size_y)
    for field, ref in enumerate((source, receiver)):
        copy(ref.at[0], now.at[field, pl.ds(REACH, rows), middle])
    for field, ref in enumerate((source_before, receiver_before)):
        copy(ref.at[0], before.at[field])
    for field in range(2):
        copy(left.at[field], now.at[field, pl.ds(0, REACH), middle])
        copy(right.at[field], now.at[field, pl.ds(rows + REACH, REACH), middle])
    copy(courant, scale)
    for one in copies:
        one.start()

    blank = jnp.zeros((REACH, size_z), F32)
    for field in range(2):
        for row in list(range(REACH)) + list(range(rows + REACH, rows + 2 * REACH)):
            after[field, row] = jnp.zeros((size_y + 2 * PAD, size_z), F32)

    def fill(row, carry):
        for field in range(2):
            got = side[row, field * REACH : (field + 1) * REACH, :]
            now[field, row + REACH, PAD - REACH : PAD, :] = jnp.where(gy == 0, blank, got)
            now[field, row + REACH, size_y + PAD : size_y + PAD + REACH, :] = jnp.where(gy == 0, got, blank)
            after[field, row + REACH, PAD - REACH : PAD, :] = blank
            after[field, row + REACH, size_y + PAD : size_y + PAD + REACH, :] = blank
        return carry

    lax.fori_loop(0, rows, fill, 0)
    for one in copies:
        one.wait()

    masks = z_weights(size_z)

    def first(row, carry):
        for field in range(2):
            for chunk in range(size_y // 8):
                at = PAD + 8 * chunk
                center = now[field, row + REACH, at : at + 8, :]
                total = (3.0 * WEIGHTS[0]) * center + z_terms(center, masks)
                for d in range(1, REACH + 1):
                    around = (
                        now[field, row + REACH + d, at : at + 8, :]
                        + now[field, row + REACH - d, at : at + 8, :]
                        + now[field, row + REACH, at + d : at + d + 8, :]
                        + now[field, row + REACH, at - d : at - d + 8, :]
                    )
                    total = total + WEIGHTS[d] * around
                here = pl.ds(8 * chunk, 8)
                after[field, row + REACH, at : at + 8, :] = (
                    2.0 * center - before[field, row, here, :] + scale[row, here, :] * total
                )
        return carry

    lax.fori_loop(0, rows, first, 0)

    def second(row, carry):
        for chunk in range(lines // 8):
            at = PAD + 8 * KEEP_EVERY * chunk
            kept = lambda start: pl.ds(start, 8, stride=KEEP_EVERY)
            line = pl.ds(8 * chunk, 8)
            scaled = scale[row, kept(at - PAD), :]
            kept_courant[row, line, :] = scaled
            for field in range(2):
                center = after[field, row + REACH, kept(at), :]
                total = (3.0 * WEIGHTS[0]) * center + z_terms(center, masks)
                for d in range(1, REACH + 1):
                    around = (
                        after[field, row + REACH + d, kept(at), :]
                        + after[field, row + REACH - d, kept(at), :]
                        + after[field, row + REACH, kept(at + d), :]
                        + after[field, row + REACH, kept(at - d), :]
                    )
                    total = total + WEIGHTS[d] * around
                partial[field, row, line, :] = (
                    2.0 * center - now[field, row + REACH, kept(at), :] + scaled * total
                )
        for field in range(2):
            lowest = WEIGHTS[REACH] * after[field, row + REACH, PAD : PAD + 1, :]
            highest = sum(
                WEIGHTS[d] * after[field, row + REACH, PAD + size_y - d : PAD + size_y - d + 1, :]
                for d in range(1, REACH + 1)
            )
            side_out[field, pl.ds(row, 1), :] = jnp.where(gy == 0, highest, lowest)
        return carry

    lax.fori_loop(0, rows, second, 0)
    kept_lines = pl.ds(PAD, lines, stride=KEEP_EVERY)
    for field in range(2):
        for row in range(REACH):
            down[field, row] = after[field, REACH + row, kept_lines, :]
            up[field, row] = after[field, rows + row, kept_lines, :]


def steps(place, source, receiver, source_before, receiver_before, courant, left, right, side):
    rows, size_y, size_z = courant.shape
    lines = size_y // KEEP_EVERY
    halo = jax.ShapeDtypeStruct((2, REACH, lines, size_z), F32)
    return pl.pallas_call(
        step_kernel,
        out_shape=(
            jax.ShapeDtypeStruct((2, rows, lines, size_z), F32),
            jax.ShapeDtypeStruct((rows, lines, size_z), F32),
            halo,
            halo,
            jax.ShapeDtypeStruct((2, rows, size_z), F32),
        ),
        in_specs=[SMEM] + [HBM] * 7 + [VMEM],
        out_specs=(VMEM,) * 5,
        scratch_shapes=[
            pltpu.VMEM((2, rows + 2 * REACH, size_y + 2 * PAD, size_z), F32),
            pltpu.VMEM((2, rows, size_y, size_z), F32),
            pltpu.VMEM((rows, size_y, size_z), F32),
            pltpu.VMEM((2, rows + 2 * REACH, size_y + 2 * PAD, size_z), F32),
            pltpu.SemaphoreType.DMA((9,)),
        ],
        compiler_params=params(40),
        cost_estimate=cost(60 * 2**20, 14 * 2**20),
        name="steps",
    )(place, source, receiver, source_before, receiver_before, courant, left, right, side)


def finish_kernel(place, partial, kept_courant, left, right, side, keep, give):
    shot, gy = place[0], place[1]
    _, rows, lines, size_z = partial.shape
    line = lax.broadcasted_iota(jnp.int32, (lines, size_z), 0)
    meets = line == jnp.where(gy == 0, lines - 1, 0)

    def one_row(row, extra):
        scaled = kept_courant[row]
        for field in range(2):
            total = jnp.where(meets, side[field, pl.ds(row, 1), :], 0.0)
            for weight, values in extra[field]:
                total = total + weight * values
            first, second = z_halves(partial[field, row] + scaled * total)
            keep[field, row] = jnp.where(shot == 0, first, second)
            give[field, row] = jnp.where(shot == 0, second, first)

    def middle(row, carry):
        one_row(row, ((), ()))
        return carry

    lax.fori_loop(REACH, rows - REACH, middle, 0)
    for row in range(REACH):
        one_row(
            row,
            [[(WEIGHTS[d], left[f, REACH + row - d]) for d in range(row + 1, REACH + 1)] for f in range(2)],
        )
        one_row(
            rows - 1 - row,
            [[(WEIGHTS[d], right[f, d - 1 - row]) for d in range(row + 1, REACH + 1)] for f in range(2)],
        )


def finish(place, partial, kept_courant, left, right, side):
    _, rows, lines, size_z = partial.shape
    half = jax.ShapeDtypeStruct((2, rows, lines // 2, size_z), F32)
    return pl.pallas_call(
        finish_kernel,
        out_shape=(half, half),
        in_specs=[SMEM] + [VMEM] * 5,
        out_specs=(VMEM,) * 2,
        compiler_params=params(24),
        cost_estimate=cost(2**20, 3 * 2**20),
        name="finish",
    )(place, partial, kept_courant, left, right, side)


def image_kernel(count, place, *refs):
    blocks, (out, rows_of, sems) = refs[:count], refs[count:]
    parity = place[2]
    rows = blocks[0].shape[1]
    step = pl.program_id(0)

    @pl.when(step == 0)
    def _():
        copies = []
        for index, ref in enumerate(blocks):
            group, kind = index // 3, index % 3
            if kind == 0:
                start = HALF
            elif kind == 1:
                start = jnp.where(parity == 0, HALF + rows, 0)
            else:
                start = jnp.where(parity == 0, 0, HALF + rows)
            copies.append(
                pltpu.make_async_copy(ref, rows_of.at[group, :, pl.ds(start, rows)], sems.at[index])
            )
        run_copies(copies)

    groups = count // 3
    lines, size_z = rows_of.shape[3], rows_of.shape[4]
    for offset in range(OFFSETS_PER_STEP):
        shift = step * OFFSETS_PER_STEP + offset
        for sample in range(rows // 4):
            for chunk in range(lines // 8):
                here = pl.ds(8 * chunk, 8)
                total = None
                for group in range(groups):
                    term = (
                        rows_of[group, 0, 2 * HALF + 4 * sample - shift, here, :]
                        * rows_of[group, 1, 4 * sample + shift, here, :]
                    )
                    total = term if total is None else total + term
                other = pltpu.roll(total, size_z // 2, 1)
                out[offset, sample, 8 * chunk : 8 * chunk + 8, :] = total[:, : size_z // 2]
                out[offset, sample, lines + 8 * chunk : lines + 8 * chunk + 8, :] = other[:, : size_z // 2]


def image(place, blocks):
    _, rows, lines, size_z = blocks[0].shape
    samples = rows // 4
    return pl.pallas_call(
        functools.partial(image_kernel, len(blocks)),
        grid=(OFFSETS // OFFSETS_PER_STEP,),
        out_shape=jax.ShapeDtypeStruct((OFFSETS, samples, 2 * lines, size_z // 2), F32),
        in_specs=[SMEM] + [HBM] * len(blocks),
        out_specs=pl.BlockSpec((OFFSETS_PER_STEP, samples, 2 * lines, size_z // 2), lambda i: (i, 0, 0, 0)),
        scratch_shapes=[
            pltpu.VMEM((len(blocks) // 3, 2, rows + 2 * HALF, lines, size_z), F32),
            pltpu.SemaphoreType.DMA((len(blocks),)),
        ],
        compiler_params=params(24),
        cost_estimate=cost(16 * 2**20, 16 * 2**20),
        name="image",
    )(place, *blocks)


def on_device(source_now, source_before, receiver_now, receiver_before, courant):
    size = lax.axis_size("gx")
    place = jnp.stack(
        [lax.axis_index("shot"), lax.axis_index("gy"), lax.axis_index("gx") % 2]
    ).astype(jnp.int32)
    up_pairs = [(i, i + 1) for i in range(size - 1)]
    down_pairs = [(j, i) for i, j in up_pairs]
    partner = [(i, i ^ 1) for i in range(size)]
    onward = [(i, i + 2) for i in range(0, size - 2, 2)] + [(i, i - 2) for i in range(3, size, 2)]
    both = [(0, 1), (1, 0)]

    def spread(keep, give):
        other = lax.ppermute(give, "shot", both)
        near = [lax.ppermute(part, "gx", partner) for part in (keep, other)]
        far = [lax.ppermute(part, "gx", onward) for part in near]
        return [keep, near[0], far[0], other, near[1], far[1]]

    up, down = edges(source_now, receiver_now)
    keep, give, side = pack(place, source_now, receiver_now)
    left = lax.ppermute(up, "gx", up_pairs)
    right = lax.ppermute(down, "gx", down_pairs)
    side = lax.ppermute(side, "gy", both)
    left, right, keep, give = lax.optimization_barrier((left, right, keep, give))
    blocks = spread(keep, give)
    partial, kept_courant, up, down, side = steps(
        place, source_now, receiver_now, source_before, receiver_before, courant, left, right, side
    )
    left = lax.ppermute(up, "gx", up_pairs)
    right = lax.ppermute(down, "gx", down_pairs)
    side = lax.ppermute(side, "gy", both)
    keep, give = finish(place, partial, kept_courant, left, right, side)
    blocks += spread(keep, give)
    return image(place, blocks)


def solution(mesh):
    in_specs = (
        P("shot", "gx", "gy", None),
        P("shot", "gx", "gy", None),
        P("shot", "gx", "gy", None),
        P("shot", "gx", "gy", None),
        P("gx", "gy", None),
    )
    out_specs = P(None, "gx", "gy", "shot")
    return jax.shard_map(
        on_device, mesh=mesh, in_specs=in_specs, out_specs=out_specs, check_vma=False
    )
```

time: 419 us -> 182 us (0.43)
  other arithmetic: 184 us -> 0.6 us
  Pallas kernels: 0 us -> 64.3 us
  waiting for transfers between devices: 117 us -> 62.2 us
  local copies, waits for them, and re-layouts: 63.6 us -> 20.2 us
  between operations: 13.7 us -> 0.19 us
  starting transfers between devices: 38.8 us -> 33.9 us
    add x4 -> x0, other arithmetic: 137 us -> none  [the longest x2 121 us: on_device(): 2.0 * fields - before + courant[None] * stencil_sum(advance_padded, fields)]
    pallas_call x0 -> x5, Pallas kernels: none -> 64.3 us  [the longest x1 32.9 us: edges(): pl.pallas_call(edge_kernel, out_shape=(shape, shape), in_specs=[HBM, HBM]...]
    concatenate x10 -> x0, other arithmetic: 47.5 us -> none  [the longest x8 44.2 us: extended(): array = jnp.concatenate([before, array, after], axis=dim)]
    reduce_scatter x1 -> x0, waiting for transfers between devices: 28.6 us -> none  [on_device(): lax.psum_scatter(image_sum, 'shot', scatter_dimension=3, tiled=True)]
    ppermute x12 -> x16, waiting for transfers between devices: 88.7 us -> 62.2 us  [the longest x4 33.3 us: spread(): near = [lax.ppermute(part, 'gx', partner) for part in (keep, other)]]
    gather x4 -> x0, local copies, waits for them, and re-layouts: 17.9 us -> none  [the longest x2 8.97 us: correlate(): source_rows = jnp.take(padded[:shot_count], source_index, axis=1)]
    slice x6 -> x0, local copies, waits for them, and re-layouts: 15.9 us -> none  [the longest x2 7.22 us: image_step(): source_part = current[:shot_count, :, ::4, :]]
    add x1 -> x0, local copies, waits for them, and re-layouts: 14.6 us -> none  [on_device(): image_sum = image_sum + image_step(fields)]
  transfers between devices with their start and end apart: 13 -> 16, of which waited for: 8 -> 8; matrix products, arithmetic and copies ran while one was open for 29% -> 0% of each run, Pallas kernels for 0% -> 5%
where the time goes in v1:
time: 182 us; the launch traced here: 181 us
  Pallas kernels  64.3 us (35%)
  waiting for transfers between devices  62.2 us (34%)
  starting transfers between devices  33.9 us (19%)
  local copies, waits for them, and re-layouts  20.2 us (11%)
    ppermute x4, waiting for transfers between devices, spread(): near = [lax.ppermute(part, 'gx', partner) for part in (keep, other)]  33.3 us
    pallas_call x1, Pallas kernels, edges(): pl.pallas_call(edge_kernel, out_shape=(shape, shape), in_specs=[HBM, HBM]...  32.9 us
    pallas_call x1, Pallas kernels, steps(): pl.pallas_call(step_kernel, out_shape=(jax.ShapeDtypeStruct((2, rows, lin...  17.8 us
    ppermute x4, starting transfers between devices, spread(): far = [lax.ppermute(part, 'gx', onward) for part in near]  14.2 us
    ppermute x2, waiting for transfers between devices, on_device(): left = lax.ppermute(up, 'gx', up_pairs)  13 us
    ppermute x4, waiting for transfers between devices, spread(): far = [lax.ppermute(part, 'gx', onward) for part in near]  11 us
    pallas_call x1, local copies, waits for them, and re-layouts, image(): pl.pallas_call(functools.partial(image_kernel, len(blocks)), grid=(OFFSET...  10.6 us
    unnamed x18, local copies, waits for them, and re-layouts  9.69 us
  transfers between devices with their start and end apart: 16, of which 8 were waited for; matrix products, arithmetic and copies ran while one was open for 0% of the time, Pallas kernels for 5%

profile of v1, /device:TPU:0, one launch (start us, length us, event | category | flops | bytes accessed | tf_op | source)
XLA Modules:
  0.0 181.5 jit_solution(11210428008391023150)
XLA Ops:
  0.0 32.9 %edges.1 = (f32[2,4,128,128]{3,2,1,0:T(8,128)}, f32[2,4,128,128]{3,2,1,0:T(8,128)}) custom-call(f32[1,32,128,128]{3,2,1,0:T(8,128)} %source.5, f32[1,32,128,128]{3,2,1,0:T(8,128)} %receiver.5), custom_call_target="tpu_custom_call" | custom-call | bytes 2097152 | tf_op jit(solution)/shard_map/edges/pallas_call | solution.py:54
  32.9 4.9 %collective-permute-start = (f32[2,4,128,128]{3,2,1,0:T(8,128)}, f32[2,4,128,128]{3,2,1,0:T(8,128)S(1)}, u32[]{:S(2)}, u32[]{:S(2)}) collective-permute-start(f32[2,4,128,128]{3,2,1,0:T(8,128)} %get-tuple-element.21), channel_id=1, source_target_pairs={{0,2},{2,4},{4,6},{6,8},{8,10},{10,12},{12,14},{1,3},{3,5},{5,7},{... | collective-permute-start | bytes 1572872 | tf_op jit(solution)/shard_map/ppermute | solution.py:386
  39.7 6.3 %pack.1 = (f32[2,32,16,128]{3,2,1,0:T(8,128)}, f32[2,32,16,128]{3,2,1,0:T(8,128)}, f32[32,8,128]{2,1,0:T(8,128)}) custom-call(s32[3]{0:T(128)} %pad_add_fusion.place, f32[1,32,128,128]{3,2,1,0:T(8,128)} %source.5, f32[1,32,128,128]{3,2,1,0:T(8,128)} %receiver.5), custom_call_target="tpu_custom_call" | custom-call | flops 1048576 | bytes 7340032 | tf_op jit(solution)/shard_map/pack/pallas_call | solution.py:97
  47.5 13.0 %collective-permute-done.left = f32[2,4,128,128]{3,2,1,0:T(8,128)S(1)} collective-permute-done((f32[2,4,128,128]{3,2,1,0:T(8,128)}, f32[2,4,128,128]{3,2,1,0:T(8,128)S(1)}, u32[]{:S(2)}, u32[]{:S(2)}) %collective-permute-start) | collective-permute-done | bytes 524320 | tf_op jit(solution)/shard_map/ppermute | solution.py:386
  62.1 1.6 copy-done.3
  66.9 17.8 %steps.1 = (f32[2,32,32,128]{3,2,1,0:T(8,128)S(1)}, f32[32,32,128]{2,1,0:T(8,128)S(1)}, f32[2,4,32,128]{3,2,1,0:T(8,128)S(1)}, f32[2,4,32,128]{3,2,1,0:T(8,128)S(1)}, f32[2,32,128]{2,1,0:T(8,128)S(1)}) custom-call(s32[3]{0:T(128)S(1)} %copy-done.7, f32[1,32,128,128]{3,2,1,0:T(8,128)S(1)} %copy-done.1, f32[1,32,128,128]{3,2,1,0:T(8,128)S(1)} %copy-done.2, ...), custom_call_target="tpu_custom_call" | custom-call | flops 62914560 | bytes 14680064 | tf_op jit(solution)/shard_map/steps/pallas_call | solution.py:237
  84.7 4.3 %collective-permute-start.8 = (f32[2,4,32,128]{3,2,1,0:T(8,128)S(1)}, f32[2,4,32,128]{3,2,1,0:T(8,128)S(1)}, u32[]{:S(2)}, u32[]{:S(2)}) collective-permute-start(f32[2,4,32,128]{3,2,1,0:T(8,128)S(1)} %get-tuple-element.32), channel_id=1, source_target_pairs={{0,2},{2,4},{4,6},{6,8},{8,10},{10,12},{12,14},{1,3},{3,5},{5,7},{... | collective-permute-start | bytes 393224 | tf_op jit(solution)/shard_map/ppermute | solution.py:394
  91.9 2.4 %collective-permute-done.10.side = f32[2,32,128]{2,1,0:T(8,128)S(1)} collective-permute-done((f32[2,32,128]{2,1,0:T(8,128)S(1)}, f32[2,32,128]{2,1,0:T(8,128)S(1)}, u32[]{:S(2)}, u32[]{:S(2)}) %collective-permute-start.10) | collective-permute-done | bytes 32800 | tf_op jit(solution)/shard_map/ppermute | solution.py:396
  94.3 2.4 %collective-permute-done.9.right = f32[2,4,32,128]{3,2,1,0:T(8,128)S(1)} collective-permute-done((f32[2,4,32,128]{3,2,1,0:T(8,128)S(1)}, f32[2,4,32,128]{3,2,1,0:T(8,128)S(1)}, u32[]{:S(2)}, u32[]{:S(2)}) %collective-permute-start.9) | collective-permute-done | bytes 131104 | tf_op jit(solution)/shard_map/ppermute | solution.py:395
  96.7 2.6 %finish.1 = (f32[2,32,16,128]{3,2,1,0:T(8,128)S(1)}, f32[2,32,16,128]{3,2,1,0:T(8,128)S(1)}) custom-call(s32[3]{0:T(128)S(1)} %copy-done.7, f32[2,32,32,128]{3,2,1,0:T(8,128)S(1)} %get-tuple-element.30.partial, f32[32,32,128]{2,1,0:T(8,128)S(1)} %get-tuple-element.31.kept_courant, f32[2,4,32,128]{3,2,1,0:T(8,128)S(1)} %collective-permute-done.8.left, ...), custom_call_target="tpu_custom_call" | custom-call | flops 1048576 | bytes 3145728 | tf_op jit(solution)/shard_map/finish/pallas_call | solution.py:296
  99.4 2.7 %collective-permute-start.2 = (f32[2,32,16,128]{3,2,1,0:T(8,128)S(1)}, f32[2,32,16,128]{3,2,1,0:T(8,128)S(1)}, u32[]{:S(2)}, u32[]{:S(2)}) collective-permute-start(f32[2,32,16,128]{3,2,1,0:T(8,128)S(1)} %copy-done.6), channel_id=1, source_target_pairs={{0,2},{2,0},{4,6},{6,4},{8,10},{10,8},{12,14},{14,12},{1,3},{3,1},... | collective-permute-start | bytes 1572872 | tf_op jit(solution)/shard_map/ppermute | solution.py:380
  102.2 1.9 %collective-permute-start.5 = (f32[2,32,16,128]{3,2,1,0:T(8,128)S(1)}, f32[2,32,16,128]{3,2,1,0:T(8,128)S(1)}, u32[]{:S(2)}, u32[]{:S(2)}) collective-permute-start(f32[2,32,16,128]{3,2,1,0:T(8,128)S(1)} %collective-permute-done.4.refs_3_), channel_id=1, source_target_pairs={{0,2},{2,0},{4,6},{6,4},{8,10},{10,8},{12,14},{14,12},{1,3},{3,1},... | collective-permute-start | bytes 1572872 | tf_op jit(solution)/shard_map/ppermute | solution.py:380
  104.2 10.6 %collective-permute-done.2.refs_1_ = f32[2,32,16,128]{3,2,1,0:T(8,128)S(1)} collective-permute-done((f32[2,32,16,128]{3,2,1,0:T(8,128)S(1)}, f32[2,32,16,128]{3,2,1,0:T(8,128)S(1)}, u32[]{:S(2)}, u32[]{:S(2)}) %collective-permute-start.2) | collective-permute-done | bytes 524320 | tf_op jit(solution)/shard_map/ppermute | solution.py:380
  114.9 3.6 %collective-permute-start.3 = (f32[2,32,16,128]{3,2,1,0:T(8,128)S(1)}, f32[2,32,16,128]{3,2,1,0:T(8,128)S(1)}, u32[]{:S(2)}, u32[]{:S(2)}) collective-permute-start(f32[2,32,16,128]{3,2,1,0:T(8,128)S(1)} %collective-permute-done.2.refs_1_), channel_id=1, source_target_pairs={{0,4},{4,8},{8,12},{6,2},{10,6},{14,10},{1,5},{5,9},{9,13},{7,3},{... | collective-permute-start | bytes 1572872 | tf_op jit(solution)/shard_map/ppermute | solution.py:381
  118.5 7.6 %collective-permute-done.11.refs_7_ = f32[2,32,16,128]{3,2,1,0:T(8,128)S(1)} collective-permute-done((f32[2,32,16,128]{3,2,1,0:T(8,128)S(1)}, f32[2,32,16,128]{3,2,1,0:T(8,128)S(1)}, u32[]{:S(2)}, u32[]{:S(2)}) %collective-permute-start.11) | collective-permute-done | bytes 524320 | tf_op jit(solution)/shard_map/ppermute | solution.py:380
  126.1 3.6 %collective-permute-start.12 = (f32[2,32,16,128]{3,2,1,0:T(8,128)S(1)}, f32[2,32,16,128]{3,2,1,0:T(8,128)S(1)}, u32[]{:S(2)}, u32[]{:S(2)}) collective-permute-start(f32[2,32,16,128]{3,2,1,0:T(8,128)S(1)} %collective-permute-done.11.refs_7_), channel_id=1, source_target_pairs={{0,4},{4,8},{8,12},{6,2},{10,6},{14,10},{1,5},{5,9},{9,13},{7,3},{... | collective-permute-start | bytes 1572872 | tf_op jit(solution)/shard_map/ppermute | solution.py:381
  129.7 7.6 %collective-permute-done.5.refs_4_ = f32[2,32,16,128]{3,2,1,0:T(8,128)S(1)} collective-permute-done((f32[2,32,16,128]{3,2,1,0:T(8,128)S(1)}, f32[2,32,16,128]{3,2,1,0:T(8,128)S(1)}, u32[]{:S(2)}, u32[]{:S(2)}) %collective-permute-start.5) | collective-permute-done | bytes 524320 | tf_op jit(solution)/shard_map/ppermute | solution.py:380
  137.3 3.6 %collective-permute-start.6 = (f32[2,32,16,128]{3,2,1,0:T(8,128)S(1)}, f32[2,32,16,128]{3,2,1,0:T(8,128)S(1)}, u32[]{:S(2)}, u32[]{:S(2)}) collective-permute-start(f32[2,32,16,128]{3,2,1,0:T(8,128)S(1)} %collective-permute-done.5.refs_4_), channel_id=1, source_target_pairs={{0,4},{4,8},{8,12},{6,2},{10,6},{14,10},{1,5},{5,9},{9,13},{7,3},{... | collective-permute-start | bytes 1572872 | tf_op jit(solution)/shard_map/ppermute | solution.py:381
  140.9 7.4 %collective-permute-done.14.refs_10_ = f32[2,32,16,128]{3,2,1,0:T(8,128)S(1)} collective-permute-done((f32[2,32,16,128]{3,2,1,0:T(8,128)S(1)}, f32[2,32,16,128]{3,2,1,0:T(8,128)S(1)}, u32[]{:S(2)}, u32[]{:S(2)}) %collective-permute-start.14) | collective-permute-done | bytes 524320 | tf_op jit(solution)/shard_map/ppermute | solution.py:380
  148.3 3.5 %collective-permute-start.15 = (f32[2,32,16,128]{3,2,1,0:T(8,128)S(1)}, f32[2,32,16,128]{3,2,1,0:T(8,128)S(1)}, u32[]{:S(2)}, u32[]{:S(2)}) collective-permute-start(f32[2,32,16,128]{3,2,1,0:T(8,128)S(1)} %collective-permute-done.14.refs_10_), channel_id=1, source_target_pairs={{0,4},{4,8},{8,12},{6,2},{10,6},{14,10},{1,5},{5,9},{9,13},{7,3},{... | collective-permute-start | bytes 1572872 | tf_op jit(solution)/shard_map/ppermute | solution.py:381
  151.9 11.0 %collective-permute-done.15.refs_11_ = f32[2,32,16,128]{3,2,1,0:T(8,128)S(1)} collective-permute-done((f32[2,32,16,128]{3,2,1,0:T(8,128)S(1)}, f32[2,32,16,128]{3,2,1,0:T(8,128)S(1)}, u32[]{:S(2)}, u32[]{:S(2)}) %collective-permute-start.15) | collective-permute-done | bytes 524320 | tf_op jit(solution)/shard_map/ppermute | solution.py:381
  162.9 4.7 %image.1 = f32[65,8,32,64]{3,2,1,0:T(8,128)S(1)} custom-call(s32[3]{0:T(128)S(1)} %copy-done.7, f32[2,32,16,128]{3,2,1,0:T(8,128)S(1)} %copy-done.6, f32[2,32,16,128]{3,2,1,0:T(8,128)S(1)} %collective-permute-done.2.refs_1_, f32[2,32,16,128]{3,2,1,0:T(8,128)S(1)} %collective-permute-done.3.refs_2_, f32[2,32,16,128]{3,2,1,0:T(8,128)S(1)} %collective-permute-done.4.refs_3_, ...), custom_call_target="tpu_custom_call" | custom-call | flops 16777216 | bytes 16777216 | tf_op jit(solution)/shard_map/image/pallas_call | solution.py:351
  167.6 3.3 %copy-done = f32[65,8,32,64]{3,2,1,0:T(8,128)} copy-done((f32[65,8,32,64]{3,2,1,0:T(8,128)}, f32[65,8,32,64]{3,2,1,0:T(8,128)S(1)}, u32[]{:S(2)}) %copy-start) | copy-done | bytes 4259864
  170.9 10.6 %copy.6 = f32[65,8,32,64]{0,3,2,1:T(8,128)} copy(f32[65,8,32,64]{3,2,1,0:T(8,128)} %copy-done) | data formatting | bytes 8519680 | tf_op jit(solution)/shard_map/image/pallas_call | solution.py:351
  (33 shorter events, 11.3 us)
Async XLA Ops:
  32.9 27.6 %collective-permute-start = (f32[2,4,128,128]{3,2,1,0:T(8,128)}, f32[2,4,128,128]{3,2,1,0:T(8,128)S(1)}, u32[]{:S(2)}, u32[]{:S(2)}) collective-permute-start(f32[2,4,128,128]{3,2,1,0:T(8,128)} %get-tuple-element.21), channel_id=1, source_target_pairs={{0,2},{2,4},{4,6},{6,8},{8,10},{10,12},{12,14},{1,3},{3,5},{5,7},{... | collective-permute-start | bytes 1572872 | tf_op jit(solution)/shard_map/ppermute | solution.py:386
  37.8 22.7 %collective-permute-start.1 = (f32[2,4,128,128]{3,2,1,0:T(8,128)}, f32[2,4,128,128]{3,2,1,0:T(8,128)S(1)}, u32[]{:S(2)}, u32[]{:S(2)}) collective-permute-start(f32[2,4,128,128]{3,2,1,0:T(8,128)} %get-tuple-element.22), channel_id=1, source_target_pairs={{2,0},{4,2},{6,4},{8,6},{10,8},{12,10},{14,12},{3,1},{5,3},{7,5},{... | collective-permute-start | bytes 1572872 | tf_op jit(solution)/shard_map/ppermute | solution.py:387
  39.7 20.8 %copy-start.1 = (f32[1,32,128,128]{3,2,1,0:T(8,128)S(1)}, f32[1,32,128,128]{3,2,1,0:T(8,128)}, u32[]{:S(2)}) copy-start(f32[1,32,128,128]{3,2,1,0:T(8,128)} %source.5) | copy-start | bytes 6291460
  39.7 20.8 %copy-start.7 = (s32[3]{0:T(128)S(1)}, s32[3]{0:T(128)}, u32[]{:S(2)}) copy-start(s32[3]{0:T(128)} %pad_add_fusion.place) | copy-start | bytes 40
  46.0 14.5 %collective-permute-start.7 = (f32[32,8,128]{2,1,0:T(8,128)}, f32[32,8,128]{2,1,0:T(8,128)S(1)}, u32[]{:S(2)}, u32[]{:S(2)}) collective-permute-start(f32[32,8,128]{2,1,0:T(8,128)} %get-tuple-element.29), channel_id=1, source_target_pairs={{0,1},{1,0},{2,3},{3,2},{4,5},{5,4},{6,7},{7,6},{8,9},{9,8},{10,11... | collective-permute-start | bytes 393224 | tf_op jit(solution)/shard_map/ppermute | solution.py:388
  60.5 1.6 copy-start.2
  62.1 1.6 copy-start.3
  63.7 1.6 copy-start.4
  66.9 25.0 %copy-start.8 = (f32[2,32,16,128]{3,2,1,0:T(8,128)S(1)}, f32[2,32,16,128]{3,2,1,0:T(8,128)}, u32[]{:S(2)}) copy-start(f32[2,32,16,128]{3,2,1,0:T(8,128)} %get-tuple-element.26) | copy-start | bytes 1572868
  66.9 32.5 %copy-start.6 = (f32[2,32,16,128]{3,2,1,0:T(8,128)S(1)}, f32[2,32,16,128]{3,2,1,0:T(8,128)}, u32[]{:S(2)}) copy-start(f32[2,32,16,128]{3,2,1,0:T(8,128)} %get-tuple-element.25.refs_0_) | copy-start | bytes 1572868
  84.7 9.6 %collective-permute-start.8 = (f32[2,4,32,128]{3,2,1,0:T(8,128)S(1)}, f32[2,4,32,128]{3,2,1,0:T(8,128)S(1)}, u32[]{:S(2)}, u32[]{:S(2)}) collective-permute-start(f32[2,4,32,128]{3,2,1,0:T(8,128)S(1)} %get-tuple-element.32), channel_id=1, source_target_pairs={{0,2},{2,4},{4,6},{6,8},{8,10},{10,12},{12,14},{1,3},{3,5},{5,7},{... | collective-permute-start | bytes 393224 | tf_op jit(solution)/shard_map/ppermute | solution.py:394
  89.0 7.7 %collective-permute-start.9 = (f32[2,4,32,128]{3,2,1,0:T(8,128)S(1)}, f32[2,4,32,128]{3,2,1,0:T(8,128)S(1)}, u32[]{:S(2)}, u32[]{:S(2)}) collective-permute-start(f32[2,4,32,128]{3,2,1,0:T(8,128)S(1)} %get-tuple-element.33), channel_id=1, source_target_pairs={{2,0},{4,2},{6,4},{8,6},{10,8},{12,10},{14,12},{3,1},{5,3},{7,5},{... | collective-permute-start | bytes 393224 | tf_op jit(solution)/shard_map/ppermute | solution.py:395
  90.3 4.0 %collective-permute-start.10 = (f32[2,32,128]{2,1,0:T(8,128)S(1)}, f32[2,32,128]{2,1,0:T(8,128)S(1)}, u32[]{:S(2)}, u32[]{:S(2)}) collective-permute-start(f32[2,32,128]{2,1,0:T(8,128)S(1)} %get-tuple-element.34), channel_id=1, source_target_pairs={{0,1},{1,0},{2,3},{3,2},{4,5},{5,4},{6,7},{7,6},{8,9},{9,8},{10,11... | collective-permute-start | bytes 98312 | tf_op jit(solution)/shard_map/ppermute | solution.py:396
  91.9 10.3 %collective-permute-start.4 = (f32[2,32,16,128]{3,2,1,0:T(8,128)S(1)}, f32[2,32,16,128]{3,2,1,0:T(8,128)S(1)}, u32[]{:S(2)}, u32[]{:S(2)}) collective-permute-start(f32[2,32,16,128]{3,2,1,0:T(8,128)S(1)} %copy-done.8), channel_id=1, source_target_pairs={{0,16},{16,0},{1,17},{17,1},{2,18},{18,2},{3,19},{19,3},{4,20},{20... | collective-permute-start | bytes 1572872 | tf_op jit(solution)/shard_map/ppermute | solution.py:379
  99.3 4.8 %collective-permute-start.13 = (f32[2,32,16,128]{3,2,1,0:T(8,128)S(1)}, f32[2,32,16,128]{3,2,1,0:T(8,128)S(1)}, u32[]{:S(2)}, u32[]{:S(2)}) collective-permute-start(f32[2,32,16,128]{3,2,1,0:T(8,128)S(1)} %get-tuple-element.36), channel_id=1, source_target_pairs={{0,16},{16,0},{1,17},{17,1},{2,18},{18,2},{3,19},{19,3},{4,20},{20... | collective-permute-start | bytes 1572872 | tf_op jit(solution)/shard_map/ppermute | solution.py:379
  99.4 15.5 %collective-permute-start.2 = (f32[2,32,16,128]{3,2,1,0:T(8,128)S(1)}, f32[2,32,16,128]{3,2,1,0:T(8,128)S(1)}, u32[]{:S(2)}, u32[]{:S(2)}) collective-permute-start(f32[2,32,16,128]{3,2,1,0:T(8,128)S(1)} %copy-done.6), channel_id=1, source_target_pairs={{0,2},{2,0},{4,6},{6,4},{8,10},{10,8},{12,14},{14,12},{1,3},{3,1},... | collective-permute-start | bytes 1572872 | tf_op jit(solution)/shard_map/ppermute | solution.py:380
  102.1 24.0 %collective-permute-start.11 = (f32[2,32,16,128]{3,2,1,0:T(8,128)S(1)}, f32[2,32,16,128]{3,2,1,0:T(8,128)S(1)}, u32[]{:S(2)}, u32[]{:S(2)}) collective-permute-start(f32[2,32,16,128]{3,2,1,0:T(8,128)S(1)} %get-tuple-element.35.refs_6_), channel_id=1, source_target_pairs={{0,2},{2,0},{4,6},{6,4},{8,10},{10,8},{12,14},{14,12},{1,3},{3,1},... | collective-permute-start | bytes 1572872 | tf_op jit(solution)/shard_map/ppermute | solution.py:380
  102.2 35.1 %collective-permute-start.5 = (f32[2,32,16,128]{3,2,1,0:T(8,128)S(1)}, f32[2,32,16,128]{3,2,1,0:T(8,128)S(1)}, u32[]{:S(2)}, u32[]{:S(2)}) collective-permute-start(f32[2,32,16,128]{3,2,1,0:T(8,128)S(1)} %collective-permute-done.4.refs_3_), channel_id=1, source_target_pairs={{0,2},{2,0},{4,6},{6,4},{8,10},{10,8},{12,14},{14,12},{1,3},{3,1},... | collective-permute-start | bytes 1572872 | tf_op jit(solution)/shard_map/ppermute | solution.py:380
  104.1 44.2 %collective-permute-start.14 = (f32[2,32,16,128]{3,2,1,0:T(8,128)S(1)}, f32[2,32,16,128]{3,2,1,0:T(8,128)S(1)}, u32[]{:S(2)}, u32[]{:S(2)}) collective-permute-start(f32[2,32,16,128]{3,2,1,0:T(8,128)S(1)} %collective-permute-done.13.refs_9_), channel_id=1, source_target_pairs={{0,2},{2,0},{4,6},{6,4},{8,10},{10,8},{12,14},{14,12},{1,3},{3,1},... | collective-permute-start | bytes 1572872 | tf_op jit(solution)/shard_map/ppermute | solution.py:380
  114.9 37.0 %collective-permute-start.3 = (f32[2,32,16,128]{3,2,1,0:T(8,128)S(1)}, f32[2,32,16,128]{3,2,1,0:T(8,128)S(1)}, u32[]{:S(2)}, u32[]{:S(2)}) collective-permute-start(f32[2,32,16,128]{3,2,1,0:T(8,128)S(1)} %collective-permute-done.2.refs_1_), channel_id=1, source_target_pairs={{0,4},{4,8},{8,12},{6,2},{10,6},{14,10},{1,5},{5,9},{9,13},{7,3},{... | collective-permute-start | bytes 1572872 | tf_op jit(solution)/shard_map/ppermute | solution.py:381
  126.1 25.7 %collective-permute-start.12 = (f32[2,32,16,128]{3,2,1,0:T(8,128)S(1)}, f32[2,32,16,128]{3,2,1,0:T(8,128)S(1)}, u32[]{:S(2)}, u32[]{:S(2)}) collective-permute-start(f32[2,32,16,128]{3,2,1,0:T(8,128)S(1)} %collective-permute-done.11.refs_7_), channel_id=1, source_target_pairs={{0,4},{4,8},{8,12},{6,2},{10,6},{14,10},{1,5},{5,9},{9,13},{7,3},{... | collective-permute-start | bytes 1572872 | tf_op jit(solution)/shard_map/ppermute | solution.py:381
  137.3 14.5 %collective-permute-start.6 = (f32[2,32,16,128]{3,2,1,0:T(8,128)S(1)}, f32[2,32,16,128]{3,2,1,0:T(8,128)S(1)}, u32[]{:S(2)}, u32[]{:S(2)}) collective-permute-start(f32[2,32,16,128]{3,2,1,0:T(8,128)S(1)} %collective-permute-done.5.refs_4_), channel_id=1, source_target_pairs={{0,4},{4,8},{8,12},{6,2},{10,6},{14,10},{1,5},{5,9},{9,13},{7,3},{... | collective-permute-start | bytes 1572872 | tf_op jit(solution)/shard_map/ppermute | solution.py:381
  148.3 14.6 %collective-permute-start.15 = (f32[2,32,16,128]{3,2,1,0:T(8,128)S(1)}, f32[2,32,16,128]{3,2,1,0:T(8,128)S(1)}, u32[]{:S(2)}, u32[]{:S(2)}) collective-permute-start(f32[2,32,16,128]{3,2,1,0:T(8,128)S(1)} %collective-permute-done.14.refs_10_), channel_id=1, source_target_pairs={{0,4},{4,8},{8,12},{6,2},{10,6},{14,10},{1,5},{5,9},{9,13},{7,3},{... | collective-permute-start | bytes 1572872 | tf_op jit(solution)/shard_map/ppermute | solution.py:381
  167.6 3.3 %copy-start = (f32[65,8,32,64]{3,2,1,0:T(8,128)}, f32[65,8,32,64]{3,2,1,0:T(8,128)S(1)}, u32[]{:S(2)}) copy-start(f32[65,8,32,64]{3,2,1,0:T(8,128)S(1)} %image.1) | copy-start | bytes 12779524
  (1 other events, 1.6 us)

commit v2 on v1

--- a/solution.py
+++ b/solution.py
@@ -11,11 +11,11 @@
 REACH = 4
 KEEP_EVERY = 4
 OFFSETS = 2 * HALF + 1
-OFFSETS_PER_STEP = 5
+OFFSET_ROWS = 72
 WEIGHTS = (-205.0 / 72.0, 8.0 / 5.0, -1.0 / 5.0, 8.0 / 315.0, -1.0 / 560.0)
 PAD = 8
 F32 = jnp.float32
-HBM = pl.BlockSpec(memory_space=pl.ANY)
+HBM = pl.BlockSpec(memory_space=pltpu.HBM)
 VMEM = pl.BlockSpec(memory_space=pltpu.VMEM)
 SMEM = pl.BlockSpec(memory_space=pltpu.SMEM)
 
@@ -35,31 +35,28 @@
         copy.wait()
 
 
-def edge_kernel(source, receiver, up, down, sems):
-    rows = source.shape[1]
-    copies = []
-    for field, ref in enumerate((source, receiver)):
-        for out, start in ((up, rows - REACH), (down, 0)):
-            copies.append(
-                pltpu.make_async_copy(
-                    ref.at[0, pl.ds(start, REACH)], out.at[field], sems.at[len(copies)]
-                )
-            )
-    run_copies(copies)
+def edge_kernel(source_low, receiver_low, source_high, receiver_high, up, down):
+    down[0] = source_low[0]
+    down[1] = receiver_low[0]
+    up[0] = source_high[0]
+    up[1] = receiver_high[0]
 
 
 def edges(source, receiver):
-    _, _, size_y, size_z = source.shape
+    _, rows, size_y, size_z = source.shape
     shape = jax.ShapeDtypeStruct((2, REACH, size_y, size_z), F32)
+    block = (1, REACH, size_y, size_z)
+    low = pl.BlockSpec(block, lambda i: (0, 0, 0, 0))
+    high = pl.BlockSpec(block, lambda i: (0, rows // REACH - 1, 0, 0))
     return pl.pallas_call(
         edge_kernel,
+        grid=(1,),
         out_shape=(shape, shape),
-        in_specs=[HBM, HBM],
-        out_specs=(HBM, HBM),
-        scratch_shapes=[pltpu.SemaphoreType.DMA((4,))],
+        in_specs=[low, low, high, high],
+        out_specs=(VMEM, VMEM),
         cost_estimate=cost(0, 2 * 2**20),
         name="edges",
-    )(source, receiver)
+    )(source, receiver, source, receiver)
 
 
 def z_halves(lines):
@@ -252,8 +249,8 @@
             pltpu.VMEM((2, rows + 2 * REACH, size_y + 2 * PAD, size_z), F32),
             pltpu.SemaphoreType.DMA((9,)),
         ],
-        compiler_params=params(40),
-        cost_estimate=cost(60 * 2**20, 14 * 2**20),
+        compiler_params=params(60),
+        cost_estimate=cost(2 * 10**10, 40 * 2**20),
         name="steps",
     )(place, source, receiver, source_before, receiver_before, courant, left, right, side)
 
@@ -305,7 +302,7 @@
 
 
 def image_kernel(count, place, *refs):
-    blocks, (out, rows_of, sems) = refs[:count], refs[count:]
+    blocks, (out, rows_of, turned, sems) = refs[:count], refs[count:]
     parity = place[2]
     rows = blocks[0].shape[1]
     step = pl.program_id(0)
@@ -328,21 +325,23 @@
 
     groups = count // 3
     lines, size_z = rows_of.shape[3], rows_of.shape[4]
-    for offset in range(OFFSETS_PER_STEP):
-        shift = step * OFFSETS_PER_STEP + offset
-        for sample in range(rows // 4):
-            for chunk in range(lines // 8):
-                here = pl.ds(8 * chunk, 8)
-                total = None
-                for group in range(groups):
-                    term = (
-                        rows_of[group, 0, 2 * HALF + 4 * sample - shift, here, :]
-                        * rows_of[group, 1, 4 * sample + shift, here, :]
-                    )
-                    total = term if total is None else total + term
-                other = pltpu.roll(total, size_z // 2, 1)
-                out[offset, sample, 8 * chunk : 8 * chunk + 8, :] = total[:, : size_z // 2]
-                out[offset, sample, lines + 8 * chunk : lines + 8 * chunk + 8, :] = other[:, : size_z // 2]
+    sample = 4 * pl.program_id(0)
+    for chunk in range(lines // 8):
+        here = pl.ds(8 * chunk, 8)
+        for shift in range(OFFSETS):
+            total = None
+            for group in range(groups):
+                term = (
+                    rows_of[group, 0, 2 * HALF + sample - shift, here, :]
+                    * rows_of[group, 1, sample + shift, here, :]
+                )
+                total = term if total is None else total + term
+            turned[pl.ds(shift, 8, stride=OFFSET_ROWS), :] = total
+        for line in range(8):
+            values = turned[line * OFFSET_ROWS : (line + 1) * OFFSET_ROWS, :].T
+            at = 8 * chunk + line
+            out[0, at] = values[: size_z // 2, :OFFSETS]
+            out[0, lines + at] = values[size_z // 2 :, :OFFSETS]
 
 
 def image(place, blocks):
@@ -350,12 +349,13 @@
     samples = rows // 4
     return pl.pallas_call(
         functools.partial(image_kernel, len(blocks)),
-        grid=(OFFSETS // OFFSETS_PER_STEP,),
-        out_shape=jax.ShapeDtypeStruct((OFFSETS, samples, 2 * lines, size_z // 2), F32),
+        grid=(samples,),
+        out_shape=jax.ShapeDtypeStruct((samples, 2 * lines, size_z // 2, OFFSETS), F32),
         in_specs=[SMEM] + [HBM] * len(blocks),
-        out_specs=pl.BlockSpec((OFFSETS_PER_STEP, samples, 2 * lines, size_z // 2), lambda i: (i, 0, 0, 0)),
+        out_specs=pl.BlockSpec((1, 2 * lines, size_z // 2, OFFSETS), lambda i: (i, 0, 0, 0)),
         scratch_shapes=[
             pltpu.VMEM((len(blocks) // 3, 2, rows + 2 * HALF, lines, size_z), F32),
+            pltpu.VMEM((8 * OFFSET_ROWS, size_z), F32),
             pltpu.SemaphoreType.DMA((len(blocks),)),
         ],
         compiler_params=params(24),
@@ -375,28 +375,37 @@
     onward = [(i, i + 2) for i in range(0, size - 2, 2)] + [(i, i - 2) for i in range(3, size, 2)]
     both = [(0, 1), (1, 0)]
 
-    def spread(keep, give):
-        other = lax.ppermute(give, "shot", both)
-        near = [lax.ppermute(part, "gx", partner) for part in (keep, other)]
-        far = [lax.ppermute(part, "gx", onward) for part in near]
-        return [keep, near[0], far[0], other, near[1], far[1]]
+    def exchange(array, axis, pairs):
+        return lax.ppermute(array, axis, pairs)
 
     up, down = edges(source_now, receiver_now)
     keep, give, side = pack(place, source_now, receiver_now)
-    left = lax.ppermute(up, "gx", up_pairs)
-    right = lax.ppermute(down, "gx", down_pairs)
-    side = lax.ppermute(side, "gy", both)
-    left, right, keep, give = lax.optimization_barrier((left, right, keep, give))
-    blocks = spread(keep, give)
+    left = exchange(up, "gx", up_pairs)
+    right = exchange(down, "gx", down_pairs)
+    side = exchange(side, "gy", both)
+    other = exchange(give, "shot", both)
+    left, right, side, other = lax.optimization_barrier((left, right, side, other))
+    near_keep = exchange(keep, "gx", partner)
+    near_other = exchange(other, "gx", partner)
     partial, kept_courant, up, down, side = steps(
         place, source_now, receiver_now, source_before, receiver_before, courant, left, right, side
     )
-    left = lax.ppermute(up, "gx", up_pairs)
-    right = lax.ppermute(down, "gx", down_pairs)
-    side = lax.ppermute(side, "gy", both)
+    up, down, side, near_keep = lax.optimization_barrier((up, down, side, near_keep))
+    left = exchange(up, "gx", up_pairs)
+    right = exchange(down, "gx", down_pairs)
+    side = exchange(side, "gy", both)
+    far_keep = exchange(near_keep, "gx", onward)
+    left, right, side, near_other = lax.optimization_barrier((left, right, side, near_other))
+    far_other = exchange(near_other, "gx", onward)
+    blocks = [keep, near_keep, far_keep, other, near_other, far_other]
     keep, give = finish(place, partial, kept_courant, left, right, side)
-    blocks += spread(keep, give)
-    return image(place, blocks)
+    other = exchange(give, "shot", both)
+    near_keep = exchange(keep, "gx", partner)
+    near_other = exchange(other, "gx", partner)
+    far_keep = exchange(near_keep, "gx", onward)
+    far_other = exchange(near_other, "gx", onward)
+    blocks += [keep, near_keep, far_keep, other, near_other, far_other]
+    return jnp.transpose(image(place, blocks), (3, 0, 1, 2))
 
 
 def solution(mesh):

time: 182 us -> 132 us (0.73)
  Pallas kernels: 64.3 us -> 41.3 us
  local copies, waits for them, and re-layouts: 20.2 us -> 2.28 us
  waiting for transfers between devices: 62.2 us -> 51.1 us
  starting transfers between devices: 33.9 us -> 36.5 us
    pallas_call x2, Pallas kernels: 37.6 us -> 9.97 us  [the longest x1 7.72 us: image(): pl.pallas_call(functools.partial(image_kernel, len(blocks)), grid=(sample...]
    ppermute x16, waiting for transfers between devices: 62.2 us -> 51.1 us  [exchange(): return lax.ppermute(array, axis, pairs)]
    pallas_call x1 -> x0, local copies, waits for them, and re-layouts: 10.6 us -> none  [image(): pl.pallas_call(functools.partial(image_kernel, len(blocks)), grid=(OFFSET...]
    unnamed x18 -> x14, local copies, waits for them, and re-layouts: 9.69 us -> 2.28 us
    pallas_call x1, Pallas kernels: 17.8 us -> 22.6 us  [steps(): pl.pallas_call(step_kernel, out_shape=(jax.ShapeDtypeStruct((2, rows, lin...]
    ppermute x16, starting transfers between devices: 33.9 us -> 36.5 us  [exchange(): return lax.ppermute(array, axis, pairs)]
  transfers between devices with their start and end apart: 16 -> 16, of which waited for: 8 -> 9; matrix products, arithmetic and copies ran while one was open for 0% -> 0% of each run, Pallas kernels for 5% -> 22%
where the time goes in v2:
time: 132 us
  waiting for transfers between devices  51.1 us (39%)
  Pallas kernels  41.3 us (31%)
  starting transfers between devices  36.5 us (28%)
  local copies, waits for them, and re-layouts  2.28 us (2%)
    ppermute x16, waiting for transfers between devices, exchange(): return lax.ppermute(array, axis, pairs)  51.1 us
    ppermute x16, starting transfers between devices, exchange(): return lax.ppermute(array, axis, pairs)  36.5 us
    pallas_call x1, Pallas kernels, steps(): pl.pallas_call(step_kernel, out_shape=(jax.ShapeDtypeStruct((2, rows, lin...  22.6 us
    pallas_call x1, Pallas kernels, image(): pl.pallas_call(functools.partial(image_kernel, len(blocks)), grid=(sample...  7.72 us
    pallas_call x1, Pallas kernels, pack(): pl.pallas_call(pack_kernel, grid=(rows // step,), out_shape=(half, half,...  6.13 us
  transfers between devices with their start and end apart: 16, of which 9 were waited for; matrix products, arithmetic and copies ran while one was open for 0% of the time, Pallas kernels for 22%

profile of v2, /device:TPU:0, one launch (start us, length us, event | category | flops | bytes accessed | tf_op | source)
XLA Modules:
  0.0 131.9 jit_solution(3777806097006350276)
XLA Ops:
  0.0 2.3 %edges.1 = (f32[2,4,128,128]{3,2,1,0:T(8,128)}, f32[2,4,128,128]{3,2,1,0:T(8,128)}) custom-call(f32[1,32,128,128]{3,2,1,0:T(8,128)} %source.3, f32[1,32,128,128]{3,2,1,0:T(8,128)} %receiver.3, f32[1,32,128,128]{3,2,1,0:T(8,128)} %source.3, f32[1,32,128,128]{3,2,1,0:T(8,128)} %receiver.3), custom_call_target="tpu_custom_call" | custom-call | bytes 2097152 | tf_op jit(solution)/shard_map/edges/pallas_call | solution.py:51
  2.3 4.9 %collective-permute-start = (f32[2,4,128,128]{3,2,1,0:T(8,128)}, f32[2,4,128,128]{3,2,1,0:T(8,128)S(1)}, u32[]{:S(2)}, u32[]{:S(2)}) collective-permute-start(f32[2,4,128,128]{3,2,1,0:T(8,128)} %get-tuple-element.30), channel_id=1, source_target_pairs={{0,2},{2,4},{4,6},{6,8},{8,10},{10,12},{12,14},{1,3},{3,5},{5,7},{... | collective-permute-start | bytes 1572872 | tf_op jit(solution)/shard_map/ppermute | solution.py:379
  9.1 6.1 %pack.1 = (f32[2,32,16,128]{3,2,1,0:T(8,128)}, f32[2,32,16,128]{3,2,1,0:T(8,128)}, f32[32,8,128]{2,1,0:T(8,128)}) custom-call(s32[3]{0:T(128)} %pad_add_fusion.place, f32[1,32,128,128]{3,2,1,0:T(8,128)} %source.3, f32[1,32,128,128]{3,2,1,0:T(8,128)} %receiver.3), custom_call_target="tpu_custom_call" | custom-call | flops 1048576 | bytes 7340032 | tf_op jit(solution)/shard_map/pack/pallas_call | solution.py:94
  16.8 2.6 %collective-permute-start.4 = (f32[2,32,16,128]{3,2,1,0:T(8,128)}, f32[2,32,16,128]{3,2,1,0:T(8,128)S(1)}, u32[]{:S(2)}, u32[]{:S(2)}) collective-permute-start(f32[2,32,16,128]{3,2,1,0:T(8,128)} %get-tuple-element.29.refs_0_), channel_id=1, source_target_pairs={{0,2},{2,0},{4,6},{6,4},{8,10},{10,8},{12,14},{14,12},{1,3},{3,1},... | collective-permute-start | bytes 1572872 | tf_op jit(solution)/shard_map/ppermute | solution.py:379
  19.4 1.9 %collective-permute-done.2.side = f32[32,8,128]{2,1,0:T(8,128)S(1)} collective-permute-done((f32[32,8,128]{2,1,0:T(8,128)}, f32[32,8,128]{2,1,0:T(8,128)S(1)}, u32[]{:S(2)}, u32[]{:S(2)}) %collective-permute-start.2) | collective-permute-done | bytes 131104 | tf_op jit(solution)/shard_map/ppermute | solution.py:379
  21.3 9.6 %collective-permute-done.left = f32[2,4,128,128]{3,2,1,0:T(8,128)S(1)} collective-permute-done((f32[2,4,128,128]{3,2,1,0:T(8,128)}, f32[2,4,128,128]{3,2,1,0:T(8,128)S(1)}, u32[]{:S(2)}, u32[]{:S(2)}) %collective-permute-start) | collective-permute-done | bytes 524320 | tf_op jit(solution)/shard_map/ppermute | solution.py:379
  31.0 2.4 %collective-permute-start.9 = (f32[2,32,16,128]{3,2,1,0:T(8,128)S(1)}, f32[2,32,16,128]{3,2,1,0:T(8,128)S(1)}, u32[]{:S(2)}, u32[]{:S(2)}) collective-permute-start(f32[2,32,16,128]{3,2,1,0:T(8,128)S(1)} %collective-permute-done.3.refs_3_), channel_id=1, source_target_pairs={{0,2},{2,0},{4,6},{6,4},{8,10},{10,8},{12,14},{14,12},{1,3},{3,1},... | collective-permute-start | bytes 1572872 | tf_op jit(solution)/shard_map/ppermute | solution.py:379
  33.4 22.6 %steps.1 = (f32[2,32,32,128]{3,2,1,0:T(8,128)}, f32[32,32,128]{2,1,0:T(8,128)}, f32[2,4,32,128]{3,2,1,0:T(8,128)}, f32[2,4,32,128]{3,2,1,0:T(8,128)}, f32[2,32,128]{2,1,0:T(8,128)}) custom-call(s32[3]{0:T(128)} %pad_add_fusion.place, f32[1,32,128,128]{3,2,1,0:T(8,128)} %source.3, f32[1,32,128,128]{3,2,1,0:T(8,128)} %receiver.3, ...), custom_call_target="tpu_custom_call" | custom-call | flops 20000000000 | bytes 41943040 | tf_op jit(solution)/shard_map/steps/pallas_call | solution.py:234
  56.1 2.8 %collective-permute-start.6 = (f32[2,4,32,128]{3,2,1,0:T(8,128)}, f32[2,4,32,128]{3,2,1,0:T(8,128)S(1)}, u32[]{:S(2)}, u32[]{:S(2)}) collective-permute-start(f32[2,4,32,128]{3,2,1,0:T(8,128)} %get-tuple-element.42), channel_id=1, source_target_pairs={{0,2},{2,4},{4,6},{6,8},{8,10},{10,12},{12,14},{1,3},{3,5},{5,7},{... | collective-permute-start | bytes 393224 | tf_op jit(solution)/shard_map/ppermute | solution.py:379
  61.7 2.6 %collective-permute-done.8.side = f32[2,32,128]{2,1,0:T(8,128)S(1)} collective-permute-done((f32[2,32,128]{2,1,0:T(8,128)}, f32[2,32,128]{2,1,0:T(8,128)S(1)}, u32[]{:S(2)}, u32[]{:S(2)}) %collective-permute-start.8) | collective-permute-done | bytes 32800 | tf_op jit(solution)/shard_map/ppermute | solution.py:379
  64.3 1.7 %collective-permute-done.7.right = f32[2,4,32,128]{3,2,1,0:T(8,128)S(1)} collective-permute-done((f32[2,4,32,128]{3,2,1,0:T(8,128)}, f32[2,4,32,128]{3,2,1,0:T(8,128)S(1)}, u32[]{:S(2)}, u32[]{:S(2)}) %collective-permute-start.7) | collective-permute-done | bytes 131104 | tf_op jit(solution)/shard_map/ppermute | solution.py:379
  68.3 2.6 %finish.1 = (f32[2,32,16,128]{3,2,1,0:T(8,128)S(1)}, f32[2,32,16,128]{3,2,1,0:T(8,128)S(1)}) custom-call(s32[3]{0:T(128)S(1)} %copy-done.3, f32[2,32,32,128]{3,2,1,0:T(8,128)S(1)} %copy-done, f32[32,32,128]{2,1,0:T(8,128)S(1)} %copy-done.2, f32[2,4,32,128]{3,2,1,0:T(8,128)S(1)} %collective-permute-done.6.left, ...), custom_call_target="tpu_custom_call" | custom-call | flops 1048576 | bytes 3145728 | tf_op jit(solution)/shard_map/finish/pallas_call | solution.py:293
  71.0 3.0 %collective-permute-start.11 = (f32[2,32,16,128]{3,2,1,0:T(8,128)S(1)}, f32[2,32,16,128]{3,2,1,0:T(8,128)S(1)}, u32[]{:S(2)}, u32[]{:S(2)}) collective-permute-start(f32[2,32,16,128]{3,2,1,0:T(8,128)S(1)} %get-tuple-element.51.refs_6_), channel_id=1, source_target_pairs={{0,2},{2,0},{4,6},{6,4},{8,10},{10,8},{12,14},{14,12},{1,3},{3,1},... | collective-permute-start | bytes 1572872 | tf_op jit(solution)/shard_map/ppermute | solution.py:379
  74.0 1.8 %collective-permute-start.14 = (f32[2,32,16,128]{3,2,1,0:T(8,128)S(1)}, f32[2,32,16,128]{3,2,1,0:T(8,128)S(1)}, u32[]{:S(2)}, u32[]{:S(2)}) collective-permute-start(f32[2,32,16,128]{3,2,1,0:T(8,128)S(1)} %collective-permute-done.13.refs_9_), channel_id=1, source_target_pairs={{0,2},{2,0},{4,6},{6,4},{8,10},{10,8},{12,14},{14,12},{1,3},{3,1},... | collective-permute-start | bytes 1572872 | tf_op jit(solution)/shard_map/ppermute | solution.py:379
  75.8 3.5 %collective-permute-start.5 = (f32[2,32,16,128]{3,2,1,0:T(8,128)S(1)}, f32[2,32,16,128]{3,2,1,0:T(8,128)S(1)}, u32[]{:S(2)}, u32[]{:S(2)}) collective-permute-start(f32[2,32,16,128]{3,2,1,0:T(8,128)S(1)} %collective-permute-done.4.refs_1_), channel_id=1, source_target_pairs={{0,4},{4,8},{8,12},{6,2},{10,6},{14,10},{1,5},{5,9},{9,13},{7,3},{... | collective-permute-start | bytes 1572872 | tf_op jit(solution)/shard_map/ppermute | solution.py:379
  79.4 2.6 %collective-permute-start.10 = (f32[2,32,16,128]{3,2,1,0:T(8,128)S(1)}, f32[2,32,16,128]{3,2,1,0:T(8,128)S(1)}, u32[]{:S(2)}, u32[]{:S(2)}) collective-permute-start(f32[2,32,16,128]{3,2,1,0:T(8,128)S(1)} %collective-permute-done.9.refs_4_), channel_id=1, source_target_pairs={{0,4},{4,8},{8,12},{6,2},{10,6},{14,10},{1,5},{5,9},{9,13},{7,3},{... | collective-permute-start | bytes 1572872 | tf_op jit(solution)/shard_map/ppermute | solution.py:379
  82.0 4.8 %collective-permute-done.11.refs_7_ = f32[2,32,16,128]{3,2,1,0:T(8,128)S(1)} collective-permute-done((f32[2,32,16,128]{3,2,1,0:T(8,128)S(1)}, f32[2,32,16,128]{3,2,1,0:T(8,128)S(1)}, u32[]{:S(2)}, u32[]{:S(2)}) %collective-permute-start.11) | collective-permute-done | bytes 524320 | tf_op jit(solution)/shard_map/ppermute | solution.py:379
  86.8 3.6 %collective-permute-start.12 = (f32[2,32,16,128]{3,2,1,0:T(8,128)S(1)}, f32[2,32,16,128]{3,2,1,0:T(8,128)S(1)}, u32[]{:S(2)}, u32[]{:S(2)}) collective-permute-start(f32[2,32,16,128]{3,2,1,0:T(8,128)S(1)} %collective-permute-done.11.refs_7_), channel_id=1, source_target_pairs={{0,4},{4,8},{8,12},{6,2},{10,6},{14,10},{1,5},{5,9},{9,13},{7,3},{... | collective-permute-start | bytes 1572872 | tf_op jit(solution)/shard_map/ppermute | solution.py:379
  90.4 7.4 %collective-permute-done.14.refs_10_ = f32[2,32,16,128]{3,2,1,0:T(8,128)S(1)} collective-permute-done((f32[2,32,16,128]{3,2,1,0:T(8,128)S(1)}, f32[2,32,16,128]{3,2,1,0:T(8,128)S(1)}, u32[]{:S(2)}, u32[]{:S(2)}) %collective-permute-start.14) | collective-permute-done | bytes 524320 | tf_op jit(solution)/shard_map/ppermute | solution.py:379
  97.8 3.5 %collective-permute-start.15 = (f32[2,32,16,128]{3,2,1,0:T(8,128)S(1)}, f32[2,32,16,128]{3,2,1,0:T(8,128)S(1)}, u32[]{:S(2)}, u32[]{:S(2)}) collective-permute-start(f32[2,32,16,128]{3,2,1,0:T(8,128)S(1)} %collective-permute-done.14.refs_10_), channel_id=1, source_target_pairs={{0,4},{4,8},{8,12},{6,2},{10,6},{14,10},{1,5},{5,9},{9,13},{7,3},{... | collective-permute-start | bytes 1572872 | tf_op jit(solution)/shard_map/ppermute | solution.py:379
  101.3 1.6 %collective-permute-done.10.refs_5_ = f32[2,32,16,128]{3,2,1,0:T(8,128)S(1)} collective-permute-done((f32[2,32,16,128]{3,2,1,0:T(8,128)S(1)}, f32[2,32,16,128]{3,2,1,0:T(8,128)S(1)}, u32[]{:S(2)}, u32[]{:S(2)}) %collective-permute-start.10) | collective-permute-done | bytes 524320 | tf_op jit(solution)/shard_map/ppermute | solution.py:379
  102.9 11.2 %collective-permute-done.12.refs_8_ = f32[2,32,16,128]{3,2,1,0:T(8,128)S(1)} collective-permute-done((f32[2,32,16,128]{3,2,1,0:T(8,128)S(1)}, f32[2,32,16,128]{3,2,1,0:T(8,128)S(1)}, u32[]{:S(2)}, u32[]{:S(2)}) %collective-permute-start.12) | collective-permute-done | bytes 524320 | tf_op jit(solution)/shard_map/ppermute | solution.py:379
  114.1 10.1 %collective-permute-done.15.refs_11_ = f32[2,32,16,128]{3,2,1,0:T(8,128)S(1)} collective-permute-done((f32[2,32,16,128]{3,2,1,0:T(8,128)S(1)}, f32[2,32,16,128]{3,2,1,0:T(8,128)S(1)}, u32[]{:S(2)}, u32[]{:S(2)}) %collective-permute-start.15) | collective-permute-done | bytes 524320 | tf_op jit(solution)/shard_map/ppermute | solution.py:379
  124.2 7.7 %image.1 = f32[8,32,64,65]{3,2,1,0:T(8,128)} custom-call(s32[3]{0:T(128)S(1)} %copy-done.3, f32[2,32,16,128]{3,2,1,0:T(8,128)S(1)} %copy-done.1, f32[2,32,16,128]{3,2,1,0:T(8,128)S(1)} %collective-permute-done.4.refs_1_, f32[2,32,16,128]{3,2,1,0:T(8,128)S(1)} %collective-permute-done.5.refs_2_, f32[2,32,16,128]{3,2,1,0:T(8,128)S(1)} %collective-permute-done.3.refs_3_, ...), custom_call_target="tpu_custom_call" | custom-call | flops 16777216 | bytes 16777216 | tf_op jit(solution)/shard_map/image/pallas_call | solution.py:350
  (28 shorter events, 8.7 us)
Async XLA Ops:
  2.3 28.7 %collective-permute-start = (f32[2,4,128,128]{3,2,1,0:T(8,128)}, f32[2,4,128,128]{3,2,1,0:T(8,128)S(1)}, u32[]{:S(2)}, u32[]{:S(2)}) collective-permute-start(f32[2,4,128,128]{3,2,1,0:T(8,128)} %get-tuple-element.30), channel_id=1, source_target_pairs={{0,2},{2,4},{4,6},{6,8},{8,10},{10,12},{12,14},{1,3},{3,5},{5,7},{... | collective-permute-start | bytes 1572872 | tf_op jit(solution)/shard_map/ppermute | solution.py:379
  7.2 23.8 %collective-permute-start.1 = (f32[2,4,128,128]{3,2,1,0:T(8,128)}, f32[2,4,128,128]{3,2,1,0:T(8,128)S(1)}, u32[]{:S(2)}, u32[]{:S(2)}) collective-permute-start(f32[2,4,128,128]{3,2,1,0:T(8,128)} %get-tuple-element.31), channel_id=1, source_target_pairs={{2,0},{4,2},{6,4},{8,6},{10,8},{12,10},{14,12},{3,1},{5,3},{7,5},{... | collective-permute-start | bytes 1572872 | tf_op jit(solution)/shard_map/ppermute | solution.py:379
  15.2 15.8 %collective-permute-start.3 = (f32[2,32,16,128]{3,2,1,0:T(8,128)}, f32[2,32,16,128]{3,2,1,0:T(8,128)S(1)}, u32[]{:S(2)}, u32[]{:S(2)}) collective-permute-start(f32[2,32,16,128]{3,2,1,0:T(8,128)} %get-tuple-element.33), channel_id=1, source_target_pairs={{0,16},{16,0},{1,17},{17,1},{2,18},{18,2},{3,19},{19,3},{4,20},{20... | collective-permute-start | bytes 1572872 | tf_op jit(solution)/shard_map/ppermute | solution.py:379
  15.2 6.1 %collective-permute-start.2 = (f32[32,8,128]{2,1,0:T(8,128)}, f32[32,8,128]{2,1,0:T(8,128)S(1)}, u32[]{:S(2)}, u32[]{:S(2)}) collective-permute-start(f32[32,8,128]{2,1,0:T(8,128)} %get-tuple-element.32), channel_id=1, source_target_pairs={{0,1},{1,0},{2,3},{3,2},{4,5},{5,4},{6,7},{7,6},{8,9},{9,8},{10,11... | collective-permute-start | bytes 393224 | tf_op jit(solution)/shard_map/ppermute | solution.py:379
  16.8 49.3 %copy-start.3 = (s32[3]{0:T(128)S(1)}, s32[3]{0:T(128)}, u32[]{:S(2)}) copy-start(s32[3]{0:T(128)} %pad_add_fusion.place) | copy-start | bytes 40
  16.8 39.3 %collective-permute-start.4 = (f32[2,32,16,128]{3,2,1,0:T(8,128)}, f32[2,32,16,128]{3,2,1,0:T(8,128)S(1)}, u32[]{:S(2)}, u32[]{:S(2)}) collective-permute-start(f32[2,32,16,128]{3,2,1,0:T(8,128)} %get-tuple-element.29.refs_0_), channel_id=1, source_target_pairs={{0,2},{2,0},{4,6},{6,4},{8,10},{10,8},{12,14},{14,12},{1,3},{3,1},... | collective-permute-start | bytes 1572872 | tf_op jit(solution)/shard_map/ppermute | solution.py:379
  21.3 12.1 %copy-start.6 = (f32[32,8,128]{2,1,0:T(8,128)}, f32[32,8,128]{2,1,0:T(8,128)S(1)}, u32[]{:S(2)}) copy-start(f32[32,8,128]{2,1,0:T(8,128)S(1)} %collective-permute-done.2.side) | copy-start | bytes 393220
  31.0 2.5 %copy-start.4 = (f32[2,4,128,128]{3,2,1,0:T(8,128)}, f32[2,4,128,128]{3,2,1,0:T(8,128)S(1)}, u32[]{:S(2)}) copy-start(f32[2,4,128,128]{3,2,1,0:T(8,128)S(1)} %collective-permute-done.left) | copy-start | bytes 1572868
  31.0 2.5 %copy-start.5 = (f32[2,4,128,128]{3,2,1,0:T(8,128)}, f32[2,4,128,128]{3,2,1,0:T(8,128)S(1)}, u32[]{:S(2)}) copy-start(f32[2,4,128,128]{3,2,1,0:T(8,128)S(1)} %collective-permute-done.1.right) | copy-start | bytes 1572868
  31.0 35.1 %collective-permute-start.9 = (f32[2,32,16,128]{3,2,1,0:T(8,128)S(1)}, f32[2,32,16,128]{3,2,1,0:T(8,128)S(1)}, u32[]{:S(2)}, u32[]{:S(2)}) collective-permute-start(f32[2,32,16,128]{3,2,1,0:T(8,128)S(1)} %collective-permute-done.3.refs_3_), channel_id=1, source_target_pairs={{0,2},{2,0},{4,6},{6,4},{8,10},{10,8},{12,14},{14,12},{1,3},{3,1},... | collective-permute-start | bytes 1572872 | tf_op jit(solution)/shard_map/ppermute | solution.py:379
  33.4 90.8 %copy-start.1 = (f32[2,32,16,128]{3,2,1,0:T(8,128)S(1)}, f32[2,32,16,128]{3,2,1,0:T(8,128)}, u32[]{:S(2)}) copy-start(f32[2,32,16,128]{3,2,1,0:T(8,128)} %get-tuple-element.29.refs_0_) | copy-start | bytes 1572868
  56.1 8.3 %collective-permute-start.6 = (f32[2,4,32,128]{3,2,1,0:T(8,128)}, f32[2,4,32,128]{3,2,1,0:T(8,128)S(1)}, u32[]{:S(2)}, u32[]{:S(2)}) collective-permute-start(f32[2,4,32,128]{3,2,1,0:T(8,128)} %get-tuple-element.42), channel_id=1, source_target_pairs={{0,2},{2,4},{4,6},{6,8},{8,10},{10,12},{12,14},{1,3},{3,5},{5,7},{... | collective-permute-start | bytes 393224 | tf_op jit(solution)/shard_map/ppermute | solution.py:379
  58.8 7.2 %collective-permute-start.7 = (f32[2,4,32,128]{3,2,1,0:T(8,128)}, f32[2,4,32,128]{3,2,1,0:T(8,128)S(1)}, u32[]{:S(2)}, u32[]{:S(2)}) collective-permute-start(f32[2,4,32,128]{3,2,1,0:T(8,128)} %get-tuple-element.43), channel_id=1, source_target_pairs={{2,0},{4,2},{6,4},{8,6},{10,8},{12,10},{14,12},{3,1},{5,3},{7,5},{... | collective-permute-start | bytes 393224 | tf_op jit(solution)/shard_map/ppermute | solution.py:379
  60.1 4.2 %collective-permute-start.8 = (f32[2,32,128]{2,1,0:T(8,128)}, f32[2,32,128]{2,1,0:T(8,128)S(1)}, u32[]{:S(2)}, u32[]{:S(2)}) collective-permute-start(f32[2,32,128]{2,1,0:T(8,128)} %get-tuple-element.44), channel_id=1, source_target_pairs={{0,1},{1,0},{2,3},{3,2},{4,5},{5,4},{6,7},{7,6},{8,9},{9,8},{10,11... | collective-permute-start | bytes 98312 | tf_op jit(solution)/shard_map/ppermute | solution.py:379
  66.1 1.2 copy-start
  67.3 1.0 copy-start.2
  71.0 3.1 %collective-permute-start.13 = (f32[2,32,16,128]{3,2,1,0:T(8,128)S(1)}, f32[2,32,16,128]{3,2,1,0:T(8,128)S(1)}, u32[]{:S(2)}, u32[]{:S(2)}) collective-permute-start(f32[2,32,16,128]{3,2,1,0:T(8,128)S(1)} %get-tuple-element.52), channel_id=1, source_target_pairs={{0,16},{16,0},{1,17},{17,1},{2,18},{18,2},{3,19},{19,3},{4,20},{20... | collective-permute-start | bytes 1572872 | tf_op jit(solution)/shard_map/ppermute | solution.py:379
  71.0 15.8 %collective-permute-start.11 = (f32[2,32,16,128]{3,2,1,0:T(8,128)S(1)}, f32[2,32,16,128]{3,2,1,0:T(8,128)S(1)}, u32[]{:S(2)}, u32[]{:S(2)}) collective-permute-start(f32[2,32,16,128]{3,2,1,0:T(8,128)S(1)} %get-tuple-element.51.refs_6_), channel_id=1, source_target_pairs={{0,2},{2,0},{4,6},{6,4},{8,10},{10,8},{12,14},{14,12},{1,3},{3,1},... | collective-permute-start | bytes 1572872 | tf_op jit(solution)/shard_map/ppermute | solution.py:379
  74.0 23.7 %collective-permute-start.14 = (f32[2,32,16,128]{3,2,1,0:T(8,128)S(1)}, f32[2,32,16,128]{3,2,1,0:T(8,128)S(1)}, u32[]{:S(2)}, u32[]{:S(2)}) collective-permute-start(f32[2,32,16,128]{3,2,1,0:T(8,128)S(1)} %collective-permute-done.13.refs_9_), channel_id=1, source_target_pairs={{0,2},{2,0},{4,6},{6,4},{8,10},{10,8},{12,14},{14,12},{1,3},{3,1},... | collective-permute-start | bytes 1572872 | tf_op jit(solution)/shard_map/ppermute | solution.py:379
  75.8 25.4 %collective-permute-start.5 = (f32[2,32,16,128]{3,2,1,0:T(8,128)S(1)}, f32[2,32,16,128]{3,2,1,0:T(8,128)S(1)}, u32[]{:S(2)}, u32[]{:S(2)}) collective-permute-start(f32[2,32,16,128]{3,2,1,0:T(8,128)S(1)} %collective-permute-done.4.refs_1_), channel_id=1, source_target_pairs={{0,4},{4,8},{8,12},{6,2},{10,6},{14,10},{1,5},{5,9},{9,13},{7,3},{... | collective-permute-start | bytes 1572872 | tf_op jit(solution)/shard_map/ppermute | solution.py:379
  79.4 23.5 %collective-permute-start.10 = (f32[2,32,16,128]{3,2,1,0:T(8,128)S(1)}, f32[2,32,16,128]{3,2,1,0:T(8,128)S(1)}, u32[]{:S(2)}, u32[]{:S(2)}) collective-permute-start(f32[2,32,16,128]{3,2,1,0:T(8,128)S(1)} %collective-permute-done.9.refs_4_), channel_id=1, source_target_pairs={{0,4},{4,8},{8,12},{6,2},{10,6},{14,10},{1,5},{5,9},{9,13},{7,3},{... | collective-permute-start | bytes 1572872 | tf_op jit(solution)/shard_map/ppermute | solution.py:379
  86.8 27.3 %collective-permute-start.12 = (f32[2,32,16,128]{3,2,1,0:T(8,128)S(1)}, f32[2,32,16,128]{3,2,1,0:T(8,128)S(1)}, u32[]{:S(2)}, u32[]{:S(2)}) collective-permute-start(f32[2,32,16,128]{3,2,1,0:T(8,128)S(1)} %collective-permute-done.11.refs_7_), channel_id=1, source_target_pairs={{0,4},{4,8},{8,12},{6,2},{10,6},{14,10},{1,5},{5,9},{9,13},{7,3},{... | collective-permute-start | bytes 1572872 | tf_op jit(solution)/shard_map/ppermute | solution.py:379
  97.8 26.4 %collective-permute-start.15 = (f32[2,32,16,128]{3,2,1,0:T(8,128)S(1)}, f32[2,32,16,128]{3,2,1,0:T(8,128)S(1)}, u32[]{:S(2)}, u32[]{:S(2)}) collective-permute-start(f32[2,32,16,128]{3,2,1,0:T(8,128)S(1)} %collective-permute-done.14.refs_10_), channel_id=1, source_target_pairs={{0,4},{4,8},{8,12},{6,2},{10,6},{14,10},{1,5},{5,9},{9,13},{7,3},{... | collective-permute-start | bytes 1572872 | tf_op jit(solution)/shard_map/ppermute | solution.py:379

commit v3 on v2

v3 whole, which is shorter than its diff:
```python
import functools

import jax
import jax.numpy as jnp
from jax import lax
from jax.experimental import pallas as pl
from jax.experimental.pallas import tpu as pltpu
from jax.sharding import PartitionSpec as P

HALF = 32
REACH = 4
KEEP_EVERY = 4
OFFSETS = 2 * HALF + 1
OFFSET_ROWS = 72
WEIGHTS = (-205.0 / 72.0, 8.0 / 5.0, -1.0 / 5.0, 8.0 / 315.0, -1.0 / 560.0)
PAD = 8
F32 = jnp.float32
HBM = pl.BlockSpec(memory_space=pltpu.HBM)
VMEM = pl.BlockSpec(memory_space=pltpu.VMEM)
SMEM = pl.BlockSpec(memory_space=pltpu.SMEM)


def params(mib):
    return pltpu.CompilerParams(vmem_limit_bytes=mib * 2**20)


def cost(flops, nbytes):
    return pl.CostEstimate(flops=flops, bytes_accessed=nbytes, transcendentals=0)


def run_copies(copies):
    for copy in copies:
        copy.start()
    for copy in copies:
        copy.wait()


def z_halves(lines):
    count, size_z = lines.shape
    top, bottom = lines[: count // 2], lines[count // 2 :]
    low = lax.broadcasted_iota(jnp.int32, top.shape, 1) < size_z // 2
    first = jnp.where(low, top, pltpu.roll(bottom, size_z // 2, 1))
    second = jnp.where(low, pltpu.roll(top, size_z // 2, 1), bottom)
    return first, second


def pack_kernel(place, source, receiver, up, down, keep, give, side):
    shot, gy = place[0], place[1]
    rows, size_y, size_z = source.shape[1:]
    lines = size_y // KEEP_EVERY
    step, steps = pl.program_id(0), pl.num_programs(0)

    @pl.when(step == 0)
    def _():
        for field, ref in enumerate((source, receiver)):
            down[field] = ref[0, :REACH]

    @pl.when(step == steps - 1)
    def _():
        for field, ref in enumerate((source, receiver)):
            up[field] = ref[0, rows - REACH :]

    for row in range(rows):
        parts = []
        for field, ref in enumerate((source, receiver)):
            first, second = z_halves(ref[0, row, pl.ds(0, lines, stride=KEEP_EVERY), :])
            keep[field, row] = jnp.where(shot == 0, first, second)
            give[field, row] = jnp.where(shot == 0, second, first)
            low = ref[0, row, 0:REACH, :]
            high = ref[0, row, size_y - REACH : size_y, :]
            parts.append(jnp.where(gy == 0, high, low))
        side[row] = jnp.concatenate(parts, axis=0)


def pack(place, source, receiver):
    _, rows, size_y, size_z = source.shape
    lines = size_y // KEEP_EVERY // 2
    step = 8
    edge = jax.ShapeDtypeStruct((2, REACH, size_y, size_z), F32)
    half = jax.ShapeDtypeStruct((2, rows, lines, size_z), F32)
    edge_spec = pl.BlockSpec((2, REACH, size_y, size_z), lambda i: (0, 0, 0, 0))
    half_spec = pl.BlockSpec((2, step, lines, size_z), lambda i: (0, i, 0, 0))
    field_spec = pl.BlockSpec((1, step, size_y, size_z), lambda i: (0, i, 0, 0))
    return pl.pallas_call(
        pack_kernel,
        grid=(rows // step,),
        out_shape=(edge, edge, half, half, jax.ShapeDtypeStruct((rows, 2 * REACH, size_z), F32)),
        in_specs=[SMEM, field_spec, field_spec],
        out_specs=(
            edge_spec,
            edge_spec,
            half_spec,
            half_spec,
            pl.BlockSpec((step, 2 * REACH, size_z), lambda i: (i, 0, 0)),
        ),
        cost_estimate=cost(10**10, 7 * 2**20),
        name="pack",
    )(place, source, receiver)


def z_weights(size_z):
    z = lax.broadcasted_iota(jnp.int32, (8, size_z), 1)
    return [
        (jnp.where(z >= d, WEIGHTS[d], 0.0), jnp.where(z < size_z - d, WEIGHTS[d], 0.0))
        for d in range(1, REACH + 1)
    ]


def z_terms(center, masks):
    size_z = center.shape[1]
    total = None
    for d, (below, above) in enumerate(masks, start=1):
        term = below * pltpu.roll(center, d, 1) + above * pltpu.roll(center, size_z - d, 1)
        total = term if total is None else total + term
    return total


def first_step(now, row, before, before_row, scale, scale_row, after, after_row, field, masks):
    size_y = before.shape[2]
    for chunk in range(size_y // 8):
        at = PAD + 8 * chunk
        center = now[field, row, at : at + 8, :]
        total = (3.0 * WEIGHTS[0]) * center + z_terms(center, masks)
        for d in range(1, REACH + 1):
            around = (
                now[field, row + d, at : at + 8, :]
                + now[field, row - d, at : at + 8, :]
                + now[field, row, at + d : at + d + 8, :]
                + now[field, row, at - d : at - d + 8, :]
            )
            total = total + WEIGHTS[d] * around
        here = pl.ds(8 * chunk, 8)
        after[field, after_row, at : at + 8, :] = (
            2.0 * center - before[field, before_row, here, :] + scale[scale_row, here, :] * total
        )


def second_step(now, row, scale, scale_row, after, after_row, field, masks, store):
    size_y = scale.shape[1]
    for chunk in range(size_y // KEEP_EVERY // 8):
        at = PAD + 8 * KEEP_EVERY * chunk
        kept = lambda start: pl.ds(start, 8, stride=KEEP_EVERY)
        center = after[field, after_row, kept(at), :]
        total = (3.0 * WEIGHTS[0]) * center + z_terms(center, masks)
        for d in range(1, REACH + 1):
            around = (
                after[field, after_row + d, kept(at), :]
                + after[field, after_row - d, kept(at), :]
                + after[field, after_row, kept(at + d), :]
                + after[field, after_row, kept(at - d), :]
            )
            total = total + WEIGHTS[d] * around
        store(
            pl.ds(8 * chunk, 8),
            2.0 * center - now[field, row, kept(at), :] + scale[scale_row, kept(at - PAD), :] * total,
        )


def side_term(after, after_row, field, size_y, gy):
    lowest = WEIGHTS[REACH] * after[field, after_row, PAD : PAD + 1, :]
    highest = sum(
        WEIGHTS[d] * after[field, after_row, PAD + size_y - d : PAD + size_y - d + 1, :]
        for d in range(1, REACH + 1)
    )
    return jnp.where(gy == 0, highest, lowest)


def fill_sides(now, row, got, field, size_y, gy):
    blank = jnp.zeros_like(got)
    now[field, row, PAD - REACH : PAD, :] = jnp.where(gy == 0, blank, got)
    now[field, row, size_y + PAD : size_y + PAD + REACH, :] = jnp.where(gy == 0, got, blank)


def blank_sides(after, row, field, size_y):
    blank = jnp.zeros((REACH, after.shape[3]), F32)
    after[field, row, PAD - REACH : PAD, :] = blank
    after[field, row, size_y + PAD : size_y + PAD + REACH, :] = blank


def inner_kernel(
    place, source, receiver, source_before, receiver_before, courant, side,
    partial, kept_courant, side_out, border, now, before, scale, after, sems, out_sems,
):
    gy = place[1]
    rows, size_y, size_z = courant.shape
    lines = size_y // KEEP_EVERY
    copies = []

    def copy(src, dst):
        copies.append(pltpu.make_async_copy(src, dst, sems.at[len(copies)]))

    middle = pl.ds(PAD, size_y)
    for field, ref in enumerate((source, receiver)):
        copy(ref.at[0], now.at[field, :, middle])
    for field, ref in enumerate((source_before, receiver_before)):
        copy(ref.at[0], before.at[field])
    copy(courant, scale)
    for one in copies:
        one.start()

    def fill(row, carry):
        for field in range(2):
            got = side[row, field * REACH : (field + 1) * REACH, :]
            fill_sides(now, row, got, field, size_y, gy)
            blank_sides(after, row, field, size_y)
        return carry

    lax.fori_loop(0, rows, fill, 0)
    side_out[...] = jnp.zeros_like(side_out)
    for one in copies:
        one.wait()
    masks = z_weights(size_z)

    def first(row, carry):
        for field in range(2):
            first_step(now, row, before, row, scale, row, after, row, field, masks)
            side_out[field, pl.ds(row, 1), :] = side_term(after, row, field, size_y, gy)
        return carry

    lax.fori_loop(REACH, rows - REACH, first, 0)
    outs = []
    for field in range(2):
        for end, start in enumerate((REACH, rows - 3 * REACH)):
            outs.append(
                pltpu.make_async_copy(
                    after.at[field, pl.ds(start, 2 * REACH), middle],
                    border.at[field, end],
                    out_sems.at[len(outs)],
                )
            )
            outs[-1].start()

    def second(row, carry):
        for field in range(2):
            def store(here, value):
                partial[field, row - 2 * REACH, here, :] = value

            second_step(now, row, scale, row, after, row, field, masks, store)
        return carry

    lax.fori_loop(2 * REACH, rows - 2 * REACH, second, 0)

    def keep(row, carry):
        kept_courant[row] = scale[row, pl.ds(0, lines, stride=KEEP_EVERY), :]
        return carry

    lax.fori_loop(0, rows, keep, 0)
    for one in outs:
        one.wait()


def inner(place, source, receiver, source_before, receiver_before, courant, side):
    rows, size_y, size_z = courant.shape
    lines = size_y // KEEP_EVERY
    return pl.pallas_call(
        inner_kernel,
        out_shape=(
            jax.ShapeDtypeStruct((2, rows - 4 * REACH, lines, size_z), F32),
            jax.ShapeDtypeStruct((rows, lines, size_z), F32),
            jax.ShapeDtypeStruct((2, rows, size_z), F32),
            jax.ShapeDtypeStruct((2, 2, 2 * REACH, size_y, size_z), F32),
        ),
        in_specs=[SMEM] + [HBM] * 5 + [VMEM],
        out_specs=(VMEM,) * 3 + (HBM,),
        scratch_shapes=[
            pltpu.VMEM((2, rows, size_y + 2 * PAD, size_z), F32),
            pltpu.VMEM((2, rows, size_y, size_z), F32),
            pltpu.VMEM((rows, size_y, size_z), F32),
            pltpu.VMEM((2, rows, size_y + 2 * PAD, size_z), F32),
            pltpu.SemaphoreType.DMA((5,)),
            pltpu.SemaphoreType.DMA((4,)),
        ],
        compiler_params=params(60),
        cost_estimate=cost(10**6, 2**20),
        name="inner",
    )(place, source, receiver, source_before, receiver_before, courant, side)


def outer_kernel(
    place, source, receiver, source_before, receiver_before, courant, border, left, right, side, side_in,
    partial, up, down, side_out, now, before, scale, after, sems,
):
    gy = place[1]
    rows, size_y, size_z = courant.shape
    lines = size_y // KEEP_EVERY
    reach2 = 2 * REACH
    copies = []

    def copy(src, dst):
        copies.append(pltpu.make_async_copy(src, dst, sems.at[len(copies)]))

    middle = pl.ds(PAD, size_y)
    for field in range(2):
        ref = (source, receiver)[field]
        copy(ref.at[0, pl.ds(0, reach2)], now.at[field, pl.ds(REACH, reach2), middle])
        copy(left.at[field], now.at[field, pl.ds(0, REACH), middle])
        copy(ref.at[0, pl.ds(rows - reach2, reach2)], now.at[2 + field, pl.ds(0, reach2), middle])
        copy(right.at[field], now.at[2 + field, pl.ds(reach2, REACH), middle])
        ref = (source_before, receiver_before)[field]
        copy(ref.at[0, pl.ds(0, REACH)], before.at[field])
        copy(ref.at[0, pl.ds(rows - REACH, REACH)], before.at[2 + field])
        copy(border.at[field, 0], after.at[field, pl.ds(reach2, reach2), middle])
        copy(border.at[field, 1], after.at[2 + field, pl.ds(0, reach2), middle])
    copy(courant.at[pl.ds(0, reach2)], scale.at[pl.ds(0, reach2)])
    copy(courant.at[pl.ds(rows - reach2, reach2)], scale.at[pl.ds(reach2, reach2)])
    for one in copies:
        one.start()

    for field in range(2):
        for row in range(REACH):
            for end in range(2):
                after[2 * end + field, 3 * REACH * end + row] = jnp.zeros((size_y + 2 * PAD, size_z), F32)
        for row in range(reach2):
            low = side[row, field * REACH : (field + 1) * REACH, :]
            fill_sides(now, REACH + row, low, field, size_y, gy)
            high = side[rows - reach2 + row, field * REACH : (field + 1) * REACH, :]
            fill_sides(now, row, high, 2 + field, size_y, gy)
            for end in range(2):
                blank_sides(after, REACH + row, 2 * end + field, size_y)
    side_out[...] = side_in[...]
    for one in copies:
        one.wait()
    masks = z_weights(size_z)

    def first(row, carry):
        for field in range(2):
            for end in range(2):
                group = 2 * end + field
                to = REACH * (1 + end) + row
                first_step(
                    now, REACH + row, before, row, scale, (2 * end + end) * REACH + row,
                    after, to, group, masks,
                )
                side_out[field, pl.ds(end * (rows - REACH) + row, 1), :] = side_term(
                    after, to, group, size_y, gy
                )
        return carry

    lax.fori_loop(0, REACH, first, 0)
    kept_lines = pl.ds(PAD, lines, stride=KEEP_EVERY)
    for field in range(2):
        for row in range(REACH):
            down[field, row] = after[field, REACH + row, kept_lines, :]
            up[field, row] = after[2 + field, reach2 + row, kept_lines, :]

    def second(row, carry):
        for field in range(2):
            for end in range(2):
                group = 2 * end + field

                def store(here, value):
                    partial[field, end, row, here, :] = value

                second_step(
                    now, (1 - end) * REACH + row, scale, end * reach2 + row, after, REACH + row, group, masks, store
                )
        return carry

    lax.fori_loop(0, reach2, second, 0)


def outer(place, source, receiver, source_before, receiver_before, courant, border, left, right, side, side_in):
    rows, size_y, size_z = courant.shape
    lines = size_y // KEEP_EVERY
    halo = jax.ShapeDtypeStruct((2, REACH, lines, size_z), F32)
    return pl.pallas_call(
        outer_kernel,
        out_shape=(
            jax.ShapeDtypeStruct((2, 2, 2 * REACH, lines, size_z), F32),
            halo,
            halo,
            jax.ShapeDtypeStruct((2, rows, size_z), F32),
        ),
        in_specs=[SMEM] + [HBM] * 8 + [VMEM] * 2,
        out_specs=(VMEM,) * 4,
        scratch_shapes=[
            pltpu.VMEM((4, 3 * REACH, size_y + 2 * PAD, size_z), F32),
            pltpu.VMEM((4, REACH, size_y, size_z), F32),
            pltpu.VMEM((4 * REACH, size_y, size_z), F32),
            pltpu.VMEM((4, 4 * REACH, size_y + 2 * PAD, size_z), F32),
            pltpu.SemaphoreType.DMA((18,)),
        ],
        compiler_params=params(60),
        cost_estimate=cost(2 * 10**10, 16 * 2**20),
        name="outer",
    )(place, source, receiver, source_before, receiver_before, courant, border, left, right, side, side_in)


def pack_row(value, field, row, shot, keep, give):
    first, second = z_halves(value)
    keep[field, row] = jnp.where(shot == 0, first, second)
    give[field, row] = jnp.where(shot == 0, second, first)


def side_lines(side, field, row, gy, lines):
    line = lax.broadcasted_iota(jnp.int32, (lines, side.shape[2]), 0)
    meets = line == jnp.where(gy == 0, lines - 1, 0)
    return jnp.where(meets, side[field, pl.ds(row, 1), :], 0.0)


def middle_kernel(place, inside, ends, kept_courant, side, keep, give):
    shot, gy = place[0], place[1]
    rows, lines, _ = kept_courant.shape

    def one_row(row, values):
        for field in range(2):
            total = side_lines(side, field, row, gy, lines)
            pack_row(values[field] + kept_courant[row] * total, field, row - REACH, shot, keep, give)

    def middle(row, carry):
        one_row(row, [inside[field, row - 2 * REACH] for field in range(2)])
        return carry

    lax.fori_loop(2 * REACH, rows - 2 * REACH, middle, 0)
    for row in range(REACH, 2 * REACH):
        one_row(row, [ends[field, 0, row] for field in range(2)])
        one_row(rows - 1 - row, [ends[field, 1, 2 * REACH - 1 - row] for field in range(2)])


def finish_middle(place, inside, ends, kept_courant, side):
    rows, lines, size_z = kept_courant.shape
    half = jax.ShapeDtypeStruct((2, rows - 2 * REACH, lines // 2, size_z), F32)
    return pl.pallas_call(
        middle_kernel,
        out_shape=(half, half),
        in_specs=[SMEM] + [VMEM] * 4,
        out_specs=(VMEM,) * 2,
        compiler_params=params(24),
        cost_estimate=cost(10**10, 3 * 2**20),
        name="finish_middle",
    )(place, inside, ends, kept_courant, side)


def ends_kernel(place, ends, kept_courant, left, right, side, keep, give):
    shot, gy = place[0], place[1]
    rows, lines, _ = kept_courant.shape
    for field in range(2):
        for row in range(REACH):
            below = above = None
            for d in range(row + 1, REACH + 1):
                term = WEIGHTS[d] * left[field, REACH + row - d]
                below = term if below is None else below + term
                term = WEIGHTS[d] * right[field, d - 1 - row]
                above = term if above is None else above + term
            far = rows - 1 - row
            below = below + side_lines(side, field, row, gy, lines)
            above = above + side_lines(side, field, far, gy, lines)
            pack_row(ends[field, 0, row] + kept_courant[row] * below, field, row, shot, keep, give)
            pack_row(
                ends[field, 1, 2 * REACH - 1 - row] + kept_courant[far] * above,
                field, 2 * REACH - 1 - row, shot, keep, give,
            )


def finish_ends(place, ends, kept_courant, left, right, side):
    _, lines, size_z = kept_courant.shape
    half = jax.ShapeDtypeStruct((2, 2 * REACH, lines // 2, size_z), F32)
    return pl.pallas_call(
        ends_kernel,
        out_shape=(half, half),
        in_specs=[SMEM] + [VMEM] * 5,
        out_specs=(VMEM,) * 2,
        compiler_params=params(24),
        cost_estimate=cost(10**10, 3 * 2**20),
        name="finish_ends",
    )(place, ends, kept_courant, left, right, side)


def image_kernel(place, *refs):
    blocks, (out, rows_of, turned, sems) = refs[:12], refs[12:]
    parity = place[2]
    rows = blocks[0].shape[2]

    @pl.when(pl.program_id(0) == 0)
    def _():
        starts = (HALF, jnp.where(parity == 0, HALF + rows, 0), jnp.where(parity == 0, 0, HALF + rows))
        copies = []

        def copy(src, group, start, count):
            dst = rows_of.at[group, :, pl.ds(start, count)]
            copies.append(pltpu.make_async_copy(src, dst, sems.at[len(copies)]))

        for part in range(2):
            for kind in range(3):
                copy(blocks[kind].at[part], part, starts[kind], rows)
                copy(blocks[3 + 3 * part + kind], 2 + part, starts[kind] + REACH, rows - 2 * REACH)
            for kind, start in enumerate((HALF, 0, HALF + rows)):
                ends = blocks[9 + kind]
                copy(ends.at[part, :, pl.ds(0, REACH)], 2 + part, start, REACH)
                copy(ends.at[part, :, pl.ds(REACH, REACH)], 2 + part, start + rows - REACH, REACH)
        run_copies(copies)

    groups = rows_of.shape[0]
    lines, size_z = rows_of.shape[3], rows_of.shape[4]
    sample = 4 * pl.program_id(0)
    for chunk in range(lines // 8):
        here = pl.ds(8 * chunk, 8)
        for shift in range(OFFSETS):
            total = None
            for group in range(groups):
                term = (
                    rows_of[group, 0, 2 * HALF + sample - shift, here, :]
                    * rows_of[group, 1, sample + shift, here, :]
                )
                total = term if total is None else total + term
            turned[pl.ds(shift, 8, stride=OFFSET_ROWS), :] = total
        for line in range(8):
            values = turned[line * OFFSET_ROWS : (line + 1) * OFFSET_ROWS, :].T
            at = 8 * chunk + line
            out[0, at] = values[: size_z // 2, :OFFSETS]
            out[0, lines + at] = values[size_z // 2 :, :OFFSETS]


def image(place, blocks):
    rows, lines, size_z = blocks[0].shape[2:]
    samples = rows // 4
    return pl.pallas_call(
        image_kernel,
        grid=(samples,),
        out_shape=jax.ShapeDtypeStruct((samples, 2 * lines, size_z // 2, OFFSETS), F32),
        in_specs=[SMEM] + [HBM] * len(blocks),
        out_specs=pl.BlockSpec((1, 2 * lines, size_z // 2, OFFSETS), lambda i: (i, 0, 0, 0)),
        scratch_shapes=[
            pltpu.VMEM((4, 2, rows + 2 * HALF, lines, size_z), F32),
            pltpu.VMEM((8 * OFFSET_ROWS, size_z), F32),
            pltpu.SemaphoreType.DMA((24,)),
        ],
        compiler_params=params(24),
        cost_estimate=cost(16 * 2**20, 16 * 2**20),
        name="image",
    )(place, *blocks)


def in_order_kernel(place, *refs):
    refs[-1][...] = place[...]


def in_order(place, *arrays):
    return pl.pallas_call(
        in_order_kernel,
        out_shape=jax.ShapeDtypeStruct((8, 128), jnp.int32),
        in_specs=[VMEM] + [HBM] * len(arrays),
        out_specs=VMEM,
        cost_estimate=cost(10**10, 2**10),
        name="in_order",
    )(jnp.broadcast_to(jnp.pad(place, (0, 125)), (8, 128)), *arrays)[0, :3]


def on_device(source_now, source_before, receiver_now, receiver_before, courant):
    size = lax.axis_size("gx")
    place = jnp.stack(
        [lax.axis_index("shot"), lax.axis_index("gy"), lax.axis_index("gx") % 2]
    ).astype(jnp.int32)
    up_pairs = [(i, i + 1) for i in range(size - 1)]
    down_pairs = [(j, i) for i, j in up_pairs]
    partner = [(i, i ^ 1) for i in range(size)]
    onward = [(i, i + 2) for i in range(0, size - 2, 2)] + [(i, i - 2) for i in range(3, size, 2)]
    both = [(0, 1), (1, 0)]

    def exchange(array, axis, pairs):
        return lax.ppermute(array, axis, pairs)

    barrier = lax.optimization_barrier
    up, down, keep, give, side = pack(place, source_now, receiver_now)
    left = exchange(up, "gx", up_pairs)
    right = exchange(down, "gx", down_pairs)
    side = exchange(side, "gy", both)
    other = exchange(give, "shot", both)
    own = jnp.stack([keep, other])
    side, own = barrier((side, own))
    near = exchange(own, "gx", partner)
    inside, kept_courant, side_in, border = inner(
        place, source_now, receiver_now, source_before, receiver_before, courant, side
    )
    ends, up, down, side = outer(
        place, source_now, receiver_now, source_before, receiver_before, courant, border, left, right, side, side_in
    )
    left = exchange(up, "gx", up_pairs)
    right = exchange(down, "gx", down_pairs)
    side = exchange(side, "gy", both)

    keep, give = finish_middle(place, inside, ends, kept_courant, side)
    keep, give, near = barrier((keep, give, near))
    far = exchange(near, "gx", onward)
    other = exchange(give, "shot", both)
    near_keep = exchange(keep, "gx", partner)
    middle = [keep, other]

    keep, give = finish_ends(place, ends, kept_courant, left, right, side)
    middle[1], keep, give = barrier((middle[1], keep, give))
    near_other = exchange(middle[1], "gx", partner)
    other = exchange(give, "shot", both)
    blocks = [own, near, far]
    other, near_keep = barrier((other, near_keep))
    own = jnp.stack([keep, other])
    left = exchange(own, "gx", up_pairs)
    right = exchange(own, "gx", down_pairs)
    near_keep, far = barrier((near_keep, far))
    blocks[2] = far
    far_keep = exchange(near_keep, "gx", onward)
    far_other = exchange(near_other, "gx", onward)
    place = in_order(place, left, right, far_keep)
    keep, other = middle
    blocks[1] = near
    blocks += [keep, near_keep, far_keep, other, near_other, far_other, own, left, right]
    return jnp.transpose(image(place, blocks), (3, 0, 1, 2))


def solution(mesh):
    in_specs = (
        P("shot", "gx", "gy", None),
        P("shot", "gx", "gy", None),
        P("shot", "gx", "gy", None),
        P("shot", "gx", "gy", None),
        P("gx", "gy", None),
    )
    out_specs = P(None, "gx", "gy", "shot")
    return jax.shard_map(
        on_device, mesh=mesh, in_specs=in_specs, out_specs=out_specs, check_vma=False
    )
```

time: 132 us -> 127 us (0.962); the launches traced: 132 us -> 125 us
  waiting for transfers between devices: 51.1 us -> 30.3 us
  local copies, waits for them, and re-layouts: 2.28 us -> 11.4 us
  Pallas kernels: 41.3 us -> 44.8 us
    ppermute x16 -> x17, waiting for transfers between devices: 51.1 us -> 30.3 us  [exchange(): return lax.ppermute(array, axis, pairs)]
    unnamed x14 -> x38, local copies, waits for them, and re-layouts: 2.28 us -> 10.1 us
    pallas_call x5 -> x7, Pallas kernels: 41.3 us -> 44.8 us  [the longest x1 17.6 us: inner(): pl.pallas_call(inner_kernel, out_shape=(jax.ShapeDtypeStruct((2, rows - 4...]
    ppermute x16 -> x17, starting transfers between devices: 36.5 us -> 37 us  [exchange(): return lax.ppermute(array, axis, pairs)]
  transfers between devices with their start and end apart: 16 -> 17, of which waited for: 9 -> 5; matrix products, arithmetic and copies ran while one was open for 0% -> 2% of each run, Pallas kernels for 22% -> 25%
where the time goes in v3:
time: 127 us; the launch traced here: 125 us
  Pallas kernels  44.8 us (35%)
  starting transfers between devices  37 us (29%)
  waiting for transfers between devices  30.3 us (24%)
  local copies, waits for them, and re-layouts  11.4 us (9%)
  other arithmetic  1.8 us (1%)
    ppermute x17, starting transfers between devices, exchange(): return lax.ppermute(array, axis, pairs)  37 us
    ppermute x17, waiting for transfers between devices, exchange(): return lax.ppermute(array, axis, pairs)  30.3 us
    pallas_call x1, Pallas kernels, inner(): pl.pallas_call(inner_kernel, out_shape=(jax.ShapeDtypeStruct((2, rows - 4...  17.6 us
    unnamed x38, local copies, waits for them, and re-layouts  10.1 us
    pallas_call x1, Pallas kernels, outer(): pl.pallas_call(outer_kernel, out_shape=(jax.ShapeDtypeStruct((2, 2, 2 * R...  9.36 us
    pallas_call x1, Pallas kernels, image(): pl.pallas_call(image_kernel, grid=(samples,), out_shape=jax.ShapeDtypeStr...  9.36 us
    pallas_call x1, Pallas kernels, pack(): pl.pallas_call(pack_kernel, grid=(rows // step,), out_shape=(edge, edge,...  4.48 us
  transfers between devices with their start and end apart: 17, of which 5 were waited for; matrix products, arithmetic and copies ran while one was open for 2% of the time, Pallas kernels for 25%

profile of v3, /device:TPU:0, one launch (start us, length us, event | category | flops | bytes accessed | tf_op | source)
XLA Modules:
  0.0 125.5 jit_solution(3211035085986829986)
XLA Ops:
  0.7 4.5 %pack.1 = (f32[2,4,128,128]{3,2,1,0:T(8,128)}, f32[2,4,128,128]{3,2,1,0:T(8,128)}, f32[2,32,16,128]{3,2,1,0:T(8,128)}, f32[2,32,16,128]{3,2,1,0:T(8,128)}, f32[32,8,128]{2,1,0:T(8,128)}) custom-call(s32[3]{0:T(128)} %pad_add_fusion.place, f32[1,32,128,128]{3,2,1,0:T(8,128)} %source.5, f32[1,32,128,128]{3,2,1,0:T(8,128)} %receiver.5), custom_call_target="tpu_custom_call" | custom-call | flops 10000000000 | bytes 7340032 | tf_op jit(solution)/shard_map/pack/pallas_call | solution.py:84
  5.6 4.5 %collective-permute-start.2 = (f32[2,4,128,128]{3,2,1,0:T(8,128)}, f32[2,4,128,128]{3,2,1,0:T(8,128)S(1)}, u32[]{:S(2)}, u32[]{:S(2)}) collective-permute-start(f32[2,4,128,128]{3,2,1,0:T(8,128)} %get-tuple-element.40), channel_id=1, source_target_pairs={{0,2},{2,4},{4,6},{6,8},{8,10},{10,12},{12,14},{1,3},{3,5},{5,7},{... | collective-permute-start | bytes 1572872 | tf_op jit(solution)/shard_map/ppermute | solution.py:561
  10.1 1.3 %collective-permute-start.3 = (f32[2,4,128,128]{3,2,1,0:T(8,128)}, f32[2,4,128,128]{3,2,1,0:T(8,128)S(1)}, u32[]{:S(2)}, u32[]{:S(2)}) collective-permute-start(f32[2,4,128,128]{3,2,1,0:T(8,128)} %get-tuple-element.41), channel_id=1, source_target_pairs={{2,0},{4,2},{6,4},{8,6},{10,8},{12,10},{14,12},{3,1},{5,3},{7,5},{... | collective-permute-start | bytes 1572872 | tf_op jit(solution)/shard_map/ppermute | solution.py:561
  11.4 1.6 %collective-permute-start = (f32[32,8,128]{2,1,0:T(8,128)}, f32[32,8,128]{2,1,0:T(8,128)S(1)}, u32[]{:S(2)}, u32[]{:S(2)}) collective-permute-start(f32[32,8,128]{2,1,0:T(8,128)} %get-tuple-element.34), channel_id=1, source_target_pairs={{0,1},{1,0},{2,3},{3,2},{4,5},{5,4},{6,7},{7,6},{8,9},{9,8},{10,11... | collective-permute-start | bytes 393224 | tf_op jit(solution)/shard_map/ppermute | solution.py:561
  14.1 3.2 %collective-permute-done.side = f32[32,8,128]{2,1,0:T(8,128)S(1)} collective-permute-done((f32[32,8,128]{2,1,0:T(8,128)}, f32[32,8,128]{2,1,0:T(8,128)S(1)}, u32[]{:S(2)}, u32[]{:S(2)}) %collective-permute-start) | collective-permute-done | bytes 131104 | tf_op jit(solution)/shard_map/ppermute | solution.py:561
  17.3 2.4 %collective-permute-start.5 = (f32[2,2,32,16,128]{4,3,2,1,0:T(8,128)S(1)}, f32[2,2,32,16,128]{4,3,2,1,0:T(8,128)S(1)}, u32[]{:S(2)}, u32[]{:S(2)}) collective-permute-start(f32[2,2,32,16,128]{4,3,2,1,0:T(8,128)S(1)} %pad_maximum_fusion.refs_0_), channel_id=1, source_target_pairs={{0,2},{2,0},{4,6},{6,4},{8,10},{10,8},{12,14},{14,12},{1,3},{3,1},... | collective-permute-start | bytes 3145736 | tf_op jit(solution)/shard_map/ppermute | solution.py:561
  19.6 17.6 %inner.1 = (f32[2,16,32,128]{3,2,1,0:T(8,128)}, f32[32,32,128]{2,1,0:T(8,128)}, f32[2,32,128]{2,1,0:T(8,128)}, f32[2,2,8,128,128]{4,3,2,1,0:T(8,128)}) custom-call(s32[3]{0:T(128)} %pad_add_fusion.place, f32[1,32,128,128]{3,2,1,0:T(8,128)} %source.5, f32[1,32,128,128]{3,2,1,0:T(8,128)} %receiver.5, f32[1,32,128,128]{3,2,1,0:T(8,128)} %source_before.3, ...), custom_call_target="tpu_custom_call" | custom-call | flops 1000000 | bytes 1048576 | tf_op jit(solution)/shard_map/inner/pallas_call | solution.py:255
  38.3 9.4 %outer.1 = (f32[2,2,8,32,128]{4,3,2,1,0:T(8,128)}, f32[2,4,32,128]{3,2,1,0:T(8,128)}, f32[2,4,32,128]{3,2,1,0:T(8,128)}, f32[2,32,128]{2,1,0:T(8,128)}) custom-call(s32[3]{0:T(128)} %pad_add_fusion.place, f32[1,32,128,128]{3,2,1,0:T(8,128)} %source.5, f32[1,32,128,128]{3,2,1,0:T(8,128)} %receiver.5, f32[1,32,128,128]{3,2,1,0:T(8,128)} %source_before.3, ...), custom_call_target="tpu_custom_call" | custom-call | flops 20000000000 | bytes 16777216 | tf_op jit(solution)/shard_map/outer/pallas_call | solution.py:366
  47.6 1.6 %collective-permute-start.4 = (f32[2,32,128]{2,1,0:T(8,128)}, f32[2,32,128]{2,1,0:T(8,128)S(1)}, u32[]{:S(2)}, u32[]{:S(2)}) collective-permute-start(f32[2,32,128]{2,1,0:T(8,128)} %get-tuple-element.45), channel_id=1, source_target_pairs={{0,1},{1,0},{2,3},{3,2},{4,5},{5,4},{6,7},{7,6},{8,9},{9,8},{10,11... | collective-permute-start | bytes 98312 | tf_op jit(solution)/shard_map/ppermute | solution.py:561
  49.2 2.5 %collective-permute-start.7 = (f32[2,4,32,128]{3,2,1,0:T(8,128)}, f32[2,4,32,128]{3,2,1,0:T(8,128)S(1)}, u32[]{:S(2)}, u32[]{:S(2)}) collective-permute-start(f32[2,4,32,128]{3,2,1,0:T(8,128)} %get-tuple-element.50), channel_id=1, source_target_pairs={{0,2},{2,4},{4,6},{6,8},{8,10},{10,12},{12,14},{1,3},{3,5},{5,7},{... | collective-permute-start | bytes 393224 | tf_op jit(solution)/shard_map/ppermute | solution.py:561
  51.7 1.3 %collective-permute-start.8 = (f32[2,4,32,128]{3,2,1,0:T(8,128)}, f32[2,4,32,128]{3,2,1,0:T(8,128)S(1)}, u32[]{:S(2)}, u32[]{:S(2)}) collective-permute-start(f32[2,4,32,128]{3,2,1,0:T(8,128)} %get-tuple-element.51), channel_id=1, source_target_pairs={{2,0},{4,2},{6,4},{8,6},{10,8},{12,10},{14,12},{3,1},{5,3},{7,5},{... | collective-permute-start | bytes 393224 | tf_op jit(solution)/shard_map/ppermute | solution.py:561
  54.1 2.0 %finish_middle.1 = (f32[2,24,16,128]{3,2,1,0:T(8,128)S(1)}, f32[2,24,16,128]{3,2,1,0:T(8,128)S(1)}) custom-call(s32[3]{0:T(128)S(1)} %copy-done.12, f32[2,16,32,128]{3,2,1,0:T(8,128)S(1)} %copy-done.14, f32[2,2,8,32,128]{4,3,2,1,0:T(8,128)S(1)} %copy-done.15, f32[32,32,128]{2,1,0:T(8,128)S(1)} %copy-done.13, f32[2,32,128]{2,1,0:T(8,128)S(1)} %collective-permute-done.4.side), custom_call_target="tpu_custom_call" | custom-call | flops 10000000000 | bytes 3145728 | tf_op jit(solution)/shard_map/finish_middle/pallas_call | solution.py:423
  56.2 1.3 %collective-permute-done.5.refs_1_ = f32[2,2,32,16,128]{4,3,2,1,0:T(8,128)S(1)} collective-permute-done((f32[2,2,32,16,128]{4,3,2,1,0:T(8,128)S(1)}, f32[2,2,32,16,128]{4,3,2,1,0:T(8,128)S(1)}, u32[]{:S(2)}, u32[]{:S(2)}) %collective-permute-start.5) | collective-permute-done | bytes 1048608 | tf_op jit(solution)/shard_map/ppermute | solution.py:561
  57.5 2.6 %collective-permute-start.10 = (f32[2,24,16,128]{3,2,1,0:T(8,128)S(1)}, f32[2,24,16,128]{3,2,1,0:T(8,128)S(1)}, u32[]{:S(2)}, u32[]{:S(2)}) collective-permute-start(f32[2,24,16,128]{3,2,1,0:T(8,128)S(1)} %get-tuple-element.56.refs_3_), channel_id=1, source_target_pairs={{0,2},{2,0},{4,6},{6,4},{8,10},{10,8},{12,14},{14,12},{1,3},{3,1},... | collective-permute-start | bytes 1179656 | tf_op jit(solution)/shard_map/ppermute | solution.py:561
  60.1 4.0 %collective-permute-start.13 = (f32[2,2,32,16,128]{4,3,2,1,0:T(8,128)S(1)}, f32[2,2,32,16,128]{4,3,2,1,0:T(8,128)S(1)}, u32[]{:S(2)}, u32[]{:S(2)}) collective-permute-start(f32[2,2,32,16,128]{4,3,2,1,0:T(8,128)S(1)} %collective-permute-done.5.refs_1_), channel_id=1, source_target_pairs={{0,4},{4,8},{8,12},{6,2},{10,6},{14,10},{1,5},{5,9},{9,13},{7,3},{... | collective-permute-start | bytes 3145736 | tf_op jit(solution)/shard_map/ppermute | solution.py:561
  65.2 5.1 %collective-permute-done.10.refs_4_ = f32[2,24,16,128]{3,2,1,0:T(8,128)S(1)} collective-permute-done((f32[2,24,16,128]{3,2,1,0:T(8,128)S(1)}, f32[2,24,16,128]{3,2,1,0:T(8,128)S(1)}, u32[]{:S(2)}, u32[]{:S(2)}) %collective-permute-start.10) | collective-permute-done | bytes 393248 | tf_op jit(solution)/shard_map/ppermute | solution.py:561
  70.3 16.8 %collective-permute-done.13.refs_2_ = f32[2,2,32,16,128]{4,3,2,1,0:T(8,128)S(1)} collective-permute-done((f32[2,2,32,16,128]{4,3,2,1,0:T(8,128)S(1)}, f32[2,2,32,16,128]{4,3,2,1,0:T(8,128)S(1)}, u32[]{:S(2)}, u32[]{:S(2)}) %collective-permute-start.13) | collective-permute-done | bytes 1048608 | tf_op jit(solution)/shard_map/ppermute | solution.py:561
  87.1 4.4 %collective-permute-start.14 = (f32[2,24,16,128]{3,2,1,0:T(8,128)S(1)}, f32[2,24,16,128]{3,2,1,0:T(8,128)S(1)}, u32[]{:S(2)}, u32[]{:S(2)}) collective-permute-start(f32[2,24,16,128]{3,2,1,0:T(8,128)S(1)} %collective-permute-done.10.refs_4_), channel_id=1, source_target_pairs={{0,4},{4,8},{8,12},{6,2},{10,6},{14,10},{1,5},{5,9},{9,13},{7,3},{... | collective-permute-start | bytes 1179656 | tf_op jit(solution)/shard_map/ppermute | solution.py:561
  92.3 1.3 %collective-permute-start.12 = (f32[2,2,8,16,128]{4,3,2,1,0:T(8,128)S(1)}, f32[2,2,8,16,128]{4,3,2,1,0:T(8,128)S(1)}, u32[]{:S(2)}, u32[]{:S(2)}) collective-permute-start(f32[2,2,8,16,128]{4,3,2,1,0:T(8,128)S(1)} %pad_maximum_fusion.1.refs_9_), channel_id=1, source_target_pairs={{2,0},{4,2},{6,4},{8,6},{10,8},{12,10},{14,12},{3,1},{5,3},{7,5},{... | collective-permute-start | bytes 786440 | tf_op jit(solution)/shard_map/ppermute | solution.py:561
  93.6 4.6 %collective-permute-start.11 = (f32[2,2,8,16,128]{4,3,2,1,0:T(8,128)S(1)}, f32[2,2,8,16,128]{4,3,2,1,0:T(8,128)S(1)}, u32[]{:S(2)}, u32[]{:S(2)}) collective-permute-start(f32[2,2,8,16,128]{4,3,2,1,0:T(8,128)S(1)} %pad_maximum_fusion.1.refs_9_), channel_id=1, source_target_pairs={{0,2},{2,4},{4,6},{6,8},{8,10},{10,12},{12,14},{1,3},{3,5},{5,7},{... | collective-permute-start | bytes 786440 | tf_op jit(solution)/shard_map/ppermute | solution.py:561
  98.2 4.2 %collective-permute-start.16 = (f32[2,24,16,128]{3,2,1,0:T(8,128)}, f32[2,24,16,128]{3,2,1,0:T(8,128)}, u32[]{:S(2)}, u32[]{:S(2)}) collective-permute-start(f32[2,24,16,128]{3,2,1,0:T(8,128)} %collective-permute-done.15.refs_7_), channel_id=1, source_target_pairs={{0,4},{4,8},{8,12},{6,2},{10,6},{14,10},{1,5},{5,9},{9,13},{7,3},{... | collective-permute-start | bytes 1179656 | tf_op jit(solution)/shard_map/ppermute | solution.py:561
  102.4 3.9 %collective-permute-done.11.refs_0_.refs_10_ = f32[2,2,8,16,128]{4,3,2,1,0:T(8,128)S(1)} collective-permute-done((f32[2,2,8,16,128]{4,3,2,1,0:T(8,128)S(1)}, f32[2,2,8,16,128]{4,3,2,1,0:T(8,128)S(1)}, u32[]{:S(2)}, u32[]{:S(2)}) %collective-permute-start.11) | collective-permute-done | bytes 262176 | tf_op jit(solution)/shard_map/ppermute | solution.py:561
  108.3 1.3 %in_order.1 = s32[8,128]{1,0:T(8,128)} custom-call(s32[8,128]{1,0:T(8,128)} %broadcast_in_dim.3.place, f32[2,2,8,16,128]{4,3,2,1,0:T(8,128)} %copy-done.10, f32[2,2,8,16,128]{4,3,2,1,0:T(8,128)} %copy-done.8, f32[2,24,16,128]{3,2,1,0:T(8,128)} %copy-done.6), custom_call_target="tpu_custom_call" | custom-call | flops 10000000000 | bytes 1024 | tf_op jit(solution)/shard_map/in_order/pallas_call | solution.py:539
  116.1 9.4 %image.1 = f32[8,32,64,65]{3,2,1,0:T(8,128)} custom-call(s32[3]{0:T(128)S(1)} %slice_bitcast_fusion.place, f32[2,2,32,16,128]{4,3,2,1,0:T(8,128)S(1)} %pad_maximum_fusion.refs_0_, f32[2,2,32,16,128]{4,3,2,1,0:T(8,128)S(1)} %collective-permute-done.5.refs_1_, f32[2,2,32,16,128]{4,3,2,1,0:T(8,128)S(1)} %collective-permute-done.13.refs_2_, ...), custom_call_target="tpu_custom_call" | custom-call | flops 16777216 | bytes 16777216 | tf_op jit(solution)/shard_map/image/pallas_call | solution.py:517
  (61 shorter events, 14.7 us)
Async XLA Ops:
  5.1 7.8 %collective-permute-start.1 = (f32[2,32,16,128]{3,2,1,0:T(8,128)}, f32[2,32,16,128]{3,2,1,0:T(8,128)S(1)}, u32[]{:S(2)}, u32[]{:S(2)}) collective-permute-start(f32[2,32,16,128]{3,2,1,0:T(8,128)} %get-tuple-element.36), channel_id=1, source_target_pairs={{0,16},{16,0},{1,17},{17,1},{2,18},{18,2},{3,19},{19,3},{4,20},{20... | collective-permute-start | bytes 1572872 | tf_op jit(solution)/shard_map/ppermute | solution.py:561
  5.6 31.6 %collective-permute-start.2 = (f32[2,4,128,128]{3,2,1,0:T(8,128)}, f32[2,4,128,128]{3,2,1,0:T(8,128)S(1)}, u32[]{:S(2)}, u32[]{:S(2)}) collective-permute-start(f32[2,4,128,128]{3,2,1,0:T(8,128)} %get-tuple-element.40), channel_id=1, source_target_pairs={{0,2},{2,4},{4,6},{6,8},{8,10},{10,12},{12,14},{1,3},{3,5},{5,7},{... | collective-permute-start | bytes 1572872 | tf_op jit(solution)/shard_map/ppermute | solution.py:561
  10.1 27.2 %collective-permute-start.3 = (f32[2,4,128,128]{3,2,1,0:T(8,128)}, f32[2,4,128,128]{3,2,1,0:T(8,128)S(1)}, u32[]{:S(2)}, u32[]{:S(2)}) collective-permute-start(f32[2,4,128,128]{3,2,1,0:T(8,128)} %get-tuple-element.41), channel_id=1, source_target_pairs={{2,0},{4,2},{6,4},{8,6},{10,8},{12,10},{14,12},{3,1},{5,3},{7,5},{... | collective-permute-start | bytes 1572872 | tf_op jit(solution)/shard_map/ppermute | solution.py:561
  11.4 5.9 %collective-permute-start = (f32[32,8,128]{2,1,0:T(8,128)}, f32[32,8,128]{2,1,0:T(8,128)S(1)}, u32[]{:S(2)}, u32[]{:S(2)}) collective-permute-start(f32[32,8,128]{2,1,0:T(8,128)} %get-tuple-element.34), channel_id=1, source_target_pairs={{0,1},{1,0},{2,3},{3,2},{4,5},{5,4},{6,7},{7,6},{8,9},{9,8},{10,11... | collective-permute-start | bytes 393224 | tf_op jit(solution)/shard_map/ppermute | solution.py:561
  17.3 2.4 %copy-start.16 = (f32[32,8,128]{2,1,0:T(8,128)}, f32[32,8,128]{2,1,0:T(8,128)S(1)}, u32[]{:S(2)}) copy-start(f32[32,8,128]{2,1,0:T(8,128)S(1)} %collective-permute-done.side) | copy-start | bytes 393220
  17.3 40.2 %collective-permute-start.5 = (f32[2,2,32,16,128]{4,3,2,1,0:T(8,128)S(1)}, f32[2,2,32,16,128]{4,3,2,1,0:T(8,128)S(1)}, u32[]{:S(2)}, u32[]{:S(2)}) collective-permute-start(f32[2,2,32,16,128]{4,3,2,1,0:T(8,128)S(1)} %pad_maximum_fusion.refs_0_), channel_id=1, source_target_pairs={{0,2},{2,0},{4,6},{6,4},{8,10},{10,8},{12,14},{14,12},{1,3},{3,1},... | collective-permute-start | bytes 3145736 | tf_op jit(solution)/shard_map/ppermute | solution.py:561
  38.3 14.8 %copy-start.12 = (s32[3]{0:T(128)S(1)}, s32[3]{0:T(128)}, u32[]{:S(2)}) copy-start(s32[3]{0:T(128)} %pad_add_fusion.place) | copy-start | bytes 40
  38.3 14.8 %copy-start.13 = (f32[32,32,128]{2,1,0:T(8,128)S(1)}, f32[32,32,128]{2,1,0:T(8,128)}, u32[]{:S(2)}) copy-start(f32[32,32,128]{2,1,0:T(8,128)} %get-tuple-element.44.kept_courant) | copy-start | bytes 1572868
  38.3 14.8 %copy-start.14 = (f32[2,16,32,128]{3,2,1,0:T(8,128)S(1)}, f32[2,16,32,128]{3,2,1,0:T(8,128)}, u32[]{:S(2)}) copy-start(f32[2,16,32,128]{3,2,1,0:T(8,128)} %get-tuple-element.38.inside) | copy-start | bytes 1572868
  47.6 5.4 %collective-permute-start.4 = (f32[2,32,128]{2,1,0:T(8,128)}, f32[2,32,128]{2,1,0:T(8,128)S(1)}, u32[]{:S(2)}, u32[]{:S(2)}) collective-permute-start(f32[2,32,128]{2,1,0:T(8,128)} %get-tuple-element.45), channel_id=1, source_target_pairs={{0,1},{1,0},{2,3},{3,2},{4,5},{5,4},{6,7},{7,6},{8,9},{9,8},{10,11... | collective-permute-start | bytes 98312 | tf_op jit(solution)/shard_map/ppermute | solution.py:561
  49.2 14.9 %collective-permute-start.7 = (f32[2,4,32,128]{3,2,1,0:T(8,128)}, f32[2,4,32,128]{3,2,1,0:T(8,128)S(1)}, u32[]{:S(2)}, u32[]{:S(2)}) collective-permute-start(f32[2,4,32,128]{3,2,1,0:T(8,128)} %get-tuple-element.50), channel_id=1, source_target_pairs={{0,2},{2,4},{4,6},{6,8},{8,10},{10,12},{12,14},{1,3},{3,5},{5,7},{... | collective-permute-start | bytes 393224 | tf_op jit(solution)/shard_map/ppermute | solution.py:561
  51.7 12.4 %collective-permute-start.8 = (f32[2,4,32,128]{3,2,1,0:T(8,128)}, f32[2,4,32,128]{3,2,1,0:T(8,128)S(1)}, u32[]{:S(2)}, u32[]{:S(2)}) collective-permute-start(f32[2,4,32,128]{3,2,1,0:T(8,128)} %get-tuple-element.51), channel_id=1, source_target_pairs={{2,0},{4,2},{6,4},{8,6},{10,8},{12,10},{14,12},{3,1},{5,3},{7,5},{... | collective-permute-start | bytes 393224 | tf_op jit(solution)/shard_map/ppermute | solution.py:561
  56.1 8.7 %copy-start = (f32[2,24,16,128]{3,2,1,0:T(8,128)}, f32[2,24,16,128]{3,2,1,0:T(8,128)S(1)}, u32[]{:S(2)}) copy-start(f32[2,24,16,128]{3,2,1,0:T(8,128)S(1)} %get-tuple-element.56.refs_3_) | copy-start | bytes 1179652
  57.5 7.4 %collective-permute-start.6 = (f32[2,24,16,128]{3,2,1,0:T(8,128)S(1)}, f32[2,24,16,128]{3,2,1,0:T(8,128)S(1)}, u32[]{:S(2)}, u32[]{:S(2)}) collective-permute-start(f32[2,24,16,128]{3,2,1,0:T(8,128)S(1)} %get-tuple-element.49), channel_id=1, source_target_pairs={{0,16},{16,0},{1,17},{17,1},{2,18},{18,2},{3,19},{19,3},{4,20},{20... | collective-permute-start | bytes 1179656 | tf_op jit(solution)/shard_map/ppermute | solution.py:561
  57.5 12.8 %collective-permute-start.10 = (f32[2,24,16,128]{3,2,1,0:T(8,128)S(1)}, f32[2,24,16,128]{3,2,1,0:T(8,128)S(1)}, u32[]{:S(2)}, u32[]{:S(2)}) collective-permute-start(f32[2,24,16,128]{3,2,1,0:T(8,128)S(1)} %get-tuple-element.56.refs_3_), channel_id=1, source_target_pairs={{0,2},{2,0},{4,6},{6,4},{8,10},{10,8},{12,14},{14,12},{1,3},{3,1},... | collective-permute-start | bytes 1179656 | tf_op jit(solution)/shard_map/ppermute | solution.py:561
  60.1 27.0 %collective-permute-start.13 = (f32[2,2,32,16,128]{4,3,2,1,0:T(8,128)S(1)}, f32[2,2,32,16,128]{4,3,2,1,0:T(8,128)S(1)}, u32[]{:S(2)}, u32[]{:S(2)}) collective-permute-start(f32[2,2,32,16,128]{4,3,2,1,0:T(8,128)S(1)} %collective-permute-done.5.refs_1_), channel_id=1, source_target_pairs={{0,4},{4,8},{8,12},{6,2},{10,6},{14,10},{1,5},{5,9},{9,13},{7,3},{... | collective-permute-start | bytes 3145736 | tf_op jit(solution)/shard_map/ppermute | solution.py:561
  64.8 41.4 %copy-start.2 = (f32[2,24,16,128]{3,2,1,0:T(8,128)}, f32[2,24,16,128]{3,2,1,0:T(8,128)S(1)}, u32[]{:S(2)}) copy-start(f32[2,24,16,128]{3,2,1,0:T(8,128)S(1)} %collective-permute-done.6.refs_6_) | copy-start | bytes 1179652
  64.8 5.4 %collective-permute-start.9 = (f32[2,8,16,128]{3,2,1,0:T(8,128)S(1)}, f32[2,8,16,128]{3,2,1,0:T(8,128)S(1)}, u32[]{:S(2)}, u32[]{:S(2)}) collective-permute-start(f32[2,8,16,128]{3,2,1,0:T(8,128)S(1)} %get-tuple-element.55), channel_id=1, source_target_pairs={{0,16},{16,0},{1,17},{17,1},{2,18},{18,2},{3,19},{19,3},{4,20},{20... | collective-permute-start | bytes 393224 | tf_op jit(solution)/shard_map/ppermute | solution.py:561
  65.1 33.0 %collective-permute-start.15 = (f32[2,24,16,128]{3,2,1,0:T(8,128)S(1)}, f32[2,24,16,128]{3,2,1,0:T(8,128)}, u32[]{:S(2)}, u32[]{:S(2)}) collective-permute-start(f32[2,24,16,128]{3,2,1,0:T(8,128)S(1)} %collective-permute-done.6.refs_6_), channel_id=1, source_target_pairs={{0,2},{2,0},{4,6},{6,4},{8,10},{10,8},{12,14},{14,12},{1,3},{3,1},... | collective-permute-start | bytes 1179656 | tf_op jit(solution)/shard_map/ppermute | solution.py:561
  87.1 19.2 %collective-permute-start.14 = (f32[2,24,16,128]{3,2,1,0:T(8,128)S(1)}, f32[2,24,16,128]{3,2,1,0:T(8,128)S(1)}, u32[]{:S(2)}, u32[]{:S(2)}) collective-permute-start(f32[2,24,16,128]{3,2,1,0:T(8,128)S(1)} %collective-permute-done.10.refs_4_), channel_id=1, source_target_pairs={{0,4},{4,8},{8,12},{6,2},{10,6},{14,10},{1,5},{5,9},{9,13},{7,3},{... | collective-permute-start | bytes 1179656 | tf_op jit(solution)/shard_map/ppermute | solution.py:561
  92.3 10.1 %collective-permute-start.12 = (f32[2,2,8,16,128]{4,3,2,1,0:T(8,128)S(1)}, f32[2,2,8,16,128]{4,3,2,1,0:T(8,128)S(1)}, u32[]{:S(2)}, u32[]{:S(2)}) collective-permute-start(f32[2,2,8,16,128]{4,3,2,1,0:T(8,128)S(1)} %pad_maximum_fusion.1.refs_9_), channel_id=1, source_target_pairs={{2,0},{4,2},{6,4},{8,6},{10,8},{12,10},{14,12},{3,1},{5,3},{7,5},{... | collective-permute-start | bytes 786440 | tf_op jit(solution)/shard_map/ppermute | solution.py:561
  93.6 12.7 %collective-permute-start.11 = (f32[2,2,8,16,128]{4,3,2,1,0:T(8,128)S(1)}, f32[2,2,8,16,128]{4,3,2,1,0:T(8,128)S(1)}, u32[]{:S(2)}, u32[]{:S(2)}) collective-permute-start(f32[2,2,8,16,128]{4,3,2,1,0:T(8,128)S(1)} %pad_maximum_fusion.1.refs_9_), channel_id=1, source_target_pairs={{0,2},{2,4},{4,6},{6,8},{8,10},{10,12},{12,14},{1,3},{3,5},{5,7},{... | collective-permute-start | bytes 786440 | tf_op jit(solution)/shard_map/ppermute | solution.py:561
  98.2 12.1 %collective-permute-start.16 = (f32[2,24,16,128]{3,2,1,0:T(8,128)}, f32[2,24,16,128]{3,2,1,0:T(8,128)}, u32[]{:S(2)}, u32[]{:S(2)}) collective-permute-start(f32[2,24,16,128]{3,2,1,0:T(8,128)} %collective-permute-done.15.refs_7_), channel_id=1, source_target_pairs={{0,4},{4,8},{8,12},{6,2},{10,6},{14,10},{1,5},{5,9},{9,13},{7,3},{... | collective-permute-start | bytes 1179656 | tf_op jit(solution)/shard_map/ppermute | solution.py:561
  102.4 3.9 %copy-start.8 = (f32[2,2,8,16,128]{4,3,2,1,0:T(8,128)}, f32[2,2,8,16,128]{4,3,2,1,0:T(8,128)S(1)}, u32[]{:S(2)}) copy-start(f32[2,2,8,16,128]{4,3,2,1,0:T(8,128)S(1)} %collective-permute-done.12.refs_1_.refs_11_) | copy-start | bytes 786436
  (12 other events, 11.0 us)

commit v4 on v3

--- a/solution.py
+++ b/solution.py
@@ -16,6 +16,7 @@
 PAD = 8
 F32 = jnp.float32
 HBM = pl.BlockSpec(memory_space=pltpu.HBM)
+ANY = pl.BlockSpec(memory_space=pl.ANY)
 VMEM = pl.BlockSpec(memory_space=pltpu.VMEM)
 SMEM = pl.BlockSpec(memory_space=pltpu.SMEM)
 
@@ -115,7 +116,7 @@
     return total
 
 
-def first_step(now, row, before, before_row, scale, scale_row, after, after_row, field, masks):
+def first_step(now, row, before, before_row, scale, scale_row, after, after_row, field, masks, zero):
     size_y = before.shape[2]
     for chunk in range(size_y // 8):
         at = PAD + 8 * chunk
@@ -125,8 +126,8 @@
             around = (
                 now[field, row + d, at : at + 8, :]
                 + now[field, row - d, at : at + 8, :]
-                + now[field, row, at + d : at + d + 8, :]
-                + now[field, row, at - d : at - d + 8, :]
+                + now[field, row, pl.ds(zero + (at + d), 8), :]
+                + now[field, row, pl.ds(zero + (at - d), 8), :]
             )
             total = total + WEIGHTS[d] * around
         here = pl.ds(8 * chunk, 8)
@@ -213,7 +214,7 @@
 
     def first(row, carry):
         for field in range(2):
-            first_step(now, row, before, row, scale, row, after, row, field, masks)
+            first_step(now, row, before, row, scale, row, after, row, field, masks, place[3])
             side_out[field, pl.ds(row, 1), :] = side_term(after, row, field, size_y, gy)
         return carry
 
@@ -271,7 +272,7 @@
             pltpu.SemaphoreType.DMA((4,)),
         ],
         compiler_params=params(60),
-        cost_estimate=cost(10**6, 2**20),
+        cost_estimate=cost(2 * 10**10, 2**20),
         name="inner",
     )(place, source, receiver, source_before, receiver_before, courant, side)
 
@@ -329,7 +330,7 @@
                 to = REACH * (1 + end) + row
                 first_step(
                     now, REACH + row, before, row, scale, (2 * end + end) * REACH + row,
-                    after, to, group, masks,
+                    after, to, group, masks, place[3],
                 )
                 side_out[field, pl.ds(end * (rows - REACH) + row, 1), :] = side_term(
                     after, to, group, size_y, gy
@@ -381,7 +382,7 @@
             pltpu.SemaphoreType.DMA((18,)),
         ],
         compiler_params=params(60),
-        cost_estimate=cost(2 * 10**10, 16 * 2**20),
+        cost_estimate=cost(10**6, 2**20),
         name="outer",
     )(place, source, receiver, source_before, receiver_before, courant, border, left, right, side, side_in)
 
@@ -466,14 +467,68 @@
     )(place, ends, kept_courant, left, right, side)
 
 
-def image_kernel(place, *refs):
-    blocks, (out, rows_of, turned, sems) = refs[:12], refs[12:]
-    parity = place[2]
-    rows = blocks[0].shape[2]
+def block_starts(place, rows):
+    even = place[2] == 0
+    return HALF, jnp.where(even, HALF + rows, 0), jnp.where(even, 0, HALF + rows)
+
+
+def products(rows_of, sample, shift, here):
+    total = None
+    for group in range(rows_of.shape[0]):
+        term = (
+            rows_of[group, 0, 2 * HALF + sample - shift, here, :]
+            * rows_of[group, 1, sample + shift, here, :]
+        )
+        total = term if total is None else total + term
+    return total
+
+
+def first_image_kernel(place, *refs):
+    blocks, (out, rows_of, sems) = refs[:6], refs[6:]
+    rows = blocks[0].shape[1]
 
     @pl.when(pl.program_id(0) == 0)
     def _():
-        starts = (HALF, jnp.where(parity == 0, HALF + rows, 0), jnp.where(parity == 0, 0, HALF + rows))
+        starts = block_starts(place, rows)
+        copies = []
+        for index, ref in enumerate(blocks):
+            dst = rows_of.at[index // 3, :, pl.ds(starts[index % 3], rows)]
+            copies.append(pltpu.make_async_copy(ref, dst, sems.at[index]))
+        run_copies(copies)
+
+    sample = 4 * pl.program_id(0)
+    for chunk in range(rows_of.shape[3] // 8):
+        here = pl.ds(8 * chunk, 8)
+        for shift in range(OFFSETS):
+            out[0, shift, here, :] = products(rows_of, sample, shift, here)
+
+
+def first_image(place, blocks):
+    _, rows, lines, size_z = blocks[0].shape
+    samples = rows // 4
+    return pl.pallas_call(
+        first_image_kernel,
+        grid=(samples,),
+        out_shape=jax.ShapeDtypeStruct((samples, OFFSETS, lines, size_z), F32),
+        in_specs=[SMEM] + [ANY] * len(blocks),
+        out_specs=pl.BlockSpec((1, OFFSETS, lines, size_z), lambda i: (i, 0, 0, 0)),
+        scratch_shapes=[
+            pltpu.VMEM((2, 2, rows + 2 * HALF, lines, size_z), F32),
+            pltpu.SemaphoreType.DMA((6,)),
+        ],
+        compiler_params=params(16),
+        cost_estimate=cost(10**10, 8 * 2**20),
+        name="first_image",
+    )(place, *blocks)
+
+
+def image_kernel(place, first, *refs):
+    blocks, (out, rows_of, turned, sems) = refs[:9], refs[9:]
+    rows = blocks[0].shape[1] + 2 * REACH
+
+    @pl.when(pl.program_id(0) == 0)
+    def _():
+        starts = block_starts(place, rows)
         copies = []
 
         def copy(src, group, start, count):
@@ -482,27 +537,19 @@
 
         for part in range(2):
             for kind in range(3):
-                copy(blocks[kind].at[part], part, starts[kind], rows)
-                copy(blocks[3 + 3 * part + kind], 2 + part, starts[kind] + REACH, rows - 2 * REACH)
+                copy(blocks[3 * part + kind], part, starts[kind] + REACH, rows - 2 * REACH)
             for kind, start in enumerate((HALF, 0, HALF + rows)):
-                ends = blocks[9 + kind]
-                copy(ends.at[part, :, pl.ds(0, REACH)], 2 + part, start, REACH)
-                copy(ends.at[part, :, pl.ds(REACH, REACH)], 2 + part, start + rows - REACH, REACH)
+                ends = blocks[6 + kind]
+                copy(ends.at[part, :, pl.ds(0, REACH)], part, start, REACH)
+                copy(ends.at[part, :, pl.ds(REACH, REACH)], part, start + rows - REACH, REACH)
         run_copies(copies)
 
-    groups = rows_of.shape[0]
     lines, size_z = rows_of.shape[3], rows_of.shape[4]
     sample = 4 * pl.program_id(0)
     for chunk in range(lines // 8):
         here = pl.ds(8 * chunk, 8)
         for shift in range(OFFSETS):
-            total = None
-            for group in range(groups):
-                term = (
-                    rows_of[group, 0, 2 * HALF + sample - shift, here, :]
-                    * rows_of[group, 1, sample + shift, here, :]
-                )
-                total = term if total is None else total + term
+            total = first[0, shift, here, :] + products(rows_of, sample, shift, here)
             turned[pl.ds(shift, 8, stride=OFFSET_ROWS), :] = total
         for line in range(8):
             values = turned[line * OFFSET_ROWS : (line + 1) * OFFSET_ROWS, :].T
@@ -511,45 +558,46 @@
             out[0, lines + at] = values[size_z // 2 :, :OFFSETS]
 
 
-def image(place, blocks):
-    rows, lines, size_z = blocks[0].shape[2:]
-    samples = rows // 4
+def image(place, first, blocks):
+    samples, _, lines, size_z = first.shape
+    rows = 4 * samples
     return pl.pallas_call(
         image_kernel,
         grid=(samples,),
         out_shape=jax.ShapeDtypeStruct((samples, 2 * lines, size_z // 2, OFFSETS), F32),
-        in_specs=[SMEM] + [HBM] * len(blocks),
+        in_specs=[SMEM, pl.BlockSpec((1, OFFSETS, lines, size_z), lambda i: (i, 0, 0, 0))] + [ANY] * len(blocks),
         out_specs=pl.BlockSpec((1, 2 * lines, size_z // 2, OFFSETS), lambda i: (i, 0, 0, 0)),
         scratch_shapes=[
-            pltpu.VMEM((4, 2, rows + 2 * HALF, lines, size_z), F32),
+            pltpu.VMEM((2, 2, rows + 2 * HALF, lines, size_z), F32),
             pltpu.VMEM((8 * OFFSET_ROWS, size_z), F32),
-            pltpu.SemaphoreType.DMA((24,)),
+            pltpu.SemaphoreType.DMA((18,)),
         ],
-        compiler_params=params(24),
-        cost_estimate=cost(16 * 2**20, 16 * 2**20),
+        compiler_params=params(20),
+        cost_estimate=cost(10**10, 16 * 2**20),
         name="image",
-    )(place, *blocks)
+    )(place, first, *blocks)
 
 
 def in_order_kernel(place, *refs):
-    refs[-1][...] = place[...]
+    for index in range(place.shape[0]):
+        refs[-1][index] = place[index]
 
 
 def in_order(place, *arrays):
     return pl.pallas_call(
         in_order_kernel,
-        out_shape=jax.ShapeDtypeStruct((8, 128), jnp.int32),
-        in_specs=[VMEM] + [HBM] * len(arrays),
-        out_specs=VMEM,
+        out_shape=jax.ShapeDtypeStruct(place.shape, jnp.int32),
+        in_specs=[SMEM] + [ANY] * len(arrays),
+        out_specs=SMEM,
         cost_estimate=cost(10**10, 2**10),
         name="in_order",
-    )(jnp.broadcast_to(jnp.pad(place, (0, 125)), (8, 128)), *arrays)[0, :3]
+    )(place, *arrays)
 
 
 def on_device(source_now, source_before, receiver_now, receiver_before, courant):
     size = lax.axis_size("gx")
     place = jnp.stack(
-        [lax.axis_index("shot"), lax.axis_index("gy"), lax.axis_index("gx") % 2]
+        [lax.axis_index("shot"), lax.axis_index("gy"), lax.axis_index("gx") % 2, 0]
     ).astype(jnp.int32)
     up_pairs = [(i, i + 1) for i in range(size - 1)]
     down_pairs = [(j, i) for i, j in up_pairs]
@@ -566,9 +614,10 @@
     right = exchange(down, "gx", down_pairs)
     side = exchange(side, "gy", both)
     other = exchange(give, "shot", both)
-    own = jnp.stack([keep, other])
-    side, own = barrier((side, own))
-    near = exchange(own, "gx", partner)
+    side, keep, other = barrier((side, keep, other))
+    near_keep = exchange(keep, "gx", partner)
+    near_other = exchange(other, "gx", partner)
+    blocks = [keep, near_keep, None, other, near_other, None]
     inside, kept_courant, side_in, border = inner(
         place, source_now, receiver_now, source_before, receiver_before, courant, side
     )
@@ -578,32 +627,30 @@
     left = exchange(up, "gx", up_pairs)
     right = exchange(down, "gx", down_pairs)
     side = exchange(side, "gy", both)
+    side, near_keep = barrier((side, near_keep))
+    far_keep = exchange(near_keep, "gx", onward)
 
     keep, give = finish_middle(place, inside, ends, kept_courant, side)
-    keep, give, near = barrier((keep, give, near))
-    far = exchange(near, "gx", onward)
+    keep, give, near_other = barrier((keep, give, near_other))
+    blocks[5] = exchange(near_other, "gx", onward)
     other = exchange(give, "shot", both)
     near_keep = exchange(keep, "gx", partner)
-    middle = [keep, other]
-
-    keep, give = finish_ends(place, ends, kept_courant, left, right, side)
-    middle[1], keep, give = barrier((middle[1], keep, give))
-    near_other = exchange(middle[1], "gx", partner)
-    other = exchange(give, "shot", both)
-    blocks = [own, near, far]
-    other, near_keep = barrier((other, near_keep))
-    own = jnp.stack([keep, other])
+
+    left, right, blocks[2] = barrier((left, right, far_keep))
+    keep_ends, give_ends = finish_ends(place, ends, kept_courant, left, right, side)
+    other, keep_ends, give_ends = barrier((other, keep_ends, give_ends))
+    near_other = exchange(other, "gx", partner)
+    other_ends = exchange(give_ends, "shot", both)
+    other_ends, near_keep = barrier((other_ends, near_keep))
+    own = jnp.stack([keep_ends, other_ends])
     left = exchange(own, "gx", up_pairs)
     right = exchange(own, "gx", down_pairs)
-    near_keep, far = barrier((near_keep, far))
-    blocks[2] = far
     far_keep = exchange(near_keep, "gx", onward)
     far_other = exchange(near_other, "gx", onward)
-    place = in_order(place, left, right, far_keep)
-    keep, other = middle
-    blocks[1] = near
-    blocks += [keep, near_keep, far_keep, other, near_other, far_other, own, left, right]
-    return jnp.transpose(image(place, blocks), (3, 0, 1, 2))
+    first = first_image(place, blocks)
+    place = in_order(place, first, left, right, far_keep)
+    blocks = [keep, near_keep, far_keep, other, near_other, far_other, own, left, right]
+    return jnp.transpose(image(place, first, blocks), (3, 0, 1, 2))
 
 
 def solution(mesh):

time: 127 us -> 117 us (0.921)
  waiting for transfers between devices: 30.3 us -> 12.4 us
  starting transfers between devices: 37 us -> 45.8 us
    ppermute x17 -> x19, waiting for transfers between devices: 30.3 us -> 12.4 us  [exchange(): return lax.ppermute(array, axis, pairs)]
    ppermute x17 -> x19, starting transfers between devices: 37 us -> 45.8 us  [exchange(): return lax.ppermute(array, axis, pairs)]
    pallas_call x1 -> x2, Pallas kernels: 1.27 us -> 3.29 us  [the longest x1 2.11 us: first_image(): pl.pallas_call(first_image_kernel, grid=(samples,), out_shape=jax.ShapeDt...]
    unnamed x38 -> x36, local copies, waits for them, and re-layouts: 10.1 us -> 11.3 us
  transfers between devices with their start and end apart: 17 -> 19, of which waited for: 5 -> 4; matrix products, arithmetic and copies ran while one was open for 2% -> 0% of each run, Pallas kernels for 25% -> 28%
where the time goes in v4:
time: 117 us; the launch traced here: 116 us
  starting transfers between devices  45.8 us (39%)
  Pallas kernels  45.7 us (39%)
  waiting for transfers between devices  12.4 us (11%)
  local copies, waits for them, and re-layouts  11.3 us (10%)
    ppermute x19, starting transfers between devices, exchange(): return lax.ppermute(array, axis, pairs)  45.8 us
    pallas_call x1, Pallas kernels, inner(): pl.pallas_call(inner_kernel, out_shape=(jax.ShapeDtypeStruct((2, rows - 4...  17.6 us
    ppermute x19, waiting for transfers between devices, exchange(): return lax.ppermute(array, axis, pairs)  12.4 us
    unnamed x36, local copies, waits for them, and re-layouts  11.3 us
    pallas_call x1, Pallas kernels, outer(): pl.pallas_call(outer_kernel, out_shape=(jax.ShapeDtypeStruct((2, 2, 2 * R...  9.38 us
    pallas_call x1, Pallas kernels, image(): pl.pallas_call(image_kernel, grid=(samples,), out_shape=jax.ShapeDtypeStr...  8.24 us
    pallas_call x1, Pallas kernels, pack(): pl.pallas_call(pack_kernel, grid=(rows // step,), out_shape=(edge, edge,...  4.48 us
  transfers between devices with their start and end apart: 19, of which 4 were waited for; matrix products, arithmetic and copies ran while one was open for 0% of the time, Pallas kernels for 28%

profile of v4, /device:TPU:0, one launch (start us, length us, event | category | flops | bytes accessed | tf_op | source)
XLA Modules:
  0.0 116.2 jit_solution(13912582296603092916)
XLA Ops:
  0.6 4.5 %pack.1 = (f32[2,4,128,128]{3,2,1,0:T(8,128)}, f32[2,4,128,128]{3,2,1,0:T(8,128)}, f32[2,32,16,128]{3,2,1,0:T(8,128)}, f32[2,32,16,128]{3,2,1,0:T(8,128)}, f32[32,8,128]{2,1,0:T(8,128)}) custom-call(s32[4]{0:T(128)} %pad_add_fusion.place, f32[1,32,128,128]{3,2,1,0:T(8,128)} %source.5, f32[1,32,128,128]{3,2,1,0:T(8,128)} %receiver.5), custom_call_target="tpu_custom_call" | custom-call | flops 10000000000 | bytes 7340032 | tf_op jit(solution)/shard_map/pack/pallas_call | solution.py:85
  5.6 2.6 %collective-permute-start = (f32[32,8,128]{2,1,0:T(8,128)}, f32[32,8,128]{2,1,0:T(8,128)S(1)}, u32[]{:S(2)}, u32[]{:S(2)}) collective-permute-start(f32[32,8,128]{2,1,0:T(8,128)} %get-tuple-element.38), channel_id=1, source_target_pairs={{0,1},{1,0},{2,3},{3,2},{4,5},{5,4},{6,7},{7,6},{8,9},{9,8},{10,11... | collective-permute-start | bytes 393224 | tf_op jit(solution)/shard_map/ppermute | solution.py:609
  8.1 3.4 %collective-permute-start.3 = (f32[2,4,128,128]{3,2,1,0:T(8,128)}, f32[2,4,128,128]{3,2,1,0:T(8,128)S(1)}, u32[]{:S(2)}, u32[]{:S(2)}) collective-permute-start(f32[2,4,128,128]{3,2,1,0:T(8,128)} %get-tuple-element.44), channel_id=1, source_target_pairs={{0,2},{2,4},{4,6},{6,8},{8,10},{10,12},{12,14},{1,3},{3,5},{5,7},{... | collective-permute-start | bytes 1572872 | tf_op jit(solution)/shard_map/ppermute | solution.py:609
  11.6 1.3 %collective-permute-start.4 = (f32[2,4,128,128]{3,2,1,0:T(8,128)}, f32[2,4,128,128]{3,2,1,0:T(8,128)S(1)}, u32[]{:S(2)}, u32[]{:S(2)}) collective-permute-start(f32[2,4,128,128]{3,2,1,0:T(8,128)} %get-tuple-element.45), channel_id=1, source_target_pairs={{2,0},{4,2},{6,4},{8,6},{10,8},{12,10},{14,12},{3,1},{5,3},{7,5},{... | collective-permute-start | bytes 1572872 | tf_op jit(solution)/shard_map/ppermute | solution.py:609
  12.9 2.7 %collective-permute-start.2 = (f32[2,32,16,128]{3,2,1,0:T(8,128)}, f32[2,32,16,128]{3,2,1,0:T(8,128)S(1)}, u32[]{:S(2)}, u32[]{:S(2)}) collective-permute-start(f32[2,32,16,128]{3,2,1,0:T(8,128)} %get-tuple-element.41.refs_0_), channel_id=1, source_target_pairs={{0,2},{2,0},{4,6},{6,4},{8,10},{10,8},{12,14},{14,12},{1,3},{3,1},... | collective-permute-start | bytes 1572872 | tf_op jit(solution)/shard_map/ppermute | solution.py:609
  15.6 17.6 %inner.1 = (f32[2,16,32,128]{3,2,1,0:T(8,128)}, f32[32,32,128]{2,1,0:T(8,128)}, f32[2,32,128]{2,1,0:T(8,128)}, f32[2,2,8,128,128]{4,3,2,1,0:T(8,128)}) custom-call(s32[4]{0:T(128)} %pad_add_fusion.place, f32[1,32,128,128]{3,2,1,0:T(8,128)} %source.5, f32[1,32,128,128]{3,2,1,0:T(8,128)} %receiver.5, f32[1,32,128,128]{3,2,1,0:T(8,128)} %source_before.3, ...), custom_call_target="tpu_custom_call" | custom-call | flops 20000000000 | bytes 1048576 | tf_op jit(solution)/shard_map/inner/pallas_call | solution.py:256
  33.3 2.1 %collective-permute-done.3.left = f32[2,4,128,128]{3,2,1,0:T(8,128)S(1)} collective-permute-done((f32[2,4,128,128]{3,2,1,0:T(8,128)}, f32[2,4,128,128]{3,2,1,0:T(8,128)S(1)}, u32[]{:S(2)}, u32[]{:S(2)}) %collective-permute-start.3) | collective-permute-done | bytes 524320 | tf_op jit(solution)/shard_map/ppermute | solution.py:609
  36.4 9.4 %outer.1 = (f32[2,2,8,32,128]{4,3,2,1,0:T(8,128)}, f32[2,4,32,128]{3,2,1,0:T(8,128)}, f32[2,4,32,128]{3,2,1,0:T(8,128)}, f32[2,32,128]{2,1,0:T(8,128)}) custom-call(s32[4]{0:T(128)} %pad_add_fusion.place, f32[1,32,128,128]{3,2,1,0:T(8,128)} %source.5, f32[1,32,128,128]{3,2,1,0:T(8,128)} %receiver.5, f32[1,32,128,128]{3,2,1,0:T(8,128)} %source_before.3, ...), custom_call_target="tpu_custom_call" | custom-call | flops 1000000 | bytes 1048576 | tf_op jit(solution)/shard_map/outer/pallas_call | solution.py:367
  46.4 2.4 %collective-permute-start.9 = (f32[2,32,16,128]{3,2,1,0:T(8,128)S(1)}, f32[2,32,16,128]{3,2,1,0:T(8,128)S(1)}, u32[]{:S(2)}, u32[]{:S(2)}) collective-permute-start(f32[2,32,16,128]{3,2,1,0:T(8,128)S(1)} %collective-permute-done.1.refs_3_), channel_id=1, source_target_pairs={{0,2},{2,0},{4,6},{6,4},{8,10},{10,8},{12,14},{14,12},{1,3},{3,1},... | collective-permute-start | bytes 1572872 | tf_op jit(solution)/shard_map/ppermute | solution.py:609
  48.7 1.9 %collective-permute-start.5 = (f32[2,4,32,128]{3,2,1,0:T(8,128)}, f32[2,4,32,128]{3,2,1,0:T(8,128)S(1)}, u32[]{:S(2)}, u32[]{:S(2)}) collective-permute-start(f32[2,4,32,128]{3,2,1,0:T(8,128)} %get-tuple-element.47), channel_id=1, source_target_pairs={{0,2},{2,4},{4,6},{6,8},{8,10},{10,12},{12,14},{1,3},{3,5},{5,7},{... | collective-permute-start | bytes 393224 | tf_op jit(solution)/shard_map/ppermute | solution.py:609
  50.7 1.3 %collective-permute-start.6 = (f32[2,4,32,128]{3,2,1,0:T(8,128)}, f32[2,4,32,128]{3,2,1,0:T(8,128)S(1)}, u32[]{:S(2)}, u32[]{:S(2)}) collective-permute-start(f32[2,4,32,128]{3,2,1,0:T(8,128)} %get-tuple-element.48), channel_id=1, source_target_pairs={{2,0},{4,2},{6,4},{8,6},{10,8},{12,10},{14,12},{3,1},{5,3},{7,5},{... | collective-permute-start | bytes 393224 | tf_op jit(solution)/shard_map/ppermute | solution.py:609
  52.0 7.0 %collective-permute-start.8 = (f32[2,32,16,128]{3,2,1,0:T(8,128)S(1)}, f32[2,32,16,128]{3,2,1,0:T(8,128)S(1)}, u32[]{:S(2)}, u32[]{:S(2)}) collective-permute-start(f32[2,32,16,128]{3,2,1,0:T(8,128)S(1)} %collective-permute-done.2.refs_1_), channel_id=1, source_target_pairs={{0,4},{4,8},{8,12},{6,2},{10,6},{14,10},{1,5},{5,9},{9,13},{7,3},{... | collective-permute-start | bytes 1572872 | tf_op jit(solution)/shard_map/ppermute | solution.py:609
  60.1 2.0 %finish_middle.1 = (f32[2,24,16,128]{3,2,1,0:T(8,128)S(1)}, f32[2,24,16,128]{3,2,1,0:T(8,128)S(1)}) custom-call(s32[4]{0:T(128)S(1)} %copy-done, f32[2,16,32,128]{3,2,1,0:T(8,128)S(1)} %copy-done.13, f32[2,2,8,32,128]{4,3,2,1,0:T(8,128)S(1)} %copy-done.2, f32[32,32,128]{2,1,0:T(8,128)S(1)} %copy-done.12, f32[2,32,128]{2,1,0:T(8,128)S(1)} %collective-permute-done.7.side), custom_call_target="tpu_custom_call" | custom-call | flops 10000000000 | bytes 3145728 | tf_op jit(solution)/shard_map/finish_middle/pallas_call | solution.py:424
  62.6 2.5 %collective-permute-start.13 = (f32[2,24,16,128]{3,2,1,0:T(8,128)S(1)}, f32[2,24,16,128]{3,2,1,0:T(8,128)S(1)}, u32[]{:S(2)}, u32[]{:S(2)}) collective-permute-start(f32[2,24,16,128]{3,2,1,0:T(8,128)S(1)} %get-tuple-element.67.refs_0_), channel_id=1, source_target_pairs={{0,2},{2,0},{4,6},{6,4},{8,10},{10,8},{12,14},{14,12},{1,3},{3,1},... | collective-permute-start | bytes 1179656 | tf_op jit(solution)/shard_map/ppermute | solution.py:609
  65.1 3.7 %collective-permute-start.10 = (f32[2,32,16,128]{3,2,1,0:T(8,128)S(1)}, f32[2,32,16,128]{3,2,1,0:T(8,128)S(1)}, u32[]{:S(2)}, u32[]{:S(2)}) collective-permute-start(f32[2,32,16,128]{3,2,1,0:T(8,128)S(1)} %collective-permute-done.9.refs_4_), channel_id=1, source_target_pairs={{0,4},{4,8},{8,12},{6,2},{10,6},{14,10},{1,5},{5,9},{9,13},{7,3},{... | collective-permute-start | bytes 1572872 | tf_op jit(solution)/shard_map/ppermute | solution.py:609
  70.4 4.7 %collective-permute-done.13.refs_1_ = f32[2,24,16,128]{3,2,1,0:T(8,128)S(1)} collective-permute-done((f32[2,24,16,128]{3,2,1,0:T(8,128)S(1)}, f32[2,24,16,128]{3,2,1,0:T(8,128)S(1)}, u32[]{:S(2)}, u32[]{:S(2)}) %collective-permute-start.13) | collective-permute-done | bytes 393248 | tf_op jit(solution)/shard_map/ppermute | solution.py:609
  76.4 4.6 %collective-permute-start.14 = (f32[2,2,8,16,128]{4,3,2,1,0:T(8,128)S(1)}, f32[2,2,8,16,128]{4,3,2,1,0:T(8,128)S(1)}, u32[]{:S(2)}, u32[]{:S(2)}) collective-permute-start(f32[2,2,8,16,128]{4,3,2,1,0:T(8,128)S(1)} %pad_maximum_fusion.refs_6_), channel_id=1, source_target_pairs={{0,2},{2,4},{4,6},{6,8},{8,10},{10,12},{12,14},{1,3},{3,5},{5,7},{... | collective-permute-start | bytes 786440 | tf_op jit(solution)/shard_map/ppermute | solution.py:609
  80.9 5.3 %collective-permute-start.16 = (f32[2,24,16,128]{3,2,1,0:T(8,128)S(1)}, f32[2,24,16,128]{3,2,1,0:T(8,128)S(1)}, u32[]{:S(2)}, u32[]{:S(2)}) collective-permute-start(f32[2,24,16,128]{3,2,1,0:T(8,128)S(1)} %collective-permute-done.13.refs_1_), channel_id=1, source_target_pairs={{0,4},{4,8},{8,12},{6,2},{10,6},{14,10},{1,5},{5,9},{9,13},{7,3},{... | collective-permute-start | bytes 1179656 | tf_op jit(solution)/shard_map/ppermute | solution.py:609
  86.2 2.1 %first_image.1.refs_0_.first = f32[8,65,16,128]{3,2,1,0:T(8,128)S(1)} custom-call(s32[4]{0:T(128)S(1)} %copy-done, f32[2,32,16,128]{3,2,1,0:T(8,128)S(1)} %copy-done.1, f32[2,32,16,128]{3,2,1,0:T(8,128)S(1)} %collective-permute-done.2.refs_1_, f32[2,32,16,128]{3,2,1,0:T(8,128)S(1)} %collective-permute-done.8.refs_2_, ...), custom_call_target="tpu_custom_call" | custom-call | flops 10000000000 | bytes 8388608 | tf_op jit(solution)/shard_map/first_image/pallas_call | solution.py:509
  88.4 2.0 %copy-done.10 = f32[8,65,16,128]{3,2,1,0:T(8,128)} copy-done((f32[8,65,16,128]{3,2,1,0:T(8,128)}, f32[8,65,16,128]{3,2,1,0:T(8,128)S(1)}, u32[]{:S(2)}) %copy-start.10) | copy-done | bytes 4259864
  90.4 4.0 %collective-permute-start.18 = (f32[2,24,16,128]{3,2,1,0:T(8,128)S(1)}, f32[2,24,16,128]{3,2,1,0:T(8,128)S(1)}, u32[]{:S(2)}, u32[]{:S(2)}) collective-permute-start(f32[2,24,16,128]{3,2,1,0:T(8,128)S(1)} %collective-permute-done.17.refs_4_), channel_id=1, source_target_pairs={{0,4},{4,8},{8,12},{6,2},{10,6},{14,10},{1,5},{5,9},{9,13},{7,3},{... | collective-permute-start | bytes 1179656 | tf_op jit(solution)/shard_map/ppermute | solution.py:609
  97.1 5.1 %collective-permute-done.18.refs_5_ = f32[2,24,16,128]{3,2,1,0:T(8,128)S(1)} collective-permute-done((f32[2,24,16,128]{3,2,1,0:T(8,128)S(1)}, f32[2,24,16,128]{3,2,1,0:T(8,128)S(1)}, u32[]{:S(2)}, u32[]{:S(2)}) %collective-permute-start.18) | collective-permute-done | bytes 393248 | tf_op jit(solution)/shard_map/ppermute | solution.py:609
  105.1 2.2 %copy-done.11 = f32[8,65,16,128]{3,2,1,0:T(8,128)S(1)} copy-done((f32[8,65,16,128]{3,2,1,0:T(8,128)S(1)}, f32[8,65,16,128]{3,2,1,0:T(8,128)}, u32[]{:S(2)}) %copy-start.11) | copy-done | bytes 4259864
  107.9 8.2 %image.1 = f32[8,32,64,65]{3,2,1,0:T(8,128)} custom-call(s32[4]{0:T(128)S(1)} %copy-done.14, f32[8,65,16,128]{3,2,1,0:T(8,128)S(1)} %copy-done.11, f32[2,24,16,128]{3,2,1,0:T(8,128)S(1)} %get-tuple-element.67.refs_0_, f32[2,24,16,128]{3,2,1,0:T(8,128)S(1)} %collective-permute-done.13.refs_1_, f32[2,24,16,128]{3,2,1,0:T(8,128)S(1)} %copy-done.5, ...), custom_call_target="tpu_custom_call" | custom-call | flops 10000000000 | bytes 16777216 | tf_op jit(solution)/shard_map/image/pallas_call | solution.py:564
  (60 shorter events, 13.3 us)
Async XLA Ops:
  5.1 7.8 %collective-permute-start.1 = (f32[2,32,16,128]{3,2,1,0:T(8,128)}, f32[2,32,16,128]{3,2,1,0:T(8,128)S(1)}, u32[]{:S(2)}, u32[]{:S(2)}) collective-permute-start(f32[2,32,16,128]{3,2,1,0:T(8,128)} %get-tuple-element.40), channel_id=1, source_target_pairs={{0,16},{16,0},{1,17},{17,1},{2,18},{18,2},{3,19},{19,3},{4,20},{20... | collective-permute-start | bytes 1572872 | tf_op jit(solution)/shard_map/ppermute | solution.py:609
  5.6 7.3 %collective-permute-start = (f32[32,8,128]{2,1,0:T(8,128)}, f32[32,8,128]{2,1,0:T(8,128)S(1)}, u32[]{:S(2)}, u32[]{:S(2)}) collective-permute-start(f32[32,8,128]{2,1,0:T(8,128)} %get-tuple-element.38), channel_id=1, source_target_pairs={{0,1},{1,0},{2,3},{3,2},{4,5},{5,4},{6,7},{7,6},{8,9},{9,8},{10,11... | collective-permute-start | bytes 393224 | tf_op jit(solution)/shard_map/ppermute | solution.py:609
  8.1 27.2 %collective-permute-start.3 = (f32[2,4,128,128]{3,2,1,0:T(8,128)}, f32[2,4,128,128]{3,2,1,0:T(8,128)S(1)}, u32[]{:S(2)}, u32[]{:S(2)}) collective-permute-start(f32[2,4,128,128]{3,2,1,0:T(8,128)} %get-tuple-element.44), channel_id=1, source_target_pairs={{0,2},{2,4},{4,6},{6,8},{8,10},{10,12},{12,14},{1,3},{3,5},{5,7},{... | collective-permute-start | bytes 1572872 | tf_op jit(solution)/shard_map/ppermute | solution.py:609
  11.6 23.8 %collective-permute-start.4 = (f32[2,4,128,128]{3,2,1,0:T(8,128)}, f32[2,4,128,128]{3,2,1,0:T(8,128)S(1)}, u32[]{:S(2)}, u32[]{:S(2)}) collective-permute-start(f32[2,4,128,128]{3,2,1,0:T(8,128)} %get-tuple-element.45), channel_id=1, source_target_pairs={{2,0},{4,2},{6,4},{8,6},{10,8},{12,10},{14,12},{3,1},{5,3},{7,5},{... | collective-permute-start | bytes 1572872 | tf_op jit(solution)/shard_map/ppermute | solution.py:609
  12.9 39.0 %collective-permute-start.2 = (f32[2,32,16,128]{3,2,1,0:T(8,128)}, f32[2,32,16,128]{3,2,1,0:T(8,128)S(1)}, u32[]{:S(2)}, u32[]{:S(2)}) collective-permute-start(f32[2,32,16,128]{3,2,1,0:T(8,128)} %get-tuple-element.41.refs_0_), channel_id=1, source_target_pairs={{0,2},{2,0},{4,6},{6,4},{8,10},{10,8},{12,14},{14,12},{1,3},{3,1},... | collective-permute-start | bytes 1572872 | tf_op jit(solution)/shard_map/ppermute | solution.py:609
  36.4 22.7 %copy-start = (s32[4]{0:T(128)S(1)}, s32[4]{0:T(128)}, u32[]{:S(2)}) copy-start(s32[4]{0:T(128)} %pad_add_fusion.place) | copy-start | bytes 52
  36.4 22.7 %copy-start.12 = (f32[32,32,128]{2,1,0:T(8,128)S(1)}, f32[32,32,128]{2,1,0:T(8,128)}, u32[]{:S(2)}) copy-start(f32[32,32,128]{2,1,0:T(8,128)} %get-tuple-element.55.kept_courant) | copy-start | bytes 1572868
  36.4 22.7 %copy-start.13 = (f32[2,16,32,128]{3,2,1,0:T(8,128)S(1)}, f32[2,16,32,128]{3,2,1,0:T(8,128)}, u32[]{:S(2)}) copy-start(f32[2,16,32,128]{3,2,1,0:T(8,128)} %get-tuple-element.53.inside) | copy-start | bytes 1572868
  45.8 6.2 %collective-permute-start.7 = (f32[2,32,128]{2,1,0:T(8,128)}, f32[2,32,128]{2,1,0:T(8,128)S(1)}, u32[]{:S(2)}, u32[]{:S(2)}) collective-permute-start(f32[2,32,128]{2,1,0:T(8,128)} %get-tuple-element.49), channel_id=1, source_target_pairs={{0,1},{1,0},{2,3},{3,2},{4,5},{5,4},{6,7},{7,6},{8,9},{9,8},{10,11... | collective-permute-start | bytes 98312 | tf_op jit(solution)/shard_map/ppermute | solution.py:609
  46.4 16.2 %collective-permute-start.9 = (f32[2,32,16,128]{3,2,1,0:T(8,128)S(1)}, f32[2,32,16,128]{3,2,1,0:T(8,128)S(1)}, u32[]{:S(2)}, u32[]{:S(2)}) collective-permute-start(f32[2,32,16,128]{3,2,1,0:T(8,128)S(1)} %collective-permute-done.1.refs_3_), channel_id=1, source_target_pairs={{0,2},{2,0},{4,6},{6,4},{8,10},{10,8},{12,14},{14,12},{1,3},{3,1},... | collective-permute-start | bytes 1572872 | tf_op jit(solution)/shard_map/ppermute | solution.py:609
  48.7 16.3 %collective-permute-start.5 = (f32[2,4,32,128]{3,2,1,0:T(8,128)}, f32[2,4,32,128]{3,2,1,0:T(8,128)S(1)}, u32[]{:S(2)}, u32[]{:S(2)}) collective-permute-start(f32[2,4,32,128]{3,2,1,0:T(8,128)} %get-tuple-element.47), channel_id=1, source_target_pairs={{0,2},{2,4},{4,6},{6,8},{8,10},{10,12},{12,14},{1,3},{3,5},{5,7},{... | collective-permute-start | bytes 393224 | tf_op jit(solution)/shard_map/ppermute | solution.py:609
  50.7 18.1 %collective-permute-start.6 = (f32[2,4,32,128]{3,2,1,0:T(8,128)}, f32[2,4,32,128]{3,2,1,0:T(8,128)S(1)}, u32[]{:S(2)}, u32[]{:S(2)}) collective-permute-start(f32[2,4,32,128]{3,2,1,0:T(8,128)} %get-tuple-element.48), channel_id=1, source_target_pairs={{2,0},{4,2},{6,4},{8,6},{10,8},{12,10},{14,12},{3,1},{5,3},{7,5},{... | collective-permute-start | bytes 393224 | tf_op jit(solution)/shard_map/ppermute | solution.py:609
  52.0 16.8 %collective-permute-start.8 = (f32[2,32,16,128]{3,2,1,0:T(8,128)S(1)}, f32[2,32,16,128]{3,2,1,0:T(8,128)S(1)}, u32[]{:S(2)}, u32[]{:S(2)}) collective-permute-start(f32[2,32,16,128]{3,2,1,0:T(8,128)S(1)} %collective-permute-done.2.refs_1_), channel_id=1, source_target_pairs={{0,4},{4,8},{8,12},{6,2},{10,6},{14,10},{1,5},{5,9},{9,13},{7,3},{... | collective-permute-start | bytes 1572872 | tf_op jit(solution)/shard_map/ppermute | solution.py:609
  60.1 8.7 %copy-start.3 = (f32[2,2,8,32,128]{4,3,2,1,0:T(8,128)S(1)}, f32[2,2,8,32,128]{4,3,2,1,0:T(8,128)}, u32[]{:S(2)}) copy-start(f32[2,2,8,32,128]{4,3,2,1,0:T(8,128)} %get-tuple-element.54.ends) | copy-start | bytes 1572868
  62.6 23.6 %copy-start.1 = (f32[2,32,16,128]{3,2,1,0:T(8,128)S(1)}, f32[2,32,16,128]{3,2,1,0:T(8,128)}, u32[]{:S(2)}) copy-start(f32[2,32,16,128]{3,2,1,0:T(8,128)} %get-tuple-element.41.refs_0_) | copy-start | bytes 1572868
  62.6 6.9 %collective-permute-start.11 = (f32[2,24,16,128]{3,2,1,0:T(8,128)S(1)}, f32[2,24,16,128]{3,2,1,0:T(8,128)S(1)}, u32[]{:S(2)}, u32[]{:S(2)}) collective-permute-start(f32[2,24,16,128]{3,2,1,0:T(8,128)S(1)} %get-tuple-element.60), channel_id=1, source_target_pairs={{0,16},{16,0},{1,17},{17,1},{2,18},{18,2},{3,19},{19,3},{4,20},{20... | collective-permute-start | bytes 1179656 | tf_op jit(solution)/shard_map/ppermute | solution.py:609
  62.6 12.4 %collective-permute-start.13 = (f32[2,24,16,128]{3,2,1,0:T(8,128)S(1)}, f32[2,24,16,128]{3,2,1,0:T(8,128)S(1)}, u32[]{:S(2)}, u32[]{:S(2)}) collective-permute-start(f32[2,24,16,128]{3,2,1,0:T(8,128)S(1)} %get-tuple-element.67.refs_0_), channel_id=1, source_target_pairs={{0,2},{2,0},{4,6},{6,4},{8,10},{10,8},{12,14},{14,12},{1,3},{3,1},... | collective-permute-start | bytes 1179656 | tf_op jit(solution)/shard_map/ppermute | solution.py:609
  65.1 21.1 %collective-permute-start.10 = (f32[2,32,16,128]{3,2,1,0:T(8,128)S(1)}, f32[2,32,16,128]{3,2,1,0:T(8,128)S(1)}, u32[]{:S(2)}, u32[]{:S(2)}) collective-permute-start(f32[2,32,16,128]{3,2,1,0:T(8,128)S(1)} %collective-permute-done.9.refs_4_), channel_id=1, source_target_pairs={{0,4},{4,8},{8,12},{6,2},{10,6},{14,10},{1,5},{5,9},{9,13},{7,3},{... | collective-permute-start | bytes 1572872 | tf_op jit(solution)/shard_map/ppermute | solution.py:609
  69.5 5.6 %collective-permute-start.12 = (f32[2,8,16,128]{3,2,1,0:T(8,128)S(1)}, f32[2,8,16,128]{3,2,1,0:T(8,128)S(1)}, u32[]{:S(2)}, u32[]{:S(2)}) collective-permute-start(f32[2,8,16,128]{3,2,1,0:T(8,128)S(1)} %get-tuple-element.66), channel_id=1, source_target_pairs={{0,16},{16,0},{1,17},{17,1},{2,18},{18,2},{3,19},{19,3},{4,20},{20... | collective-permute-start | bytes 393224 | tf_op jit(solution)/shard_map/ppermute | solution.py:609
  69.6 20.8 %collective-permute-start.17 = (f32[2,24,16,128]{3,2,1,0:T(8,128)S(1)}, f32[2,24,16,128]{3,2,1,0:T(8,128)S(1)}, u32[]{:S(2)}, u32[]{:S(2)}) collective-permute-start(f32[2,24,16,128]{3,2,1,0:T(8,128)S(1)} %collective-permute-done.11.refs_3_), channel_id=1, source_target_pairs={{0,2},{2,0},{4,6},{6,4},{8,10},{10,8},{12,14},{14,12},{1,3},{3,1},... | collective-permute-start | bytes 1179656 | tf_op jit(solution)/shard_map/ppermute | solution.py:609
  75.1 19.3 %collective-permute-start.15 = (f32[2,2,8,16,128]{4,3,2,1,0:T(8,128)S(1)}, f32[2,2,8,16,128]{4,3,2,1,0:T(8,128)S(1)}, u32[]{:S(2)}, u32[]{:S(2)}) collective-permute-start(f32[2,2,8,16,128]{4,3,2,1,0:T(8,128)S(1)} %pad_maximum_fusion.refs_6_), channel_id=1, source_target_pairs={{2,0},{4,2},{6,4},{8,6},{10,8},{12,10},{14,12},{3,1},{5,3},{7,5},{... | collective-permute-start | bytes 786440 | tf_op jit(solution)/shard_map/ppermute | solution.py:609
  76.4 18.0 %collective-permute-start.14 = (f32[2,2,8,16,128]{4,3,2,1,0:T(8,128)S(1)}, f32[2,2,8,16,128]{4,3,2,1,0:T(8,128)S(1)}, u32[]{:S(2)}, u32[]{:S(2)}) collective-permute-start(f32[2,2,8,16,128]{4,3,2,1,0:T(8,128)S(1)} %pad_maximum_fusion.refs_6_), channel_id=1, source_target_pairs={{0,2},{2,4},{4,6},{6,8},{8,10},{10,12},{12,14},{1,3},{3,5},{5,7},{... | collective-permute-start | bytes 786440 | tf_op jit(solution)/shard_map/ppermute | solution.py:609
  80.9 13.5 %collective-permute-start.16 = (f32[2,24,16,128]{3,2,1,0:T(8,128)S(1)}, f32[2,24,16,128]{3,2,1,0:T(8,128)S(1)}, u32[]{:S(2)}, u32[]{:S(2)}) collective-permute-start(f32[2,24,16,128]{3,2,1,0:T(8,128)S(1)} %collective-permute-done.13.refs_1_), channel_id=1, source_target_pairs={{0,4},{4,8},{8,12},{6,2},{10,6},{14,10},{1,5},{5,9},{9,13},{7,3},{... | collective-permute-start | bytes 1179656 | tf_op jit(solution)/shard_map/ppermute | solution.py:609
  90.4 11.8 %collective-permute-start.18 = (f32[2,24,16,128]{3,2,1,0:T(8,128)S(1)}, f32[2,24,16,128]{3,2,1,0:T(8,128)S(1)}, u32[]{:S(2)}, u32[]{:S(2)}) collective-permute-start(f32[2,24,16,128]{3,2,1,0:T(8,128)S(1)} %collective-permute-done.17.refs_4_), channel_id=1, source_target_pairs={{0,4},{4,8},{8,12},{6,2},{10,6},{14,10},{1,5},{5,9},{9,13},{7,3},{... | collective-permute-start | bytes 1179656 | tf_op jit(solution)/shard_map/ppermute | solution.py:609
  (13 other events, 15.6 us)

commit v5 on v4

--- a/solution.py
+++ b/solution.py
@@ -12,6 +12,7 @@
 KEEP_EVERY = 4
 OFFSETS = 2 * HALF + 1
 OFFSET_ROWS = 72
+LINES = 32
 WEIGHTS = (-205.0 / 72.0, 8.0 / 5.0, -1.0 / 5.0, 8.0 / 315.0, -1.0 / 560.0)
 PAD = 8
 F32 = jnp.float32
@@ -45,8 +46,8 @@
     return first, second
 
 
-def pack_kernel(place, source, receiver, up, down, keep, give, side):
-    shot, gy = place[0], place[1]
+def pack_kernel(source, receiver, up, down, keep, give, side):
+    shot, gy = lax.axis_index("shot"), lax.axis_index("gy")
     rows, size_y, size_z = source.shape[1:]
     lines = size_y // KEEP_EVERY
     step, steps = pl.program_id(0), pl.num_programs(0)
@@ -73,7 +74,7 @@
         side[row] = jnp.concatenate(parts, axis=0)
 
 
-def pack(place, source, receiver):
+def pack(source, receiver):
     _, rows, size_y, size_z = source.shape
     lines = size_y // KEEP_EVERY // 2
     step = 8
@@ -86,7 +87,7 @@
         pack_kernel,
         grid=(rows // step,),
         out_shape=(edge, edge, half, half, jax.ShapeDtypeStruct((rows, 2 * REACH, size_z), F32)),
-        in_specs=[SMEM, field_spec, field_spec],
+        in_specs=[field_spec, field_spec],
         out_specs=(
             edge_spec,
             edge_spec,
@@ -96,7 +97,7 @@
         ),
         cost_estimate=cost(10**10, 7 * 2**20),
         name="pack",
-    )(place, source, receiver)
+    )(source, receiver)
 
 
 def z_weights(size_z):
@@ -109,52 +110,49 @@
 
 def z_terms(center, masks):
     size_z = center.shape[1]
+    center = center.reshape(-1, 8, size_z)
     total = None
     for d, (below, above) in enumerate(masks, start=1):
-        term = below * pltpu.roll(center, d, 1) + above * pltpu.roll(center, size_z - d, 1)
+        term = below * pltpu.roll(center, d, 2) + above * pltpu.roll(center, size_z - d, 2)
         total = term if total is None else total + term
-    return total
-
-
-def first_step(now, row, before, before_row, scale, scale_row, after, after_row, field, masks, zero):
+    return total.reshape(-1, size_z)
+
+
+def first_step(now, row, before, before_row, scale, scale_row, after, after_row, field, masks):
     size_y = before.shape[2]
-    for chunk in range(size_y // 8):
-        at = PAD + 8 * chunk
-        center = now[field, row, at : at + 8, :]
+    for chunk in range(size_y // LINES):
+        at = PAD + LINES * chunk
+        center = now[field, row, at : at + LINES, :]
         total = (3.0 * WEIGHTS[0]) * center + z_terms(center, masks)
         for d in range(1, REACH + 1):
             around = (
-                now[field, row + d, at : at + 8, :]
-                + now[field, row - d, at : at + 8, :]
-                + now[field, row, pl.ds(zero + (at + d), 8), :]
-                + now[field, row, pl.ds(zero + (at - d), 8), :]
+                now[field, row + d, at : at + LINES, :]
+                + now[field, row - d, at : at + LINES, :]
+                + now[field, row, at + d : at + d + LINES, :]
+                + now[field, row, at - d : at - d + LINES, :]
             )
             total = total + WEIGHTS[d] * around
-        here = pl.ds(8 * chunk, 8)
-        after[field, after_row, at : at + 8, :] = (
+        here = pl.ds(LINES * chunk, LINES)
+        after[field, after_row, at : at + LINES, :] = (
             2.0 * center - before[field, before_row, here, :] + scale[scale_row, here, :] * total
         )
 
 
 def second_step(now, row, scale, scale_row, after, after_row, field, masks, store):
     size_y = scale.shape[1]
-    for chunk in range(size_y // KEEP_EVERY // 8):
-        at = PAD + 8 * KEEP_EVERY * chunk
-        kept = lambda start: pl.ds(start, 8, stride=KEEP_EVERY)
-        center = after[field, after_row, kept(at), :]
-        total = (3.0 * WEIGHTS[0]) * center + z_terms(center, masks)
-        for d in range(1, REACH + 1):
-            around = (
-                after[field, after_row + d, kept(at), :]
-                + after[field, after_row - d, kept(at), :]
-                + after[field, after_row, kept(at + d), :]
-                + after[field, after_row, kept(at - d), :]
-            )
-            total = total + WEIGHTS[d] * around
-        store(
-            pl.ds(8 * chunk, 8),
-            2.0 * center - now[field, row, kept(at), :] + scale[scale_row, kept(at - PAD), :] * total,
+    lines = size_y // KEEP_EVERY
+    kept = lambda start: pl.ds(start, lines, stride=KEEP_EVERY)
+    center = after[field, after_row, kept(PAD), :]
+    total = (3.0 * WEIGHTS[0]) * center + z_terms(center, masks)
+    for d in range(1, REACH + 1):
+        around = (
+            after[field, after_row + d, kept(PAD), :]
+            + after[field, after_row - d, kept(PAD), :]
+            + after[field, after_row, kept(PAD + d), :]
+            + after[field, after_row, kept(PAD - d), :]
         )
+        total = total + WEIGHTS[d] * around
+    store(2.0 * center - now[field, row, kept(PAD), :] + scale[scale_row, kept(0), :] * total)
 
 
 def side_term(after, after_row, field, size_y, gy):
@@ -179,10 +177,10 @@
 
 
 def inner_kernel(
-    place, source, receiver, source_before, receiver_before, courant, side,
+    source, receiver, source_before, receiver_before, courant, side,
     partial, kept_courant, side_out, border, now, before, scale, after, sems, out_sems,
 ):
-    gy = place[1]
+    gy = lax.axis_index("gy")
     rows, size_y, size_z = courant.shape
     lines = size_y // KEEP_EVERY
     copies = []
@@ -214,7 +212,7 @@
 
     def first(row, carry):
         for field in range(2):
-            first_step(now, row, before, row, scale, row, after, row, field, masks, place[3])
+            first_step(now, row, before, row, scale, row, after, row, field, masks)
             side_out[field, pl.ds(row, 1), :] = side_term(after, row, field, size_y, gy)
         return carry
 
@@ -233,8 +231,8 @@
 
     def second(row, carry):
         for field in range(2):
-            def store(here, value):
-                partial[field, row - 2 * REACH, here, :] = value
+            def store(value):
+                partial[field, row - 2 * REACH] = value
 
             second_step(now, row, scale, row, after, row, field, masks, store)
         return carry
@@ -250,7 +248,7 @@
         one.wait()
 
 
-def inner(place, source, receiver, source_before, receiver_before, courant, side):
+def inner(source, receiver, source_before, receiver_before, courant, side):
     rows, size_y, size_z = courant.shape
     lines = size_y // KEEP_EVERY
     return pl.pallas_call(
@@ -261,7 +259,7 @@
             jax.ShapeDtypeStruct((2, rows, size_z), F32),
             jax.ShapeDtypeStruct((2, 2, 2 * REACH, size_y, size_z), F32),
         ),
-        in_specs=[SMEM] + [HBM] * 5 + [VMEM],
+        in_specs=[HBM] * 5 + [VMEM],
         out_specs=(VMEM,) * 3 + (HBM,),
         scratch_shapes=[
             pltpu.VMEM((2, rows, size_y + 2 * PAD, size_z), F32),
@@ -274,14 +272,14 @@
         compiler_params=params(60),
         cost_estimate=cost(2 * 10**10, 2**20),
         name="inner",
-    )(place, source, receiver, source_before, receiver_before, courant, side)
+    )(source, receiver, source_before, receiver_before, courant, side)
 
 
 def outer_kernel(
-    place, source, receiver, source_before, receiver_before, courant, border, left, right, side, side_in,
+    source, receiver, source_before, receiver_before, courant, border, left, right, side, side_in,
     partial, up, down, side_out, now, before, scale, after, sems,
 ):
-    gy = place[1]
+    gy = lax.axis_index("gy")
     rows, size_y, size_z = courant.shape
     lines = size_y // KEEP_EVERY
     reach2 = 2 * REACH
@@ -330,7 +328,7 @@
                 to = REACH * (1 + end) + row
                 first_step(
                     now, REACH + row, before, row, scale, (2 * end + end) * REACH + row,
-                    after, to, group, masks, place[3],
+                    after, to, group, masks,
                 )
                 side_out[field, pl.ds(end * (rows - REACH) + row, 1), :] = side_term(
                     after, to, group, size_y, gy
@@ -349,8 +347,8 @@
             for end in range(2):
                 group = 2 * end + field
 
-                def store(here, value):
-                    partial[field, end, row, here, :] = value
+                def store(value):
+                    partial[field, end, row] = value
 
                 second_step(
                     now, (1 - end) * REACH + row, scale, end * reach2 + row, after, REACH + row, group, masks, store
@@ -360,7 +358,7 @@
     lax.fori_loop(0, reach2, second, 0)
 
 
-def outer(place, source, receiver, source_before, receiver_before, courant, border, left, right, side, side_in):
+def outer(source, receiver, source_before, receiver_before, courant, border, left, right, side, side_in):
     rows, size_y, size_z = courant.shape
     lines = size_y // KEEP_EVERY
     halo = jax.ShapeDtypeStruct((2, REACH, lines, size_z), F32)
@@ -372,7 +370,7 @@
             halo,
             jax.ShapeDtypeStruct((2, rows, size_z), F32),
         ),
-        in_specs=[SMEM] + [HBM] * 8 + [VMEM] * 2,
+        in_specs=[HBM] * 8 + [VMEM] * 2,
         out_specs=(VMEM,) * 4,
         scratch_shapes=[
             pltpu.VMEM((4, 3 * REACH, size_y + 2 * PAD, size_z), F32),
@@ -384,7 +382,7 @@
         compiler_params=params(60),
         cost_estimate=cost(10**6, 2**20),
         name="outer",
-    )(place, source, receiver, source_before, receiver_before, courant, border, left, right, side, side_in)
+    )(source, receiver, source_before, receiver_before, courant, border, left, right, side, side_in)
 
 
 def pack_row(value, field, row, shot, keep, give):
@@ -399,8 +397,8 @@
     return jnp.where(meets, side[field, pl.ds(row, 1), :], 0.0)
 
 
-def middle_kernel(place, inside, ends, kept_courant, side, keep, give):
-    shot, gy = place[0], place[1]
+def middle_kernel(inside, ends, kept_courant, side, keep, give):
+    shot, gy = lax.axis_index("shot"), lax.axis_index("gy")
     rows, lines, _ = kept_courant.shape
 
     def one_row(row, values):
@@ -418,22 +416,22 @@
         one_row(rows - 1 - row, [ends[field, 1, 2 * REACH - 1 - row] for field in range(2)])
 
 
-def finish_middle(place, inside, ends, kept_courant, side):
+def finish_middle(inside, ends, kept_courant, side):
     rows, lines, size_z = kept_courant.shape
     half = jax.ShapeDtypeStruct((2, rows - 2 * REACH, lines // 2, size_z), F32)
     return pl.pallas_call(
         middle_kernel,
         out_shape=(half, half),
-        in_specs=[SMEM] + [VMEM] * 4,
+        in_specs=[VMEM] * 4,
         out_specs=(VMEM,) * 2,
         compiler_params=params(24),
         cost_estimate=cost(10**10, 3 * 2**20),
         name="finish_middle",
-    )(place, inside, ends, kept_courant, side)
-
-
-def ends_kernel(place, ends, kept_courant, left, right, side, keep, give):
-    shot, gy = place[0], place[1]
+    )(inside, ends, kept_courant, side)
+
+
+def ends_kernel(ends, kept_courant, left, right, side, keep, give):
+    shot, gy = lax.axis_index("shot"), lax.axis_index("gy")
     rows, lines, _ = kept_courant.shape
     for field in range(2):
         for row in range(REACH):
@@ -453,22 +451,22 @@
             )
 
 
-def finish_ends(place, ends, kept_courant, left, right, side):
+def finish_ends(ends, kept_courant, left, right, side):
     _, lines, size_z = kept_courant.shape
     half = jax.ShapeDtypeStruct((2, 2 * REACH, lines // 2, size_z), F32)
     return pl.pallas_call(
         ends_kernel,
         out_shape=(half, half),
-        in_specs=[SMEM] + [VMEM] * 5,
+        in_specs=[VMEM] * 5,
         out_specs=(VMEM,) * 2,
         compiler_params=params(24),
         cost_estimate=cost(10**10, 3 * 2**20),
         name="finish_ends",
-    )(place, ends, kept_courant, left, right, side)
-
-
-def block_starts(place, rows):
-    even = place[2] == 0
+    )(ends, kept_courant, left, right, side)
+
+
+def block_starts(rows):
+    even = lax.axis_index("gx") % 2 == 0
     return HALF, jnp.where(even, HALF + rows, 0), jnp.where(even, 0, HALF + rows)
 
 
@@ -483,13 +481,13 @@
     return total
 
 
-def first_image_kernel(place, *refs):
+def first_image_kernel(*refs):
     blocks, (out, rows_of, sems) = refs[:6], refs[6:]
     rows = blocks[0].shape[1]
 
     @pl.when(pl.program_id(0) == 0)
     def _():
-        starts = block_starts(place, rows)
+        starts = block_starts(rows)
         copies = []
         for index, ref in enumerate(blocks):
             dst = rows_of.at[index // 3, :, pl.ds(starts[index % 3], rows)]
@@ -503,14 +501,14 @@
             out[0, shift, here, :] = products(rows_of, sample, shift, here)
 
 
-def first_image(place, blocks):
+def first_image(blocks):
     _, rows, lines, size_z = blocks[0].shape
     samples = rows // 4
     return pl.pallas_call(
         first_image_kernel,
         grid=(samples,),
         out_shape=jax.ShapeDtypeStruct((samples, OFFSETS, lines, size_z), F32),
-        in_specs=[SMEM] + [ANY] * len(blocks),
+        in_specs=[ANY] * len(blocks),
         out_specs=pl.BlockSpec((1, OFFSETS, lines, size_z), lambda i: (i, 0, 0, 0)),
         scratch_shapes=[
             pltpu.VMEM((2, 2, rows + 2 * HALF, lines, size_z), F32),
@@ -519,16 +517,16 @@
         compiler_params=params(16),
         cost_estimate=cost(10**10, 8 * 2**20),
         name="first_image",
-    )(place, *blocks)
-
-
-def image_kernel(place, first, *refs):
+    )(*blocks)
+
+
+def image_kernel(token, first, *refs):
     blocks, (out, rows_of, turned, sems) = refs[:9], refs[9:]
     rows = blocks[0].shape[1] + 2 * REACH
 
     @pl.when(pl.program_id(0) == 0)
     def _():
-        starts = block_starts(place, rows)
+        starts = block_starts(rows)
         copies = []
 
         def copy(src, group, start, count):
@@ -550,15 +548,15 @@
         here = pl.ds(8 * chunk, 8)
         for shift in range(OFFSETS):
             total = first[0, shift, here, :] + products(rows_of, sample, shift, here)
-            turned[pl.ds(shift, 8, stride=OFFSET_ROWS), :] = total
+            turned[chunk, pl.ds(shift, 8, stride=OFFSET_ROWS), :] = total
         for line in range(8):
-            values = turned[line * OFFSET_ROWS : (line + 1) * OFFSET_ROWS, :].T
+            values = turned[chunk, line * OFFSET_ROWS : (line + 1) * OFFSET_ROWS, :].T
             at = 8 * chunk + line
             out[0, at] = values[: size_z // 2, :OFFSETS]
             out[0, lines + at] = values[size_z // 2 :, :OFFSETS]
 
 
-def image(place, first, blocks):
+def image(token, first, blocks):
     samples, _, lines, size_z = first.shape
     rows = 4 * samples
     return pl.pallas_call(
@@ -569,36 +567,33 @@
         out_specs=pl.BlockSpec((1, 2 * lines, size_z // 2, OFFSETS), lambda i: (i, 0, 0, 0)),
         scratch_shapes=[
             pltpu.VMEM((2, 2, rows + 2 * HALF, lines, size_z), F32),
-            pltpu.VMEM((8 * OFFSET_ROWS, size_z), F32),
+            pltpu.VMEM((lines // 8, 8 * OFFSET_ROWS, size_z), F32),
             pltpu.SemaphoreType.DMA((18,)),
         ],
         compiler_params=params(20),
         cost_estimate=cost(10**10, 16 * 2**20),
         name="image",
-    )(place, first, *blocks)
-
-
-def in_order_kernel(place, *refs):
-    for index in range(place.shape[0]):
-        refs[-1][index] = place[index]
-
-
-def in_order(place, *arrays):
+    )(token, first, *blocks)
+
+
+def in_order_kernel(*refs):
+    refs[-1][0] = 0
+
+
+def in_order(*arrays):
     return pl.pallas_call(
         in_order_kernel,
-        out_shape=jax.ShapeDtypeStruct(place.shape, jnp.int32),
-        in_specs=[SMEM] + [ANY] * len(arrays),
+        out_shape=jax.ShapeDtypeStruct((1,), jnp.int32),
+        in_specs=[ANY] * len(arrays),
         out_specs=SMEM,
-        cost_estimate=cost(10**10, 2**10),
+        compiler_params=params(1),
+        cost_estimate=cost(1, 1),
         name="in_order",
-    )(place, *arrays)
+    )(*arrays)
 
 
 def on_device(source_now, source_before, receiver_now, receiver_before, courant):
     size = lax.axis_size("gx")
-    place = jnp.stack(
-        [lax.axis_index("shot"), lax.axis_index("gy"), lax.axis_index("gx") % 2, 0]
-    ).astype(jnp.int32)
     up_pairs = [(i, i + 1) for i in range(size - 1)]
     down_pairs = [(j, i) for i, j in up_pairs]
     partner = [(i, i ^ 1) for i in range(size)]
@@ -609,7 +604,7 @@
         return lax.ppermute(array, axis, pairs)
 
     barrier = lax.optimization_barrier
-    up, down, keep, give, side = pack(place, source_now, receiver_now)
+    up, down, keep, give, side = pack(source_now, receiver_now)
     left = exchange(up, "gx", up_pairs)
     right = exchange(down, "gx", down_pairs)
     side = exchange(side, "gy", both)
@@ -619,10 +614,10 @@
     near_other = exchange(other, "gx", partner)
     blocks = [keep, near_keep, None, other, near_other, None]
     inside, kept_courant, side_in, border = inner(
-        place, source_now, receiver_now, source_before, receiver_before, courant, side
+        source_now, receiver_now, source_before, receiver_before, courant, side
     )
     ends, up, down, side = outer(
-        place, source_now, receiver_now, source_before, receiver_before, courant, border, left, right, side, side_in
+        source_now, receiver_now, source_before, receiver_before, courant, border, left, right, side, side_in
     )
     left = exchange(up, "gx", up_pairs)
     right = exchange(down, "gx", down_pairs)
@@ -630,14 +625,14 @@
     side, near_keep = barrier((side, near_keep))
     far_keep = exchange(near_keep, "gx", onward)
 
-    keep, give = finish_middle(place, inside, ends, kept_courant, side)
+    keep, give = finish_middle(inside, ends, kept_courant, side)
     keep, give, near_other = barrier((keep, give, near_other))
     blocks[5] = exchange(near_other, "gx", onward)
     other = exchange(give, "shot", both)
     near_keep = exchange(keep, "gx", partner)
 
     left, right, blocks[2] = barrier((left, right, far_keep))
-    keep_ends, give_ends = finish_ends(place, ends, kept_courant, left, right, side)
+    keep_ends, give_ends = finish_ends(ends, kept_courant, left, right, side)
     other, keep_ends, give_ends = barrier((other, keep_ends, give_ends))
     near_other = exchange(other, "gx", partner)
     other_ends = exchange(give_ends, "shot", both)
@@ -647,10 +642,10 @@
     right = exchange(own, "gx", down_pairs)
     far_keep = exchange(near_keep, "gx", onward)
     far_other = exchange(near_other, "gx", onward)
-    first = first_image(place, blocks)
-    place = in_order(place, first, left, right, far_keep)
+    first = first_image(blocks)
+    token = in_order(first, left, right, far_keep)
     blocks = [keep, near_keep, far_keep, other, near_other, far_other, own, left, right]
-    return jnp.transpose(image(place, first, blocks), (3, 0, 1, 2))
+    return jnp.transpose(image(token, first, blocks), (3, 0, 1, 2))
 
 
 def solution(mesh):

time: 117 us -> 110 us (0.940)
  local copies, waits for them, and re-layouts: 11.3 us -> 2.04 us
  waiting for transfers between devices: 12.4 us -> 16.3 us
  Pallas kernels: 45.7 us -> 43.7 us
  starting transfers between devices: 45.8 us -> 47.5 us
    unnamed x36 -> x16, local copies, waits for them, and re-layouts: 11.3 us -> 2.04 us
    ppermute x19, waiting for transfers between devices: 12.4 us -> 16.3 us  [exchange(): return lax.ppermute(array, axis, pairs)]
    pallas_call x3, Pallas kernels: 3.89 us -> 2.13 us  [the longest x1 1.46 us: finish_middle(): pl.pallas_call(middle_kernel, out_shape=(half, half), in_specs=[VMEM] * 4...]
    ppermute x19, starting transfers between devices: 45.8 us -> 47.5 us  [exchange(): return lax.ppermute(array, axis, pairs)]
  transfers between devices with their start and end apart: 19 -> 19, of which waited for: 4 -> 5; matrix products, arithmetic and copies ran while one was open for 0% -> 0% of each run, Pallas kernels for 28% -> 28%
where the time goes in v5:
time: 110 us
  starting transfers between devices  47.5 us (43%)
  Pallas kernels  43.7 us (40%)
  waiting for transfers between devices  16.3 us (15%)
  local copies, waits for them, and re-layouts  2.04 us (2%)
    ppermute x19, starting transfers between devices, exchange(): return lax.ppermute(array, axis, pairs)  47.5 us
    pallas_call x1, Pallas kernels, inner(): pl.pallas_call(inner_kernel, out_shape=(jax.ShapeDtypeStruct((2, rows - 4...  17.9 us
    ppermute x19, waiting for transfers between devices, exchange(): return lax.ppermute(array, axis, pairs)  16.3 us
    pallas_call x1, Pallas kernels, outer(): pl.pallas_call(outer_kernel, out_shape=(jax.ShapeDtypeStruct((2, 2, 2 * R...  9.44 us
    pallas_call x1, Pallas kernels, image(): pl.pallas_call(image_kernel, grid=(samples,), out_shape=jax.ShapeDtypeStr...  8.22 us
    pallas_call x1, Pallas kernels, pack(): pl.pallas_call(pack_kernel, grid=(rows // step,), out_shape=(edge, edge,...  4.5 us
  transfers between devices with their start and end apart: 19, of which 5 were waited for; matrix products, arithmetic and copies ran while one was open for 0% of the time, Pallas kernels for 28%

profile of v5, /device:TPU:0, one launch (start us, length us, event | category | flops | bytes accessed | tf_op | source)
XLA Modules:
  0.0 109.9 jit_solution(17891564998452498587)
XLA Ops:
  0.0 4.5 %pack.1 = (f32[2,4,128,128]{3,2,1,0:T(8,128)}, f32[2,4,128,128]{3,2,1,0:T(8,128)}, f32[2,32,16,128]{3,2,1,0:T(8,128)}, f32[2,32,16,128]{3,2,1,0:T(8,128)}, f32[32,8,128]{2,1,0:T(8,128)}) custom-call(f32[1,32,128,128]{3,2,1,0:T(8,128)} %source.5, f32[1,32,128,128]{3,2,1,0:T(8,128)} %receiver.5), custom_call_target="tpu_custom_call" | custom-call | flops 10000000000 | bytes 7340032 | tf_op jit(solution)/shard_map/pack/pallas_call | solution.py:86
  5.0 2.6 %collective-permute-start = (f32[32,8,128]{2,1,0:T(8,128)}, f32[32,8,128]{2,1,0:T(8,128)S(1)}, u32[]{:S(2)}, u32[]{:S(2)}) collective-permute-start(f32[32,8,128]{2,1,0:T(8,128)} %get-tuple-element.38), channel_id=1, source_target_pairs={{0,1},{1,0},{2,3},{3,2},{4,5},{5,4},{6,7},{7,6},{8,9},{9,8},{10,11... | collective-permute-start | bytes 393224 | tf_op jit(solution)/shard_map/ppermute | solution.py:604
  7.5 3.4 %collective-permute-start.3 = (f32[2,4,128,128]{3,2,1,0:T(8,128)}, f32[2,4,128,128]{3,2,1,0:T(8,128)S(1)}, u32[]{:S(2)}, u32[]{:S(2)}) collective-permute-start(f32[2,4,128,128]{3,2,1,0:T(8,128)} %get-tuple-element.44), channel_id=1, source_target_pairs={{0,2},{2,4},{4,6},{6,8},{8,10},{10,12},{12,14},{1,3},{3,5},{5,7},{... | collective-permute-start | bytes 1572872 | tf_op jit(solution)/shard_map/ppermute | solution.py:604
  11.0 1.3 %collective-permute-start.4 = (f32[2,4,128,128]{3,2,1,0:T(8,128)}, f32[2,4,128,128]{3,2,1,0:T(8,128)S(1)}, u32[]{:S(2)}, u32[]{:S(2)}) collective-permute-start(f32[2,4,128,128]{3,2,1,0:T(8,128)} %get-tuple-element.45), channel_id=1, source_target_pairs={{2,0},{4,2},{6,4},{8,6},{10,8},{12,10},{14,12},{3,1},{5,3},{7,5},{... | collective-permute-start | bytes 1572872 | tf_op jit(solution)/shard_map/ppermute | solution.py:604
  12.3 2.7 %collective-permute-start.2 = (f32[2,32,16,128]{3,2,1,0:T(8,128)}, f32[2,32,16,128]{3,2,1,0:T(8,128)S(1)}, u32[]{:S(2)}, u32[]{:S(2)}) collective-permute-start(f32[2,32,16,128]{3,2,1,0:T(8,128)} %get-tuple-element.41.refs_0_), channel_id=1, source_target_pairs={{0,2},{2,0},{4,6},{6,4},{8,10},{10,8},{12,14},{14,12},{1,3},{3,1},... | collective-permute-start | bytes 1572872 | tf_op jit(solution)/shard_map/ppermute | solution.py:604
  15.0 17.9 %inner.1 = (f32[2,16,32,128]{3,2,1,0:T(8,128)}, f32[32,32,128]{2,1,0:T(8,128)}, f32[2,32,128]{2,1,0:T(8,128)}, f32[2,2,8,128,128]{4,3,2,1,0:T(8,128)}) custom-call(f32[1,32,128,128]{3,2,1,0:T(8,128)} %source.5, f32[1,32,128,128]{3,2,1,0:T(8,128)} %receiver.5, f32[1,32,128,128]{3,2,1,0:T(8,128)} %source_before.3, f32[1,32,128,128]{3,2,1,0:T(8,128)} %receiver_before.3, ...), custom_call_target="tpu_custom_call" | custom-call | flops 20000000000 | bytes 1048576 | tf_op jit(solution)/shard_map/inner/pallas_call | solution.py:254
  33.0 1.8 %collective-permute-done.3.left = f32[2,4,128,128]{3,2,1,0:T(8,128)S(1)} collective-permute-done((f32[2,4,128,128]{3,2,1,0:T(8,128)}, f32[2,4,128,128]{3,2,1,0:T(8,128)S(1)}, u32[]{:S(2)}, u32[]{:S(2)}) %collective-permute-start.3) | collective-permute-done | bytes 524320 | tf_op jit(solution)/shard_map/ppermute | solution.py:604
  35.8 9.4 %outer.1 = (f32[2,2,8,32,128]{4,3,2,1,0:T(8,128)}, f32[2,4,32,128]{3,2,1,0:T(8,128)}, f32[2,4,32,128]{3,2,1,0:T(8,128)}, f32[2,32,128]{2,1,0:T(8,128)}) custom-call(f32[1,32,128,128]{3,2,1,0:T(8,128)} %source.5, f32[1,32,128,128]{3,2,1,0:T(8,128)} %receiver.5, f32[1,32,128,128]{3,2,1,0:T(8,128)} %source_before.3, f32[1,32,128,128]{3,2,1,0:T(8,128)} %receiver_before.3, ...), custom_call_target="tpu_custom_call" | custom-call | flops 1000000 | bytes 1048576 | tf_op jit(solution)/shard_map/outer/pallas_call | solution.py:365
  45.8 2.4 %collective-permute-start.9 = (f32[2,32,16,128]{3,2,1,0:T(8,128)S(1)}, f32[2,32,16,128]{3,2,1,0:T(8,128)S(1)}, u32[]{:S(2)}, u32[]{:S(2)}) collective-permute-start(f32[2,32,16,128]{3,2,1,0:T(8,128)S(1)} %collective-permute-done.1.refs_3_), channel_id=1, source_target_pairs={{0,2},{2,0},{4,6},{6,4},{8,10},{10,8},{12,14},{14,12},{1,3},{3,1},... | collective-permute-start | bytes 1572872 | tf_op jit(solution)/shard_map/ppermute | solution.py:604
  48.2 1.9 %collective-permute-start.5 = (f32[2,4,32,128]{3,2,1,0:T(8,128)}, f32[2,4,32,128]{3,2,1,0:T(8,128)S(1)}, u32[]{:S(2)}, u32[]{:S(2)}) collective-permute-start(f32[2,4,32,128]{3,2,1,0:T(8,128)} %get-tuple-element.47), channel_id=1, source_target_pairs={{0,2},{2,4},{4,6},{6,8},{8,10},{10,12},{12,14},{1,3},{3,5},{5,7},{... | collective-permute-start | bytes 393224 | tf_op jit(solution)/shard_map/ppermute | solution.py:604
  50.1 1.3 %collective-permute-start.6 = (f32[2,4,32,128]{3,2,1,0:T(8,128)}, f32[2,4,32,128]{3,2,1,0:T(8,128)S(1)}, u32[]{:S(2)}, u32[]{:S(2)}) collective-permute-start(f32[2,4,32,128]{3,2,1,0:T(8,128)} %get-tuple-element.48), channel_id=1, source_target_pairs={{2,0},{4,2},{6,4},{8,6},{10,8},{12,10},{14,12},{3,1},{5,3},{7,5},{... | collective-permute-start | bytes 393224 | tf_op jit(solution)/shard_map/ppermute | solution.py:604
  51.4 7.0 %collective-permute-start.8 = (f32[2,32,16,128]{3,2,1,0:T(8,128)S(1)}, f32[2,32,16,128]{3,2,1,0:T(8,128)S(1)}, u32[]{:S(2)}, u32[]{:S(2)}) collective-permute-start(f32[2,32,16,128]{3,2,1,0:T(8,128)S(1)} %collective-permute-done.2.refs_1_), channel_id=1, source_target_pairs={{0,4},{4,8},{8,12},{6,2},{10,6},{14,10},{1,5},{5,9},{9,13},{7,3},{... | collective-permute-start | bytes 1572872 | tf_op jit(solution)/shard_map/ppermute | solution.py:604
  59.5 1.5 %finish_middle.1 = (f32[2,24,16,128]{3,2,1,0:T(8,128)S(1)}, f32[2,24,16,128]{3,2,1,0:T(8,128)S(1)}) custom-call(f32[2,16,32,128]{3,2,1,0:T(8,128)S(1)} %copy-done.4, f32[2,2,8,32,128]{4,3,2,1,0:T(8,128)S(1)} %copy-done.1, f32[32,32,128]{2,1,0:T(8,128)S(1)} %copy-done.3, f32[2,32,128]{2,1,0:T(8,128)S(1)} %collective-permute-done.7.side), custom_call_target="tpu_custom_call" | custom-call | flops 10000000000 | bytes 3145728 | tf_op jit(solution)/shard_map/finish_middle/pallas_call | solution.py:422
  62.0 2.5 %collective-permute-start.13 = (f32[2,24,16,128]{3,2,1,0:T(8,128)S(1)}, f32[2,24,16,128]{3,2,1,0:T(8,128)S(1)}, u32[]{:S(2)}, u32[]{:S(2)}) collective-permute-start(f32[2,24,16,128]{3,2,1,0:T(8,128)S(1)} %get-tuple-element.67.refs_0_), channel_id=1, source_target_pairs={{0,2},{2,0},{4,6},{6,4},{8,10},{10,8},{12,14},{14,12},{1,3},{3,1},... | collective-permute-start | bytes 1179656 | tf_op jit(solution)/shard_map/ppermute | solution.py:604
  64.5 3.6 %collective-permute-start.10 = (f32[2,32,16,128]{3,2,1,0:T(8,128)S(1)}, f32[2,32,16,128]{3,2,1,0:T(8,128)S(1)}, u32[]{:S(2)}, u32[]{:S(2)}) collective-permute-start(f32[2,32,16,128]{3,2,1,0:T(8,128)S(1)} %collective-permute-done.9.refs_4_), channel_id=1, source_target_pairs={{0,4},{4,8},{8,12},{6,2},{10,6},{14,10},{1,5},{5,9},{9,13},{7,3},{... | collective-permute-start | bytes 1572872 | tf_op jit(solution)/shard_map/ppermute | solution.py:604
  69.2 5.3 %collective-permute-done.13.refs_1_ = f32[2,24,16,128]{3,2,1,0:T(8,128)S(1)} collective-permute-done((f32[2,24,16,128]{3,2,1,0:T(8,128)S(1)}, f32[2,24,16,128]{3,2,1,0:T(8,128)S(1)}, u32[]{:S(2)}, u32[]{:S(2)}) %collective-permute-start.13) | collective-permute-done | bytes 393248 | tf_op jit(solution)/shard_map/ppermute | solution.py:604
  74.5 1.3 %collective-permute-start.15 = (f32[2,2,8,16,128]{4,3,2,1,0:T(8,128)S(1)}, f32[2,2,8,16,128]{4,3,2,1,0:T(8,128)S(1)}, u32[]{:S(2)}, u32[]{:S(2)}) collective-permute-start(f32[2,2,8,16,128]{4,3,2,1,0:T(8,128)S(1)} %pad_maximum_fusion.refs_6_), channel_id=1, source_target_pairs={{2,0},{4,2},{6,4},{8,6},{10,8},{12,10},{14,12},{3,1},{5,3},{7,5},{... | collective-permute-start | bytes 786440 | tf_op jit(solution)/shard_map/ppermute | solution.py:604
  75.8 4.6 %collective-permute-start.14 = (f32[2,2,8,16,128]{4,3,2,1,0:T(8,128)S(1)}, f32[2,2,8,16,128]{4,3,2,1,0:T(8,128)S(1)}, u32[]{:S(2)}, u32[]{:S(2)}) collective-permute-start(f32[2,2,8,16,128]{4,3,2,1,0:T(8,128)S(1)} %pad_maximum_fusion.refs_6_), channel_id=1, source_target_pairs={{0,2},{2,4},{4,6},{6,8},{8,10},{10,12},{12,14},{1,3},{3,5},{5,7},{... | collective-permute-start | bytes 786440 | tf_op jit(solution)/shard_map/ppermute | solution.py:604
  80.4 5.3 %collective-permute-start.16 = (f32[2,24,16,128]{3,2,1,0:T(8,128)S(1)}, f32[2,24,16,128]{3,2,1,0:T(8,128)S(1)}, u32[]{:S(2)}, u32[]{:S(2)}) collective-permute-start(f32[2,24,16,128]{3,2,1,0:T(8,128)S(1)} %collective-permute-done.13.refs_1_), channel_id=1, source_target_pairs={{0,4},{4,8},{8,12},{6,2},{10,6},{14,10},{1,5},{5,9},{9,13},{7,3},{... | collective-permute-start | bytes 1179656 | tf_op jit(solution)/shard_map/ppermute | solution.py:604
  85.7 2.3 %collective-permute-done.17.refs_4_ = f32[2,24,16,128]{3,2,1,0:T(8,128)S(1)} collective-permute-done((f32[2,24,16,128]{3,2,1,0:T(8,128)S(1)}, f32[2,24,16,128]{3,2,1,0:T(8,128)S(1)}, u32[]{:S(2)}, u32[]{:S(2)}) %collective-permute-start.17) | collective-permute-done | bytes 393248 | tf_op jit(solution)/shard_map/ppermute | solution.py:604
  88.0 5.8 %collective-permute-start.18 = (f32[2,24,16,128]{3,2,1,0:T(8,128)S(1)}, f32[2,24,16,128]{3,2,1,0:T(8,128)S(1)}, u32[]{:S(2)}, u32[]{:S(2)}) collective-permute-start(f32[2,24,16,128]{3,2,1,0:T(8,128)S(1)} %collective-permute-done.17.refs_4_), channel_id=1, source_target_pairs={{0,4},{4,8},{8,12},{6,2},{10,6},{14,10},{1,5},{5,9},{9,13},{7,3},{... | collective-permute-start | bytes 1179656 | tf_op jit(solution)/shard_map/ppermute | solution.py:604
  93.8 1.5 %first_image.1.refs_0_.first = f32[8,65,16,128]{3,2,1,0:T(8,128)S(1)} custom-call(f32[2,32,16,128]{3,2,1,0:T(8,128)S(1)} %copy-done, f32[2,32,16,128]{3,2,1,0:T(8,128)S(1)} %collective-permute-done.2.refs_1_, f32[2,32,16,128]{3,2,1,0:T(8,128)S(1)} %collective-permute-done.8.refs_2_, f32[2,32,16,128]{3,2,1,0:T(8,128)S(1)} %collective-permute-done.1.refs_3_, ...), custom_call_target="tpu_custom_call" | custom-call | flops 10000000000 | bytes 8388608 | tf_op jit(solution)/shard_map/first_image/pallas_call | solution.py:507
  95.9 5.8 %collective-permute-done.18.refs_5_ = f32[2,24,16,128]{3,2,1,0:T(8,128)S(1)} collective-permute-done((f32[2,24,16,128]{3,2,1,0:T(8,128)S(1)}, f32[2,24,16,128]{3,2,1,0:T(8,128)S(1)}, u32[]{:S(2)}, u32[]{:S(2)}) %collective-permute-start.18) | collective-permute-done | bytes 393248 | tf_op jit(solution)/shard_map/ppermute | solution.py:604
  101.6 8.2 %image.1 = f32[8,32,64,65]{3,2,1,0:T(8,128)} custom-call(s32[1]{0:T(128)} %in_order.1.token, f32[8,65,16,128]{3,2,1,0:T(8,128)S(1)} %first_image.1.refs_0_.first, f32[2,24,16,128]{3,2,1,0:T(8,128)S(1)} %get-tuple-element.67.refs_0_, f32[2,24,16,128]{3,2,1,0:T(8,128)S(1)} %collective-permute-done.13.refs_1_, ...), custom_call_target="tpu_custom_call" | custom-call | flops 10000000000 | bytes 16777216 | tf_op jit(solution)/shard_map/image/pallas_call | solution.py:562
  (39 shorter events, 5.7 us)
Async XLA Ops:
  4.5 7.8 %collective-permute-start.1 = (f32[2,32,16,128]{3,2,1,0:T(8,128)}, f32[2,32,16,128]{3,2,1,0:T(8,128)S(1)}, u32[]{:S(2)}, u32[]{:S(2)}) collective-permute-start(f32[2,32,16,128]{3,2,1,0:T(8,128)} %get-tuple-element.40), channel_id=1, source_target_pairs={{0,16},{16,0},{1,17},{17,1},{2,18},{18,2},{3,19},{19,3},{4,20},{20... | collective-permute-start | bytes 1572872 | tf_op jit(solution)/shard_map/ppermute | solution.py:604
  5.0 7.3 %collective-permute-start = (f32[32,8,128]{2,1,0:T(8,128)}, f32[32,8,128]{2,1,0:T(8,128)S(1)}, u32[]{:S(2)}, u32[]{:S(2)}) collective-permute-start(f32[32,8,128]{2,1,0:T(8,128)} %get-tuple-element.38), channel_id=1, source_target_pairs={{0,1},{1,0},{2,3},{3,2},{4,5},{5,4},{6,7},{7,6},{8,9},{9,8},{10,11... | collective-permute-start | bytes 393224 | tf_op jit(solution)/shard_map/ppermute | solution.py:604
  7.5 27.2 %collective-permute-start.3 = (f32[2,4,128,128]{3,2,1,0:T(8,128)}, f32[2,4,128,128]{3,2,1,0:T(8,128)S(1)}, u32[]{:S(2)}, u32[]{:S(2)}) collective-permute-start(f32[2,4,128,128]{3,2,1,0:T(8,128)} %get-tuple-element.44), channel_id=1, source_target_pairs={{0,2},{2,4},{4,6},{6,8},{8,10},{10,12},{12,14},{1,3},{3,5},{5,7},{... | collective-permute-start | bytes 1572872 | tf_op jit(solution)/shard_map/ppermute | solution.py:604
  11.0 23.8 %collective-permute-start.4 = (f32[2,4,128,128]{3,2,1,0:T(8,128)}, f32[2,4,128,128]{3,2,1,0:T(8,128)S(1)}, u32[]{:S(2)}, u32[]{:S(2)}) collective-permute-start(f32[2,4,128,128]{3,2,1,0:T(8,128)} %get-tuple-element.45), channel_id=1, source_target_pairs={{2,0},{4,2},{6,4},{8,6},{10,8},{12,10},{14,12},{3,1},{5,3},{7,5},{... | collective-permute-start | bytes 1572872 | tf_op jit(solution)/shard_map/ppermute | solution.py:604
  12.3 2.7 %copy-start.7 = (f32[32,8,128]{2,1,0:T(8,128)}, f32[32,8,128]{2,1,0:T(8,128)S(1)}, u32[]{:S(2)}) copy-start(f32[32,8,128]{2,1,0:T(8,128)S(1)} %collective-permute-done.side) | copy-start | bytes 393220
  12.3 39.1 %collective-permute-start.2 = (f32[2,32,16,128]{3,2,1,0:T(8,128)}, f32[2,32,16,128]{3,2,1,0:T(8,128)S(1)}, u32[]{:S(2)}, u32[]{:S(2)}) collective-permute-start(f32[2,32,16,128]{3,2,1,0:T(8,128)} %get-tuple-element.41.refs_0_), channel_id=1, source_target_pairs={{0,2},{2,0},{4,6},{6,4},{8,10},{10,8},{12,14},{14,12},{1,3},{3,1},... | collective-permute-start | bytes 1572872 | tf_op jit(solution)/shard_map/ppermute | solution.py:604
  35.8 22.7 %copy-start.3 = (f32[32,32,128]{2,1,0:T(8,128)S(1)}, f32[32,32,128]{2,1,0:T(8,128)}, u32[]{:S(2)}) copy-start(f32[32,32,128]{2,1,0:T(8,128)} %get-tuple-element.55.kept_courant) | copy-start | bytes 1572868
  35.8 22.7 %copy-start.4 = (f32[2,16,32,128]{3,2,1,0:T(8,128)S(1)}, f32[2,16,32,128]{3,2,1,0:T(8,128)}, u32[]{:S(2)}) copy-start(f32[2,16,32,128]{3,2,1,0:T(8,128)} %get-tuple-element.53.inside) | copy-start | bytes 1572868
  45.2 6.2 %collective-permute-start.7 = (f32[2,32,128]{2,1,0:T(8,128)}, f32[2,32,128]{2,1,0:T(8,128)S(1)}, u32[]{:S(2)}, u32[]{:S(2)}) collective-permute-start(f32[2,32,128]{2,1,0:T(8,128)} %get-tuple-element.49), channel_id=1, source_target_pairs={{0,1},{1,0},{2,3},{3,2},{4,5},{5,4},{6,7},{7,6},{8,9},{9,8},{10,11... | collective-permute-start | bytes 98312 | tf_op jit(solution)/shard_map/ppermute | solution.py:604
  45.8 16.2 %collective-permute-start.9 = (f32[2,32,16,128]{3,2,1,0:T(8,128)S(1)}, f32[2,32,16,128]{3,2,1,0:T(8,128)S(1)}, u32[]{:S(2)}, u32[]{:S(2)}) collective-permute-start(f32[2,32,16,128]{3,2,1,0:T(8,128)S(1)} %collective-permute-done.1.refs_3_), channel_id=1, source_target_pairs={{0,2},{2,0},{4,6},{6,4},{8,10},{10,8},{12,14},{14,12},{1,3},{3,1},... | collective-permute-start | bytes 1572872 | tf_op jit(solution)/shard_map/ppermute | solution.py:604
  48.2 16.3 %collective-permute-start.5 = (f32[2,4,32,128]{3,2,1,0:T(8,128)}, f32[2,4,32,128]{3,2,1,0:T(8,128)S(1)}, u32[]{:S(2)}, u32[]{:S(2)}) collective-permute-start(f32[2,4,32,128]{3,2,1,0:T(8,128)} %get-tuple-element.47), channel_id=1, source_target_pairs={{0,2},{2,4},{4,6},{6,8},{8,10},{10,12},{12,14},{1,3},{3,5},{5,7},{... | collective-permute-start | bytes 393224 | tf_op jit(solution)/shard_map/ppermute | solution.py:604
  50.1 18.1 %collective-permute-start.6 = (f32[2,4,32,128]{3,2,1,0:T(8,128)}, f32[2,4,32,128]{3,2,1,0:T(8,128)S(1)}, u32[]{:S(2)}, u32[]{:S(2)}) collective-permute-start(f32[2,4,32,128]{3,2,1,0:T(8,128)} %get-tuple-element.48), channel_id=1, source_target_pairs={{2,0},{4,2},{6,4},{8,6},{10,8},{12,10},{14,12},{3,1},{5,3},{7,5},{... | collective-permute-start | bytes 393224 | tf_op jit(solution)/shard_map/ppermute | solution.py:604
  51.4 16.8 %collective-permute-start.8 = (f32[2,32,16,128]{3,2,1,0:T(8,128)S(1)}, f32[2,32,16,128]{3,2,1,0:T(8,128)S(1)}, u32[]{:S(2)}, u32[]{:S(2)}) collective-permute-start(f32[2,32,16,128]{3,2,1,0:T(8,128)S(1)} %collective-permute-done.2.refs_1_), channel_id=1, source_target_pairs={{0,4},{4,8},{8,12},{6,2},{10,6},{14,10},{1,5},{5,9},{9,13},{7,3},{... | collective-permute-start | bytes 1572872 | tf_op jit(solution)/shard_map/ppermute | solution.py:604
  59.5 8.7 %copy-start.2 = (f32[2,2,8,32,128]{4,3,2,1,0:T(8,128)S(1)}, f32[2,2,8,32,128]{4,3,2,1,0:T(8,128)}, u32[]{:S(2)}) copy-start(f32[2,2,8,32,128]{4,3,2,1,0:T(8,128)} %get-tuple-element.54.ends) | copy-start | bytes 1572868
  62.0 31.8 %copy-start = (f32[2,32,16,128]{3,2,1,0:T(8,128)S(1)}, f32[2,32,16,128]{3,2,1,0:T(8,128)}, u32[]{:S(2)}) copy-start(f32[2,32,16,128]{3,2,1,0:T(8,128)} %get-tuple-element.41.refs_0_) | copy-start | bytes 1572868
  62.0 6.3 %collective-permute-start.11 = (f32[2,24,16,128]{3,2,1,0:T(8,128)S(1)}, f32[2,24,16,128]{3,2,1,0:T(8,128)S(1)}, u32[]{:S(2)}, u32[]{:S(2)}) collective-permute-start(f32[2,24,16,128]{3,2,1,0:T(8,128)S(1)} %get-tuple-element.60), channel_id=1, source_target_pairs={{0,16},{16,0},{1,17},{17,1},{2,18},{18,2},{3,19},{19,3},{4,20},{20... | collective-permute-start | bytes 1179656 | tf_op jit(solution)/shard_map/ppermute | solution.py:604
  62.0 12.4 %collective-permute-start.13 = (f32[2,24,16,128]{3,2,1,0:T(8,128)S(1)}, f32[2,24,16,128]{3,2,1,0:T(8,128)S(1)}, u32[]{:S(2)}, u32[]{:S(2)}) collective-permute-start(f32[2,24,16,128]{3,2,1,0:T(8,128)S(1)} %get-tuple-element.67.refs_0_), channel_id=1, source_target_pairs={{0,2},{2,0},{4,6},{6,4},{8,10},{10,8},{12,14},{14,12},{1,3},{3,1},... | collective-permute-start | bytes 1179656 | tf_op jit(solution)/shard_map/ppermute | solution.py:604
  64.5 29.3 %collective-permute-start.10 = (f32[2,32,16,128]{3,2,1,0:T(8,128)S(1)}, f32[2,32,16,128]{3,2,1,0:T(8,128)S(1)}, u32[]{:S(2)}, u32[]{:S(2)}) collective-permute-start(f32[2,32,16,128]{3,2,1,0:T(8,128)S(1)} %collective-permute-done.9.refs_4_), channel_id=1, source_target_pairs={{0,4},{4,8},{8,12},{6,2},{10,6},{14,10},{1,5},{5,9},{9,13},{7,3},{... | collective-permute-start | bytes 1572872 | tf_op jit(solution)/shard_map/ppermute | solution.py:604
  68.4 19.6 %collective-permute-start.17 = (f32[2,24,16,128]{3,2,1,0:T(8,128)S(1)}, f32[2,24,16,128]{3,2,1,0:T(8,128)S(1)}, u32[]{:S(2)}, u32[]{:S(2)}) collective-permute-start(f32[2,24,16,128]{3,2,1,0:T(8,128)S(1)} %collective-permute-done.11.refs_3_), channel_id=1, source_target_pairs={{0,2},{2,0},{4,6},{6,4},{8,10},{10,8},{12,14},{14,12},{1,3},{3,1},... | collective-permute-start | bytes 1179656 | tf_op jit(solution)/shard_map/ppermute | solution.py:604
  69.2 5.3 %collective-permute-start.12 = (f32[2,8,16,128]{3,2,1,0:T(8,128)S(1)}, f32[2,8,16,128]{3,2,1,0:T(8,128)S(1)}, u32[]{:S(2)}, u32[]{:S(2)}) collective-permute-start(f32[2,8,16,128]{3,2,1,0:T(8,128)S(1)} %get-tuple-element.66), channel_id=1, source_target_pairs={{0,16},{16,0},{1,17},{17,1},{2,18},{18,2},{3,19},{19,3},{4,20},{20... | collective-permute-start | bytes 393224 | tf_op jit(solution)/shard_map/ppermute | solution.py:604
  74.5 20.8 %collective-permute-start.15 = (f32[2,2,8,16,128]{4,3,2,1,0:T(8,128)S(1)}, f32[2,2,8,16,128]{4,3,2,1,0:T(8,128)S(1)}, u32[]{:S(2)}, u32[]{:S(2)}) collective-permute-start(f32[2,2,8,16,128]{4,3,2,1,0:T(8,128)S(1)} %pad_maximum_fusion.refs_6_), channel_id=1, source_target_pairs={{2,0},{4,2},{6,4},{8,6},{10,8},{12,10},{14,12},{3,1},{5,3},{7,5},{... | collective-permute-start | bytes 786440 | tf_op jit(solution)/shard_map/ppermute | solution.py:604
  75.8 19.5 %collective-permute-start.14 = (f32[2,2,8,16,128]{4,3,2,1,0:T(8,128)S(1)}, f32[2,2,8,16,128]{4,3,2,1,0:T(8,128)S(1)}, u32[]{:S(2)}, u32[]{:S(2)}) collective-permute-start(f32[2,2,8,16,128]{4,3,2,1,0:T(8,128)S(1)} %pad_maximum_fusion.refs_6_), channel_id=1, source_target_pairs={{0,2},{2,4},{4,6},{6,8},{8,10},{10,12},{12,14},{1,3},{3,5},{5,7},{... | collective-permute-start | bytes 786440 | tf_op jit(solution)/shard_map/ppermute | solution.py:604
  80.4 15.0 %collective-permute-start.16 = (f32[2,24,16,128]{3,2,1,0:T(8,128)S(1)}, f32[2,24,16,128]{3,2,1,0:T(8,128)S(1)}, u32[]{:S(2)}, u32[]{:S(2)}) collective-permute-start(f32[2,24,16,128]{3,2,1,0:T(8,128)S(1)} %collective-permute-done.13.refs_1_), channel_id=1, source_target_pairs={{0,4},{4,8},{8,12},{6,2},{10,6},{14,10},{1,5},{5,9},{9,13},{7,3},{... | collective-permute-start | bytes 1179656 | tf_op jit(solution)/shard_map/ppermute | solution.py:604
  88.0 13.6 %collective-permute-start.18 = (f32[2,24,16,128]{3,2,1,0:T(8,128)S(1)}, f32[2,24,16,128]{3,2,1,0:T(8,128)S(1)}, u32[]{:S(2)}, u32[]{:S(2)}) collective-permute-start(f32[2,24,16,128]{3,2,1,0:T(8,128)S(1)} %collective-permute-done.17.refs_4_), channel_id=1, source_target_pairs={{0,4},{4,8},{8,12},{6,2},{10,6},{14,10},{1,5},{5,9},{9,13},{7,3},{... | collective-permute-start | bytes 1179656 | tf_op jit(solution)/shard_map/ppermute | solution.py:604
  (3 other events, 2.8 us)

commit v6 on v5

--- a/solution.py
+++ b/solution.py
@@ -13,6 +13,7 @@
 OFFSETS = 2 * HALF + 1
 OFFSET_ROWS = 72
 LINES = 32
+STEPS_MIB = 40
 WEIGHTS = (-205.0 / 72.0, 8.0 / 5.0, -1.0 / 5.0, 8.0 / 315.0, -1.0 / 560.0)
 PAD = 8
 F32 = jnp.float32
@@ -176,213 +177,184 @@
     after[field, row, size_y + PAD : size_y + PAD + REACH, :] = blank
 
 
-def inner_kernel(
+def steps_kernel(
     source, receiver, source_before, receiver_before, courant, side,
-    partial, kept_courant, side_out, border, now, before, scale, after, sems, out_sems,
+    partial, kept_courant, edge_courant, edge, side_out, now, before, scale, after, sems,
 ):
     gy = lax.axis_index("gy")
     rows, size_y, size_z = courant.shape
     lines = size_y // KEEP_EVERY
-    copies = []
-
-    def copy(src, dst):
-        copies.append(pltpu.make_async_copy(src, dst, sems.at[len(copies)]))
-
+    piece = 2 * REACH
     middle = pl.ds(PAD, size_y)
-    for field, ref in enumerate((source, receiver)):
-        copy(ref.at[0], now.at[field, :, middle])
-    for field, ref in enumerate((source_before, receiver_before)):
-        copy(ref.at[0], before.at[field])
-    copy(courant, scale)
-    for one in copies:
-        one.start()
+
+    def copies(index):
+        part = pl.ds(piece * index, piece)
+        found = []
+        for field in range(2):
+            src = (source, receiver)[field].at[0, part]
+            dst = now.at[field, pl.ds(REACH + piece * index, piece), middle]
+            found.append(pltpu.make_async_copy(src, dst, sems.at[index, field]))
+        for field in range(2):
+            src = (source_before, receiver_before)[field].at[0, part]
+            found.append(pltpu.make_async_copy(src, before.at[field, part], sems.at[index, 2 + field]))
+        found.append(pltpu.make_async_copy(courant.at[part], scale.at[part], sems.at[index, 4]))
+        return found
+
+    for index in range(rows // piece):
+        for one in copies(index):
+            one.start()
+
+    for field in range(2):
+        for row in list(range(REACH)) + list(range(rows + REACH, rows + 2 * REACH)):
+            now[field, row] = jnp.zeros((size_y + 2 * PAD, size_z), F32)
+            after[field, row] = jnp.zeros((size_y + 2 * PAD, size_z), F32)
 
     def fill(row, carry):
         for field in range(2):
             got = side[row, field * REACH : (field + 1) * REACH, :]
-            fill_sides(now, row, got, field, size_y, gy)
-            blank_sides(after, row, field, size_y)
+            fill_sides(now, row + REACH, got, field, size_y, gy)
+            blank_sides(after, row + REACH, field, size_y)
         return carry
 
     lax.fori_loop(0, rows, fill, 0)
-    side_out[...] = jnp.zeros_like(side_out)
-    for one in copies:
+    masks = z_weights(size_z)
+    for one in copies(0)[:2]:
         one.wait()
-    masks = z_weights(size_z)
 
     def first(row, carry):
+        @pl.when(row % piece == 0)
+        def _():
+            index = row // piece
+            for one in copies(index)[2:]:
+                one.wait()
+
+            @pl.when(index + 1 < rows // piece)
+            def _():
+                for one in copies(index + 1)[:2]:
+                    one.wait()
+
+        at = row + REACH
         for field in range(2):
-            first_step(now, row, before, row, scale, row, after, row, field, masks)
-            side_out[field, pl.ds(row, 1), :] = side_term(after, row, field, size_y, gy)
+            first_step(now, at, before, row, scale, row, after, at, field, masks)
+            side_out[field, pl.ds(row, 1), :] = side_term(after, at, field, size_y, gy)
         return carry
 
-    lax.fori_loop(REACH, rows - REACH, first, 0)
-    outs = []
-    for field in range(2):
-        for end, start in enumerate((REACH, rows - 3 * REACH)):
-            outs.append(
-                pltpu.make_async_copy(
-                    after.at[field, pl.ds(start, 2 * REACH), middle],
-                    border.at[field, end],
-                    out_sems.at[len(outs)],
-                )
-            )
-            outs[-1].start()
+    lax.fori_loop(0, rows, first, 0)
 
     def second(row, carry):
+        at = row + REACH
+        kept_courant[row] = scale[row, pl.ds(0, lines, stride=KEEP_EVERY), :]
         for field in range(2):
             def store(value):
-                partial[field, row - 2 * REACH] = value
-
-            second_step(now, row, scale, row, after, row, field, masks, store)
+                partial[field, row] = value
+
+            second_step(now, at, scale, row, after, at, field, masks, store)
         return carry
 
-    lax.fori_loop(2 * REACH, rows - 2 * REACH, second, 0)
-
-    def keep(row, carry):
-        kept_courant[row] = scale[row, pl.ds(0, lines, stride=KEEP_EVERY), :]
-        return carry
-
-    lax.fori_loop(0, rows, keep, 0)
-    for one in outs:
-        one.wait()
-
-
-def inner(source, receiver, source_before, receiver_before, courant, side):
+    lax.fori_loop(0, rows, second, 0)
+    for end in range(2):
+        for row in range(REACH):
+            at = rows - 1 - row if end else row
+            edge_courant[end, row] = scale[at]
+            for field in range(2):
+                edge[field, end, row] = after[field, REACH + at, pl.ds(PAD, lines, stride=KEEP_EVERY), :]
+
+
+def steps(source, receiver, source_before, receiver_before, courant, side):
     rows, size_y, size_z = courant.shape
     lines = size_y // KEEP_EVERY
     return pl.pallas_call(
-        inner_kernel,
+        steps_kernel,
         out_shape=(
-            jax.ShapeDtypeStruct((2, rows - 4 * REACH, lines, size_z), F32),
+            jax.ShapeDtypeStruct((2, rows, lines, size_z), F32),
             jax.ShapeDtypeStruct((rows, lines, size_z), F32),
+            jax.ShapeDtypeStruct((2, REACH, size_y, size_z), F32),
+            jax.ShapeDtypeStruct((2, 2, REACH, lines, size_z), F32),
             jax.ShapeDtypeStruct((2, rows, size_z), F32),
-            jax.ShapeDtypeStruct((2, 2, 2 * REACH, size_y, size_z), F32),
         ),
         in_specs=[HBM] * 5 + [VMEM],
-        out_specs=(VMEM,) * 3 + (HBM,),
+        out_specs=(VMEM,) * 5,
         scratch_shapes=[
-            pltpu.VMEM((2, rows, size_y + 2 * PAD, size_z), F32),
+            pltpu.VMEM((2, rows + 2 * REACH, size_y + 2 * PAD, size_z), F32),
             pltpu.VMEM((2, rows, size_y, size_z), F32),
             pltpu.VMEM((rows, size_y, size_z), F32),
-            pltpu.VMEM((2, rows, size_y + 2 * PAD, size_z), F32),
-            pltpu.SemaphoreType.DMA((5,)),
-            pltpu.SemaphoreType.DMA((4,)),
+            pltpu.VMEM((2, rows + 2 * REACH, size_y + 2 * PAD, size_z), F32),
+            pltpu.SemaphoreType.DMA((rows // (2 * REACH), 5)),
         ],
-        compiler_params=params(60),
+        compiler_params=params(STEPS_MIB),
         cost_estimate=cost(2 * 10**10, 2**20),
-        name="inner",
+        name="steps",
     )(source, receiver, source_before, receiver_before, courant, side)
 
 
-def outer_kernel(
-    source, receiver, source_before, receiver_before, courant, border, left, right, side, side_in,
-    partial, up, down, side_out, now, before, scale, after, sems,
+def mend_kernel(
+    left, right, partial, kept_courant, edge_courant, edge, side_in,
+    ends, up, down, side_out, added,
 ):
     gy = lax.axis_index("gy")
-    rows, size_y, size_z = courant.shape
-    lines = size_y // KEEP_EVERY
-    reach2 = 2 * REACH
-    copies = []
-
-    def copy(src, dst):
-        copies.append(pltpu.make_async_copy(src, dst, sems.at[len(copies)]))
-
-    middle = pl.ds(PAD, size_y)
-    for field in range(2):
-        ref = (source, receiver)[field]
-        copy(ref.at[0, pl.ds(0, reach2)], now.at[field, pl.ds(REACH, reach2), middle])
-        copy(left.at[field], now.at[field, pl.ds(0, REACH), middle])
-        copy(ref.at[0, pl.ds(rows - reach2, reach2)], now.at[2 + field, pl.ds(0, reach2), middle])
-        copy(right.at[field], now.at[2 + field, pl.ds(reach2, REACH), middle])
-        ref = (source_before, receiver_before)[field]
-        copy(ref.at[0, pl.ds(0, REACH)], before.at[field])
-        copy(ref.at[0, pl.ds(rows - REACH, REACH)], before.at[2 + field])
-        copy(border.at[field, 0], after.at[field, pl.ds(reach2, reach2), middle])
-        copy(border.at[field, 1], after.at[2 + field, pl.ds(0, reach2), middle])
-    copy(courant.at[pl.ds(0, reach2)], scale.at[pl.ds(0, reach2)])
-    copy(courant.at[pl.ds(rows - reach2, reach2)], scale.at[pl.ds(reach2, reach2)])
-    for one in copies:
-        one.start()
-
-    for field in range(2):
-        for row in range(REACH):
-            for end in range(2):
-                after[2 * end + field, 3 * REACH * end + row] = jnp.zeros((size_y + 2 * PAD, size_z), F32)
-        for row in range(reach2):
-            low = side[row, field * REACH : (field + 1) * REACH, :]
-            fill_sides(now, REACH + row, low, field, size_y, gy)
-            high = side[rows - reach2 + row, field * REACH : (field + 1) * REACH, :]
-            fill_sides(now, row, high, 2 + field, size_y, gy)
-            for end in range(2):
-                blank_sides(after, REACH + row, 2 * end + field, size_y)
+    rows, lines, size_z = kept_courant.shape
+    size_y = KEEP_EVERY * lines
+    masks = z_weights(size_z)
+    kept = lambda start: pl.ds(start, lines, stride=KEEP_EVERY)
     side_out[...] = side_in[...]
-    for one in copies:
-        one.wait()
-    masks = z_weights(size_z)
-
-    def first(row, carry):
+    for end in range(2):
         for field in range(2):
-            for end in range(2):
-                group = 2 * end + field
-                to = REACH * (1 + end) + row
-                first_step(
-                    now, REACH + row, before, row, scale, (2 * end + end) * REACH + row,
-                    after, to, group, masks,
-                )
-                side_out[field, pl.ds(end * (rows - REACH) + row, 1), :] = side_term(
-                    after, to, group, size_y, gy
-                )
-        return carry
-
-    lax.fori_loop(0, REACH, first, 0)
-    kept_lines = pl.ds(PAD, lines, stride=KEEP_EVERY)
-    for field in range(2):
-        for row in range(REACH):
-            down[field, row] = after[field, REACH + row, kept_lines, :]
-            up[field, row] = after[2 + field, reach2 + row, kept_lines, :]
-
-    def second(row, carry):
-        for field in range(2):
-            for end in range(2):
-                group = 2 * end + field
-
-                def store(value):
-                    partial[field, end, row] = value
-
-                second_step(
-                    now, (1 - end) * REACH + row, scale, end * reach2 + row, after, REACH + row, group, masks, store
-                )
-        return carry
-
-    lax.fori_loop(0, reach2, second, 0)
-
-
-def outer(source, receiver, source_before, receiver_before, courant, border, left, right, side, side_in):
-    rows, size_y, size_z = courant.shape
-    lines = size_y // KEEP_EVERY
+            group = 2 * end + field
+            for row in range(REACH):
+                blank_sides(added, row, group, size_y)
+                for chunk in range(size_y // LINES):
+                    here = pl.ds(LINES * chunk, LINES)
+                    total = None
+                    for d in range(row + 1, REACH + 1):
+                        beyond = d - row - 1
+                        halo = right[field, beyond, here, :] if end else left[field, REACH - 1 - beyond, here, :]
+                        term = WEIGHTS[d] * halo
+                        total = term if total is None else total + term
+                    added[group, row, pl.ds(PAD + LINES * chunk, LINES), :] = edge_courant[end, row, here, :] * total
+            for row in range(2 * REACH):
+                at = rows - 1 - row if end else row
+                total = None
+                for other in range(REACH):
+                    if 0 < abs(row - other) <= REACH:
+                        term = WEIGHTS[abs(row - other)] * added[group, other, kept(PAD), :]
+                        total = term if total is None else total + term
+                value = partial[field, at]
+                if row < REACH:
+                    center = added[group, row, kept(PAD), :]
+                    total = total + (3.0 * WEIGHTS[0]) * center + z_terms(center, masks)
+                    for d in range(1, REACH + 1):
+                        around = added[group, row, kept(PAD + d), :] + added[group, row, kept(PAD - d), :]
+                        total = total + WEIGHTS[d] * around
+                    value = value + 2.0 * center
+                    first = edge[field, end, row] + center
+                    if end:
+                        up[field, REACH - 1 - row] = first
+                    else:
+                        down[field, row] = first
+                    side_out[field, at : at + 1, :] = side_in[field, at : at + 1, :] + side_term(
+                        added, row, group, size_y, gy
+                    )
+                ends[field, end, row] = value + kept_courant[at] * total
+
+
+def mend(left, right, partial, kept_courant, edge_courant, edge, side_in):
+    rows, lines, size_z = kept_courant.shape
     halo = jax.ShapeDtypeStruct((2, REACH, lines, size_z), F32)
     return pl.pallas_call(
-        outer_kernel,
+        mend_kernel,
         out_shape=(
             jax.ShapeDtypeStruct((2, 2, 2 * REACH, lines, size_z), F32),
             halo,
             halo,
             jax.ShapeDtypeStruct((2, rows, size_z), F32),
         ),
-        in_specs=[HBM] * 8 + [VMEM] * 2,
+        in_specs=[VMEM] * 7,
         out_specs=(VMEM,) * 4,
-        scratch_shapes=[
-            pltpu.VMEM((4, 3 * REACH, size_y + 2 * PAD, size_z), F32),
-            pltpu.VMEM((4, REACH, size_y, size_z), F32),
-            pltpu.VMEM((4 * REACH, size_y, size_z), F32),
-            pltpu.VMEM((4, 4 * REACH, size_y + 2 * PAD, size_z), F32),
-            pltpu.SemaphoreType.DMA((18,)),
-        ],
-        compiler_params=params(60),
+        scratch_shapes=[pltpu.VMEM((4, REACH, KEEP_EVERY * lines + 2 * PAD, size_z), F32)],
+        compiler_params=params(24),
         cost_estimate=cost(10**6, 2**20),
-        name="outer",
-    )(source, receiver, source_before, receiver_before, courant, border, left, right, side, side_in)
+        name="mend",
+    )(left, right, partial, kept_courant, edge_courant, edge, side_in)
 
 
 def pack_row(value, field, row, shot, keep, give):
@@ -397,7 +369,7 @@
     return jnp.where(meets, side[field, pl.ds(row, 1), :], 0.0)
 
 
-def middle_kernel(inside, ends, kept_courant, side, keep, give):
+def middle_kernel(partial, ends, kept_courant, side, keep, give):
     shot, gy = lax.axis_index("shot"), lax.axis_index("gy")
     rows, lines, _ = kept_courant.shape
 
@@ -407,16 +379,16 @@
             pack_row(values[field] + kept_courant[row] * total, field, row - REACH, shot, keep, give)
 
     def middle(row, carry):
-        one_row(row, [inside[field, row - 2 * REACH] for field in range(2)])
+        one_row(row, [partial[field, row] for field in range(2)])
         return carry
 
     lax.fori_loop(2 * REACH, rows - 2 * REACH, middle, 0)
     for row in range(REACH, 2 * REACH):
         one_row(row, [ends[field, 0, row] for field in range(2)])
-        one_row(rows - 1 - row, [ends[field, 1, 2 * REACH - 1 - row] for field in range(2)])
-
-
-def finish_middle(inside, ends, kept_courant, side):
+        one_row(rows - 1 - row, [ends[field, 1, row] for field in range(2)])
+
+
+def finish_middle(partial, ends, kept_courant, side):
     rows, lines, size_z = kept_courant.shape
     half = jax.ShapeDtypeStruct((2, rows - 2 * REACH, lines // 2, size_z), F32)
     return pl.pallas_call(
@@ -427,7 +399,7 @@
         compiler_params=params(24),
         cost_estimate=cost(10**10, 3 * 2**20),
         name="finish_middle",
-    )(inside, ends, kept_courant, side)
+    )(partial, ends, kept_courant, side)
 
 
 def ends_kernel(ends, kept_courant, left, right, side, keep, give):
@@ -446,7 +418,7 @@
             above = above + side_lines(side, field, far, gy, lines)
             pack_row(ends[field, 0, row] + kept_courant[row] * below, field, row, shot, keep, give)
             pack_row(
-                ends[field, 1, 2 * REACH - 1 - row] + kept_courant[far] * above,
+                ends[field, 1, row] + kept_courant[far] * above,
                 field, 2 * REACH - 1 - row, shot, keep, give,
             )
 
@@ -613,19 +585,17 @@
     near_keep = exchange(keep, "gx", partner)
     near_other = exchange(other, "gx", partner)
     blocks = [keep, near_keep, None, other, near_other, None]
-    inside, kept_courant, side_in, border = inner(
+    partial, kept_courant, edge_courant, edge, side = steps(
         source_now, receiver_now, source_before, receiver_before, courant, side
     )
-    ends, up, down, side = outer(
-        source_now, receiver_now, source_before, receiver_before, courant, border, left, right, side, side_in
-    )
+    ends, up, down, side = mend(left, right, partial, kept_courant, edge_courant, edge, side)
     left = exchange(up, "gx", up_pairs)
     right = exchange(down, "gx", down_pairs)
     side = exchange(side, "gy", both)
     side, near_keep = barrier((side, near_keep))
     far_keep = exchange(near_keep, "gx", onward)
 
-    keep, give = finish_middle(inside, ends, kept_courant, side)
+    keep, give = finish_middle(partial, ends, kept_courant, side)
     keep, give, near_other = barrier((keep, give, near_other))
     blocks[5] = exchange(near_other, "gx", onward)
     other = exchange(give, "shot", both)

time: 110 us -> 107 us (0.973)
  Pallas kernels: 43.7 us -> 35.5 us
  waiting for transfers between devices: 16.3 us -> 20.8 us
  local copies, waits for them, and re-layouts: 2.04 us -> 6.37 us
  starting transfers between devices: 47.5 us -> 43.5 us
    pallas_call x2, Pallas kernels: 27.4 us -> 19.1 us  [the longest x1 18.3 us: steps(): pl.pallas_call(steps_kernel, out_shape=(jax.ShapeDtypeStruct((2, rows, li...]
    ppermute x19, waiting for transfers between devices: 16.3 us -> 20.8 us  [exchange(): return lax.ppermute(array, axis, pairs)]
    unnamed x16 -> x12, local copies, waits for them, and re-layouts: 2.04 us -> 6.37 us
    ppermute x19, starting transfers between devices: 47.5 us -> 43.5 us  [exchange(): return lax.ppermute(array, axis, pairs)]
  transfers between devices with their start and end apart: 19 -> 19, of which waited for: 5 -> 4; matrix products, arithmetic and copies ran while one was open for 0% -> 0% of each run, Pallas kernels for 28% -> 21%
where the time goes in v6:
time: 107 us; the launch traced here: 106 us
  starting transfers between devices  43.5 us (41%)
  Pallas kernels  35.5 us (33%)
  waiting for transfers between devices  20.8 us (19%)
  local copies, waits for them, and re-layouts  6.37 us (6%)
    ppermute x19, starting transfers between devices, exchange(): return lax.ppermute(array, axis, pairs)  43.5 us
    ppermute x19, waiting for transfers between devices, exchange(): return lax.ppermute(array, axis, pairs)  20.8 us
    pallas_call x1, Pallas kernels, steps(): pl.pallas_call(steps_kernel, out_shape=(jax.ShapeDtypeStruct((2, rows, li...  18.3 us
    pallas_call x1, Pallas kernels, image(): pl.pallas_call(image_kernel, grid=(samples,), out_shape=jax.ShapeDtypeStr...  8.16 us
    unnamed x12, local copies, waits for them, and re-layouts  6.37 us
    pallas_call x1, Pallas kernels, pack(): pl.pallas_call(pack_kernel, grid=(rows // step,), out_shape=(edge, edge,...  4.66 us
  transfers between devices with their start and end apart: 19, of which 4 were waited for; matrix products, arithmetic and copies ran while one was open for 0% of the time, Pallas kernels for 21%

profile of v6, /device:TPU:0, one launch (start us, length us, event | category | flops | bytes accessed | tf_op | source)
XLA Modules:
  0.0 106.5 jit_solution(5789987433739608340)
XLA Ops:
  0.0 4.7 %pack.1 = (f32[2,4,128,128]{3,2,1,0:T(8,128)}, f32[2,4,128,128]{3,2,1,0:T(8,128)}, f32[2,32,16,128]{3,2,1,0:T(8,128)}, f32[2,32,16,128]{3,2,1,0:T(8,128)}, f32[32,8,128]{2,1,0:T(8,128)}) custom-call(f32[1,32,128,128]{3,2,1,0:T(8,128)} %source.3, f32[1,32,128,128]{3,2,1,0:T(8,128)} %receiver.3), custom_call_target="tpu_custom_call" | custom-call | flops 10000000000 | bytes 7340032 | tf_op jit(solution)/shard_map/pack/pallas_call | solution.py:87
  5.1 2.6 %collective-permute-start = (f32[32,8,128]{2,1,0:T(8,128)}, f32[32,8,128]{2,1,0:T(8,128)S(1)}, u32[]{:S(2)}, u32[]{:S(2)}) collective-permute-start(f32[32,8,128]{2,1,0:T(8,128)} %get-tuple-element.39), channel_id=1, source_target_pairs={{0,1},{1,0},{2,3},{3,2},{4,5},{5,4},{6,7},{7,6},{8,9},{9,8},{10,11... | collective-permute-start | bytes 393224 | tf_op jit(solution)/shard_map/ppermute | solution.py:576
  7.7 3.4 %collective-permute-start.3 = (f32[2,4,128,128]{3,2,1,0:T(8,128)}, f32[2,4,128,128]{3,2,1,0:T(8,128)S(1)}, u32[]{:S(2)}, u32[]{:S(2)}) collective-permute-start(f32[2,4,128,128]{3,2,1,0:T(8,128)} %get-tuple-element.43), channel_id=1, source_target_pairs={{0,2},{2,4},{4,6},{6,8},{8,10},{10,12},{12,14},{1,3},{3,5},{5,7},{... | collective-permute-start | bytes 1572872 | tf_op jit(solution)/shard_map/ppermute | solution.py:576
  11.2 1.3 %collective-permute-start.4 = (f32[2,4,128,128]{3,2,1,0:T(8,128)}, f32[2,4,128,128]{3,2,1,0:T(8,128)S(1)}, u32[]{:S(2)}, u32[]{:S(2)}) collective-permute-start(f32[2,4,128,128]{3,2,1,0:T(8,128)} %get-tuple-element.44), channel_id=1, source_target_pairs={{2,0},{4,2},{6,4},{8,6},{10,8},{12,10},{14,12},{3,1},{5,3},{7,5},{... | collective-permute-start | bytes 1572872 | tf_op jit(solution)/shard_map/ppermute | solution.py:576
  12.5 2.7 %collective-permute-start.2 = (f32[2,32,16,128]{3,2,1,0:T(8,128)}, f32[2,32,16,128]{3,2,1,0:T(8,128)S(1)}, u32[]{:S(2)}, u32[]{:S(2)}) collective-permute-start(f32[2,32,16,128]{3,2,1,0:T(8,128)} %get-tuple-element.42.refs_0_), channel_id=1, source_target_pairs={{0,2},{2,0},{4,6},{6,4},{8,10},{10,8},{12,14},{14,12},{1,3},{3,1},... | collective-permute-start | bytes 1572872 | tf_op jit(solution)/shard_map/ppermute | solution.py:576
  15.2 1.6 %copy-done.1 = f32[1,32,128,128]{3,2,1,0:T(8,128)S(1)} copy-done((f32[1,32,128,128]{3,2,1,0:T(8,128)S(1)}, f32[1,32,128,128]{3,2,1,0:T(8,128)}, u32[]{:S(2)}) %copy-start.1) | copy-done | bytes 2097176
  16.8 1.6 %copy-done.2 = f32[1,32,128,128]{3,2,1,0:T(8,128)S(1)} copy-done((f32[1,32,128,128]{3,2,1,0:T(8,128)S(1)}, f32[1,32,128,128]{3,2,1,0:T(8,128)}, u32[]{:S(2)}) %copy-start.2) | copy-done | bytes 2097176
  18.4 1.6 %copy-done.3 = f32[1,32,128,128]{3,2,1,0:T(8,128)S(1)} copy-done((f32[1,32,128,128]{3,2,1,0:T(8,128)S(1)}, f32[1,32,128,128]{3,2,1,0:T(8,128)}, u32[]{:S(2)}) %copy-start.3) | copy-done | bytes 2097176
  20.0 1.6 %copy-done.4 = f32[32,128,128]{2,1,0:T(8,128)S(1)} copy-done((f32[32,128,128]{2,1,0:T(8,128)S(1)}, f32[32,128,128]{2,1,0:T(8,128)}, u32[]{:S(2)}) %copy-start.4) | copy-done | bytes 2097176
  21.6 18.3 %steps.1 = (f32[2,32,32,128]{3,2,1,0:T(8,128)S(1)}, f32[32,32,128]{2,1,0:T(8,128)S(1)}, f32[2,4,128,128]{3,2,1,0:T(8,128)S(1)}, f32[2,2,4,32,128]{4,3,2,1,0:T(8,128)S(1)}, f32[2,32,128]{2,1,0:T(8,128)S(1)}) custom-call(f32[1,32,128,128]{3,2,1,0:T(8,128)S(1)} %copy-done, f32[1,32,128,128]{3,2,1,0:T(8,128)S(1)} %copy-done.1, ...), custom_call_target="tpu_custom_call" | custom-call | flops 20000000000 | bytes 1048576 | tf_op jit(solution)/shard_map/steps/pallas_call | solution.py:266
  41.4 3.9 %collective-permute-start.5 = (f32[2,4,32,128]{3,2,1,0:T(8,128)S(1)}, f32[2,4,32,128]{3,2,1,0:T(8,128)S(1)}, u32[]{:S(2)}, u32[]{:S(2)}) collective-permute-start(f32[2,4,32,128]{3,2,1,0:T(8,128)S(1)} %get-tuple-element.51), channel_id=1, source_target_pairs={{0,2},{2,4},{4,6},{6,8},{8,10},{10,12},{12,14},{1,3},{3,5},{5,7},{... | collective-permute-start | bytes 393224 | tf_op jit(solution)/shard_map/ppermute | solution.py:576
  46.5 6.4 %collective-permute-start.8 = (f32[2,32,16,128]{3,2,1,0:T(8,128)S(1)}, f32[2,32,16,128]{3,2,1,0:T(8,128)S(1)}, u32[]{:S(2)}, u32[]{:S(2)}) collective-permute-start(f32[2,32,16,128]{3,2,1,0:T(8,128)S(1)} %collective-permute-done.2.refs_1_), channel_id=1, source_target_pairs={{0,4},{4,8},{8,12},{6,2},{10,6},{14,10},{1,5},{5,9},{9,13},{7,3},{... | collective-permute-start | bytes 1572872 | tf_op jit(solution)/shard_map/ppermute | solution.py:576
  53.0 1.5 %finish_middle.1 = (f32[2,24,16,128]{3,2,1,0:T(8,128)S(1)}, f32[2,24,16,128]{3,2,1,0:T(8,128)S(1)}) custom-call(f32[2,32,32,128]{3,2,1,0:T(8,128)S(1)} %get-tuple-element.46.partial, f32[2,2,8,32,128]{4,3,2,1,0:T(8,128)S(1)} %get-tuple-element.57.ends, f32[32,32,128]{2,1,0:T(8,128)S(1)} %get-tuple-element.47.kept_courant, ...), custom_call_target="tpu_custom_call" | custom-call | flops 10000000000 | bytes 3145728 | tf_op jit(solution)/shard_map/finish_middle/pallas_call | solution.py:394
  54.4 5.7 %collective-permute-done.9.refs_4_ = f32[2,32,16,128]{3,2,1,0:T(8,128)S(1)} collective-permute-done((f32[2,32,16,128]{3,2,1,0:T(8,128)S(1)}, f32[2,32,16,128]{3,2,1,0:T(8,128)S(1)}, u32[]{:S(2)}, u32[]{:S(2)}) %collective-permute-start.9) | collective-permute-done | bytes 524320 | tf_op jit(solution)/shard_map/ppermute | solution.py:576
  60.1 2.5 %collective-permute-start.13 = (f32[2,24,16,128]{3,2,1,0:T(8,128)S(1)}, f32[2,24,16,128]{3,2,1,0:T(8,128)S(1)}, u32[]{:S(2)}, u32[]{:S(2)}) collective-permute-start(f32[2,24,16,128]{3,2,1,0:T(8,128)S(1)} %get-tuple-element.69.refs_0_), channel_id=1, source_target_pairs={{0,2},{2,0},{4,6},{6,4},{8,10},{10,8},{12,14},{14,12},{1,3},{3,1},... | collective-permute-start | bytes 1179656 | tf_op jit(solution)/shard_map/ppermute | solution.py:576
  62.6 3.5 %collective-permute-start.10 = (f32[2,32,16,128]{3,2,1,0:T(8,128)S(1)}, f32[2,32,16,128]{3,2,1,0:T(8,128)S(1)}, u32[]{:S(2)}, u32[]{:S(2)}) collective-permute-start(f32[2,32,16,128]{3,2,1,0:T(8,128)S(1)} %collective-permute-done.9.refs_4_), channel_id=1, source_target_pairs={{0,4},{4,8},{8,12},{6,2},{10,6},{14,10},{1,5},{5,9},{9,13},{7,3},{... | collective-permute-start | bytes 1572872 | tf_op jit(solution)/shard_map/ppermute | solution.py:576
  66.5 6.1 %collective-permute-done.13.refs_1_ = f32[2,24,16,128]{3,2,1,0:T(8,128)S(1)} collective-permute-done((f32[2,24,16,128]{3,2,1,0:T(8,128)S(1)}, f32[2,24,16,128]{3,2,1,0:T(8,128)S(1)}, u32[]{:S(2)}, u32[]{:S(2)}) %collective-permute-start.13) | collective-permute-done | bytes 393248 | tf_op jit(solution)/shard_map/ppermute | solution.py:576
  73.9 4.6 %collective-permute-start.14 = (f32[2,2,8,16,128]{4,3,2,1,0:T(8,128)S(1)}, f32[2,2,8,16,128]{4,3,2,1,0:T(8,128)S(1)}, u32[]{:S(2)}, u32[]{:S(2)}) collective-permute-start(f32[2,2,8,16,128]{4,3,2,1,0:T(8,128)S(1)} %pad_maximum_fusion.refs_6_), channel_id=1, source_target_pairs={{0,2},{2,4},{4,6},{6,8},{8,10},{10,12},{12,14},{1,3},{3,5},{5,7},{... | collective-permute-start | bytes 786440 | tf_op jit(solution)/shard_map/ppermute | solution.py:576
  78.5 4.1 %collective-permute-start.16 = (f32[2,24,16,128]{3,2,1,0:T(8,128)S(1)}, f32[2,24,16,128]{3,2,1,0:T(8,128)S(1)}, u32[]{:S(2)}, u32[]{:S(2)}) collective-permute-start(f32[2,24,16,128]{3,2,1,0:T(8,128)S(1)} %collective-permute-done.13.refs_1_), channel_id=1, source_target_pairs={{0,4},{4,8},{8,12},{6,2},{10,6},{14,10},{1,5},{5,9},{9,13},{7,3},{... | collective-permute-start | bytes 1179656 | tf_op jit(solution)/shard_map/ppermute | solution.py:576
  82.6 3.5 %collective-permute-done.17.refs_4_ = f32[2,24,16,128]{3,2,1,0:T(8,128)S(1)} collective-permute-done((f32[2,24,16,128]{3,2,1,0:T(8,128)S(1)}, f32[2,24,16,128]{3,2,1,0:T(8,128)S(1)}, u32[]{:S(2)}, u32[]{:S(2)}) %collective-permute-start.17) | collective-permute-done | bytes 393248 | tf_op jit(solution)/shard_map/ppermute | solution.py:576
  86.1 4.7 %collective-permute-start.18 = (f32[2,24,16,128]{3,2,1,0:T(8,128)S(1)}, f32[2,24,16,128]{3,2,1,0:T(8,128)S(1)}, u32[]{:S(2)}, u32[]{:S(2)}) collective-permute-start(f32[2,24,16,128]{3,2,1,0:T(8,128)S(1)} %collective-permute-done.17.refs_4_), channel_id=1, source_target_pairs={{0,4},{4,8},{8,12},{6,2},{10,6},{14,10},{1,5},{5,9},{9,13},{7,3},{... | collective-permute-start | bytes 1179656 | tf_op jit(solution)/shard_map/ppermute | solution.py:576
  90.8 1.5 %first_image.1.refs_0_.first = f32[8,65,16,128]{3,2,1,0:T(8,128)S(1)} custom-call(f32[2,32,16,128]{3,2,1,0:T(8,128)S(1)} %copy-done.5, f32[2,32,16,128]{3,2,1,0:T(8,128)S(1)} %collective-permute-done.2.refs_1_, f32[2,32,16,128]{3,2,1,0:T(8,128)S(1)} %collective-permute-done.8.refs_2_, f32[2,32,16,128]{3,2,1,0:T(8,128)S(1)} %collective-permute-done.1.refs_3_, ...), custom_call_target="tpu_custom_call" | custom-call | flops 10000000000 | bytes 8388608 | tf_op jit(solution)/shard_map/first_image/pallas_call | solution.py:479
  92.8 5.5 %collective-permute-done.18.refs_5_ = f32[2,24,16,128]{3,2,1,0:T(8,128)S(1)} collective-permute-done((f32[2,24,16,128]{3,2,1,0:T(8,128)S(1)}, f32[2,24,16,128]{3,2,1,0:T(8,128)S(1)}, u32[]{:S(2)}, u32[]{:S(2)}) %collective-permute-start.18) | collective-permute-done | bytes 393248 | tf_op jit(solution)/shard_map/ppermute | solution.py:576
  98.3 8.2 %image.1 = f32[8,32,64,65]{3,2,1,0:T(8,128)} custom-call(s32[1]{0:T(128)} %in_order.1.token, f32[8,65,16,128]{3,2,1,0:T(8,128)S(1)} %first_image.1.refs_0_.first, f32[2,24,16,128]{3,2,1,0:T(8,128)S(1)} %get-tuple-element.69.refs_0_, f32[2,24,16,128]{3,2,1,0:T(8,128)S(1)} %collective-permute-done.13.refs_1_, ...), custom_call_target="tpu_custom_call" | custom-call | flops 10000000000 | bytes 16777216 | tf_op jit(solution)/shard_map/image/pallas_call | solution.py:534
  (35 shorter events, 5.4 us)
Async XLA Ops:
  0.0 15.2 %copy-start = (f32[1,32,128,128]{3,2,1,0:T(8,128)S(1)}, f32[1,32,128,128]{3,2,1,0:T(8,128)}, u32[]{:S(2)}) copy-start(f32[1,32,128,128]{3,2,1,0:T(8,128)} %source.3) | copy-start | bytes 6291460
  4.7 7.8 %collective-permute-start.1 = (f32[2,32,16,128]{3,2,1,0:T(8,128)}, f32[2,32,16,128]{3,2,1,0:T(8,128)S(1)}, u32[]{:S(2)}, u32[]{:S(2)}) collective-permute-start(f32[2,32,16,128]{3,2,1,0:T(8,128)} %get-tuple-element.41), channel_id=1, source_target_pairs={{0,16},{16,0},{1,17},{17,1},{2,18},{18,2},{3,19},{19,3},{4,20},{20... | collective-permute-start | bytes 1572872 | tf_op jit(solution)/shard_map/ppermute | solution.py:576
  5.1 7.3 %collective-permute-start = (f32[32,8,128]{2,1,0:T(8,128)}, f32[32,8,128]{2,1,0:T(8,128)S(1)}, u32[]{:S(2)}, u32[]{:S(2)}) collective-permute-start(f32[32,8,128]{2,1,0:T(8,128)} %get-tuple-element.39), channel_id=1, source_target_pairs={{0,1},{1,0},{2,3},{3,2},{4,5},{5,4},{6,7},{7,6},{8,9},{9,8},{10,11... | collective-permute-start | bytes 393224 | tf_op jit(solution)/shard_map/ppermute | solution.py:576
  7.7 32.1 %collective-permute-start.3 = (f32[2,4,128,128]{3,2,1,0:T(8,128)}, f32[2,4,128,128]{3,2,1,0:T(8,128)S(1)}, u32[]{:S(2)}, u32[]{:S(2)}) collective-permute-start(f32[2,4,128,128]{3,2,1,0:T(8,128)} %get-tuple-element.43), channel_id=1, source_target_pairs={{0,2},{2,4},{4,6},{6,8},{8,10},{10,12},{12,14},{1,3},{3,5},{5,7},{... | collective-permute-start | bytes 1572872 | tf_op jit(solution)/shard_map/ppermute | solution.py:576
  11.2 28.7 %collective-permute-start.4 = (f32[2,4,128,128]{3,2,1,0:T(8,128)}, f32[2,4,128,128]{3,2,1,0:T(8,128)S(1)}, u32[]{:S(2)}, u32[]{:S(2)}) collective-permute-start(f32[2,4,128,128]{3,2,1,0:T(8,128)} %get-tuple-element.44), channel_id=1, source_target_pairs={{2,0},{4,2},{6,4},{8,6},{10,8},{12,10},{14,12},{3,1},{5,3},{7,5},{... | collective-permute-start | bytes 1572872 | tf_op jit(solution)/shard_map/ppermute | solution.py:576
  12.5 34.1 %collective-permute-start.2 = (f32[2,32,16,128]{3,2,1,0:T(8,128)}, f32[2,32,16,128]{3,2,1,0:T(8,128)S(1)}, u32[]{:S(2)}, u32[]{:S(2)}) collective-permute-start(f32[2,32,16,128]{3,2,1,0:T(8,128)} %get-tuple-element.42.refs_0_), channel_id=1, source_target_pairs={{0,2},{2,0},{4,6},{6,4},{8,10},{10,8},{12,14},{14,12},{1,3},{3,1},... | collective-permute-start | bytes 1572872 | tf_op jit(solution)/shard_map/ppermute | solution.py:576
  15.2 1.6 %copy-start.1 = (f32[1,32,128,128]{3,2,1,0:T(8,128)S(1)}, f32[1,32,128,128]{3,2,1,0:T(8,128)}, u32[]{:S(2)}) copy-start(f32[1,32,128,128]{3,2,1,0:T(8,128)} %receiver.3) | copy-start | bytes 6291460
  16.8 1.6 %copy-start.2 = (f32[1,32,128,128]{3,2,1,0:T(8,128)S(1)}, f32[1,32,128,128]{3,2,1,0:T(8,128)}, u32[]{:S(2)}) copy-start(f32[1,32,128,128]{3,2,1,0:T(8,128)} %source_before.1) | copy-start | bytes 6291460
  18.4 1.6 %copy-start.3 = (f32[1,32,128,128]{3,2,1,0:T(8,128)S(1)}, f32[1,32,128,128]{3,2,1,0:T(8,128)}, u32[]{:S(2)}) copy-start(f32[1,32,128,128]{3,2,1,0:T(8,128)} %receiver_before.1) | copy-start | bytes 6291460
  40.7 5.8 %collective-permute-start.7 = (f32[2,32,128]{2,1,0:T(8,128)S(1)}, f32[2,32,128]{2,1,0:T(8,128)S(1)}, u32[]{:S(2)}, u32[]{:S(2)}) collective-permute-start(f32[2,32,128]{2,1,0:T(8,128)S(1)} %get-tuple-element.53), channel_id=1, source_target_pairs={{0,1},{1,0},{2,3},{3,2},{4,5},{5,4},{6,7},{7,6},{8,9},{9,8},{10,11... | collective-permute-start | bytes 98312 | tf_op jit(solution)/shard_map/ppermute | solution.py:576
  41.3 18.8 %collective-permute-start.9 = (f32[2,32,16,128]{3,2,1,0:T(8,128)S(1)}, f32[2,32,16,128]{3,2,1,0:T(8,128)S(1)}, u32[]{:S(2)}, u32[]{:S(2)}) collective-permute-start(f32[2,32,16,128]{3,2,1,0:T(8,128)S(1)} %collective-permute-done.1.refs_3_), channel_id=1, source_target_pairs={{0,2},{2,0},{4,6},{6,4},{8,10},{10,8},{12,14},{14,12},{1,3},{3,1},... | collective-permute-start | bytes 1572872 | tf_op jit(solution)/shard_map/ppermute | solution.py:576
  41.4 21.2 %collective-permute-start.5 = (f32[2,4,32,128]{3,2,1,0:T(8,128)S(1)}, f32[2,4,32,128]{3,2,1,0:T(8,128)S(1)}, u32[]{:S(2)}, u32[]{:S(2)}) collective-permute-start(f32[2,4,32,128]{3,2,1,0:T(8,128)S(1)} %get-tuple-element.51), channel_id=1, source_target_pairs={{0,2},{2,4},{4,6},{6,8},{8,10},{10,12},{12,14},{1,3},{3,5},{5,7},{... | collective-permute-start | bytes 393224 | tf_op jit(solution)/shard_map/ppermute | solution.py:576
  45.2 20.9 %collective-permute-start.6 = (f32[2,4,32,128]{3,2,1,0:T(8,128)S(1)}, f32[2,4,32,128]{3,2,1,0:T(8,128)S(1)}, u32[]{:S(2)}, u32[]{:S(2)}) collective-permute-start(f32[2,4,32,128]{3,2,1,0:T(8,128)S(1)} %get-tuple-element.52), channel_id=1, source_target_pairs={{2,0},{4,2},{6,4},{8,6},{10,8},{12,10},{14,12},{3,1},{5,3},{7,5},{... | collective-permute-start | bytes 393224 | tf_op jit(solution)/shard_map/ppermute | solution.py:576
  46.5 19.6 %collective-permute-start.8 = (f32[2,32,16,128]{3,2,1,0:T(8,128)S(1)}, f32[2,32,16,128]{3,2,1,0:T(8,128)S(1)}, u32[]{:S(2)}, u32[]{:S(2)}) collective-permute-start(f32[2,32,16,128]{3,2,1,0:T(8,128)S(1)} %collective-permute-done.2.refs_1_), channel_id=1, source_target_pairs={{0,4},{4,8},{8,12},{6,2},{10,6},{14,10},{1,5},{5,9},{9,13},{7,3},{... | collective-permute-start | bytes 1572872 | tf_op jit(solution)/shard_map/ppermute | solution.py:576
  60.1 30.7 %copy-start.5 = (f32[2,32,16,128]{3,2,1,0:T(8,128)S(1)}, f32[2,32,16,128]{3,2,1,0:T(8,128)}, u32[]{:S(2)}) copy-start(f32[2,32,16,128]{3,2,1,0:T(8,128)} %get-tuple-element.42.refs_0_) | copy-start | bytes 1572868
  60.1 6.2 %collective-permute-start.11 = (f32[2,24,16,128]{3,2,1,0:T(8,128)S(1)}, f32[2,24,16,128]{3,2,1,0:T(8,128)S(1)}, u32[]{:S(2)}, u32[]{:S(2)}) collective-permute-start(f32[2,24,16,128]{3,2,1,0:T(8,128)S(1)} %get-tuple-element.62), channel_id=1, source_target_pairs={{0,16},{16,0},{1,17},{17,1},{2,18},{18,2},{3,19},{19,3},{4,20},{20... | collective-permute-start | bytes 1179656 | tf_op jit(solution)/shard_map/ppermute | solution.py:576
  60.1 12.4 %collective-permute-start.13 = (f32[2,24,16,128]{3,2,1,0:T(8,128)S(1)}, f32[2,24,16,128]{3,2,1,0:T(8,128)S(1)}, u32[]{:S(2)}, u32[]{:S(2)}) collective-permute-start(f32[2,24,16,128]{3,2,1,0:T(8,128)S(1)} %get-tuple-element.69.refs_0_), channel_id=1, source_target_pairs={{0,2},{2,0},{4,6},{6,4},{8,10},{10,8},{12,14},{14,12},{1,3},{3,1},... | collective-permute-start | bytes 1179656 | tf_op jit(solution)/shard_map/ppermute | solution.py:576
  62.6 28.2 %collective-permute-start.10 = (f32[2,32,16,128]{3,2,1,0:T(8,128)S(1)}, f32[2,32,16,128]{3,2,1,0:T(8,128)S(1)}, u32[]{:S(2)}, u32[]{:S(2)}) collective-permute-start(f32[2,32,16,128]{3,2,1,0:T(8,128)S(1)} %collective-permute-done.9.refs_4_), channel_id=1, source_target_pairs={{0,4},{4,8},{8,12},{6,2},{10,6},{14,10},{1,5},{5,9},{9,13},{7,3},{... | collective-permute-start | bytes 1572872 | tf_op jit(solution)/shard_map/ppermute | solution.py:576
  66.3 19.8 %collective-permute-start.17 = (f32[2,24,16,128]{3,2,1,0:T(8,128)S(1)}, f32[2,24,16,128]{3,2,1,0:T(8,128)S(1)}, u32[]{:S(2)}, u32[]{:S(2)}) collective-permute-start(f32[2,24,16,128]{3,2,1,0:T(8,128)S(1)} %collective-permute-done.11.refs_3_), channel_id=1, source_target_pairs={{0,2},{2,0},{4,6},{6,4},{8,10},{10,8},{12,14},{14,12},{1,3},{3,1},... | collective-permute-start | bytes 1179656 | tf_op jit(solution)/shard_map/ppermute | solution.py:576
  66.4 6.2 %collective-permute-start.12 = (f32[2,8,16,128]{3,2,1,0:T(8,128)S(1)}, f32[2,8,16,128]{3,2,1,0:T(8,128)S(1)}, u32[]{:S(2)}, u32[]{:S(2)}) collective-permute-start(f32[2,8,16,128]{3,2,1,0:T(8,128)S(1)} %get-tuple-element.68), channel_id=1, source_target_pairs={{0,16},{16,0},{1,17},{17,1},{2,18},{18,2},{3,19},{19,3},{4,20},{20... | collective-permute-start | bytes 393224 | tf_op jit(solution)/shard_map/ppermute | solution.py:576
  72.6 19.7 %collective-permute-start.15 = (f32[2,2,8,16,128]{4,3,2,1,0:T(8,128)S(1)}, f32[2,2,8,16,128]{4,3,2,1,0:T(8,128)S(1)}, u32[]{:S(2)}, u32[]{:S(2)}) collective-permute-start(f32[2,2,8,16,128]{4,3,2,1,0:T(8,128)S(1)} %pad_maximum_fusion.refs_6_), channel_id=1, source_target_pairs={{2,0},{4,2},{6,4},{8,6},{10,8},{12,10},{14,12},{3,1},{5,3},{7,5},{... | collective-permute-start | bytes 786440 | tf_op jit(solution)/shard_map/ppermute | solution.py:576
  73.9 18.4 %collective-permute-start.14 = (f32[2,2,8,16,128]{4,3,2,1,0:T(8,128)S(1)}, f32[2,2,8,16,128]{4,3,2,1,0:T(8,128)S(1)}, u32[]{:S(2)}, u32[]{:S(2)}) collective-permute-start(f32[2,2,8,16,128]{4,3,2,1,0:T(8,128)S(1)} %pad_maximum_fusion.refs_6_), channel_id=1, source_target_pairs={{0,2},{2,4},{4,6},{6,8},{8,10},{10,12},{12,14},{1,3},{3,5},{5,7},{... | collective-permute-start | bytes 786440 | tf_op jit(solution)/shard_map/ppermute | solution.py:576
  78.5 13.8 %collective-permute-start.16 = (f32[2,24,16,128]{3,2,1,0:T(8,128)S(1)}, f32[2,24,16,128]{3,2,1,0:T(8,128)S(1)}, u32[]{:S(2)}, u32[]{:S(2)}) collective-permute-start(f32[2,24,16,128]{3,2,1,0:T(8,128)S(1)} %collective-permute-done.13.refs_1_), channel_id=1, source_target_pairs={{0,4},{4,8},{8,12},{6,2},{10,6},{14,10},{1,5},{5,9},{9,13},{7,3},{... | collective-permute-start | bytes 1179656 | tf_op jit(solution)/shard_map/ppermute | solution.py:576
  86.1 12.2 %collective-permute-start.18 = (f32[2,24,16,128]{3,2,1,0:T(8,128)S(1)}, f32[2,24,16,128]{3,2,1,0:T(8,128)S(1)}, u32[]{:S(2)}, u32[]{:S(2)}) collective-permute-start(f32[2,24,16,128]{3,2,1,0:T(8,128)S(1)} %collective-permute-done.17.refs_4_), channel_id=1, source_target_pairs={{0,4},{4,8},{8,12},{6,2},{10,6},{14,10},{1,5},{5,9},{9,13},{7,3},{... | collective-permute-start | bytes 1179656 | tf_op jit(solution)/shard_map/ppermute | solution.py:576
  (1 other events, 1.6 us)

commit v7 on v6

--- a/solution.py
+++ b/solution.py
@@ -13,7 +13,7 @@
 OFFSETS = 2 * HALF + 1
 OFFSET_ROWS = 72
 LINES = 32
-STEPS_MIB = 40
+STEPS_MIB = 50
 WEIGHTS = (-205.0 / 72.0, 8.0 / 5.0, -1.0 / 5.0, 8.0 / 315.0, -1.0 / 560.0)
 PAD = 8
 F32 = jnp.float32
@@ -47,55 +47,59 @@
     return first, second
 
 
-def pack_kernel(source, receiver, up, down, keep, give, side):
+def pack_kernel(source, receiver, up, down, keep, give, side, fields, sems):
     shot, gy = lax.axis_index("shot"), lax.axis_index("gy")
-    rows, size_y, size_z = source.shape[1:]
+    _, rows, size_y, _ = fields.shape
     lines = size_y // KEEP_EVERY
-    step, steps = pl.program_id(0), pl.num_programs(0)
-
-    @pl.when(step == 0)
-    def _():
+    pieces = sems.shape[0]
+    count = rows // pieces
+    order = [0, pieces - 1] + list(range(1, pieces - 1))
+    copies = {}
+    for index in order:
+        part = pl.ds(count * index, count)
         for field, ref in enumerate((source, receiver)):
-            down[field] = ref[0, :REACH]
-
-    @pl.when(step == steps - 1)
-    def _():
-        for field, ref in enumerate((source, receiver)):
-            up[field] = ref[0, rows - REACH :]
-
-    for row in range(rows):
+            copies[index, field] = pltpu.make_async_copy(
+                ref.at[0, part], fields.at[field, part], sems.at[index, field]
+            )
+            copies[index, field].start()
+
+    def one_row(row, carry):
         parts = []
-        for field, ref in enumerate((source, receiver)):
-            first, second = z_halves(ref[0, row, pl.ds(0, lines, stride=KEEP_EVERY), :])
+        for field in range(2):
+            first, second = z_halves(fields[field, row, pl.ds(0, lines, stride=KEEP_EVERY), :])
             keep[field, row] = jnp.where(shot == 0, first, second)
             give[field, row] = jnp.where(shot == 0, second, first)
-            low = ref[0, row, 0:REACH, :]
-            high = ref[0, row, size_y - REACH : size_y, :]
+            low = fields[field, row, 0:REACH, :]
+            high = fields[field, row, size_y - REACH : size_y, :]
             parts.append(jnp.where(gy == 0, high, low))
         side[row] = jnp.concatenate(parts, axis=0)
+        return carry
+
+    for index in order:
+        for field in range(2):
+            copies[index, field].wait()
+            if index == 0:
+                down[field] = fields[field, :REACH]
+            if index == pieces - 1:
+                up[field] = fields[field, rows - REACH :]
+        lax.fori_loop(count * index, count * (index + 1), one_row, 0, unroll=4)
 
 
 def pack(source, receiver):
     _, rows, size_y, size_z = source.shape
     lines = size_y // KEEP_EVERY // 2
-    step = 8
     edge = jax.ShapeDtypeStruct((2, REACH, size_y, size_z), F32)
     half = jax.ShapeDtypeStruct((2, rows, lines, size_z), F32)
-    edge_spec = pl.BlockSpec((2, REACH, size_y, size_z), lambda i: (0, 0, 0, 0))
-    half_spec = pl.BlockSpec((2, step, lines, size_z), lambda i: (0, i, 0, 0))
-    field_spec = pl.BlockSpec((1, step, size_y, size_z), lambda i: (0, i, 0, 0))
     return pl.pallas_call(
         pack_kernel,
-        grid=(rows // step,),
         out_shape=(edge, edge, half, half, jax.ShapeDtypeStruct((rows, 2 * REACH, size_z), F32)),
-        in_specs=[field_spec, field_spec],
-        out_specs=(
-            edge_spec,
-            edge_spec,
-            half_spec,
-            half_spec,
-            pl.BlockSpec((step, 2 * REACH, size_z), lambda i: (i, 0, 0)),
-        ),
+        in_specs=[HBM, HBM],
+        out_specs=(VMEM,) * 5,
+        scratch_shapes=[
+            pltpu.VMEM((2, rows, size_y, size_z), F32),
+            pltpu.SemaphoreType.DMA((4, 2)),
+        ],
+        compiler_params=params(48),
         cost_estimate=cost(10**10, 7 * 2**20),
         name="pack",
     )(source, receiver)
@@ -493,10 +497,11 @@
 
 
 def image_kernel(token, first, *refs):
-    blocks, (out, rows_of, turned, sems) = refs[:9], refs[9:]
+    blocks, (out, rows_of, turned, staged, sems, out_sems) = refs[:9], refs[9:]
     rows = blocks[0].shape[1] + 2 * REACH
-
-    @pl.when(pl.program_id(0) == 0)
+    step, steps_in_all = pl.program_id(0), pl.num_programs(0)
+
+    @pl.when(step == 0)
     def _():
         starts = block_starts(rows)
         copies = []
@@ -515,17 +520,39 @@
         run_copies(copies)
 
     lines, size_z = rows_of.shape[3], rows_of.shape[4]
-    sample = 4 * pl.program_id(0)
-    for chunk in range(lines // 8):
+    chunks = lines // 8
+
+    def leave(at_step, chunk, half):
+        slot = at_step % 2
+        here = pl.ds(half * lines + 8 * chunk, 8)
+        return pltpu.make_async_copy(staged.at[slot, here], out.at[at_step, here], out_sems.at[slot, chunk, half])
+
+    sample = 4 * step
+    for chunk in range(chunks):
         here = pl.ds(8 * chunk, 8)
         for shift in range(OFFSETS):
             total = first[0, shift, here, :] + products(rows_of, sample, shift, here)
             turned[chunk, pl.ds(shift, 8, stride=OFFSET_ROWS), :] = total
+
+        @pl.when(step >= 2)
+        def _():
+            for half in range(2):
+                leave(step - 2, chunk, half).wait()
+
         for line in range(8):
             values = turned[chunk, line * OFFSET_ROWS : (line + 1) * OFFSET_ROWS, :].T
             at = 8 * chunk + line
-            out[0, at] = values[: size_z // 2, :OFFSETS]
-            out[0, lines + at] = values[size_z // 2 :, :OFFSETS]
+            staged[step % 2, at] = values[: size_z // 2, :OFFSETS]
+            staged[step % 2, lines + at] = values[size_z // 2 :, :OFFSETS]
+        for half in range(2):
+            leave(step, chunk, half).start()
+
+    @pl.when(step == steps_in_all - 1)
+    def _():
+        for back in (1, 0):
+            for chunk in range(chunks):
+                for half in range(2):
+                    leave(step - back, chunk, half).wait()
 
 
 def image(token, first, blocks):
@@ -536,11 +563,13 @@
         grid=(samples,),
         out_shape=jax.ShapeDtypeStruct((samples, 2 * lines, size_z // 2, OFFSETS), F32),
         in_specs=[SMEM, pl.BlockSpec((1, OFFSETS, lines, size_z), lambda i: (i, 0, 0, 0))] + [ANY] * len(blocks),
-        out_specs=pl.BlockSpec((1, 2 * lines, size_z // 2, OFFSETS), lambda i: (i, 0, 0, 0)),
+        out_specs=HBM,
         scratch_shapes=[
             pltpu.VMEM((2, 2, rows + 2 * HALF, lines, size_z), F32),
             pltpu.VMEM((lines // 8, 8 * OFFSET_ROWS, size_z), F32),
+            pltpu.VMEM((2, 2 * lines, size_z // 2, OFFSETS), F32),
             pltpu.SemaphoreType.DMA((18,)),
+            pltpu.SemaphoreType.DMA((2, lines // 8, 2)),
         ],
         compiler_params=params(20),
         cost_estimate=cost(10**10, 16 * 2**20),
@@ -608,12 +637,13 @@
     other_ends = exchange(give_ends, "shot", both)
     other_ends, near_keep = barrier((other_ends, near_keep))
     own = jnp.stack([keep_ends, other_ends])
+    far_keep = exchange(near_keep, "gx", onward)
     left = exchange(own, "gx", up_pairs)
     right = exchange(own, "gx", down_pairs)
-    far_keep = exchange(near_keep, "gx", onward)
     far_other = exchange(near_other, "gx", onward)
+    blocks[5], far_keep = lax.optimization_barrier((blocks[5], far_keep))
     first = first_image(blocks)
-    token = in_order(first, left, right, far_keep)
+    token = in_order(left, right, first)
     blocks = [keep, near_keep, far_keep, other, near_other, far_other, own, left, right]
     return jnp.transpose(image(token, first, blocks), (3, 0, 1, 2))
 

time: 107 us -> 105 us (0.981)
  waiting for transfers between devices: 20.8 us -> 25.9 us
  local copies, waits for them, and re-layouts: 6.37 us -> 1.59 us
  Pallas kernels: 35.5 us -> 33.2 us
    ppermute x19, waiting for transfers between devices: 20.8 us -> 25.9 us  [exchange(): return lax.ppermute(array, axis, pairs)]
    unnamed x12 -> x2, local copies, waits for them, and re-layouts: 6.37 us -> 1.59 us
    pallas_call x1, Pallas kernels: 4.66 us -> 2.05 us  [pack(): pl.pallas_call(pack_kernel, out_shape=(edge, edge, half, half, jax.ShapeD...]
  transfers between devices with their start and end apart: 19 -> 19, of which waited for: 4 -> 8; matrix products, arithmetic and copies ran while one was open for 0% -> 0% of each run, Pallas kernels for 21% -> 23%
where the time goes in v7:
time: 105 us
  starting transfers between devices  43.6 us (42%)
  Pallas kernels  33.2 us (32%)
  waiting for transfers between devices  25.9 us (25%)
  local copies, waits for them, and re-layouts  1.59 us (2%)
    ppermute x19, starting transfers between devices, exchange(): return lax.ppermute(array, axis, pairs)  43.6 us
    ppermute x19, waiting for transfers between devices, exchange(): return lax.ppermute(array, axis, pairs)  25.9 us
    pallas_call x1, Pallas kernels, steps(): pl.pallas_call(steps_kernel, out_shape=(jax.ShapeDtypeStruct((2, rows, li...  19.1 us
    pallas_call x1, Pallas kernels, image(): pl.pallas_call(image_kernel, grid=(samples,), out_shape=jax.ShapeDtypeStr...  7.64 us
  transfers between devices with their start and end apart: 19, of which 8 were waited for; matrix products, arithmetic and copies ran while one was open for 0% of the time, Pallas kernels for 23%

profile of v7, /device:TPU:0, one launch (start us, length us, event | category | flops | bytes accessed | tf_op | source)
XLA Modules:
  0.0 104.6 jit_solution(9496798015381208368)
XLA Ops:
  0.0 1.6 %copy-done = f32[1,32,128,128]{3,2,1,0:T(8,128)S(1)} copy-done((f32[1,32,128,128]{3,2,1,0:T(8,128)S(1)}, f32[1,32,128,128]{3,2,1,0:T(8,128)}, u32[]{:S(2)}) %copy-start) | copy-done | bytes 2097176
  1.6 2.1 %pack.1 = (f32[2,4,128,128]{3,2,1,0:T(8,128)S(1)}, f32[2,4,128,128]{3,2,1,0:T(8,128)S(1)}, f32[2,32,16,128]{3,2,1,0:T(8,128)S(1)}, f32[2,32,16,128]{3,2,1,0:T(8,128)S(1)}, f32[32,8,128]{2,1,0:T(8,128)S(1)}) custom-call(f32[1,32,128,128]{3,2,1,0:T(8,128)S(1)} %copy-done, f32[1,32,128,128]{3,2,1,0:T(8,128)} %receiver.3), custom_call_target="tpu_custom_call" | custom-call | flops 10000000000 | bytes 7340032 | tf_op jit(solution)/shard_map/pack/pallas_call | solution.py:93
  4.2 2.6 %collective-permute-start = (f32[32,8,128]{2,1,0:T(8,128)S(1)}, f32[32,8,128]{2,1,0:T(8,128)S(1)}, u32[]{:S(2)}, u32[]{:S(2)}) collective-permute-start(f32[32,8,128]{2,1,0:T(8,128)S(1)} %get-tuple-element.41), channel_id=1, source_target_pairs={{0,1},{1,0},{2,3},{3,2},{4,5},{5,4},{6,7},{7,6},{8,9},{9,8},{10,11... | collective-permute-start | bytes 393224 | tf_op jit(solution)/shard_map/ppermute | solution.py:605
  6.7 3.4 %collective-permute-start.2 = (f32[2,4,128,128]{3,2,1,0:T(8,128)S(1)}, f32[2,4,128,128]{3,2,1,0:T(8,128)S(1)}, u32[]{:S(2)}, u32[]{:S(2)}) collective-permute-start(f32[2,4,128,128]{3,2,1,0:T(8,128)S(1)} %get-tuple-element.46), channel_id=1, source_target_pairs={{0,2},{2,4},{4,6},{6,8},{8,10},{10,12},{12,14},{1,3},{3,5},{5,7},{... | collective-permute-start | bytes 1572872 | tf_op jit(solution)/shard_map/ppermute | solution.py:605
  10.2 1.3 %collective-permute-start.3 = (f32[2,4,128,128]{3,2,1,0:T(8,128)S(1)}, f32[2,4,128,128]{3,2,1,0:T(8,128)S(1)}, u32[]{:S(2)}, u32[]{:S(2)}) collective-permute-start(f32[2,4,128,128]{3,2,1,0:T(8,128)S(1)} %get-tuple-element.47), channel_id=1, source_target_pairs={{2,0},{4,2},{6,4},{8,6},{10,8},{12,10},{14,12},{3,1},{5,3},{7,5},{... | collective-permute-start | bytes 1572872 | tf_op jit(solution)/shard_map/ppermute | solution.py:605
  11.5 2.7 %collective-permute-start.5 = (f32[2,32,16,128]{3,2,1,0:T(8,128)S(1)}, f32[2,32,16,128]{3,2,1,0:T(8,128)S(1)}, u32[]{:S(2)}, u32[]{:S(2)}) collective-permute-start(f32[2,32,16,128]{3,2,1,0:T(8,128)S(1)} %get-tuple-element.54.refs_0_), channel_id=1, source_target_pairs={{0,2},{2,0},{4,6},{6,4},{8,10},{10,8},{12,14},{14,12},{1,3},{3,1},... | collective-permute-start | bytes 1572872 | tf_op jit(solution)/shard_map/ppermute | solution.py:605
  14.2 19.1 %steps.1 = (f32[2,32,32,128]{3,2,1,0:T(8,128)S(1)}, f32[32,32,128]{2,1,0:T(8,128)S(1)}, f32[2,4,128,128]{3,2,1,0:T(8,128)S(1)}, f32[2,2,4,32,128]{4,3,2,1,0:T(8,128)S(1)}, f32[2,32,128]{2,1,0:T(8,128)S(1)}) custom-call(f32[1,32,128,128]{3,2,1,0:T(8,128)} %source.3, f32[1,32,128,128]{3,2,1,0:T(8,128)} %receiver.3, f32[1,32,128,128]{3,2,1,0:T(8,128)} %source_before.1, ...), custom_call_target="tpu_custom_call" | custom-call | flops 20000000000 | bytes 1048576 | tf_op jit(solution)/shard_map/steps/pallas_call | solution.py:270
  35.1 2.5 %collective-permute-start.6 = (f32[2,32,16,128]{3,2,1,0:T(8,128)S(1)}, f32[2,32,16,128]{3,2,1,0:T(8,128)S(1)}, u32[]{:S(2)}, u32[]{:S(2)}) collective-permute-start(f32[2,32,16,128]{3,2,1,0:T(8,128)S(1)} %collective-permute-done.1.refs_3_), channel_id=1, source_target_pairs={{0,2},{2,0},{4,6},{6,4},{8,10},{10,8},{12,14},{14,12},{1,3},{3,1},... | collective-permute-start | bytes 1572872 | tf_op jit(solution)/shard_map/ppermute | solution.py:605
  37.6 1.9 %collective-permute-start.8 = (f32[2,4,32,128]{3,2,1,0:T(8,128)S(1)}, f32[2,4,32,128]{3,2,1,0:T(8,128)S(1)}, u32[]{:S(2)}, u32[]{:S(2)}) collective-permute-start(f32[2,4,32,128]{3,2,1,0:T(8,128)S(1)} %get-tuple-element.60), channel_id=1, source_target_pairs={{0,2},{2,4},{4,6},{6,8},{8,10},{10,12},{12,14},{1,3},{3,5},{5,7},{... | collective-permute-start | bytes 393224 | tf_op jit(solution)/shard_map/ppermute | solution.py:605
  40.8 5.5 %collective-permute-done.5.refs_1_ = f32[2,32,16,128]{3,2,1,0:T(8,128)S(1)} collective-permute-done((f32[2,32,16,128]{3,2,1,0:T(8,128)S(1)}, f32[2,32,16,128]{3,2,1,0:T(8,128)S(1)}, u32[]{:S(2)}, u32[]{:S(2)}) %collective-permute-start.5) | collective-permute-done | bytes 524320 | tf_op jit(solution)/shard_map/ppermute | solution.py:605
  46.3 6.1 %collective-permute-start.10 = (f32[2,32,16,128]{3,2,1,0:T(8,128)S(1)}, f32[2,32,16,128]{3,2,1,0:T(8,128)S(1)}, u32[]{:S(2)}, u32[]{:S(2)}) collective-permute-start(f32[2,32,16,128]{3,2,1,0:T(8,128)S(1)} %collective-permute-done.5.refs_1_), channel_id=1, source_target_pairs={{0,4},{4,8},{8,12},{6,2},{10,6},{14,10},{1,5},{5,9},{9,13},{7,3},{... | collective-permute-start | bytes 1572872 | tf_op jit(solution)/shard_map/ppermute | solution.py:605
  52.4 1.5 %finish_middle.1 = (f32[2,24,16,128]{3,2,1,0:T(8,128)S(1)}, f32[2,24,16,128]{3,2,1,0:T(8,128)S(1)}) custom-call(f32[2,32,32,128]{3,2,1,0:T(8,128)S(1)} %get-tuple-element.45.partial, f32[2,2,8,32,128]{4,3,2,1,0:T(8,128)S(1)} %get-tuple-element.52.ends, f32[32,32,128]{2,1,0:T(8,128)S(1)} %get-tuple-element.48.kept_courant, ...), custom_call_target="tpu_custom_call" | custom-call | flops 10000000000 | bytes 3145728 | tf_op jit(solution)/shard_map/finish_middle/pallas_call | solution.py:398
  53.9 5.1 %collective-permute-done.6.refs_4_ = f32[2,32,16,128]{3,2,1,0:T(8,128)S(1)} collective-permute-done((f32[2,32,16,128]{3,2,1,0:T(8,128)S(1)}, f32[2,32,16,128]{3,2,1,0:T(8,128)S(1)}, u32[]{:S(2)}, u32[]{:S(2)}) %collective-permute-start.6) | collective-permute-done | bytes 524320 | tf_op jit(solution)/shard_map/ppermute | solution.py:605
  58.9 2.5 %collective-permute-start.12 = (f32[2,24,16,128]{3,2,1,0:T(8,128)S(1)}, f32[2,24,16,128]{3,2,1,0:T(8,128)S(1)}, u32[]{:S(2)}, u32[]{:S(2)}) collective-permute-start(f32[2,24,16,128]{3,2,1,0:T(8,128)S(1)} %get-tuple-element.69.refs_0_), channel_id=1, source_target_pairs={{0,2},{2,0},{4,6},{6,4},{8,10},{10,8},{12,14},{14,12},{1,3},{3,1},... | collective-permute-start | bytes 1179656 | tf_op jit(solution)/shard_map/ppermute | solution.py:605
  61.4 2.2 %collective-permute-done.10.refs_2_ = f32[2,32,16,128]{3,2,1,0:T(8,128)S(1)} collective-permute-done((f32[2,32,16,128]{3,2,1,0:T(8,128)S(1)}, f32[2,32,16,128]{3,2,1,0:T(8,128)S(1)}, u32[]{:S(2)}, u32[]{:S(2)}) %collective-permute-start.10) | collective-permute-done | bytes 524320 | tf_op jit(solution)/shard_map/ppermute | solution.py:605
  63.9 4.4 %collective-permute-start.15 = (f32[2,32,16,128]{3,2,1,0:T(8,128)S(1)}, f32[2,32,16,128]{3,2,1,0:T(8,128)S(1)}, u32[]{:S(2)}, u32[]{:S(2)}) collective-permute-start(f32[2,32,16,128]{3,2,1,0:T(8,128)S(1)} %collective-permute-done.6.refs_4_), channel_id=1, source_target_pairs={{0,4},{4,8},{8,12},{6,2},{10,6},{14,10},{1,5},{5,9},{9,13},{7,3},{... | collective-permute-start | bytes 1572872 | tf_op jit(solution)/shard_map/ppermute | solution.py:605
  68.4 2.8 %collective-permute-done.12.refs_1_ = f32[2,24,16,128]{3,2,1,0:T(8,128)S(1)} collective-permute-done((f32[2,24,16,128]{3,2,1,0:T(8,128)S(1)}, f32[2,24,16,128]{3,2,1,0:T(8,128)S(1)}, u32[]{:S(2)}, u32[]{:S(2)}) %collective-permute-start.12) | collective-permute-done | bytes 393248 | tf_op jit(solution)/shard_map/ppermute | solution.py:605
  71.2 4.3 %collective-permute-start.16 = (f32[2,24,16,128]{3,2,1,0:T(8,128)S(1)}, f32[2,24,16,128]{3,2,1,0:T(8,128)S(1)}, u32[]{:S(2)}, u32[]{:S(2)}) collective-permute-start(f32[2,24,16,128]{3,2,1,0:T(8,128)S(1)} %collective-permute-done.12.refs_1_), channel_id=1, source_target_pairs={{0,4},{4,8},{8,12},{6,2},{10,6},{14,10},{1,5},{5,9},{9,13},{7,3},{... | collective-permute-start | bytes 1179656 | tf_op jit(solution)/shard_map/ppermute | solution.py:605
  76.9 4.6 %collective-permute-start.13 = (f32[2,2,8,16,128]{4,3,2,1,0:T(8,128)S(1)}, f32[2,2,8,16,128]{4,3,2,1,0:T(8,128)S(1)}, u32[]{:S(2)}, u32[]{:S(2)}) collective-permute-start(f32[2,2,8,16,128]{4,3,2,1,0:T(8,128)S(1)} %pad_maximum_fusion.refs_6_), channel_id=1, source_target_pairs={{0,2},{2,4},{4,6},{6,8},{8,10},{10,12},{12,14},{1,3},{3,5},{5,7},{... | collective-permute-start | bytes 786440 | tf_op jit(solution)/shard_map/ppermute | solution.py:605
  81.4 3.5 %collective-permute-done.17.refs_4_ = f32[2,24,16,128]{3,2,1,0:T(8,128)S(1)} collective-permute-done((f32[2,24,16,128]{3,2,1,0:T(8,128)S(1)}, f32[2,24,16,128]{3,2,1,0:T(8,128)S(1)}, u32[]{:S(2)}, u32[]{:S(2)}) %collective-permute-start.17) | collective-permute-done | bytes 393248 | tf_op jit(solution)/shard_map/ppermute | solution.py:605
  84.9 3.5 %collective-permute-start.18 = (f32[2,24,16,128]{3,2,1,0:T(8,128)S(1)}, f32[2,24,16,128]{3,2,1,0:T(8,128)S(1)}, u32[]{:S(2)}, u32[]{:S(2)}) collective-permute-start(f32[2,24,16,128]{3,2,1,0:T(8,128)S(1)} %collective-permute-done.17.refs_4_), channel_id=1, source_target_pairs={{0,4},{4,8},{8,12},{6,2},{10,6},{14,10},{1,5},{5,9},{9,13},{7,3},{... | collective-permute-start | bytes 1179656 | tf_op jit(solution)/shard_map/ppermute | solution.py:605
  88.9 1.5 %first_image.1.refs_2_.first = f32[8,65,16,128]{3,2,1,0:T(8,128)S(1)} custom-call(f32[2,32,16,128]{3,2,1,0:T(8,128)S(1)} %get-tuple-element.54.refs_0_, f32[2,32,16,128]{3,2,1,0:T(8,128)S(1)} %collective-permute-done.5.refs_1_, f32[2,32,16,128]{3,2,1,0:T(8,128)S(1)} %collective-permute-done.10.refs_2_, ...), custom_call_target="tpu_custom_call" | custom-call | flops 10000000000 | bytes 8388608 | tf_op jit(solution)/shard_map/first_image/pallas_call | solution.py:483
  90.9 6.0 %collective-permute-done.18.refs_5_ = f32[2,24,16,128]{3,2,1,0:T(8,128)S(1)} collective-permute-done((f32[2,24,16,128]{3,2,1,0:T(8,128)S(1)}, f32[2,24,16,128]{3,2,1,0:T(8,128)S(1)}, u32[]{:S(2)}, u32[]{:S(2)}) %collective-permute-start.18) | collective-permute-done | bytes 393248 | tf_op jit(solution)/shard_map/ppermute | solution.py:605
  96.9 7.6 %image.1 = f32[8,32,64,65]{3,2,1,0:T(8,128)} custom-call(s32[1]{0:T(128)} %in_order.1.token, f32[8,65,16,128]{3,2,1,0:T(8,128)S(1)} %first_image.1.refs_2_.first, f32[2,24,16,128]{3,2,1,0:T(8,128)S(1)} %get-tuple-element.69.refs_0_, f32[2,24,16,128]{3,2,1,0:T(8,128)S(1)} %collective-permute-done.12.refs_1_, ...), custom_call_target="tpu_custom_call" | custom-call | flops 10000000000 | bytes 16777216 | tf_op jit(solution)/shard_map/image/pallas_call | solution.py:561
  (25 shorter events, 6.2 us)
Async XLA Ops:
  0.0 1.6 %copy-start = (f32[1,32,128,128]{3,2,1,0:T(8,128)S(1)}, f32[1,32,128,128]{3,2,1,0:T(8,128)}, u32[]{:S(2)}) copy-start(f32[1,32,128,128]{3,2,1,0:T(8,128)} %source.3) | copy-start | bytes 6291460
  3.7 7.8 %collective-permute-start.1 = (f32[2,32,16,128]{3,2,1,0:T(8,128)S(1)}, f32[2,32,16,128]{3,2,1,0:T(8,128)S(1)}, u32[]{:S(2)}, u32[]{:S(2)}) collective-permute-start(f32[2,32,16,128]{3,2,1,0:T(8,128)S(1)} %get-tuple-element.43), channel_id=1, source_target_pairs={{0,16},{16,0},{1,17},{17,1},{2,18},{18,2},{3,19},{19,3},{4,20},{20... | collective-permute-start | bytes 1572872 | tf_op jit(solution)/shard_map/ppermute | solution.py:605
  4.2 7.3 %collective-permute-start = (f32[32,8,128]{2,1,0:T(8,128)S(1)}, f32[32,8,128]{2,1,0:T(8,128)S(1)}, u32[]{:S(2)}, u32[]{:S(2)}) collective-permute-start(f32[32,8,128]{2,1,0:T(8,128)S(1)} %get-tuple-element.41), channel_id=1, source_target_pairs={{0,1},{1,0},{2,3},{3,2},{4,5},{5,4},{6,7},{7,6},{8,9},{9,8},{10,11... | collective-permute-start | bytes 393224 | tf_op jit(solution)/shard_map/ppermute | solution.py:605
  6.7 26.9 %collective-permute-start.2 = (f32[2,4,128,128]{3,2,1,0:T(8,128)S(1)}, f32[2,4,128,128]{3,2,1,0:T(8,128)S(1)}, u32[]{:S(2)}, u32[]{:S(2)}) collective-permute-start(f32[2,4,128,128]{3,2,1,0:T(8,128)S(1)} %get-tuple-element.46), channel_id=1, source_target_pairs={{0,2},{2,4},{4,6},{6,8},{8,10},{10,12},{12,14},{1,3},{3,5},{5,7},{... | collective-permute-start | bytes 1572872 | tf_op jit(solution)/shard_map/ppermute | solution.py:605
  10.2 23.5 %collective-permute-start.3 = (f32[2,4,128,128]{3,2,1,0:T(8,128)S(1)}, f32[2,4,128,128]{3,2,1,0:T(8,128)S(1)}, u32[]{:S(2)}, u32[]{:S(2)}) collective-permute-start(f32[2,4,128,128]{3,2,1,0:T(8,128)S(1)} %get-tuple-element.47), channel_id=1, source_target_pairs={{2,0},{4,2},{6,4},{8,6},{10,8},{12,10},{14,12},{3,1},{5,3},{7,5},{... | collective-permute-start | bytes 1572872 | tf_op jit(solution)/shard_map/ppermute | solution.py:605
  11.5 34.8 %collective-permute-start.5 = (f32[2,32,16,128]{3,2,1,0:T(8,128)S(1)}, f32[2,32,16,128]{3,2,1,0:T(8,128)S(1)}, u32[]{:S(2)}, u32[]{:S(2)}) collective-permute-start(f32[2,32,16,128]{3,2,1,0:T(8,128)S(1)} %get-tuple-element.54.refs_0_), channel_id=1, source_target_pairs={{0,2},{2,0},{4,6},{6,4},{8,10},{10,8},{12,14},{14,12},{1,3},{3,1},... | collective-permute-start | bytes 1572872 | tf_op jit(solution)/shard_map/ppermute | solution.py:605
  34.5 6.3 %collective-permute-start.4 = (f32[2,32,128]{2,1,0:T(8,128)S(1)}, f32[2,32,128]{2,1,0:T(8,128)S(1)}, u32[]{:S(2)}, u32[]{:S(2)}) collective-permute-start(f32[2,32,128]{2,1,0:T(8,128)S(1)} %get-tuple-element.53), channel_id=1, source_target_pairs={{0,1},{1,0},{2,3},{3,2},{4,5},{5,4},{6,7},{7,6},{8,9},{9,8},{10,11... | collective-permute-start | bytes 98312 | tf_op jit(solution)/shard_map/ppermute | solution.py:605
  35.1 23.9 %collective-permute-start.6 = (f32[2,32,16,128]{3,2,1,0:T(8,128)S(1)}, f32[2,32,16,128]{3,2,1,0:T(8,128)S(1)}, u32[]{:S(2)}, u32[]{:S(2)}) collective-permute-start(f32[2,32,16,128]{3,2,1,0:T(8,128)S(1)} %collective-permute-done.1.refs_3_), channel_id=1, source_target_pairs={{0,2},{2,0},{4,6},{6,4},{8,10},{10,8},{12,14},{14,12},{1,3},{3,1},... | collective-permute-start | bytes 1572872 | tf_op jit(solution)/shard_map/ppermute | solution.py:605
  37.6 23.9 %collective-permute-start.8 = (f32[2,4,32,128]{3,2,1,0:T(8,128)S(1)}, f32[2,4,32,128]{3,2,1,0:T(8,128)S(1)}, u32[]{:S(2)}, u32[]{:S(2)}) collective-permute-start(f32[2,4,32,128]{3,2,1,0:T(8,128)S(1)} %get-tuple-element.60), channel_id=1, source_target_pairs={{0,2},{2,4},{4,6},{6,8},{8,10},{10,12},{12,14},{1,3},{3,5},{5,7},{... | collective-permute-start | bytes 393224 | tf_op jit(solution)/shard_map/ppermute | solution.py:605
  39.5 21.9 %collective-permute-start.9 = (f32[2,4,32,128]{3,2,1,0:T(8,128)S(1)}, f32[2,4,32,128]{3,2,1,0:T(8,128)S(1)}, u32[]{:S(2)}, u32[]{:S(2)}) collective-permute-start(f32[2,4,32,128]{3,2,1,0:T(8,128)S(1)} %get-tuple-element.61), channel_id=1, source_target_pairs={{2,0},{4,2},{6,4},{8,6},{10,8},{12,10},{14,12},{3,1},{5,3},{7,5},{... | collective-permute-start | bytes 393224 | tf_op jit(solution)/shard_map/ppermute | solution.py:605
  46.3 17.3 %collective-permute-start.10 = (f32[2,32,16,128]{3,2,1,0:T(8,128)S(1)}, f32[2,32,16,128]{3,2,1,0:T(8,128)S(1)}, u32[]{:S(2)}, u32[]{:S(2)}) collective-permute-start(f32[2,32,16,128]{3,2,1,0:T(8,128)S(1)} %collective-permute-done.5.refs_1_), channel_id=1, source_target_pairs={{0,4},{4,8},{8,12},{6,2},{10,6},{14,10},{1,5},{5,9},{9,13},{7,3},{... | collective-permute-start | bytes 1572872 | tf_op jit(solution)/shard_map/ppermute | solution.py:605
  58.9 4.8 %collective-permute-start.7 = (f32[2,24,16,128]{3,2,1,0:T(8,128)S(1)}, f32[2,24,16,128]{3,2,1,0:T(8,128)S(1)}, u32[]{:S(2)}, u32[]{:S(2)}) collective-permute-start(f32[2,24,16,128]{3,2,1,0:T(8,128)S(1)} %get-tuple-element.59), channel_id=1, source_target_pairs={{0,16},{16,0},{1,17},{17,1},{2,18},{18,2},{3,19},{19,3},{4,20},{20... | collective-permute-start | bytes 1179656 | tf_op jit(solution)/shard_map/ppermute | solution.py:605
  58.9 12.3 %collective-permute-start.12 = (f32[2,24,16,128]{3,2,1,0:T(8,128)S(1)}, f32[2,24,16,128]{3,2,1,0:T(8,128)S(1)}, u32[]{:S(2)}, u32[]{:S(2)}) collective-permute-start(f32[2,24,16,128]{3,2,1,0:T(8,128)S(1)} %get-tuple-element.69.refs_0_), channel_id=1, source_target_pairs={{0,2},{2,0},{4,6},{6,4},{8,10},{10,8},{12,14},{14,12},{1,3},{3,1},... | collective-permute-start | bytes 1179656 | tf_op jit(solution)/shard_map/ppermute | solution.py:605
  63.8 7.4 %collective-permute-start.11 = (f32[2,8,16,128]{3,2,1,0:T(8,128)S(1)}, f32[2,8,16,128]{3,2,1,0:T(8,128)S(1)}, u32[]{:S(2)}, u32[]{:S(2)}) collective-permute-start(f32[2,8,16,128]{3,2,1,0:T(8,128)S(1)} %get-tuple-element.68), channel_id=1, source_target_pairs={{0,16},{16,0},{1,17},{17,1},{2,18},{18,2},{3,19},{19,3},{4,20},{20... | collective-permute-start | bytes 393224 | tf_op jit(solution)/shard_map/ppermute | solution.py:605
  63.9 24.5 %collective-permute-start.15 = (f32[2,32,16,128]{3,2,1,0:T(8,128)S(1)}, f32[2,32,16,128]{3,2,1,0:T(8,128)S(1)}, u32[]{:S(2)}, u32[]{:S(2)}) collective-permute-start(f32[2,32,16,128]{3,2,1,0:T(8,128)S(1)} %collective-permute-done.6.refs_4_), channel_id=1, source_target_pairs={{0,4},{4,8},{8,12},{6,2},{10,6},{14,10},{1,5},{5,9},{9,13},{7,3},{... | collective-permute-start | bytes 1572872 | tf_op jit(solution)/shard_map/ppermute | solution.py:605
  68.3 16.6 %collective-permute-start.17 = (f32[2,24,16,128]{3,2,1,0:T(8,128)S(1)}, f32[2,24,16,128]{3,2,1,0:T(8,128)S(1)}, u32[]{:S(2)}, u32[]{:S(2)}) collective-permute-start(f32[2,24,16,128]{3,2,1,0:T(8,128)S(1)} %collective-permute-done.7.refs_3_), channel_id=1, source_target_pairs={{0,2},{2,0},{4,6},{6,4},{8,10},{10,8},{12,14},{14,12},{1,3},{3,1},... | collective-permute-start | bytes 1179656 | tf_op jit(solution)/shard_map/ppermute | solution.py:605
  71.2 17.7 %collective-permute-start.16 = (f32[2,24,16,128]{3,2,1,0:T(8,128)S(1)}, f32[2,24,16,128]{3,2,1,0:T(8,128)S(1)}, u32[]{:S(2)}, u32[]{:S(2)}) collective-permute-start(f32[2,24,16,128]{3,2,1,0:T(8,128)S(1)} %collective-permute-done.12.refs_1_), channel_id=1, source_target_pairs={{0,4},{4,8},{8,12},{6,2},{10,6},{14,10},{1,5},{5,9},{9,13},{7,3},{... | collective-permute-start | bytes 1179656 | tf_op jit(solution)/shard_map/ppermute | solution.py:605
  75.6 14.8 %collective-permute-start.14 = (f32[2,2,8,16,128]{4,3,2,1,0:T(8,128)S(1)}, f32[2,2,8,16,128]{4,3,2,1,0:T(8,128)S(1)}, u32[]{:S(2)}, u32[]{:S(2)}) collective-permute-start(f32[2,2,8,16,128]{4,3,2,1,0:T(8,128)S(1)} %pad_maximum_fusion.refs_6_), channel_id=1, source_target_pairs={{2,0},{4,2},{6,4},{8,6},{10,8},{12,10},{14,12},{3,1},{5,3},{7,5},{... | collective-permute-start | bytes 786440 | tf_op jit(solution)/shard_map/ppermute | solution.py:605
  76.9 13.5 %collective-permute-start.13 = (f32[2,2,8,16,128]{4,3,2,1,0:T(8,128)S(1)}, f32[2,2,8,16,128]{4,3,2,1,0:T(8,128)S(1)}, u32[]{:S(2)}, u32[]{:S(2)}) collective-permute-start(f32[2,2,8,16,128]{4,3,2,1,0:T(8,128)S(1)} %pad_maximum_fusion.refs_6_), channel_id=1, source_target_pairs={{0,2},{2,4},{4,6},{6,8},{8,10},{10,12},{12,14},{1,3},{3,5},{5,7},{... | collective-permute-start | bytes 786440 | tf_op jit(solution)/shard_map/ppermute | solution.py:605
  84.9 12.0 %collective-permute-start.18 = (f32[2,24,16,128]{3,2,1,0:T(8,128)S(1)}, f32[2,24,16,128]{3,2,1,0:T(8,128)S(1)}, u32[]{:S(2)}, u32[]{:S(2)}) collective-permute-start(f32[2,24,16,128]{3,2,1,0:T(8,128)S(1)} %collective-permute-done.17.refs_4_), channel_id=1, source_target_pairs={{0,4},{4,8},{8,12},{6,2},{10,6},{14,10},{1,5},{5,9},{9,13},{7,3},{... | collective-permute-start | bytes 1179656 | tf_op jit(solution)/shard_map/ppermute | solution.py:605

commit v8 on v7

--- a/solution.py
+++ b/solution.py
@@ -2,6 +2,7 @@
 
 import jax
 import jax.numpy as jnp
+import numpy as np
 from jax import lax
 from jax.experimental import pallas as pl
 from jax.experimental.pallas import tpu as pltpu
@@ -47,7 +48,9 @@
     return first, second
 
 
-def pack_kernel(source, receiver, up, down, keep, give, side, fields, sems):
+def pack_kernel(
+    source, receiver, up, down, edge, keep, keep_ends, give, give_ends, side, fields, sems
+):
     shot, gy = lax.axis_index("shot"), lax.axis_index("gy")
     _, rows, size_y, _ = fields.shape
     lines = size_y // KEEP_EVERY
@@ -63,43 +66,69 @@
             )
             copies[index, field].start()
 
-    def one_row(row, carry):
+    def one_row(row, keep_ref, give_ref, to):
         parts = []
         for field in range(2):
             first, second = z_halves(fields[field, row, pl.ds(0, lines, stride=KEEP_EVERY), :])
-            keep[field, row] = jnp.where(shot == 0, first, second)
-            give[field, row] = jnp.where(shot == 0, second, first)
+            keep_ref[field, to] = jnp.where(shot == 0, first, second)
+            give_ref[field, to] = jnp.where(shot == 0, second, first)
             low = fields[field, row, 0:REACH, :]
             high = fields[field, row, size_y - REACH : size_y, :]
             parts.append(jnp.where(gy == 0, high, low))
         side[row] = jnp.concatenate(parts, axis=0)
+
+    def middle_row(row, carry):
+        one_row(row, keep, give, row - REACH)
         return carry
 
+    def end_rows(out, start, to):
+        for row in range(REACH):
+            for field in range(2):
+                edge[field, to + row] = fields[field, start + row, pl.ds(0, lines, stride=KEEP_EVERY), :]
+                for phase in range(1, KEEP_EVERY):
+                    out[field, row, (phase - 1) * lines : phase * lines, :] = fields[
+                        field, start + row, pl.ds(phase, lines, stride=KEEP_EVERY), :
+                    ]
+            one_row(start + row, keep_ends, give_ends, to + row)
+
     for index in order:
         for field in range(2):
             copies[index, field].wait()
-            if index == 0:
-                down[field] = fields[field, :REACH]
-            if index == pieces - 1:
-                up[field] = fields[field, rows - REACH :]
-        lax.fori_loop(count * index, count * (index + 1), one_row, 0, unroll=4)
+        low, high = count * index, count * (index + 1)
+        if index == 0:
+            end_rows(down, 0, 0)
+            low += REACH
+        if index == pieces - 1:
+            end_rows(up, rows - REACH, REACH)
+            high -= REACH
+        lax.fori_loop(low, high, middle_row, 0, unroll=4)
 
 
 def pack(source, receiver):
     _, rows, size_y, size_z = source.shape
-    lines = size_y // KEEP_EVERY // 2
-    edge = jax.ShapeDtypeStruct((2, REACH, size_y, size_z), F32)
-    half = jax.ShapeDtypeStruct((2, rows, lines, size_z), F32)
+    lines = size_y // KEEP_EVERY
+    apart = jax.ShapeDtypeStruct((2, REACH, size_y - lines, size_z), F32)
+    middle = jax.ShapeDtypeStruct((2, rows - 2 * REACH, lines // 2, size_z), F32)
+    ends = jax.ShapeDtypeStruct((2, 2 * REACH, lines // 2, size_z), F32)
     return pl.pallas_call(
         pack_kernel,
-        out_shape=(edge, edge, half, half, jax.ShapeDtypeStruct((rows, 2 * REACH, size_z), F32)),
+        out_shape=(
+            apart,
+            apart,
+            jax.ShapeDtypeStruct((2, 2 * REACH, lines, size_z), F32),
+            middle,
+            ends,
+            middle,
+            ends,
+            jax.ShapeDtypeStruct((rows, 2 * REACH, size_z), F32),
+        ),
         in_specs=[HBM, HBM],
-        out_specs=(VMEM,) * 5,
+        out_specs=(VMEM,) * 8,
         scratch_shapes=[
             pltpu.VMEM((2, rows, size_y, size_z), F32),
             pltpu.SemaphoreType.DMA((4, 2)),
         ],
-        compiler_params=params(48),
+        compiler_params=params(56),
         cost_estimate=cost(10**10, 7 * 2**20),
         name="pack",
     )(source, receiver)
@@ -123,41 +152,61 @@
     return total.reshape(-1, size_z)
 
 
-def first_step(now, row, before, before_row, scale, scale_row, after, after_row, field, masks):
+def z_matrix(size_z):
+    z = np.arange(size_z)
+    apart = np.abs(z[:, None] - z[None, :])
+    weights = np.array((0.0,) + WEIGHTS[1:] + (0.0,), np.float32)[np.minimum(apart, REACH + 1)]
+    high = weights.astype(jnp.bfloat16)
+    low = (weights - high.astype(np.float32)).astype(jnp.bfloat16)
+    return jnp.asarray(np.block([[high, low], [high, np.zeros_like(low)]]))
+
+
+def z_product(lines, matrix):
+    size_z = lines.shape[1]
+    high = lines.astype(jnp.bfloat16)
+    low = (lines - high.astype(F32)).astype(jnp.bfloat16)
+    both = jnp.dot(jnp.concatenate([high, low], axis=1), matrix, preferred_element_type=F32)
+    return both[:, :size_z] + both[:, size_z:]
+
+
+def first_step(now, row, z_sums, before, before_row, scale, scale_row, after, field):
     size_y = before.shape[2]
-    for chunk in range(size_y // LINES):
-        at = PAD + LINES * chunk
-        center = now[field, row, at : at + LINES, :]
-        total = (3.0 * WEIGHTS[0]) * center + z_terms(center, masks)
+    lines = size_y // KEEP_EVERY
+    for phase in range(KEEP_EVERY):
+        kept = lambda start: pl.ds(start, lines, stride=KEEP_EVERY)
+        at = PAD + phase
+        center = now[field, row, kept(at), :]
+        total = (3.0 * WEIGHTS[0]) * center + z_sums[field, kept(phase), :]
         for d in range(1, REACH + 1):
             around = (
-                now[field, row + d, at : at + LINES, :]
-                + now[field, row - d, at : at + LINES, :]
-                + now[field, row, at + d : at + d + LINES, :]
-                + now[field, row, at - d : at - d + LINES, :]
+                now[field, row + d, kept(at), :]
+                + now[field, row - d, kept(at), :]
+                + now[field, row, kept(at + d), :]
+                + now[field, row, kept(at - d), :]
             )
             total = total + WEIGHTS[d] * around
-        here = pl.ds(LINES * chunk, LINES)
-        after[field, after_row, at : at + LINES, :] = (
-            2.0 * center - before[field, before_row, here, :] + scale[scale_row, here, :] * total
+        after[field, row, kept(at), :] = (
+            2.0 * center
+            - before[field, before_row, kept(phase), :]
+            + scale[scale_row, kept(phase), :] * total
         )
 
 
-def second_step(now, row, scale, scale_row, after, after_row, field, masks, store):
+def second_step(now, row, scale, scale_row, after, field, z_sum):
     size_y = scale.shape[1]
     lines = size_y // KEEP_EVERY
     kept = lambda start: pl.ds(start, lines, stride=KEEP_EVERY)
-    center = after[field, after_row, kept(PAD), :]
-    total = (3.0 * WEIGHTS[0]) * center + z_terms(center, masks)
+    center = after[field, row, kept(PAD), :]
+    total = (3.0 * WEIGHTS[0]) * center + z_sum
     for d in range(1, REACH + 1):
         around = (
-            after[field, after_row + d, kept(PAD), :]
-            + after[field, after_row - d, kept(PAD), :]
-            + after[field, after_row, kept(PAD + d), :]
-            + after[field, after_row, kept(PAD - d), :]
+            after[field, row + d, kept(PAD), :]
+            + after[field, row - d, kept(PAD), :]
+            + after[field, row, kept(PAD + d), :]
+            + after[field, row, kept(PAD - d), :]
         )
         total = total + WEIGHTS[d] * around
-    store(2.0 * center - now[field, row, kept(PAD), :] + scale[scale_row, kept(0), :] * total)
+    return 2.0 * center - now[field, row, kept(PAD), :] + scale[scale_row, kept(0), :] * total
 
 
 def side_term(after, after_row, field, size_y, gy):
@@ -182,8 +231,8 @@
 
 
 def steps_kernel(
-    source, receiver, source_before, receiver_before, courant, side,
-    partial, kept_courant, edge_courant, edge, side_out, now, before, scale, after, sems,
+    source, receiver, source_before, receiver_before, courant, side, matrix,
+    partial, kept_courant, edge_courant, edge, side_out, now, before, scale, after, z_sums, sems,
 ):
     gy = lax.axis_index("gy")
     rows, size_y, size_z = courant.shape
@@ -221,9 +270,17 @@
         return carry
 
     lax.fori_loop(0, rows, fill, 0)
-    masks = z_weights(size_z)
     for one in copies(0)[:2]:
         one.wait()
+
+    def z_next(row):
+        found = z_product(
+            jnp.concatenate([now[field, row + REACH, middle, :] for field in range(2)], axis=0), matrix[...]
+        )
+        for field in range(2):
+            z_sums[row % 2, field] = found[field * size_y : (field + 1) * size_y]
+
+    z_next(0)
 
     def first(row, carry):
         @pl.when(row % piece == 0)
@@ -239,7 +296,9 @@
 
         at = row + REACH
         for field in range(2):
-            first_step(now, at, before, row, scale, row, after, at, field, masks)
+            first_step(now, at, z_sums.at[row % 2], before, row, scale, row, after, field)
+        z_next(row + 1)
+        for field in range(2):
             side_out[field, pl.ds(row, 1), :] = side_term(after, at, field, size_y, gy)
         return carry
 
@@ -248,14 +307,15 @@
     def second(row, carry):
         at = row + REACH
         kept_courant[row] = scale[row, pl.ds(0, lines, stride=KEEP_EVERY), :]
-        for field in range(2):
-            def store(value):
-                partial[field, row] = value
-
-            second_step(now, at, scale, row, after, at, field, masks, store)
+        centers = [after[field, at, pl.ds(PAD, lines, stride=KEEP_EVERY), :] for field in range(2)]
+        z_sum = z_product(jnp.concatenate(centers, axis=0), matrix[...])
+        for field in range(2):
+            partial[field, row] = second_step(
+                now, at, scale, row, after, field, z_sum[field * lines : (field + 1) * lines]
+            )
         return carry
 
-    lax.fori_loop(0, rows, second, 0)
+    lax.fori_loop(0, rows, second, 0, unroll=2)
     for end in range(2):
         for row in range(REACH):
             at = rows - 1 - row if end else row
@@ -276,26 +336,28 @@
             jax.ShapeDtypeStruct((2, 2, REACH, lines, size_z), F32),
             jax.ShapeDtypeStruct((2, rows, size_z), F32),
         ),
-        in_specs=[HBM] * 5 + [VMEM],
+        in_specs=[HBM] * 5 + [VMEM] * 2,
         out_specs=(VMEM,) * 5,
         scratch_shapes=[
             pltpu.VMEM((2, rows + 2 * REACH, size_y + 2 * PAD, size_z), F32),
             pltpu.VMEM((2, rows, size_y, size_z), F32),
             pltpu.VMEM((rows, size_y, size_z), F32),
             pltpu.VMEM((2, rows + 2 * REACH, size_y + 2 * PAD, size_z), F32),
+            pltpu.VMEM((2, 2, size_y, size_z), F32),
             pltpu.SemaphoreType.DMA((rows // (2 * REACH), 5)),
         ],
         compiler_params=params(STEPS_MIB),
         cost_estimate=cost(2 * 10**10, 2**20),
         name="steps",
-    )(source, receiver, source_before, receiver_before, courant, side)
+    )(source, receiver, source_before, receiver_before, courant, side, z_matrix(size_z))
 
 
 def mend_kernel(
-    left, right, partial, kept_courant, edge_courant, edge, side_in,
-    ends, up, down, side_out, added,
+    left, right, near, far, partial, kept_courant, edge_courant, edge, side_in,
+    ends, up, down, side_out, keep, give, added,
 ):
-    gy = lax.axis_index("gy")
+    gy, shot = lax.axis_index("gy"), lax.axis_index("shot")
+    even = lax.axis_index("gx") % 2 == 0
     rows, lines, size_z = kept_courant.shape
     size_y = KEEP_EVERY * lines
     masks = z_weights(size_z)
@@ -306,15 +368,21 @@
             group = 2 * end + field
             for row in range(REACH):
                 blank_sides(added, row, group, size_y)
-                for chunk in range(size_y // LINES):
-                    here = pl.ds(LINES * chunk, LINES)
+                for phase in range(KEEP_EVERY):
                     total = None
                     for d in range(row + 1, REACH + 1):
                         beyond = d - row - 1
-                        halo = right[field, beyond, here, :] if end else left[field, REACH - 1 - beyond, here, :]
+                        at = beyond if end else REACH - 1 - beyond
+                        if phase:
+                            halo = (right if end else left)[field, at, (phase - 1) * lines : phase * lines, :]
+                        elif end:
+                            halo = jnp.where(even, near[field, at], far[field, at])
+                        else:
+                            halo = jnp.where(even, far[field, REACH + at], near[field, REACH + at])
                         term = WEIGHTS[d] * halo
                         total = term if total is None else total + term
-                    added[group, row, pl.ds(PAD + LINES * chunk, LINES), :] = edge_courant[end, row, here, :] * total
+                    scaled = edge_courant[end, row, pl.ds(phase, lines, stride=KEEP_EVERY), :]
+                    added[group, row, kept(PAD + phase), :] = scaled * total
             for row in range(2 * REACH):
                 at = rows - 1 - row if end else row
                 total = None
@@ -339,11 +407,16 @@
                         added, row, group, size_y, gy
                     )
                 ends[field, end, row] = value + kept_courant[at] * total
-
-
-def mend(left, right, partial, kept_courant, edge_courant, edge, side_in):
+    for kind, ref in enumerate((near, far)):
+        for field in range(2):
+            for row in range(2 * REACH):
+                pack_row(ref[field, row], field, row, shot, keep.at[kind], give.at[kind])
+
+
+def mend(left, right, near, far, partial, kept_courant, edge_courant, edge, side_in):
     rows, lines, size_z = kept_courant.shape
     halo = jax.ShapeDtypeStruct((2, REACH, lines, size_z), F32)
+    half = jax.ShapeDtypeStruct((2, 2, 2 * REACH, lines // 2, size_z), F32)
     return pl.pallas_call(
         mend_kernel,
         out_shape=(
@@ -351,14 +424,16 @@
             halo,
             halo,
             jax.ShapeDtypeStruct((2, rows, size_z), F32),
+            half,
+            half,
         ),
-        in_specs=[VMEM] * 7,
-        out_specs=(VMEM,) * 4,
+        in_specs=[VMEM] * 9,
+        out_specs=(VMEM,) * 6,
         scratch_shapes=[pltpu.VMEM((4, REACH, KEEP_EVERY * lines + 2 * PAD, size_z), F32)],
         compiler_params=params(24),
         cost_estimate=cost(10**6, 2**20),
         name="mend",
-    )(left, right, partial, kept_courant, edge_courant, edge, side_in)
+    )(left, right, near, far, partial, kept_courant, edge_courant, edge, side_in)
 
 
 def pack_row(value, field, row, shot, keep, give):
@@ -457,18 +532,32 @@
     return total
 
 
+def layout_copies(middles, ends, middle_starts, end_starts, rows_of, sems):
+    copies = []
+
+    def copy(src, part, start, count):
+        dst = rows_of.at[part, :, pl.ds(start, count)]
+        copies.append(pltpu.make_async_copy(src, dst, sems.at[len(copies)]))
+
+    count = middles[0][0].shape[1]
+    for part in range(2):
+        for src, start in zip(middles[part], middle_starts):
+            copy(src, part, start + REACH, count)
+        for src, start in zip(ends[part], end_starts):
+            copy(src.at[:, pl.ds(0, REACH)], part, start, REACH)
+            copy(src.at[:, pl.ds(REACH, REACH)], part, start + REACH + count, REACH)
+    return copies
+
+
 def first_image_kernel(*refs):
-    blocks, (out, rows_of, sems) = refs[:6], refs[6:]
-    rows = blocks[0].shape[1]
+    blocks, (out, rows_of, sems) = refs[:10], refs[10:]
+    rows = blocks[0].shape[1] + 2 * REACH
 
     @pl.when(pl.program_id(0) == 0)
     def _():
         starts = block_starts(rows)
-        copies = []
-        for index, ref in enumerate(blocks):
-            dst = rows_of.at[index // 3, :, pl.ds(starts[index % 3], rows)]
-            copies.append(pltpu.make_async_copy(ref, dst, sems.at[index]))
-        run_copies(copies)
+        ends = [[blocks[6 + part], blocks[8 + part].at[0], blocks[8 + part].at[1]] for part in range(2)]
+        run_copies(layout_copies([blocks[:3], blocks[3:6]], ends, starts, starts, rows_of, sems))
 
     sample = 4 * pl.program_id(0)
     for chunk in range(rows_of.shape[3] // 8):
@@ -478,7 +567,8 @@
 
 
 def first_image(blocks):
-    _, rows, lines, size_z = blocks[0].shape
+    _, middle_rows, lines, size_z = blocks[0].shape
+    rows = middle_rows + 2 * REACH
     samples = rows // 4
     return pl.pallas_call(
         first_image_kernel,
@@ -488,7 +578,7 @@
         out_specs=pl.BlockSpec((1, OFFSETS, lines, size_z), lambda i: (i, 0, 0, 0)),
         scratch_shapes=[
             pltpu.VMEM((2, 2, rows + 2 * HALF, lines, size_z), F32),
-            pltpu.SemaphoreType.DMA((6,)),
+            pltpu.SemaphoreType.DMA((18,)),
         ],
         compiler_params=params(16),
         cost_estimate=cost(10**10, 8 * 2**20),
@@ -503,21 +593,11 @@
 
     @pl.when(step == 0)
     def _():
-        starts = block_starts(rows)
-        copies = []
-
-        def copy(src, group, start, count):
-            dst = rows_of.at[group, :, pl.ds(start, count)]
-            copies.append(pltpu.make_async_copy(src, dst, sems.at[len(copies)]))
-
-        for part in range(2):
-            for kind in range(3):
-                copy(blocks[3 * part + kind], part, starts[kind] + REACH, rows - 2 * REACH)
-            for kind, start in enumerate((HALF, 0, HALF + rows)):
-                ends = blocks[6 + kind]
-                copy(ends.at[part, :, pl.ds(0, REACH)], part, start, REACH)
-                copy(ends.at[part, :, pl.ds(REACH, REACH)], part, start + rows - REACH, REACH)
-        run_copies(copies)
+        ends = [[ref.at[part] for ref in blocks[6:]] for part in range(2)]
+        end_starts = (HALF, 0, HALF + rows)
+        run_copies(
+            layout_copies([blocks[:3], blocks[3:6]], ends, block_starts(rows), end_starts, rows_of, sems)
+        )
 
     lines, size_z = rows_of.shape[3], rows_of.shape[4]
     chunks = lines // 8
@@ -605,23 +685,29 @@
         return lax.ppermute(array, axis, pairs)
 
     barrier = lax.optimization_barrier
-    up, down, keep, give, side = pack(source_now, receiver_now)
+    up, down, edge, keep, keep_ends, give, give_ends, side = pack(source_now, receiver_now)
+    near_edge = exchange(edge, "gx", partner)
     left = exchange(up, "gx", up_pairs)
     right = exchange(down, "gx", down_pairs)
     side = exchange(side, "gy", both)
     other = exchange(give, "shot", both)
+    other_ends = exchange(give_ends, "shot", both)
     side, keep, other = barrier((side, keep, other))
     near_keep = exchange(keep, "gx", partner)
     near_other = exchange(other, "gx", partner)
-    blocks = [keep, near_keep, None, other, near_other, None]
+    far_edge = exchange(near_edge, "gx", onward)
+    blocks = [keep, near_keep, None, other, near_other, None, keep_ends, other_ends]
     partial, kept_courant, edge_courant, edge, side = steps(
         source_now, receiver_now, source_before, receiver_before, courant, side
     )
-    ends, up, down, side = mend(left, right, partial, kept_courant, edge_courant, edge, side)
+    ends, up, down, side, keep_edges, give_edges = mend(
+        left, right, near_edge, far_edge, partial, kept_courant, edge_courant, edge, side
+    )
+    blocks += [keep_edges, exchange(give_edges, "shot", both)]
     left = exchange(up, "gx", up_pairs)
     right = exchange(down, "gx", down_pairs)
     side = exchange(side, "gy", both)
-    side, near_keep = barrier((side, near_keep))
+    side, near_keep, blocks[7], blocks[9] = barrier((side, near_keep, blocks[7], blocks[9]))
     far_keep = exchange(near_keep, "gx", onward)
 
     keep, give = finish_middle(partial, ends, kept_courant, side)

time: 105 us -> 103 us (0.981)
  starting transfers between devices: 43.6 us -> 55.2 us
  waiting for transfers between devices: 25.9 us -> 16.3 us
  Pallas kernels: 33.2 us -> 30.1 us
  local copies, waits for them, and re-layouts: 1.59 us -> 0.02 us
    ppermute x19 -> x23, starting transfers between devices: 43.6 us -> 55.2 us  [exchange(): return lax.ppermute(array, axis, pairs)]
    ppermute x19 -> x23, waiting for transfers between devices: 25.9 us -> 16.3 us  [exchange(): return lax.ppermute(array, axis, pairs)]
    pallas_call x1, Pallas kernels: 19.1 us -> 13 us  [steps(): pl.pallas_call(steps_kernel, out_shape=(jax.ShapeDtypeStruct((2, rows, li...]
    pallas_call x1, Pallas kernels: 2.05 us -> 3.78 us  [pack(): pl.pallas_call(pack_kernel, out_shape=(apart, apart, jax.ShapeDtypeStruct...]
    unnamed x2 -> x8, local copies, waits for them, and re-layouts: 1.59 us -> 0.02 us
    pallas_call x1, Pallas kernels: 1.46 us -> 2.53 us  [first_image(): pl.pallas_call(first_image_kernel, grid=(samples,), out_shape=jax.ShapeDt...]
  transfers between devices with their start and end apart: 19 -> 23, of which waited for: 8 -> 6; matrix products, arithmetic and copies ran while one was open for 0% -> 0% of each run, Pallas kernels for 23% -> 18%
where the time goes in v8:
time: 103 us; the launch traced here: 102 us
  starting transfers between devices  55.2 us (54%)
  Pallas kernels  30.1 us (29%)
  waiting for transfers between devices  16.3 us (16%)
    ppermute x23, starting transfers between devices, exchange(): return lax.ppermute(array, axis, pairs)  55.2 us
    ppermute x23, waiting for transfers between devices, exchange(): return lax.ppermute(array, axis, pairs)  16.3 us
    pallas_call x1, Pallas kernels, steps(): pl.pallas_call(steps_kernel, out_shape=(jax.ShapeDtypeStruct((2, rows, li...  13 us
    pallas_call x1, Pallas kernels, image(): pl.pallas_call(image_kernel, grid=(samples,), out_shape=jax.ShapeDtypeStr...  7.71 us
    pallas_call x1, Pallas kernels, pack(): pl.pallas_call(pack_kernel, out_shape=(apart, apart, jax.ShapeDtypeStruct...  3.78 us
    pallas_call x1, Pallas kernels, first_image(): pl.pallas_call(first_image_kernel, grid=(samples,), out_shape=jax.ShapeDt...  2.53 us
  transfers between devices with their start and end apart: 23, of which 6 were waited for; matrix products, arithmetic and copies ran while one was open for 0% of the time, Pallas kernels for 18%

profile of v8, /device:TPU:0, one launch (start us, length us, event | category | flops | bytes accessed | tf_op | source)
XLA Modules:
  0.0 102.0 jit_solution(17638807440101713975)
XLA Ops:
  0.0 3.8 %pack.1 = (f32[2,4,96,128]{3,2,1,0:T(8,128)}, f32[2,4,96,128]{3,2,1,0:T(8,128)}, f32[2,8,32,128]{3,2,1,0:T(8,128)}, f32[2,24,16,128]{3,2,1,0:T(8,128)}, f32[2,8,...) custom-call(f32[1,32,128,128]{3,2,1,0:T(8,128)} %source.3, ...), custom_call_target="tpu_custom_call" | custom-call | flops 10000000000 | bytes 7340032 | tf_op jit(solution)/shard_map/pack/pallas_call | solution.py:113
  4.3 2.6 %collective-permute-start.4 = (f32[2,8,32,128]{3,2,1,0:T(8,128)}, f32[2,8,32,128]{3,2,1,0:T(8,128)S(1)}, u32[]{:S(2)}, u32[]{:S(2)}) collective-permute-start(f32[2,8,32,128]{3,2,1,0:T(8,128)} %get-tuple-element.55), channel_id=1, source_target_pairs={{0,2},{2,0},{4,6},{6,4},{8,10},{10,8},{12,14},{14,12},{1,3},{3,1},... | collective-permute-start | bytes 786440 | tf_op jit(solution)/shard_map/ppermute | solution.py:685
  6.9 1.5 %collective-permute-start = (f32[32,8,128]{2,1,0:T(8,128)}, f32[32,8,128]{2,1,0:T(8,128)S(1)}, u32[]{:S(2)}, u32[]{:S(2)}) collective-permute-start(f32[32,8,128]{2,1,0:T(8,128)} %get-tuple-element.48), channel_id=1, source_target_pairs={{0,1},{1,0},{2,3},{3,2},{4,5},{5,4},{6,7},{7,6},{8,9},{9,8},{10,11... | collective-permute-start | bytes 393224 | tf_op jit(solution)/shard_map/ppermute | solution.py:685
  8.4 2.4 %collective-permute-start.2 = (f32[2,4,96,128]{3,2,1,0:T(8,128)}, f32[2,4,96,128]{3,2,1,0:T(8,128)S(1)}, u32[]{:S(2)}, u32[]{:S(2)}) collective-permute-start(f32[2,4,96,128]{3,2,1,0:T(8,128)} %get-tuple-element.53), channel_id=1, source_target_pairs={{0,2},{2,4},{4,6},{6,8},{8,10},{10,12},{12,14},{1,3},{3,5},{5,7},{... | collective-permute-start | bytes 1179656 | tf_op jit(solution)/shard_map/ppermute | solution.py:685
  10.8 1.3 %collective-permute-start.3 = (f32[2,4,96,128]{3,2,1,0:T(8,128)}, f32[2,4,96,128]{3,2,1,0:T(8,128)S(1)}, u32[]{:S(2)}, u32[]{:S(2)}) collective-permute-start(f32[2,4,96,128]{3,2,1,0:T(8,128)} %get-tuple-element.54), channel_id=1, source_target_pairs={{2,0},{4,2},{6,4},{8,6},{10,8},{12,10},{14,12},{3,1},{5,3},{7,5},{... | collective-permute-start | bytes 1179656 | tf_op jit(solution)/shard_map/ppermute | solution.py:685
  12.1 1.9 %collective-permute-done.4.near = f32[2,8,32,128]{3,2,1,0:T(8,128)S(1)} collective-permute-done((f32[2,8,32,128]{3,2,1,0:T(8,128)}, f32[2,8,32,128]{3,2,1,0:T(8,128)S(1)}, u32[]{:S(2)}, u32[]{:S(2)}) %collective-permute-start.4) | collective-permute-done | bytes 262176 | tf_op jit(solution)/shard_map/ppermute | solution.py:685
  14.0 12.4 %collective-permute-start.5 = (f32[2,8,32,128]{3,2,1,0:T(8,128)S(1)}, f32[2,8,32,128]{3,2,1,0:T(8,128)S(1)}, u32[]{:S(2)}, u32[]{:S(2)}) collective-permute-start(f32[2,8,32,128]{3,2,1,0:T(8,128)S(1)} %collective-permute-done.4.near), channel_id=1, source_target_pairs={{0,4},{4,8},{8,12},{6,2},{10,6},{14,10},{1,5},{5,9},{9,13},{7,3},{... | collective-permute-start | bytes 786440 | tf_op jit(solution)/shard_map/ppermute | solution.py:685
  26.5 13.0 %steps.1 = (f32[2,32,32,128]{3,2,1,0:T(8,128)S(1)}, f32[32,32,128]{2,1,0:T(8,128)S(1)}, f32[2,4,128,128]{3,2,1,0:T(8,128)S(1)}, f32[2,2,4,32,128]{4,3,2,1,0:T(8,128)S(1)}, f32[2,32,128]{2,1,0:T(8,128)S(1)}) custom-call(f32[1,32,128,128]{3,2,1,0:T(8,128)} %source.3, f32[1,32,128,128]{3,2,1,0:T(8,128)} %receiver.3, f32[1,32,128,128]{3,2,1,0:T(8,128)} %source_before.1, ...), custom_call_target="tpu_custom_call" | custom-call | flops 20000000000 | bytes 1048576 | tf_op jit(solution)/shard_map/steps/pallas_call | solution.py:330
  41.1 1.7 %collective-permute-start.6 = (f32[2,32,128]{2,1,0:T(8,128)S(1)}, f32[2,32,128]{2,1,0:T(8,128)S(1)}, u32[]{:S(2)}, u32[]{:S(2)}) collective-permute-start(f32[2,32,128]{2,1,0:T(8,128)S(1)} %get-tuple-element.61), channel_id=1, source_target_pairs={{0,1},{1,0},{2,3},{3,2},{4,5},{5,4},{6,7},{7,6},{8,9},{9,8},{10,11... | collective-permute-start | bytes 98312 | tf_op jit(solution)/shard_map/ppermute | solution.py:685
  42.8 2.0 %collective-permute-start.10 = (f32[2,24,16,128]{3,2,1,0:T(8,128)S(1)}, f32[2,24,16,128]{3,2,1,0:T(8,128)S(1)}, u32[]{:S(2)}, u32[]{:S(2)}) collective-permute-start(f32[2,24,16,128]{3,2,1,0:T(8,128)S(1)} %collective-permute-done.1.refs_3_), channel_id=1, source_target_pairs={{0,2},{2,0},{4,6},{6,4},{8,10},{10,8},{12,14},{14,12},{1,3},{3,1},... | collective-permute-start | bytes 1179656 | tf_op jit(solution)/shard_map/ppermute | solution.py:685
  44.8 1.9 %collective-permute-start.12 = (f32[2,4,32,128]{3,2,1,0:T(8,128)S(1)}, f32[2,4,32,128]{3,2,1,0:T(8,128)S(1)}, u32[]{:S(2)}, u32[]{:S(2)}) collective-permute-start(f32[2,4,32,128]{3,2,1,0:T(8,128)S(1)} %get-tuple-element.70), channel_id=1, source_target_pairs={{0,2},{2,4},{4,6},{6,8},{8,10},{10,12},{12,14},{1,3},{3,5},{5,7},{... | collective-permute-start | bytes 393224 | tf_op jit(solution)/shard_map/ppermute | solution.py:685
  48.1 7.0 %collective-permute-start.14 = (f32[2,24,16,128]{3,2,1,0:T(8,128)S(1)}, f32[2,24,16,128]{3,2,1,0:T(8,128)S(1)}, u32[]{:S(2)}, u32[]{:S(2)}) collective-permute-start(f32[2,24,16,128]{3,2,1,0:T(8,128)S(1)} %collective-permute-done.7.refs_1_), channel_id=1, source_target_pairs={{0,4},{4,8},{8,12},{6,2},{10,6},{14,10},{1,5},{5,9},{9,13},{7,3},{... | collective-permute-start | bytes 1179656 | tf_op jit(solution)/shard_map/ppermute | solution.py:685
  55.1 1.5 %finish_middle.1 = (f32[2,24,16,128]{3,2,1,0:T(8,128)S(1)}, f32[2,24,16,128]{3,2,1,0:T(8,128)S(1)}) custom-call(f32[2,32,32,128]{3,2,1,0:T(8,128)S(1)} %get-tuple-element.52.partial, f32[2,2,8,32,128]{4,3,2,1,0:T(8,128)S(1)} %get-tuple-element.60.ends, f32[32,32,128]{2,1,0:T(8,128)S(1)} %get-tuple-element.56.kept_courant, ...), custom_call_target="tpu_custom_call" | custom-call | flops 10000000000 | bytes 3145728 | tf_op jit(solution)/shard_map/finish_middle/pallas_call | solution.py:473
  57.2 2.5 %collective-permute-start.16 = (f32[2,24,16,128]{3,2,1,0:T(8,128)S(1)}, f32[2,24,16,128]{3,2,1,0:T(8,128)S(1)}, u32[]{:S(2)}, u32[]{:S(2)}) collective-permute-start(f32[2,24,16,128]{3,2,1,0:T(8,128)S(1)} %get-tuple-element.79.refs_0_), channel_id=1, source_target_pairs={{0,2},{2,0},{4,6},{6,4},{8,10},{10,8},{12,14},{14,12},{1,3},{3,1},... | collective-permute-start | bytes 1179656 | tf_op jit(solution)/shard_map/ppermute | solution.py:685
  59.7 2.9 %collective-permute-done.14.refs_2_ = f32[2,24,16,128]{3,2,1,0:T(8,128)S(1)} collective-permute-done((f32[2,24,16,128]{3,2,1,0:T(8,128)S(1)}, f32[2,24,16,128]{3,2,1,0:T(8,128)S(1)}, u32[]{:S(2)}, u32[]{:S(2)}) %collective-permute-start.14) | collective-permute-done | bytes 393248 | tf_op jit(solution)/shard_map/ppermute | solution.py:685
  62.8 4.4 %collective-permute-start.19 = (f32[2,24,16,128]{3,2,1,0:T(8,128)S(1)}, f32[2,24,16,128]{3,2,1,0:T(8,128)S(1)}, u32[]{:S(2)}, u32[]{:S(2)}) collective-permute-start(f32[2,24,16,128]{3,2,1,0:T(8,128)S(1)} %collective-permute-done.10.refs_4_), channel_id=1, source_target_pairs={{0,4},{4,8},{8,12},{6,2},{10,6},{14,10},{1,5},{5,9},{9,13},{7,3},{... | collective-permute-start | bytes 1179656 | tf_op jit(solution)/shard_map/ppermute | solution.py:685
  67.3 2.1 %collective-permute-done.16.refs_1_ = f32[2,24,16,128]{3,2,1,0:T(8,128)S(1)} collective-permute-done((f32[2,24,16,128]{3,2,1,0:T(8,128)S(1)}, f32[2,24,16,128]{3,2,1,0:T(8,128)S(1)}, u32[]{:S(2)}, u32[]{:S(2)}) %collective-permute-start.16) | collective-permute-done | bytes 393248 | tf_op jit(solution)/shard_map/ppermute | solution.py:685
  69.5 3.5 %collective-permute-start.20 = (f32[2,24,16,128]{3,2,1,0:T(8,128)S(1)}, f32[2,24,16,128]{3,2,1,0:T(8,128)S(1)}, u32[]{:S(2)}, u32[]{:S(2)}) collective-permute-start(f32[2,24,16,128]{3,2,1,0:T(8,128)S(1)} %collective-permute-done.16.refs_1_), channel_id=1, source_target_pairs={{0,4},{4,8},{8,12},{6,2},{10,6},{14,10},{1,5},{5,9},{9,13},{7,3},{... | collective-permute-start | bytes 1179656 | tf_op jit(solution)/shard_map/ppermute | solution.py:685
  74.3 4.6 %collective-permute-start.17 = (f32[2,2,8,16,128]{4,3,2,1,0:T(8,128)S(1)}, f32[2,2,8,16,128]{4,3,2,1,0:T(8,128)S(1)}, u32[]{:S(2)}, u32[]{:S(2)}) collective-permute-start(f32[2,2,8,16,128]{4,3,2,1,0:T(8,128)S(1)} %pad_maximum_fusion.refs_6_), channel_id=1, source_target_pairs={{0,2},{2,4},{4,6},{6,8},{8,10},{10,12},{12,14},{1,3},{3,5},{5,7},{... | collective-permute-start | bytes 786440 | tf_op jit(solution)/shard_map/ppermute | solution.py:685
  78.8 4.4 %collective-permute-done.21.refs_4_ = f32[2,24,16,128]{3,2,1,0:T(8,128)S(1)} collective-permute-done((f32[2,24,16,128]{3,2,1,0:T(8,128)S(1)}, f32[2,24,16,128]{3,2,1,0:T(8,128)S(1)}, u32[]{:S(2)}, u32[]{:S(2)}) %collective-permute-start.21) | collective-permute-done | bytes 393248 | tf_op jit(solution)/shard_map/ppermute | solution.py:685
  83.2 3.5 %collective-permute-start.22 = (f32[2,24,16,128]{3,2,1,0:T(8,128)S(1)}, f32[2,24,16,128]{3,2,1,0:T(8,128)S(1)}, u32[]{:S(2)}, u32[]{:S(2)}) collective-permute-start(f32[2,24,16,128]{3,2,1,0:T(8,128)S(1)} %collective-permute-done.21.refs_4_), channel_id=1, source_target_pairs={{0,4},{4,8},{8,12},{6,2},{10,6},{14,10},{1,5},{5,9},{9,13},{7,3},{... | collective-permute-start | bytes 1179656 | tf_op jit(solution)/shard_map/ppermute | solution.py:685
  86.7 2.5 %first_image.1.refs_2_.first = f32[8,65,16,128]{3,2,1,0:T(8,128)S(1)} custom-call(f32[2,24,16,128]{3,2,1,0:T(8,128)S(1)} %copy-done, f32[2,24,16,128]{3,2,1,0:T(8,128)S(1)} %collective-permute-done.7.refs_1_, f32[2,24,16,128]{3,2,1,0:T(8,128)S(1)} %collective-permute-done.14.refs_2_, f32[2,24,16,128]{3,2,1,0:T(8,128)S(1)} %collective-permute-done.1.refs_3_, ...), custom_call_target="tpu_custom_call" | custom-call | flops 10000000000 | bytes 8388608 | tf_op jit(solution)/shard_map/first_image/pallas_call | solution.py:573
  89.8 4.4 %collective-permute-done.22.refs_5_ = f32[2,24,16,128]{3,2,1,0:T(8,128)S(1)} collective-permute-done((f32[2,24,16,128]{3,2,1,0:T(8,128)S(1)}, f32[2,24,16,128]{3,2,1,0:T(8,128)S(1)}, u32[]{:S(2)}, u32[]{:S(2)}) %collective-permute-start.22) | collective-permute-done | bytes 393248 | tf_op jit(solution)/shard_map/ppermute | solution.py:685
  94.3 7.7 %image.1 = f32[8,32,64,65]{3,2,1,0:T(8,128)} custom-call(s32[1]{0:T(128)} %in_order.1.token, f32[8,65,16,128]{3,2,1,0:T(8,128)S(1)} %first_image.1.refs_2_.first, f32[2,24,16,128]{3,2,1,0:T(8,128)S(1)} %get-tuple-element.79.refs_0_, f32[2,24,16,128]{3,2,1,0:T(8,128)S(1)} %collective-permute-done.16.refs_1_, ...), custom_call_target="tpu_custom_call" | custom-call | flops 10000000000 | bytes 16777216 | tf_op jit(solution)/shard_map/image/pallas_call | solution.py:641
  (39 shorter events, 6.2 us)
Async XLA Ops:
  3.8 22.6 %collective-permute-start.1 = (f32[2,24,16,128]{3,2,1,0:T(8,128)}, f32[2,24,16,128]{3,2,1,0:T(8,128)S(1)}, u32[]{:S(2)}, u32[]{:S(2)}) collective-permute-start(f32[2,24,16,128]{3,2,1,0:T(8,128)} %get-tuple-element.50), channel_id=1, source_target_pairs={{0,16},{16,0},{1,17},{17,1},{2,18},{18,2},{3,19},{19,3},{4,20},{20... | collective-permute-start | bytes 1179656 | tf_op jit(solution)/shard_map/ppermute | solution.py:685
  4.3 9.7 %collective-permute-start.4 = (f32[2,8,32,128]{3,2,1,0:T(8,128)}, f32[2,8,32,128]{3,2,1,0:T(8,128)S(1)}, u32[]{:S(2)}, u32[]{:S(2)}) collective-permute-start(f32[2,8,32,128]{3,2,1,0:T(8,128)} %get-tuple-element.55), channel_id=1, source_target_pairs={{0,2},{2,0},{4,6},{6,4},{8,10},{10,8},{12,14},{14,12},{1,3},{3,1},... | collective-permute-start | bytes 786440 | tf_op jit(solution)/shard_map/ppermute | solution.py:685
  6.9 19.5 %collective-permute-start = (f32[32,8,128]{2,1,0:T(8,128)}, f32[32,8,128]{2,1,0:T(8,128)S(1)}, u32[]{:S(2)}, u32[]{:S(2)}) collective-permute-start(f32[32,8,128]{2,1,0:T(8,128)} %get-tuple-element.48), channel_id=1, source_target_pairs={{0,1},{1,0},{2,3},{3,2},{4,5},{5,4},{6,7},{7,6},{8,9},{9,8},{10,11... | collective-permute-start | bytes 393224 | tf_op jit(solution)/shard_map/ppermute | solution.py:685
  8.4 31.1 %collective-permute-start.2 = (f32[2,4,96,128]{3,2,1,0:T(8,128)}, f32[2,4,96,128]{3,2,1,0:T(8,128)S(1)}, u32[]{:S(2)}, u32[]{:S(2)}) collective-permute-start(f32[2,4,96,128]{3,2,1,0:T(8,128)} %get-tuple-element.53), channel_id=1, source_target_pairs={{0,2},{2,4},{4,6},{6,8},{8,10},{10,12},{12,14},{1,3},{3,5},{5,7},{... | collective-permute-start | bytes 1179656 | tf_op jit(solution)/shard_map/ppermute | solution.py:685
  10.8 28.7 %collective-permute-start.3 = (f32[2,4,96,128]{3,2,1,0:T(8,128)}, f32[2,4,96,128]{3,2,1,0:T(8,128)S(1)}, u32[]{:S(2)}, u32[]{:S(2)}) collective-permute-start(f32[2,4,96,128]{3,2,1,0:T(8,128)} %get-tuple-element.54), channel_id=1, source_target_pairs={{2,0},{4,2},{6,4},{8,6},{10,8},{12,10},{14,12},{3,1},{5,3},{7,5},{... | collective-permute-start | bytes 1179656 | tf_op jit(solution)/shard_map/ppermute | solution.py:685
  14.0 25.5 %collective-permute-start.5 = (f32[2,8,32,128]{3,2,1,0:T(8,128)S(1)}, f32[2,8,32,128]{3,2,1,0:T(8,128)S(1)}, u32[]{:S(2)}, u32[]{:S(2)}) collective-permute-start(f32[2,8,32,128]{3,2,1,0:T(8,128)S(1)} %collective-permute-done.4.near), channel_id=1, source_target_pairs={{0,4},{4,8},{8,12},{6,2},{10,6},{14,10},{1,5},{5,9},{9,13},{7,3},{... | collective-permute-start | bytes 786440 | tf_op jit(solution)/shard_map/ppermute | solution.py:685
  26.4 21.7 %collective-permute-start.7 = (f32[2,24,16,128]{3,2,1,0:T(8,128)}, f32[2,24,16,128]{3,2,1,0:T(8,128)S(1)}, u32[]{:S(2)}, u32[]{:S(2)}) collective-permute-start(f32[2,24,16,128]{3,2,1,0:T(8,128)} %get-tuple-element.62.refs_0_), channel_id=1, source_target_pairs={{0,2},{2,0},{4,6},{6,4},{8,10},{10,8},{12,14},{14,12},{1,3},{3,1},... | collective-permute-start | bytes 1179656 | tf_op jit(solution)/shard_map/ppermute | solution.py:685
  40.5 7.6 %collective-permute-start.9 = (f32[2,2,8,16,128]{4,3,2,1,0:T(8,128)S(1)}, f32[2,2,8,16,128]{4,3,2,1,0:T(8,128)S(1)}, u32[]{:S(2)}, u32[]{:S(2)}) collective-permute-start(f32[2,2,8,16,128]{4,3,2,1,0:T(8,128)S(1)} %get-tuple-element.64), channel_id=1, source_target_pairs={{0,16},{16,0},{1,17},{17,1},{2,18},{18,2},{3,19},{19,3},{4,20},{20... | collective-permute-start | bytes 786440 | tf_op jit(solution)/shard_map/ppermute | solution.py:685
  40.6 4.2 %collective-permute-start.8 = (f32[2,8,16,128]{3,2,1,0:T(8,128)S(1)}, f32[2,8,16,128]{3,2,1,0:T(8,128)S(1)}, u32[]{:S(2)}, u32[]{:S(2)}) collective-permute-start(f32[2,8,16,128]{3,2,1,0:T(8,128)S(1)} %copy-done.3), channel_id=1, source_target_pairs={{0,16},{16,0},{1,17},{17,1},{2,18},{18,2},{3,19},{19,3},{4,20},{20... | collective-permute-start | bytes 393224 | tf_op jit(solution)/shard_map/ppermute | solution.py:685
  41.1 5.7 %collective-permute-start.6 = (f32[2,32,128]{2,1,0:T(8,128)S(1)}, f32[2,32,128]{2,1,0:T(8,128)S(1)}, u32[]{:S(2)}, u32[]{:S(2)}) collective-permute-start(f32[2,32,128]{2,1,0:T(8,128)S(1)} %get-tuple-element.61), channel_id=1, source_target_pairs={{0,1},{1,0},{2,3},{3,2},{4,5},{5,4},{6,7},{7,6},{8,9},{9,8},{10,11... | collective-permute-start | bytes 98312 | tf_op jit(solution)/shard_map/ppermute | solution.py:685
  42.8 14.3 %collective-permute-start.10 = (f32[2,24,16,128]{3,2,1,0:T(8,128)S(1)}, f32[2,24,16,128]{3,2,1,0:T(8,128)S(1)}, u32[]{:S(2)}, u32[]{:S(2)}) collective-permute-start(f32[2,24,16,128]{3,2,1,0:T(8,128)S(1)} %collective-permute-done.1.refs_3_), channel_id=1, source_target_pairs={{0,2},{2,0},{4,6},{6,4},{8,10},{10,8},{12,14},{14,12},{1,3},{3,1},... | collective-permute-start | bytes 1179656 | tf_op jit(solution)/shard_map/ppermute | solution.py:685
  44.8 14.9 %collective-permute-start.12 = (f32[2,4,32,128]{3,2,1,0:T(8,128)S(1)}, f32[2,4,32,128]{3,2,1,0:T(8,128)S(1)}, u32[]{:S(2)}, u32[]{:S(2)}) collective-permute-start(f32[2,4,32,128]{3,2,1,0:T(8,128)S(1)} %get-tuple-element.70), channel_id=1, source_target_pairs={{0,2},{2,4},{4,6},{6,8},{8,10},{10,12},{12,14},{1,3},{3,5},{5,7},{... | collective-permute-start | bytes 393224 | tf_op jit(solution)/shard_map/ppermute | solution.py:685
  46.8 12.9 %collective-permute-start.13 = (f32[2,4,32,128]{3,2,1,0:T(8,128)S(1)}, f32[2,4,32,128]{3,2,1,0:T(8,128)S(1)}, u32[]{:S(2)}, u32[]{:S(2)}) collective-permute-start(f32[2,4,32,128]{3,2,1,0:T(8,128)S(1)} %get-tuple-element.71), channel_id=1, source_target_pairs={{2,0},{4,2},{6,4},{8,6},{10,8},{12,10},{14,12},{3,1},{5,3},{7,5},{... | collective-permute-start | bytes 393224 | tf_op jit(solution)/shard_map/ppermute | solution.py:685
  48.1 14.5 %collective-permute-start.14 = (f32[2,24,16,128]{3,2,1,0:T(8,128)S(1)}, f32[2,24,16,128]{3,2,1,0:T(8,128)S(1)}, u32[]{:S(2)}, u32[]{:S(2)}) collective-permute-start(f32[2,24,16,128]{3,2,1,0:T(8,128)S(1)} %collective-permute-done.7.refs_1_), channel_id=1, source_target_pairs={{0,4},{4,8},{8,12},{6,2},{10,6},{14,10},{1,5},{5,9},{9,13},{7,3},{... | collective-permute-start | bytes 1179656 | tf_op jit(solution)/shard_map/ppermute | solution.py:685
  57.2 29.6 %copy-start.2 = (f32[2,8,16,128]{3,2,1,0:T(8,128)S(1)}, f32[2,8,16,128]{3,2,1,0:T(8,128)}, u32[]{:S(2)}) copy-start(f32[2,8,16,128]{3,2,1,0:T(8,128)} %get-tuple-element.85.refs_6_) | copy-start | bytes 393220
  57.2 5.6 %collective-permute-start.11 = (f32[2,24,16,128]{3,2,1,0:T(8,128)S(1)}, f32[2,24,16,128]{3,2,1,0:T(8,128)S(1)}, u32[]{:S(2)}, u32[]{:S(2)}) collective-permute-start(f32[2,24,16,128]{3,2,1,0:T(8,128)S(1)} %get-tuple-element.69), channel_id=1, source_target_pairs={{0,16},{16,0},{1,17},{17,1},{2,18},{18,2},{3,19},{19,3},{4,20},{20... | collective-permute-start | bytes 1179656 | tf_op jit(solution)/shard_map/ppermute | solution.py:685
  57.2 12.3 %collective-permute-start.16 = (f32[2,24,16,128]{3,2,1,0:T(8,128)S(1)}, f32[2,24,16,128]{3,2,1,0:T(8,128)S(1)}, u32[]{:S(2)}, u32[]{:S(2)}) collective-permute-start(f32[2,24,16,128]{3,2,1,0:T(8,128)S(1)} %get-tuple-element.79.refs_0_), channel_id=1, source_target_pairs={{0,2},{2,0},{4,6},{6,4},{8,10},{10,8},{12,14},{14,12},{1,3},{3,1},... | collective-permute-start | bytes 1179656 | tf_op jit(solution)/shard_map/ppermute | solution.py:685
  62.8 6.7 %collective-permute-start.15 = (f32[2,8,16,128]{3,2,1,0:T(8,128)S(1)}, f32[2,8,16,128]{3,2,1,0:T(8,128)S(1)}, u32[]{:S(2)}, u32[]{:S(2)}) collective-permute-start(f32[2,8,16,128]{3,2,1,0:T(8,128)S(1)} %get-tuple-element.78), channel_id=1, source_target_pairs={{0,16},{16,0},{1,17},{17,1},{2,18},{18,2},{3,19},{19,3},{4,20},{20... | collective-permute-start | bytes 393224 | tf_op jit(solution)/shard_map/ppermute | solution.py:685
  62.8 23.9 %collective-permute-start.19 = (f32[2,24,16,128]{3,2,1,0:T(8,128)S(1)}, f32[2,24,16,128]{3,2,1,0:T(8,128)S(1)}, u32[]{:S(2)}, u32[]{:S(2)}) collective-permute-start(f32[2,24,16,128]{3,2,1,0:T(8,128)S(1)} %collective-permute-done.10.refs_4_), channel_id=1, source_target_pairs={{0,4},{4,8},{8,12},{6,2},{10,6},{14,10},{1,5},{5,9},{9,13},{7,3},{... | collective-permute-start | bytes 1179656 | tf_op jit(solution)/shard_map/ppermute | solution.py:685
  67.2 16.0 %collective-permute-start.21 = (f32[2,24,16,128]{3,2,1,0:T(8,128)S(1)}, f32[2,24,16,128]{3,2,1,0:T(8,128)S(1)}, u32[]{:S(2)}, u32[]{:S(2)}) collective-permute-start(f32[2,24,16,128]{3,2,1,0:T(8,128)S(1)} %collective-permute-done.11.refs_3_), channel_id=1, source_target_pairs={{0,2},{2,0},{4,6},{6,4},{8,10},{10,8},{12,14},{14,12},{1,3},{3,1},... | collective-permute-start | bytes 1179656 | tf_op jit(solution)/shard_map/ppermute | solution.py:685
  69.5 17.3 %collective-permute-start.20 = (f32[2,24,16,128]{3,2,1,0:T(8,128)S(1)}, f32[2,24,16,128]{3,2,1,0:T(8,128)S(1)}, u32[]{:S(2)}, u32[]{:S(2)}) collective-permute-start(f32[2,24,16,128]{3,2,1,0:T(8,128)S(1)} %collective-permute-done.16.refs_1_), channel_id=1, source_target_pairs={{0,4},{4,8},{8,12},{6,2},{10,6},{14,10},{1,5},{5,9},{9,13},{7,3},{... | collective-permute-start | bytes 1179656 | tf_op jit(solution)/shard_map/ppermute | solution.py:685
  73.0 16.3 %collective-permute-start.18 = (f32[2,2,8,16,128]{4,3,2,1,0:T(8,128)S(1)}, f32[2,2,8,16,128]{4,3,2,1,0:T(8,128)S(1)}, u32[]{:S(2)}, u32[]{:S(2)}) collective-permute-start(f32[2,2,8,16,128]{4,3,2,1,0:T(8,128)S(1)} %pad_maximum_fusion.refs_6_), channel_id=1, source_target_pairs={{2,0},{4,2},{6,4},{8,6},{10,8},{12,10},{14,12},{3,1},{5,3},{7,5},{... | collective-permute-start | bytes 786440 | tf_op jit(solution)/shard_map/ppermute | solution.py:685
  74.3 15.0 %collective-permute-start.17 = (f32[2,2,8,16,128]{4,3,2,1,0:T(8,128)S(1)}, f32[2,2,8,16,128]{4,3,2,1,0:T(8,128)S(1)}, u32[]{:S(2)}, u32[]{:S(2)}) collective-permute-start(f32[2,2,8,16,128]{4,3,2,1,0:T(8,128)S(1)} %pad_maximum_fusion.refs_6_), channel_id=1, source_target_pairs={{0,2},{2,4},{4,6},{6,8},{8,10},{10,12},{12,14},{1,3},{3,5},{5,7},{... | collective-permute-start | bytes 786440 | tf_op jit(solution)/shard_map/ppermute | solution.py:685
  83.2 11.1 %collective-permute-start.22 = (f32[2,24,16,128]{3,2,1,0:T(8,128)S(1)}, f32[2,24,16,128]{3,2,1,0:T(8,128)S(1)}, u32[]{:S(2)}, u32[]{:S(2)}) collective-permute-start(f32[2,24,16,128]{3,2,1,0:T(8,128)S(1)} %collective-permute-done.21.refs_4_), channel_id=1, source_target_pairs={{0,4},{4,8},{8,12},{6,2},{10,6},{14,10},{1,5},{5,9},{9,13},{7,3},{... | collective-permute-start | bytes 1179656 | tf_op jit(solution)/shard_map/ppermute | solution.py:685
  (3 other events, 57.2 us)

commit v9 on v8

--- a/solution.py
+++ b/solution.py
@@ -695,11 +695,12 @@
     side, keep, other = barrier((side, keep, other))
     near_keep = exchange(keep, "gx", partner)
     near_other = exchange(other, "gx", partner)
-    far_edge = exchange(near_edge, "gx", onward)
     blocks = [keep, near_keep, None, other, near_other, None, keep_ends, other_ends]
     partial, kept_courant, edge_courant, edge, side = steps(
         source_now, receiver_now, source_before, receiver_before, courant, side
     )
+    near_edge, side = barrier((near_edge, side))
+    far_edge = exchange(near_edge, "gx", onward)
     ends, up, down, side, keep_edges, give_edges = mend(
         left, right, near_edge, far_edge, partial, kept_courant, edge_courant, edge, side
     )
@@ -707,11 +708,10 @@
     left = exchange(up, "gx", up_pairs)
     right = exchange(down, "gx", down_pairs)
     side = exchange(side, "gy", both)
-    side, near_keep, blocks[7], blocks[9] = barrier((side, near_keep, blocks[7], blocks[9]))
+    side, near_keep, near_other, blocks[7], blocks[9] = barrier((side, near_keep, near_other, blocks[7], blocks[9]))
     far_keep = exchange(near_keep, "gx", onward)
 
     keep, give = finish_middle(partial, ends, kept_courant, side)
-    keep, give, near_other = barrier((keep, give, near_other))
     blocks[5] = exchange(near_other, "gx", onward)
     other = exchange(give, "shot", both)
     near_keep = exchange(keep, "gx", partner)

time: 103 us -> 103 us (level)
  waiting for transfers between devices: 16.3 us -> 26.1 us
  starting transfers between devices: 55.2 us -> 45.8 us
    ppermute x23, waiting for transfers between devices: 16.3 us -> 26.1 us  [exchange(): return lax.ppermute(array, axis, pairs)]
    ppermute x23, starting transfers between devices: 55.2 us -> 45.8 us  [exchange(): return lax.ppermute(array, axis, pairs)]
  transfers between devices with their start and end apart: 23 -> 23, of which waited for: 6 -> 7; matrix products, arithmetic and copies ran while one was open for 0% -> 0% of each run, Pallas kernels for 18% -> 18%
where the time goes in v9:
time: 103 us; the launch traced here: 102 us
  starting transfers between devices  45.8 us (44%)
  Pallas kernels  30.2 us (29%)
  waiting for transfers between devices  26.1 us (25%)
    ppermute x23, starting transfers between devices, exchange(): return lax.ppermute(array, axis, pairs)  45.8 us
    ppermute x23, waiting for transfers between devices, exchange(): return lax.ppermute(array, axis, pairs)  26.1 us
    pallas_call x1, Pallas kernels, steps(): pl.pallas_call(steps_kernel, out_shape=(jax.ShapeDtypeStruct((2, rows, li...  13 us
    pallas_call x1, Pallas kernels, image(): pl.pallas_call(image_kernel, grid=(samples,), out_shape=jax.ShapeDtypeStr...  7.71 us
    pallas_call x1, Pallas kernels, pack(): pl.pallas_call(pack_kernel, out_shape=(apart, apart, jax.ShapeDtypeStruct...  3.78 us
    pallas_call x1, Pallas kernels, first_image(): pl.pallas_call(first_image_kernel, grid=(samples,), out_shape=jax.ShapeDt...  2.53 us
  transfers between devices with their start and end apart: 23, of which 7 were waited for; matrix products, arithmetic and copies ran while one was open for 0% of the time, Pallas kernels for 18%

profile of v9, /device:TPU:0, one launch (start us, length us, event | category | flops | bytes accessed | tf_op | source)
XLA Modules:
  0.0 102.4 jit_solution(15673701187874508700)
XLA Ops:
  0.0 3.8 %pack.1 = (f32[2,4,96,128]{3,2,1,0:T(8,128)}, f32[2,4,96,128]{3,2,1,0:T(8,128)}, f32[2,8,32,128]{3,2,1,0:T(8,128)}, f32[2,24,16,128]{3,2,1,0:T(8,128)}, f32[2,8,...) custom-call(f32[1,32,128,128]{3,2,1,0:T(8,128)} %source.3, ...), custom_call_target="tpu_custom_call" | custom-call | flops 10000000000 | bytes 7340032 | tf_op jit(solution)/shard_map/pack/pallas_call | solution.py:113
  4.3 2.6 %collective-permute-start = (f32[32,8,128]{2,1,0:T(8,128)}, f32[32,8,128]{2,1,0:T(8,128)S(1)}, u32[]{:S(2)}, u32[]{:S(2)}) collective-permute-start(f32[32,8,128]{2,1,0:T(8,128)} %get-tuple-element.48), channel_id=1, source_target_pairs={{0,1},{1,0},{2,3},{3,2},{4,5},{5,4},{6,7},{7,6},{8,9},{9,8},{10,11... | collective-permute-start | bytes 393224 | tf_op jit(solution)/shard_map/ppermute | solution.py:685
  6.9 1.5 %collective-permute-start.4 = (f32[2,8,32,128]{3,2,1,0:T(8,128)}, f32[2,8,32,128]{3,2,1,0:T(8,128)S(1)}, u32[]{:S(2)}, u32[]{:S(2)}) collective-permute-start(f32[2,8,32,128]{3,2,1,0:T(8,128)} %get-tuple-element.55), channel_id=1, source_target_pairs={{0,2},{2,0},{4,6},{6,4},{8,10},{10,8},{12,14},{14,12},{1,3},{3,1},... | collective-permute-start | bytes 786440 | tf_op jit(solution)/shard_map/ppermute | solution.py:685
  8.4 2.4 %collective-permute-start.2 = (f32[2,4,96,128]{3,2,1,0:T(8,128)}, f32[2,4,96,128]{3,2,1,0:T(8,128)S(1)}, u32[]{:S(2)}, u32[]{:S(2)}) collective-permute-start(f32[2,4,96,128]{3,2,1,0:T(8,128)} %get-tuple-element.53), channel_id=1, source_target_pairs={{0,2},{2,4},{4,6},{6,8},{8,10},{10,12},{12,14},{1,3},{3,5},{5,7},{... | collective-permute-start | bytes 1179656 | tf_op jit(solution)/shard_map/ppermute | solution.py:685
  10.8 1.3 %collective-permute-start.3 = (f32[2,4,96,128]{3,2,1,0:T(8,128)}, f32[2,4,96,128]{3,2,1,0:T(8,128)S(1)}, u32[]{:S(2)}, u32[]{:S(2)}) collective-permute-start(f32[2,4,96,128]{3,2,1,0:T(8,128)} %get-tuple-element.54), channel_id=1, source_target_pairs={{2,0},{4,2},{6,4},{8,6},{10,8},{12,10},{14,12},{3,1},{5,3},{7,5},{... | collective-permute-start | bytes 1179656 | tf_op jit(solution)/shard_map/ppermute | solution.py:685
  12.2 13.0 %steps.1 = (f32[2,32,32,128]{3,2,1,0:T(8,128)S(1)}, f32[32,32,128]{2,1,0:T(8,128)S(1)}, f32[2,4,128,128]{3,2,1,0:T(8,128)S(1)}, f32[2,2,4,32,128]{4,3,2,1,0:T(8,128)S(1)}, f32[2,32,128]{2,1,0:T(8,128)S(1)}) custom-call(f32[1,32,128,128]{3,2,1,0:T(8,128)} %source.3, f32[1,32,128,128]{3,2,1,0:T(8,128)} %receiver.3, f32[1,32,128,128]{3,2,1,0:T(8,128)} %source_before.1, ...), custom_call_target="tpu_custom_call" | custom-call | flops 20000000000 | bytes 1048576 | tf_op jit(solution)/shard_map/steps/pallas_call | solution.py:330
  25.2 6.6 %collective-permute-start.5 = (f32[2,8,32,128]{3,2,1,0:T(8,128)S(1)}, f32[2,8,32,128]{3,2,1,0:T(8,128)S(1)}, u32[]{:S(2)}, u32[]{:S(2)}) collective-permute-start(f32[2,8,32,128]{3,2,1,0:T(8,128)S(1)} %collective-permute-done.4.near), channel_id=1, source_target_pairs={{0,4},{4,8},{8,12},{6,2},{10,6},{14,10},{1,5},{5,9},{9,13},{7,3},{... | collective-permute-start | bytes 786440 | tf_op jit(solution)/shard_map/ppermute | solution.py:685
  32.0 2.0 %collective-permute-start.8 = (f32[2,24,16,128]{3,2,1,0:T(8,128)S(1)}, f32[2,24,16,128]{3,2,1,0:T(8,128)S(1)}, u32[]{:S(2)}, u32[]{:S(2)}) collective-permute-start(f32[2,24,16,128]{3,2,1,0:T(8,128)S(1)} %collective-permute-done.1.refs_3_), channel_id=1, source_target_pairs={{0,2},{2,0},{4,6},{6,4},{8,10},{10,8},{12,14},{14,12},{1,3},{3,1},... | collective-permute-start | bytes 1179656 | tf_op jit(solution)/shard_map/ppermute | solution.py:685
  34.0 2.9 %collective-permute-done.5.far = f32[2,8,32,128]{3,2,1,0:T(8,128)S(1)} collective-permute-done((f32[2,8,32,128]{3,2,1,0:T(8,128)S(1)}, f32[2,8,32,128]{3,2,1,0:T(8,128)S(1)}, u32[]{:S(2)}, u32[]{:S(2)}) %collective-permute-start.5) | collective-permute-done | bytes 262176 | tf_op jit(solution)/shard_map/ppermute | solution.py:685
  39.7 3.2 %collective-permute-start.12 = (f32[2,4,32,128]{3,2,1,0:T(8,128)S(1)}, f32[2,4,32,128]{3,2,1,0:T(8,128)S(1)}, u32[]{:S(2)}, u32[]{:S(2)}) collective-permute-start(f32[2,4,32,128]{3,2,1,0:T(8,128)S(1)} %get-tuple-element.70), channel_id=1, source_target_pairs={{0,2},{2,4},{4,6},{6,8},{8,10},{10,12},{12,14},{1,3},{3,5},{5,7},{... | collective-permute-start | bytes 393224 | tf_op jit(solution)/shard_map/ppermute | solution.py:685
  44.2 8.2 %collective-permute-done.8.refs_4_ = f32[2,24,16,128]{3,2,1,0:T(8,128)S(1)} collective-permute-done((f32[2,24,16,128]{3,2,1,0:T(8,128)S(1)}, f32[2,24,16,128]{3,2,1,0:T(8,128)S(1)}, u32[]{:S(2)}, u32[]{:S(2)}) %collective-permute-start.8) | collective-permute-done | bytes 393248 | tf_op jit(solution)/shard_map/ppermute | solution.py:685
  52.5 5.7 %collective-permute-start.14 = (f32[2,24,16,128]{3,2,1,0:T(8,128)S(1)}, f32[2,24,16,128]{3,2,1,0:T(8,128)S(1)}, u32[]{:S(2)}, u32[]{:S(2)}) collective-permute-start(f32[2,24,16,128]{3,2,1,0:T(8,128)S(1)} %collective-permute-done.7.refs_1_), channel_id=1, source_target_pairs={{0,4},{4,8},{8,12},{6,2},{10,6},{14,10},{1,5},{5,9},{9,13},{7,3},{... | collective-permute-start | bytes 1179656 | tf_op jit(solution)/shard_map/ppermute | solution.py:685
  58.1 1.5 %finish_middle.1 = (f32[2,24,16,128]{3,2,1,0:T(8,128)S(1)}, f32[2,24,16,128]{3,2,1,0:T(8,128)S(1)}) custom-call(f32[2,32,32,128]{3,2,1,0:T(8,128)S(1)} %get-tuple-element.52.partial, f32[2,2,8,32,128]{4,3,2,1,0:T(8,128)S(1)} %get-tuple-element.62.ends, f32[32,32,128]{2,1,0:T(8,128)S(1)} %get-tuple-element.58.kept_courant, ...), custom_call_target="tpu_custom_call" | custom-call | flops 10000000000 | bytes 3145728 | tf_op jit(solution)/shard_map/finish_middle/pallas_call | solution.py:473
  59.8 3.6 %collective-permute-done.14.refs_2_ = f32[2,24,16,128]{3,2,1,0:T(8,128)S(1)} collective-permute-done((f32[2,24,16,128]{3,2,1,0:T(8,128)S(1)}, f32[2,24,16,128]{3,2,1,0:T(8,128)S(1)}, u32[]{:S(2)}, u32[]{:S(2)}) %collective-permute-start.14) | collective-permute-done | bytes 393248 | tf_op jit(solution)/shard_map/ppermute | solution.py:685
  63.6 4.4 %collective-permute-start.19 = (f32[2,24,16,128]{3,2,1,0:T(8,128)S(1)}, f32[2,24,16,128]{3,2,1,0:T(8,128)S(1)}, u32[]{:S(2)}, u32[]{:S(2)}) collective-permute-start(f32[2,24,16,128]{3,2,1,0:T(8,128)S(1)} %collective-permute-done.8.refs_4_), channel_id=1, source_target_pairs={{0,4},{4,8},{8,12},{6,2},{10,6},{14,10},{1,5},{5,9},{9,13},{7,3},{... | collective-permute-start | bytes 1179656 | tf_op jit(solution)/shard_map/ppermute | solution.py:685
  68.1 3.3 %collective-permute-done.16.refs_1_ = f32[2,24,16,128]{3,2,1,0:T(8,128)S(1)} collective-permute-done((f32[2,24,16,128]{3,2,1,0:T(8,128)S(1)}, f32[2,24,16,128]{3,2,1,0:T(8,128)S(1)}, u32[]{:S(2)}, u32[]{:S(2)}) %collective-permute-start.16) | collective-permute-done | bytes 393248 | tf_op jit(solution)/shard_map/ppermute | solution.py:685
  71.4 3.5 %collective-permute-start.20 = (f32[2,24,16,128]{3,2,1,0:T(8,128)S(1)}, f32[2,24,16,128]{3,2,1,0:T(8,128)S(1)}, u32[]{:S(2)}, u32[]{:S(2)}) collective-permute-start(f32[2,24,16,128]{3,2,1,0:T(8,128)S(1)} %collective-permute-done.16.refs_1_), channel_id=1, source_target_pairs={{0,4},{4,8},{8,12},{6,2},{10,6},{14,10},{1,5},{5,9},{9,13},{7,3},{... | collective-permute-start | bytes 1179656 | tf_op jit(solution)/shard_map/ppermute | solution.py:685
  75.0 1.3 %collective-permute-start.18 = (f32[2,2,8,16,128]{4,3,2,1,0:T(8,128)S(1)}, f32[2,2,8,16,128]{4,3,2,1,0:T(8,128)S(1)}, u32[]{:S(2)}, u32[]{:S(2)}) collective-permute-start(f32[2,2,8,16,128]{4,3,2,1,0:T(8,128)S(1)} %pad_maximum_fusion.refs_6_), channel_id=1, source_target_pairs={{2,0},{4,2},{6,4},{8,6},{10,8},{12,10},{14,12},{3,1},{5,3},{7,5},{... | collective-permute-start | bytes 786440 | tf_op jit(solution)/shard_map/ppermute | solution.py:685
  76.3 4.6 %collective-permute-start.17 = (f32[2,2,8,16,128]{4,3,2,1,0:T(8,128)S(1)}, f32[2,2,8,16,128]{4,3,2,1,0:T(8,128)S(1)}, u32[]{:S(2)}, u32[]{:S(2)}) collective-permute-start(f32[2,2,8,16,128]{4,3,2,1,0:T(8,128)S(1)} %pad_maximum_fusion.refs_6_), channel_id=1, source_target_pairs={{0,2},{2,4},{4,6},{6,8},{8,10},{10,12},{12,14},{1,3},{3,5},{5,7},{... | collective-permute-start | bytes 786440 | tf_op jit(solution)/shard_map/ppermute | solution.py:685
  80.8 2.5 %collective-permute-done.21.refs_4_ = f32[2,24,16,128]{3,2,1,0:T(8,128)S(1)} collective-permute-done((f32[2,24,16,128]{3,2,1,0:T(8,128)S(1)}, f32[2,24,16,128]{3,2,1,0:T(8,128)S(1)}, u32[]{:S(2)}, u32[]{:S(2)}) %collective-permute-start.21) | collective-permute-done | bytes 393248 | tf_op jit(solution)/shard_map/ppermute | solution.py:685
  83.3 3.5 %collective-permute-start.22 = (f32[2,24,16,128]{3,2,1,0:T(8,128)S(1)}, f32[2,24,16,128]{3,2,1,0:T(8,128)S(1)}, u32[]{:S(2)}, u32[]{:S(2)}) collective-permute-start(f32[2,24,16,128]{3,2,1,0:T(8,128)S(1)} %collective-permute-done.21.refs_4_), channel_id=1, source_target_pairs={{0,4},{4,8},{8,12},{6,2},{10,6},{14,10},{1,5},{5,9},{9,13},{7,3},{... | collective-permute-start | bytes 1179656 | tf_op jit(solution)/shard_map/ppermute | solution.py:685
  86.8 2.5 %first_image.1.refs_2_.first = f32[8,65,16,128]{3,2,1,0:T(8,128)S(1)} custom-call(f32[2,24,16,128]{3,2,1,0:T(8,128)S(1)} %copy-done, f32[2,24,16,128]{3,2,1,0:T(8,128)S(1)} %collective-permute-done.7.refs_1_, f32[2,24,16,128]{3,2,1,0:T(8,128)S(1)} %collective-permute-done.14.refs_2_, f32[2,24,16,128]{3,2,1,0:T(8,128)S(1)} %collective-permute-done.1.refs_3_, ...), custom_call_target="tpu_custom_call" | custom-call | flops 10000000000 | bytes 8388608 | tf_op jit(solution)/shard_map/first_image/pallas_call | solution.py:573
  89.9 4.8 %collective-permute-done.22.refs_5_ = f32[2,24,16,128]{3,2,1,0:T(8,128)S(1)} collective-permute-done((f32[2,24,16,128]{3,2,1,0:T(8,128)S(1)}, f32[2,24,16,128]{3,2,1,0:T(8,128)S(1)}, u32[]{:S(2)}, u32[]{:S(2)}) %collective-permute-start.22) | collective-permute-done | bytes 393248 | tf_op jit(solution)/shard_map/ppermute | solution.py:685
  94.7 7.7 %image.1 = f32[8,32,64,65]{3,2,1,0:T(8,128)} custom-call(s32[1]{0:T(128)} %in_order.1.token, f32[8,65,16,128]{3,2,1,0:T(8,128)S(1)} %first_image.1.refs_2_.first, f32[2,24,16,128]{3,2,1,0:T(8,128)S(1)} %get-tuple-element.79.refs_0_, f32[2,24,16,128]{3,2,1,0:T(8,128)S(1)} %collective-permute-done.16.refs_1_, ...), custom_call_target="tpu_custom_call" | custom-call | flops 10000000000 | bytes 16777216 | tf_op jit(solution)/shard_map/image/pallas_call | solution.py:641
  (39 shorter events, 5.7 us)
Async XLA Ops:
  3.8 8.3 %collective-permute-start.1 = (f32[2,24,16,128]{3,2,1,0:T(8,128)}, f32[2,24,16,128]{3,2,1,0:T(8,128)S(1)}, u32[]{:S(2)}, u32[]{:S(2)}) collective-permute-start(f32[2,24,16,128]{3,2,1,0:T(8,128)} %get-tuple-element.50), channel_id=1, source_target_pairs={{0,16},{16,0},{1,17},{17,1},{2,18},{18,2},{3,19},{19,3},{4,20},{20... | collective-permute-start | bytes 1179656 | tf_op jit(solution)/shard_map/ppermute | solution.py:685
  4.3 7.8 %collective-permute-start = (f32[32,8,128]{2,1,0:T(8,128)}, f32[32,8,128]{2,1,0:T(8,128)S(1)}, u32[]{:S(2)}, u32[]{:S(2)}) collective-permute-start(f32[32,8,128]{2,1,0:T(8,128)} %get-tuple-element.48), channel_id=1, source_target_pairs={{0,1},{1,0},{2,3},{3,2},{4,5},{5,4},{6,7},{7,6},{8,9},{9,8},{10,11... | collective-permute-start | bytes 393224 | tf_op jit(solution)/shard_map/ppermute | solution.py:685
  6.9 18.3 %collective-permute-start.4 = (f32[2,8,32,128]{3,2,1,0:T(8,128)}, f32[2,8,32,128]{3,2,1,0:T(8,128)S(1)}, u32[]{:S(2)}, u32[]{:S(2)}) collective-permute-start(f32[2,8,32,128]{3,2,1,0:T(8,128)} %get-tuple-element.55), channel_id=1, source_target_pairs={{0,2},{2,0},{4,6},{6,4},{8,10},{10,8},{12,14},{14,12},{1,3},{3,1},... | collective-permute-start | bytes 786440 | tf_op jit(solution)/shard_map/ppermute | solution.py:685
  8.4 25.6 %collective-permute-start.2 = (f32[2,4,96,128]{3,2,1,0:T(8,128)}, f32[2,4,96,128]{3,2,1,0:T(8,128)S(1)}, u32[]{:S(2)}, u32[]{:S(2)}) collective-permute-start(f32[2,4,96,128]{3,2,1,0:T(8,128)} %get-tuple-element.53), channel_id=1, source_target_pairs={{0,2},{2,4},{4,6},{6,8},{8,10},{10,12},{12,14},{1,3},{3,5},{5,7},{... | collective-permute-start | bytes 1179656 | tf_op jit(solution)/shard_map/ppermute | solution.py:685
  10.8 23.2 %collective-permute-start.3 = (f32[2,4,96,128]{3,2,1,0:T(8,128)}, f32[2,4,96,128]{3,2,1,0:T(8,128)S(1)}, u32[]{:S(2)}, u32[]{:S(2)}) collective-permute-start(f32[2,4,96,128]{3,2,1,0:T(8,128)} %get-tuple-element.54), channel_id=1, source_target_pairs={{2,0},{4,2},{6,4},{8,6},{10,8},{12,10},{14,12},{3,1},{5,3},{7,5},{... | collective-permute-start | bytes 1179656 | tf_op jit(solution)/shard_map/ppermute | solution.py:685
  25.2 11.7 %collective-permute-start.5 = (f32[2,8,32,128]{3,2,1,0:T(8,128)S(1)}, f32[2,8,32,128]{3,2,1,0:T(8,128)S(1)}, u32[]{:S(2)}, u32[]{:S(2)}) collective-permute-start(f32[2,8,32,128]{3,2,1,0:T(8,128)S(1)} %collective-permute-done.4.near), channel_id=1, source_target_pairs={{0,4},{4,8},{8,12},{6,2},{10,6},{14,10},{1,5},{5,9},{9,13},{7,3},{... | collective-permute-start | bytes 786440 | tf_op jit(solution)/shard_map/ppermute | solution.py:685
  31.9 12.3 %collective-permute-start.7 = (f32[2,24,16,128]{3,2,1,0:T(8,128)S(1)}, f32[2,24,16,128]{3,2,1,0:T(8,128)S(1)}, u32[]{:S(2)}, u32[]{:S(2)}) collective-permute-start(f32[2,24,16,128]{3,2,1,0:T(8,128)S(1)} %copy-done), channel_id=1, source_target_pairs={{0,2},{2,0},{4,6},{6,4},{8,10},{10,8},{12,14},{14,12},{1,3},{3,1},... | collective-permute-start | bytes 1179656 | tf_op jit(solution)/shard_map/ppermute | solution.py:685
  32.0 20.5 %collective-permute-start.8 = (f32[2,24,16,128]{3,2,1,0:T(8,128)S(1)}, f32[2,24,16,128]{3,2,1,0:T(8,128)S(1)}, u32[]{:S(2)}, u32[]{:S(2)}) collective-permute-start(f32[2,24,16,128]{3,2,1,0:T(8,128)S(1)} %collective-permute-done.1.refs_3_), channel_id=1, source_target_pairs={{0,2},{2,0},{4,6},{6,4},{8,10},{10,8},{12,14},{14,12},{1,3},{3,1},... | collective-permute-start | bytes 1179656 | tf_op jit(solution)/shard_map/ppermute | solution.py:685
  37.9 14.6 %collective-permute-start.10 = (f32[2,2,8,16,128]{4,3,2,1,0:T(8,128)S(1)}, f32[2,2,8,16,128]{4,3,2,1,0:T(8,128)S(1)}, u32[]{:S(2)}, u32[]{:S(2)}) collective-permute-start(f32[2,2,8,16,128]{4,3,2,1,0:T(8,128)S(1)} %get-tuple-element.67), channel_id=1, source_target_pairs={{0,16},{16,0},{1,17},{17,1},{2,18},{18,2},{3,19},{19,3},{4,20},{20... | collective-permute-start | bytes 786440 | tf_op jit(solution)/shard_map/ppermute | solution.py:685
  38.0 1.7 %collective-permute-start.9 = (f32[2,8,16,128]{3,2,1,0:T(8,128)S(1)}, f32[2,8,16,128]{3,2,1,0:T(8,128)S(1)}, u32[]{:S(2)}, u32[]{:S(2)}) collective-permute-start(f32[2,8,16,128]{3,2,1,0:T(8,128)S(1)} %copy-done.3), channel_id=1, source_target_pairs={{0,16},{16,0},{1,17},{17,1},{2,18},{18,2},{3,19},{19,3},{4,20},{20... | collective-permute-start | bytes 393224 | tf_op jit(solution)/shard_map/ppermute | solution.py:685
  38.5 4.4 %collective-permute-start.6 = (f32[2,32,128]{2,1,0:T(8,128)S(1)}, f32[2,32,128]{2,1,0:T(8,128)S(1)}, u32[]{:S(2)}, u32[]{:S(2)}) collective-permute-start(f32[2,32,128]{2,1,0:T(8,128)S(1)} %get-tuple-element.63), channel_id=1, source_target_pairs={{0,1},{1,0},{2,3},{3,2},{4,5},{5,4},{6,7},{7,6},{8,9},{9,8},{10,11... | collective-permute-start | bytes 98312 | tf_op jit(solution)/shard_map/ppermute | solution.py:685
  39.7 20.1 %collective-permute-start.12 = (f32[2,4,32,128]{3,2,1,0:T(8,128)S(1)}, f32[2,4,32,128]{3,2,1,0:T(8,128)S(1)}, u32[]{:S(2)}, u32[]{:S(2)}) collective-permute-start(f32[2,4,32,128]{3,2,1,0:T(8,128)S(1)} %get-tuple-element.70), channel_id=1, source_target_pairs={{0,2},{2,4},{4,6},{6,8},{8,10},{10,12},{12,14},{1,3},{3,5},{5,7},{... | collective-permute-start | bytes 393224 | tf_op jit(solution)/shard_map/ppermute | solution.py:685
  42.9 16.9 %collective-permute-start.13 = (f32[2,4,32,128]{3,2,1,0:T(8,128)S(1)}, f32[2,4,32,128]{3,2,1,0:T(8,128)S(1)}, u32[]{:S(2)}, u32[]{:S(2)}) collective-permute-start(f32[2,4,32,128]{3,2,1,0:T(8,128)S(1)} %get-tuple-element.71), channel_id=1, source_target_pairs={{2,0},{4,2},{6,4},{8,6},{10,8},{12,10},{14,12},{3,1},{5,3},{7,5},{... | collective-permute-start | bytes 393224 | tf_op jit(solution)/shard_map/ppermute | solution.py:685
  52.5 10.9 %collective-permute-start.14 = (f32[2,24,16,128]{3,2,1,0:T(8,128)S(1)}, f32[2,24,16,128]{3,2,1,0:T(8,128)S(1)}, u32[]{:S(2)}, u32[]{:S(2)}) collective-permute-start(f32[2,24,16,128]{3,2,1,0:T(8,128)S(1)} %collective-permute-done.7.refs_1_), channel_id=1, source_target_pairs={{0,4},{4,8},{8,12},{6,2},{10,6},{14,10},{1,5},{5,9},{9,13},{7,3},{... | collective-permute-start | bytes 1179656 | tf_op jit(solution)/shard_map/ppermute | solution.py:685
  59.6 4.0 %collective-permute-start.11 = (f32[2,24,16,128]{3,2,1,0:T(8,128)S(1)}, f32[2,24,16,128]{3,2,1,0:T(8,128)S(1)}, u32[]{:S(2)}, u32[]{:S(2)}) collective-permute-start(f32[2,24,16,128]{3,2,1,0:T(8,128)S(1)} %get-tuple-element.69), channel_id=1, source_target_pairs={{0,16},{16,0},{1,17},{17,1},{2,18},{18,2},{3,19},{19,3},{4,20},{20... | collective-permute-start | bytes 1179656 | tf_op jit(solution)/shard_map/ppermute | solution.py:685
  59.7 27.1 %copy-start.2 = (f32[2,8,16,128]{3,2,1,0:T(8,128)S(1)}, f32[2,8,16,128]{3,2,1,0:T(8,128)}, u32[]{:S(2)}) copy-start(f32[2,8,16,128]{3,2,1,0:T(8,128)} %get-tuple-element.85.refs_6_) | copy-start | bytes 393220
  59.7 11.7 %collective-permute-start.16 = (f32[2,24,16,128]{3,2,1,0:T(8,128)S(1)}, f32[2,24,16,128]{3,2,1,0:T(8,128)S(1)}, u32[]{:S(2)}, u32[]{:S(2)}) collective-permute-start(f32[2,24,16,128]{3,2,1,0:T(8,128)S(1)} %get-tuple-element.79.refs_0_), channel_id=1, source_target_pairs={{0,2},{2,0},{4,6},{6,4},{8,10},{10,8},{12,14},{14,12},{1,3},{3,1},... | collective-permute-start | bytes 1179656 | tf_op jit(solution)/shard_map/ppermute | solution.py:685
  63.6 7.9 %collective-permute-start.15 = (f32[2,8,16,128]{3,2,1,0:T(8,128)S(1)}, f32[2,8,16,128]{3,2,1,0:T(8,128)S(1)}, u32[]{:S(2)}, u32[]{:S(2)}) collective-permute-start(f32[2,8,16,128]{3,2,1,0:T(8,128)S(1)} %get-tuple-element.78), channel_id=1, source_target_pairs={{0,16},{16,0},{1,17},{17,1},{2,18},{18,2},{3,19},{19,3},{4,20},{20... | collective-permute-start | bytes 393224 | tf_op jit(solution)/shard_map/ppermute | solution.py:685
  63.6 23.2 %collective-permute-start.19 = (f32[2,24,16,128]{3,2,1,0:T(8,128)S(1)}, f32[2,24,16,128]{3,2,1,0:T(8,128)S(1)}, u32[]{:S(2)}, u32[]{:S(2)}) collective-permute-start(f32[2,24,16,128]{3,2,1,0:T(8,128)S(1)} %collective-permute-done.8.refs_4_), channel_id=1, source_target_pairs={{0,4},{4,8},{8,12},{6,2},{10,6},{14,10},{1,5},{5,9},{9,13},{7,3},{... | collective-permute-start | bytes 1179656 | tf_op jit(solution)/shard_map/ppermute | solution.py:685
  68.1 15.3 %collective-permute-start.21 = (f32[2,24,16,128]{3,2,1,0:T(8,128)S(1)}, f32[2,24,16,128]{3,2,1,0:T(8,128)S(1)}, u32[]{:S(2)}, u32[]{:S(2)}) collective-permute-start(f32[2,24,16,128]{3,2,1,0:T(8,128)S(1)} %collective-permute-done.11.refs_3_), channel_id=1, source_target_pairs={{0,2},{2,0},{4,6},{6,4},{8,10},{10,8},{12,14},{14,12},{1,3},{3,1},... | collective-permute-start | bytes 1179656 | tf_op jit(solution)/shard_map/ppermute | solution.py:685
  71.4 15.4 %collective-permute-start.20 = (f32[2,24,16,128]{3,2,1,0:T(8,128)S(1)}, f32[2,24,16,128]{3,2,1,0:T(8,128)S(1)}, u32[]{:S(2)}, u32[]{:S(2)}) collective-permute-start(f32[2,24,16,128]{3,2,1,0:T(8,128)S(1)} %collective-permute-done.16.refs_1_), channel_id=1, source_target_pairs={{0,4},{4,8},{8,12},{6,2},{10,6},{14,10},{1,5},{5,9},{9,13},{7,3},{... | collective-permute-start | bytes 1179656 | tf_op jit(solution)/shard_map/ppermute | solution.py:685
  75.0 14.4 %collective-permute-start.18 = (f32[2,2,8,16,128]{4,3,2,1,0:T(8,128)S(1)}, f32[2,2,8,16,128]{4,3,2,1,0:T(8,128)S(1)}, u32[]{:S(2)}, u32[]{:S(2)}) collective-permute-start(f32[2,2,8,16,128]{4,3,2,1,0:T(8,128)S(1)} %pad_maximum_fusion.refs_6_), channel_id=1, source_target_pairs={{2,0},{4,2},{6,4},{8,6},{10,8},{12,10},{14,12},{3,1},{5,3},{7,5},{... | collective-permute-start | bytes 786440 | tf_op jit(solution)/shard_map/ppermute | solution.py:685
  76.3 13.1 %collective-permute-start.17 = (f32[2,2,8,16,128]{4,3,2,1,0:T(8,128)S(1)}, f32[2,2,8,16,128]{4,3,2,1,0:T(8,128)S(1)}, u32[]{:S(2)}, u32[]{:S(2)}) collective-permute-start(f32[2,2,8,16,128]{4,3,2,1,0:T(8,128)S(1)} %pad_maximum_fusion.refs_6_), channel_id=1, source_target_pairs={{0,2},{2,4},{4,6},{6,8},{8,10},{10,12},{12,14},{1,3},{3,5},{5,7},{... | collective-permute-start | bytes 786440 | tf_op jit(solution)/shard_map/ppermute | solution.py:685
  83.3 11.4 %collective-permute-start.22 = (f32[2,24,16,128]{3,2,1,0:T(8,128)S(1)}, f32[2,24,16,128]{3,2,1,0:T(8,128)S(1)}, u32[]{:S(2)}, u32[]{:S(2)}) collective-permute-start(f32[2,24,16,128]{3,2,1,0:T(8,128)S(1)} %collective-permute-done.21.refs_4_), channel_id=1, source_target_pairs={{0,4},{4,8},{8,12},{6,2},{10,6},{14,10},{1,5},{5,9},{9,13},{7,3},{... | collective-permute-start | bytes 1179656 | tf_op jit(solution)/shard_map/ppermute | solution.py:685
  (3 other events, 44.6 us)

commit v10 on v9

--- a/solution.py
+++ b/solution.py
@@ -476,7 +476,7 @@
         in_specs=[VMEM] * 4,
         out_specs=(VMEM,) * 2,
         compiler_params=params(24),
-        cost_estimate=cost(10**10, 3 * 2**20),
+        cost_estimate=cost(1, 1),
         name="finish_middle",
     )(partial, ends, kept_courant, side)
 
@@ -708,15 +708,15 @@
     left = exchange(up, "gx", up_pairs)
     right = exchange(down, "gx", down_pairs)
     side = exchange(side, "gy", both)
-    side, near_keep, near_other, blocks[7], blocks[9] = barrier((side, near_keep, near_other, blocks[7], blocks[9]))
+    side, near_keep, blocks[7], blocks[9] = barrier((side, near_keep, blocks[7], blocks[9]))
     far_keep = exchange(near_keep, "gx", onward)
 
     keep, give = finish_middle(partial, ends, kept_courant, side)
-    blocks[5] = exchange(near_other, "gx", onward)
     other = exchange(give, "shot", both)
     near_keep = exchange(keep, "gx", partner)
 
-    left, right, blocks[2] = barrier((left, right, far_keep))
+    left, right, blocks[2], blocks[4] = barrier((left, right, far_keep, near_other))
+    blocks[5] = exchange(blocks[4], "gx", onward)
     keep_ends, give_ends = finish_ends(ends, kept_courant, left, right, side)
     other, keep_ends, give_ends = barrier((other, keep_ends, give_ends))
     near_other = exchange(other, "gx", partner)

time: 103 us -> 100 us (0.971)
  waiting for transfers between devices: 26.1 us -> 21.1 us
  starting transfers between devices: 45.8 us -> 47.5 us
    ppermute x23, waiting for transfers between devices: 26.1 us -> 21.1 us  [exchange(): return lax.ppermute(array, axis, pairs)]
    ppermute x23, starting transfers between devices: 45.8 us -> 47.5 us  [exchange(): return lax.ppermute(array, axis, pairs)]
  transfers between devices with their start and end apart: 23 -> 23, of which waited for: 7 -> 7; matrix products, arithmetic and copies ran while one was open for 0% -> 0% of each run, Pallas kernels for 18% -> 19%
where the time goes in v10:
time: 100 us; the launch traced here: 99.1 us
  starting transfers between devices  47.5 us (48%)
  Pallas kernels  30.2 us (30%)
  waiting for transfers between devices  21.1 us (21%)
    ppermute x23, starting transfers between devices, exchange(): return lax.ppermute(array, axis, pairs)  47.5 us
    ppermute x23, waiting for transfers between devices, exchange(): return lax.ppermute(array, axis, pairs)  21.1 us
    pallas_call x1, Pallas kernels, steps(): pl.pallas_call(steps_kernel, out_shape=(jax.ShapeDtypeStruct((2, rows, li...  13 us
    pallas_call x1, Pallas kernels, image(): pl.pallas_call(image_kernel, grid=(samples,), out_shape=jax.ShapeDtypeStr...  7.71 us
    pallas_call x1, Pallas kernels, pack(): pl.pallas_call(pack_kernel, out_shape=(apart, apart, jax.ShapeDtypeStruct...  3.78 us
    pallas_call x1, Pallas kernels, first_image(): pl.pallas_call(first_image_kernel, grid=(samples,), out_shape=jax.ShapeDt...  2.53 us
  transfers between devices with their start and end apart: 23, of which 7 were waited for; matrix products, arithmetic and copies ran while one was open for 0% of the time, Pallas kernels for 19%

profile of v10, /device:TPU:0, one launch (start us, length us, event | category | flops | bytes accessed | tf_op | source)
XLA Modules:
  0.0 99.1 jit_solution(10608469627134052620)
XLA Ops:
  0.0 3.8 %pack.1 = (f32[2,4,96,128]{3,2,1,0:T(8,128)}, f32[2,4,96,128]{3,2,1,0:T(8,128)}, f32[2,8,32,128]{3,2,1,0:T(8,128)}, f32[2,24,16,128]{3,2,1,0:T(8,128)}, f32[2,8,...) custom-call(f32[1,32,128,128]{3,2,1,0:T(8,128)} %source.3, ...), custom_call_target="tpu_custom_call" | custom-call | flops 10000000000 | bytes 7340032 | tf_op jit(solution)/shard_map/pack/pallas_call | solution.py:113
  4.3 2.6 %collective-permute-start = (f32[32,8,128]{2,1,0:T(8,128)}, f32[32,8,128]{2,1,0:T(8,128)S(1)}, u32[]{:S(2)}, u32[]{:S(2)}) collective-permute-start(f32[32,8,128]{2,1,0:T(8,128)} %get-tuple-element.48), channel_id=1, source_target_pairs={{0,1},{1,0},{2,3},{3,2},{4,5},{5,4},{6,7},{7,6},{8,9},{9,8},{10,11... | collective-permute-start | bytes 393224 | tf_op jit(solution)/shard_map/ppermute | solution.py:685
  6.9 1.5 %collective-permute-start.4 = (f32[2,8,32,128]{3,2,1,0:T(8,128)}, f32[2,8,32,128]{3,2,1,0:T(8,128)S(1)}, u32[]{:S(2)}, u32[]{:S(2)}) collective-permute-start(f32[2,8,32,128]{3,2,1,0:T(8,128)} %get-tuple-element.55), channel_id=1, source_target_pairs={{0,2},{2,0},{4,6},{6,4},{8,10},{10,8},{12,14},{14,12},{1,3},{3,1},... | collective-permute-start | bytes 786440 | tf_op jit(solution)/shard_map/ppermute | solution.py:685
  8.4 2.4 %collective-permute-start.2 = (f32[2,4,96,128]{3,2,1,0:T(8,128)}, f32[2,4,96,128]{3,2,1,0:T(8,128)S(1)}, u32[]{:S(2)}, u32[]{:S(2)}) collective-permute-start(f32[2,4,96,128]{3,2,1,0:T(8,128)} %get-tuple-element.53), channel_id=1, source_target_pairs={{0,2},{2,4},{4,6},{6,8},{8,10},{10,12},{12,14},{1,3},{3,5},{5,7},{... | collective-permute-start | bytes 1179656 | tf_op jit(solution)/shard_map/ppermute | solution.py:685
  10.8 1.3 %collective-permute-start.3 = (f32[2,4,96,128]{3,2,1,0:T(8,128)}, f32[2,4,96,128]{3,2,1,0:T(8,128)S(1)}, u32[]{:S(2)}, u32[]{:S(2)}) collective-permute-start(f32[2,4,96,128]{3,2,1,0:T(8,128)} %get-tuple-element.54), channel_id=1, source_target_pairs={{2,0},{4,2},{6,4},{8,6},{10,8},{12,10},{14,12},{3,1},{5,3},{7,5},{... | collective-permute-start | bytes 1179656 | tf_op jit(solution)/shard_map/ppermute | solution.py:685
  12.2 13.0 %steps.1 = (f32[2,32,32,128]{3,2,1,0:T(8,128)S(1)}, f32[32,32,128]{2,1,0:T(8,128)S(1)}, f32[2,4,128,128]{3,2,1,0:T(8,128)S(1)}, f32[2,2,4,32,128]{4,3,2,1,0:T(8,128)S(1)}, f32[2,32,128]{2,1,0:T(8,128)S(1)}) custom-call(f32[1,32,128,128]{3,2,1,0:T(8,128)} %source.3, f32[1,32,128,128]{3,2,1,0:T(8,128)} %receiver.3, f32[1,32,128,128]{3,2,1,0:T(8,128)} %source_before.1, ...), custom_call_target="tpu_custom_call" | custom-call | flops 20000000000 | bytes 1048576 | tf_op jit(solution)/shard_map/steps/pallas_call | solution.py:330
  25.2 6.6 %collective-permute-start.5 = (f32[2,8,32,128]{3,2,1,0:T(8,128)S(1)}, f32[2,8,32,128]{3,2,1,0:T(8,128)S(1)}, u32[]{:S(2)}, u32[]{:S(2)}) collective-permute-start(f32[2,8,32,128]{3,2,1,0:T(8,128)S(1)} %collective-permute-done.4.near), channel_id=1, source_target_pairs={{0,4},{4,8},{8,12},{6,2},{10,6},{14,10},{1,5},{5,9},{9,13},{7,3},{... | collective-permute-start | bytes 786440 | tf_op jit(solution)/shard_map/ppermute | solution.py:685
  32.0 4.9 %collective-permute-done.5.far = f32[2,8,32,128]{3,2,1,0:T(8,128)S(1)} collective-permute-done((f32[2,8,32,128]{3,2,1,0:T(8,128)S(1)}, f32[2,8,32,128]{3,2,1,0:T(8,128)S(1)}, u32[]{:S(2)}, u32[]{:S(2)}) %collective-permute-start.5) | collective-permute-done | bytes 262176 | tf_op jit(solution)/shard_map/ppermute | solution.py:685
  39.0 1.3 %collective-permute-start.14 = (f32[2,24,16,128]{3,2,1,0:T(8,128)S(1)}, f32[2,24,16,128]{3,2,1,0:T(8,128)S(1)}, u32[]{:S(2)}, u32[]{:S(2)}) collective-permute-start(f32[2,24,16,128]{3,2,1,0:T(8,128)S(1)} %collective-permute-done.1.refs_3_), channel_id=1, source_target_pairs={{0,2},{2,0},{4,6},{6,4},{8,10},{10,8},{12,14},{14,12},{1,3},{3,1},... | collective-permute-start | bytes 1179656 | tf_op jit(solution)/shard_map/ppermute | solution.py:685
  40.3 2.1 %collective-permute-done.6.side = f32[2,32,128]{2,1,0:T(8,128)S(1)} collective-permute-done((f32[2,32,128]{2,1,0:T(8,128)S(1)}, f32[2,32,128]{2,1,0:T(8,128)S(1)}, u32[]{:S(2)}, u32[]{:S(2)}) %collective-permute-start.6) | collective-permute-done | bytes 32800 | tf_op jit(solution)/shard_map/ppermute | solution.py:685
  42.6 4.2 %collective-permute-start.13 = (f32[2,24,16,128]{3,2,1,0:T(8,128)S(1)}, f32[2,24,16,128]{3,2,1,0:T(8,128)S(1)}, u32[]{:S(2)}, u32[]{:S(2)}) collective-permute-start(f32[2,24,16,128]{3,2,1,0:T(8,128)S(1)} %collective-permute-done.7.refs_1_), channel_id=1, source_target_pairs={{0,4},{4,8},{8,12},{6,2},{10,6},{14,10},{1,5},{5,9},{9,13},{7,3},{... | collective-permute-start | bytes 1179656 | tf_op jit(solution)/shard_map/ppermute | solution.py:685
  46.8 1.3 %collective-permute-start.11 = (f32[2,4,32,128]{3,2,1,0:T(8,128)S(1)}, f32[2,4,32,128]{3,2,1,0:T(8,128)S(1)}, u32[]{:S(2)}, u32[]{:S(2)}) collective-permute-start(f32[2,4,32,128]{3,2,1,0:T(8,128)S(1)} %get-tuple-element.69), channel_id=1, source_target_pairs={{0,2},{2,4},{4,6},{6,8},{8,10},{10,12},{12,14},{1,3},{3,5},{5,7},{... | collective-permute-start | bytes 393224 | tf_op jit(solution)/shard_map/ppermute | solution.py:685
  48.1 1.3 %collective-permute-start.12 = (f32[2,4,32,128]{3,2,1,0:T(8,128)S(1)}, f32[2,4,32,128]{3,2,1,0:T(8,128)S(1)}, u32[]{:S(2)}, u32[]{:S(2)}) collective-permute-start(f32[2,4,32,128]{3,2,1,0:T(8,128)S(1)} %get-tuple-element.70), channel_id=1, source_target_pairs={{2,0},{4,2},{6,4},{8,6},{10,8},{12,10},{14,12},{3,1},{5,3},{7,5},{... | collective-permute-start | bytes 393224 | tf_op jit(solution)/shard_map/ppermute | solution.py:685
  49.4 1.5 %finish_middle.1 = (f32[2,24,16,128]{3,2,1,0:T(8,128)S(1)}, f32[2,24,16,128]{3,2,1,0:T(8,128)S(1)}) custom-call(f32[2,32,32,128]{3,2,1,0:T(8,128)S(1)} %get-tuple-element.52.partial, f32[2,2,8,32,128]{4,3,2,1,0:T(8,128)S(1)} %get-tuple-element.62.ends, f32[32,32,128]{2,1,0:T(8,128)S(1)} %get-tuple-element.58.kept_courant, ...), custom_call_target="tpu_custom_call" | custom-call | flops 1 | bytes 1 | tf_op jit(solution)/shard_map/finish_middle/pallas_call | solution.py:473
  51.0 4.3 %collective-permute-start.16 = (f32[2,24,16,128]{3,2,1,0:T(8,128)S(1)}, f32[2,24,16,128]{3,2,1,0:T(8,128)S(1)}, u32[]{:S(2)}, u32[]{:S(2)}) collective-permute-start(f32[2,24,16,128]{3,2,1,0:T(8,128)S(1)} %get-tuple-element.79.refs_0_), channel_id=1, source_target_pairs={{0,2},{2,0},{4,6},{6,4},{8,10},{10,8},{12,14},{14,12},{1,3},{3,1},... | collective-permute-start | bytes 1179656 | tf_op jit(solution)/shard_map/ppermute | solution.py:685
  56.8 4.0 %collective-permute-start.19 = (f32[2,24,16,128]{3,2,1,0:T(8,128)S(1)}, f32[2,24,16,128]{3,2,1,0:T(8,128)S(1)}, u32[]{:S(2)}, u32[]{:S(2)}) collective-permute-start(f32[2,24,16,128]{3,2,1,0:T(8,128)S(1)} %collective-permute-done.14.refs_4_), channel_id=1, source_target_pairs={{0,4},{4,8},{8,12},{6,2},{10,6},{14,10},{1,5},{5,9},{9,13},{7,3},{... | collective-permute-start | bytes 1179656 | tf_op jit(solution)/shard_map/ppermute | solution.py:685
  61.2 4.3 %collective-permute-done.16.refs_1_ = f32[2,24,16,128]{3,2,1,0:T(8,128)S(1)} collective-permute-done((f32[2,24,16,128]{3,2,1,0:T(8,128)S(1)}, f32[2,24,16,128]{3,2,1,0:T(8,128)S(1)}, u32[]{:S(2)}, u32[]{:S(2)}) %collective-permute-start.16) | collective-permute-done | bytes 393248 | tf_op jit(solution)/shard_map/ppermute | solution.py:685
  65.5 5.1 %collective-permute-start.20 = (f32[2,24,16,128]{3,2,1,0:T(8,128)S(1)}, f32[2,24,16,128]{3,2,1,0:T(8,128)S(1)}, u32[]{:S(2)}, u32[]{:S(2)}) collective-permute-start(f32[2,24,16,128]{3,2,1,0:T(8,128)S(1)} %collective-permute-done.16.refs_1_), channel_id=1, source_target_pairs={{0,4},{4,8},{8,12},{6,2},{10,6},{14,10},{1,5},{5,9},{9,13},{7,3},{... | collective-permute-start | bytes 1179656 | tf_op jit(solution)/shard_map/ppermute | solution.py:685
  71.9 4.6 %collective-permute-start.17 = (f32[2,2,8,16,128]{4,3,2,1,0:T(8,128)S(1)}, f32[2,2,8,16,128]{4,3,2,1,0:T(8,128)S(1)}, u32[]{:S(2)}, u32[]{:S(2)}) collective-permute-start(f32[2,2,8,16,128]{4,3,2,1,0:T(8,128)S(1)} %pad_maximum_fusion.refs_6_), channel_id=1, source_target_pairs={{0,2},{2,4},{4,6},{6,8},{8,10},{10,12},{12,14},{1,3},{3,5},{5,7},{... | collective-permute-start | bytes 786440 | tf_op jit(solution)/shard_map/ppermute | solution.py:685
  76.5 3.0 %collective-permute-done.21.refs_4_ = f32[2,24,16,128]{3,2,1,0:T(8,128)S(1)} collective-permute-done((f32[2,24,16,128]{3,2,1,0:T(8,128)S(1)}, f32[2,24,16,128]{3,2,1,0:T(8,128)S(1)}, u32[]{:S(2)}, u32[]{:S(2)}) %collective-permute-start.21) | collective-permute-done | bytes 393248 | tf_op jit(solution)/shard_map/ppermute | solution.py:685
  79.5 3.5 %collective-permute-start.22 = (f32[2,24,16,128]{3,2,1,0:T(8,128)S(1)}, f32[2,24,16,128]{3,2,1,0:T(8,128)S(1)}, u32[]{:S(2)}, u32[]{:S(2)}) collective-permute-start(f32[2,24,16,128]{3,2,1,0:T(8,128)S(1)} %collective-permute-done.21.refs_4_), channel_id=1, source_target_pairs={{0,4},{4,8},{8,12},{6,2},{10,6},{14,10},{1,5},{5,9},{9,13},{7,3},{... | collective-permute-start | bytes 1179656 | tf_op jit(solution)/shard_map/ppermute | solution.py:685
  83.1 2.5 %first_image.1.refs_2_.first = f32[8,65,16,128]{3,2,1,0:T(8,128)S(1)} custom-call(f32[2,24,16,128]{3,2,1,0:T(8,128)S(1)} %copy-done, f32[2,24,16,128]{3,2,1,0:T(8,128)S(1)} %collective-permute-done.7.refs_1_, f32[2,24,16,128]{3,2,1,0:T(8,128)S(1)} %collective-permute-done.13.refs_2_, f32[2,24,16,128]{3,2,1,0:T(8,128)S(1)} %collective-permute-done.1.refs_3_, ...), custom_call_target="tpu_custom_call" | custom-call | flops 10000000000 | bytes 8388608 | tf_op jit(solution)/shard_map/first_image/pallas_call | solution.py:573
  86.1 5.3 %collective-permute-done.22.refs_5_ = f32[2,24,16,128]{3,2,1,0:T(8,128)S(1)} collective-permute-done((f32[2,24,16,128]{3,2,1,0:T(8,128)S(1)}, f32[2,24,16,128]{3,2,1,0:T(8,128)S(1)}, u32[]{:S(2)}, u32[]{:S(2)}) %collective-permute-start.22) | collective-permute-done | bytes 393248 | tf_op jit(solution)/shard_map/ppermute | solution.py:685
  91.4 7.7 %image.1 = f32[8,32,64,65]{3,2,1,0:T(8,128)} custom-call(s32[1]{0:T(128)} %in_order.1.token, f32[8,65,16,128]{3,2,1,0:T(8,128)S(1)} %first_image.1.refs_2_.first, f32[2,24,16,128]{3,2,1,0:T(8,128)S(1)} %get-tuple-element.79.refs_0_, f32[2,24,16,128]{3,2,1,0:T(8,128)S(1)} %collective-permute-done.16.refs_1_, ...), custom_call_target="tpu_custom_call" | custom-call | flops 10000000000 | bytes 16777216 | tf_op jit(solution)/shard_map/image/pallas_call | solution.py:641
  (39 shorter events, 6.7 us)
Async XLA Ops:
  3.8 8.3 %collective-permute-start.1 = (f32[2,24,16,128]{3,2,1,0:T(8,128)}, f32[2,24,16,128]{3,2,1,0:T(8,128)S(1)}, u32[]{:S(2)}, u32[]{:S(2)}) collective-permute-start(f32[2,24,16,128]{3,2,1,0:T(8,128)} %get-tuple-element.50), channel_id=1, source_target_pairs={{0,16},{16,0},{1,17},{17,1},{2,18},{18,2},{3,19},{19,3},{4,20},{20... | collective-permute-start | bytes 1179656 | tf_op jit(solution)/shard_map/ppermute | solution.py:685
  4.3 7.8 %collective-permute-start = (f32[32,8,128]{2,1,0:T(8,128)}, f32[32,8,128]{2,1,0:T(8,128)S(1)}, u32[]{:S(2)}, u32[]{:S(2)}) collective-permute-start(f32[32,8,128]{2,1,0:T(8,128)} %get-tuple-element.48), channel_id=1, source_target_pairs={{0,1},{1,0},{2,3},{3,2},{4,5},{5,4},{6,7},{7,6},{8,9},{9,8},{10,11... | collective-permute-start | bytes 393224 | tf_op jit(solution)/shard_map/ppermute | solution.py:685
  6.9 18.3 %collective-permute-start.4 = (f32[2,8,32,128]{3,2,1,0:T(8,128)}, f32[2,8,32,128]{3,2,1,0:T(8,128)S(1)}, u32[]{:S(2)}, u32[]{:S(2)}) collective-permute-start(f32[2,8,32,128]{3,2,1,0:T(8,128)} %get-tuple-element.55), channel_id=1, source_target_pairs={{0,2},{2,0},{4,6},{6,4},{8,10},{10,8},{12,14},{14,12},{1,3},{3,1},... | collective-permute-start | bytes 786440 | tf_op jit(solution)/shard_map/ppermute | solution.py:685
  8.4 23.6 %collective-permute-start.2 = (f32[2,4,96,128]{3,2,1,0:T(8,128)}, f32[2,4,96,128]{3,2,1,0:T(8,128)S(1)}, u32[]{:S(2)}, u32[]{:S(2)}) collective-permute-start(f32[2,4,96,128]{3,2,1,0:T(8,128)} %get-tuple-element.53), channel_id=1, source_target_pairs={{0,2},{2,4},{4,6},{6,8},{8,10},{10,12},{12,14},{1,3},{3,5},{5,7},{... | collective-permute-start | bytes 1179656 | tf_op jit(solution)/shard_map/ppermute | solution.py:685
  10.8 21.1 %collective-permute-start.3 = (f32[2,4,96,128]{3,2,1,0:T(8,128)}, f32[2,4,96,128]{3,2,1,0:T(8,128)S(1)}, u32[]{:S(2)}, u32[]{:S(2)}) collective-permute-start(f32[2,4,96,128]{3,2,1,0:T(8,128)} %get-tuple-element.54), channel_id=1, source_target_pairs={{2,0},{4,2},{6,4},{8,6},{10,8},{12,10},{14,12},{3,1},{5,3},{7,5},{... | collective-permute-start | bytes 1179656 | tf_op jit(solution)/shard_map/ppermute | solution.py:685
  25.2 11.7 %collective-permute-start.5 = (f32[2,8,32,128]{3,2,1,0:T(8,128)S(1)}, f32[2,8,32,128]{3,2,1,0:T(8,128)S(1)}, u32[]{:S(2)}, u32[]{:S(2)}) collective-permute-start(f32[2,8,32,128]{3,2,1,0:T(8,128)S(1)} %collective-permute-done.4.near), channel_id=1, source_target_pairs={{0,4},{4,8},{8,12},{6,2},{10,6},{14,10},{1,5},{5,9},{9,13},{7,3},{... | collective-permute-start | bytes 786440 | tf_op jit(solution)/shard_map/ppermute | solution.py:685
  31.9 10.7 %collective-permute-start.7 = (f32[2,24,16,128]{3,2,1,0:T(8,128)S(1)}, f32[2,24,16,128]{3,2,1,0:T(8,128)S(1)}, u32[]{:S(2)}, u32[]{:S(2)}) collective-permute-start(f32[2,24,16,128]{3,2,1,0:T(8,128)S(1)} %copy-done), channel_id=1, source_target_pairs={{0,2},{2,0},{4,6},{6,4},{8,10},{10,8},{12,14},{14,12},{1,3},{3,1},... | collective-permute-start | bytes 1179656 | tf_op jit(solution)/shard_map/ppermute | solution.py:685
  37.9 4.7 %collective-permute-start.9 = (f32[2,2,8,16,128]{4,3,2,1,0:T(8,128)S(1)}, f32[2,2,8,16,128]{4,3,2,1,0:T(8,128)S(1)}, u32[]{:S(2)}, u32[]{:S(2)}) collective-permute-start(f32[2,2,8,16,128]{4,3,2,1,0:T(8,128)S(1)} %get-tuple-element.66), channel_id=1, source_target_pairs={{0,16},{16,0},{1,17},{17,1},{2,18},{18,2},{3,19},{19,3},{4,20},{20... | collective-permute-start | bytes 786440 | tf_op jit(solution)/shard_map/ppermute | solution.py:685
  38.0 2.3 %collective-permute-start.8 = (f32[2,8,16,128]{3,2,1,0:T(8,128)S(1)}, f32[2,8,16,128]{3,2,1,0:T(8,128)S(1)}, u32[]{:S(2)}, u32[]{:S(2)}) collective-permute-start(f32[2,8,16,128]{3,2,1,0:T(8,128)S(1)} %copy-done.3), channel_id=1, source_target_pairs={{0,16},{16,0},{1,17},{17,1},{2,18},{18,2},{3,19},{19,3},{4,20},{20... | collective-permute-start | bytes 393224 | tf_op jit(solution)/shard_map/ppermute | solution.py:685
  38.5 3.9 %collective-permute-start.6 = (f32[2,32,128]{2,1,0:T(8,128)S(1)}, f32[2,32,128]{2,1,0:T(8,128)S(1)}, u32[]{:S(2)}, u32[]{:S(2)}) collective-permute-start(f32[2,32,128]{2,1,0:T(8,128)S(1)} %get-tuple-element.63), channel_id=1, source_target_pairs={{0,1},{1,0},{2,3},{3,2},{4,5},{5,4},{6,7},{7,6},{8,9},{9,8},{10,11... | collective-permute-start | bytes 98312 | tf_op jit(solution)/shard_map/ppermute | solution.py:685
  39.0 11.9 %collective-permute-start.14 = (f32[2,24,16,128]{3,2,1,0:T(8,128)S(1)}, f32[2,24,16,128]{3,2,1,0:T(8,128)S(1)}, u32[]{:S(2)}, u32[]{:S(2)}) collective-permute-start(f32[2,24,16,128]{3,2,1,0:T(8,128)S(1)} %collective-permute-done.1.refs_3_), channel_id=1, source_target_pairs={{0,2},{2,0},{4,6},{6,4},{8,10},{10,8},{12,14},{14,12},{1,3},{3,1},... | collective-permute-start | bytes 1179656 | tf_op jit(solution)/shard_map/ppermute | solution.py:685
  42.6 14.0 %collective-permute-start.13 = (f32[2,24,16,128]{3,2,1,0:T(8,128)S(1)}, f32[2,24,16,128]{3,2,1,0:T(8,128)S(1)}, u32[]{:S(2)}, u32[]{:S(2)}) collective-permute-start(f32[2,24,16,128]{3,2,1,0:T(8,128)S(1)} %collective-permute-done.7.refs_1_), channel_id=1, source_target_pairs={{0,4},{4,8},{8,12},{6,2},{10,6},{14,10},{1,5},{5,9},{9,13},{7,3},{... | collective-permute-start | bytes 1179656 | tf_op jit(solution)/shard_map/ppermute | solution.py:685
  46.8 8.5 %collective-permute-start.11 = (f32[2,4,32,128]{3,2,1,0:T(8,128)S(1)}, f32[2,4,32,128]{3,2,1,0:T(8,128)S(1)}, u32[]{:S(2)}, u32[]{:S(2)}) collective-permute-start(f32[2,4,32,128]{3,2,1,0:T(8,128)S(1)} %get-tuple-element.69), channel_id=1, source_target_pairs={{0,2},{2,4},{4,6},{6,8},{8,10},{10,12},{12,14},{1,3},{3,5},{5,7},{... | collective-permute-start | bytes 393224 | tf_op jit(solution)/shard_map/ppermute | solution.py:685
  48.1 8.5 %collective-permute-start.12 = (f32[2,4,32,128]{3,2,1,0:T(8,128)S(1)}, f32[2,4,32,128]{3,2,1,0:T(8,128)S(1)}, u32[]{:S(2)}, u32[]{:S(2)}) collective-permute-start(f32[2,4,32,128]{3,2,1,0:T(8,128)S(1)} %get-tuple-element.70), channel_id=1, source_target_pairs={{2,0},{4,2},{6,4},{8,6},{10,8},{12,10},{14,12},{3,1},{5,3},{7,5},{... | collective-permute-start | bytes 393224 | tf_op jit(solution)/shard_map/ppermute | solution.py:685
  50.9 5.9 %collective-permute-start.10 = (f32[2,24,16,128]{3,2,1,0:T(8,128)S(1)}, f32[2,24,16,128]{3,2,1,0:T(8,128)S(1)}, u32[]{:S(2)}, u32[]{:S(2)}) collective-permute-start(f32[2,24,16,128]{3,2,1,0:T(8,128)S(1)} %get-tuple-element.68), channel_id=1, source_target_pairs={{0,16},{16,0},{1,17},{17,1},{2,18},{18,2},{3,19},{19,3},{4,20},{20... | collective-permute-start | bytes 1179656 | tf_op jit(solution)/shard_map/ppermute | solution.py:685
  51.0 32.1 %copy-start.2 = (f32[2,8,16,128]{3,2,1,0:T(8,128)S(1)}, f32[2,8,16,128]{3,2,1,0:T(8,128)}, u32[]{:S(2)}) copy-start(f32[2,8,16,128]{3,2,1,0:T(8,128)} %get-tuple-element.85.refs_6_) | copy-start | bytes 393220
  51.0 14.5 %collective-permute-start.16 = (f32[2,24,16,128]{3,2,1,0:T(8,128)S(1)}, f32[2,24,16,128]{3,2,1,0:T(8,128)S(1)}, u32[]{:S(2)}, u32[]{:S(2)}) collective-permute-start(f32[2,24,16,128]{3,2,1,0:T(8,128)S(1)} %get-tuple-element.79.refs_0_), channel_id=1, source_target_pairs={{0,2},{2,0},{4,6},{6,4},{8,10},{10,8},{12,14},{14,12},{1,3},{3,1},... | collective-permute-start | bytes 1179656 | tf_op jit(solution)/shard_map/ppermute | solution.py:685
  56.8 8.7 %collective-permute-start.15 = (f32[2,8,16,128]{3,2,1,0:T(8,128)S(1)}, f32[2,8,16,128]{3,2,1,0:T(8,128)S(1)}, u32[]{:S(2)}, u32[]{:S(2)}) collective-permute-start(f32[2,8,16,128]{3,2,1,0:T(8,128)S(1)} %get-tuple-element.78), channel_id=1, source_target_pairs={{0,16},{16,0},{1,17},{17,1},{2,18},{18,2},{3,19},{19,3},{4,20},{20... | collective-permute-start | bytes 393224 | tf_op jit(solution)/shard_map/ppermute | solution.py:685
  56.8 26.2 %collective-permute-start.19 = (f32[2,24,16,128]{3,2,1,0:T(8,128)S(1)}, f32[2,24,16,128]{3,2,1,0:T(8,128)S(1)}, u32[]{:S(2)}, u32[]{:S(2)}) collective-permute-start(f32[2,24,16,128]{3,2,1,0:T(8,128)S(1)} %collective-permute-done.14.refs_4_), channel_id=1, source_target_pairs={{0,4},{4,8},{8,12},{6,2},{10,6},{14,10},{1,5},{5,9},{9,13},{7,3},{... | collective-permute-start | bytes 1179656 | tf_op jit(solution)/shard_map/ppermute | solution.py:685
  60.8 18.7 %collective-permute-start.21 = (f32[2,24,16,128]{3,2,1,0:T(8,128)S(1)}, f32[2,24,16,128]{3,2,1,0:T(8,128)S(1)}, u32[]{:S(2)}, u32[]{:S(2)}) collective-permute-start(f32[2,24,16,128]{3,2,1,0:T(8,128)S(1)} %collective-permute-done.10.refs_3_), channel_id=1, source_target_pairs={{0,2},{2,0},{4,6},{6,4},{8,10},{10,8},{12,14},{14,12},{1,3},{3,1},... | collective-permute-start | bytes 1179656 | tf_op jit(solution)/shard_map/ppermute | solution.py:685
  65.5 17.5 %collective-permute-start.20 = (f32[2,24,16,128]{3,2,1,0:T(8,128)S(1)}, f32[2,24,16,128]{3,2,1,0:T(8,128)S(1)}, u32[]{:S(2)}, u32[]{:S(2)}) collective-permute-start(f32[2,24,16,128]{3,2,1,0:T(8,128)S(1)} %collective-permute-done.16.refs_1_), channel_id=1, source_target_pairs={{0,4},{4,8},{8,12},{6,2},{10,6},{14,10},{1,5},{5,9},{9,13},{7,3},{... | collective-permute-start | bytes 1179656 | tf_op jit(solution)/shard_map/ppermute | solution.py:685
  70.6 15.0 %collective-permute-start.18 = (f32[2,2,8,16,128]{4,3,2,1,0:T(8,128)S(1)}, f32[2,2,8,16,128]{4,3,2,1,0:T(8,128)S(1)}, u32[]{:S(2)}, u32[]{:S(2)}) collective-permute-start(f32[2,2,8,16,128]{4,3,2,1,0:T(8,128)S(1)} %pad_maximum_fusion.refs_6_), channel_id=1, source_target_pairs={{2,0},{4,2},{6,4},{8,6},{10,8},{12,10},{14,12},{3,1},{5,3},{7,5},{... | collective-permute-start | bytes 786440 | tf_op jit(solution)/shard_map/ppermute | solution.py:685
  71.9 13.7 %collective-permute-start.17 = (f32[2,2,8,16,128]{4,3,2,1,0:T(8,128)S(1)}, f32[2,2,8,16,128]{4,3,2,1,0:T(8,128)S(1)}, u32[]{:S(2)}, u32[]{:S(2)}) collective-permute-start(f32[2,2,8,16,128]{4,3,2,1,0:T(8,128)S(1)} %pad_maximum_fusion.refs_6_), channel_id=1, source_target_pairs={{0,2},{2,4},{4,6},{6,8},{8,10},{10,12},{12,14},{1,3},{3,5},{5,7},{... | collective-permute-start | bytes 786440 | tf_op jit(solution)/shard_map/ppermute | solution.py:685
  79.5 11.9 %collective-permute-start.22 = (f32[2,24,16,128]{3,2,1,0:T(8,128)S(1)}, f32[2,24,16,128]{3,2,1,0:T(8,128)S(1)}, u32[]{:S(2)}, u32[]{:S(2)}) collective-permute-start(f32[2,24,16,128]{3,2,1,0:T(8,128)S(1)} %collective-permute-done.21.refs_4_), channel_id=1, source_target_pairs={{0,4},{4,8},{8,12},{6,2},{10,6},{14,10},{1,5},{5,9},{9,13},{7,3},{... | collective-permute-start | bytes 1179656 | tf_op jit(solution)/shard_map/ppermute | solution.py:685
  (3 other events, 44.6 us)

commit v11 on v10

--- a/solution.py
+++ b/solution.py
@@ -607,6 +607,12 @@
         here = pl.ds(half * lines + 8 * chunk, 8)
         return pltpu.make_async_copy(staged.at[slot, here], out.at[at_step, here], out_sems.at[slot, chunk, half])
 
+    @pl.when(step >= 2)
+    def _():
+        for chunk in range(chunks):
+            for half in range(2):
+                leave(step - 2, chunk, half).wait()
+
     sample = 4 * step
     for chunk in range(chunks):
         here = pl.ds(8 * chunk, 8)
@@ -614,16 +620,12 @@
             total = first[0, shift, here, :] + products(rows_of, sample, shift, here)
             turned[chunk, pl.ds(shift, 8, stride=OFFSET_ROWS), :] = total
 
-        @pl.when(step >= 2)
-        def _():
-            for half in range(2):
-                leave(step - 2, chunk, half).wait()
-
         for line in range(8):
             values = turned[chunk, line * OFFSET_ROWS : (line + 1) * OFFSET_ROWS, :].T
             at = 8 * chunk + line
             staged[step % 2, at] = values[: size_z // 2, :OFFSETS]
             staged[step % 2, lines + at] = values[size_z // 2 :, :OFFSETS]
+    for chunk in range(chunks):
         for half in range(2):
             leave(step, chunk, half).start()
 
@@ -724,12 +726,13 @@
     other_ends, near_keep = barrier((other_ends, near_keep))
     own = jnp.stack([keep_ends, other_ends])
     far_keep = exchange(near_keep, "gx", onward)
-    left = exchange(own, "gx", up_pairs)
     right = exchange(own, "gx", down_pairs)
+    late, near_other = barrier((keep_ends, near_other))
     far_other = exchange(near_other, "gx", onward)
+    left = exchange(jnp.stack([late, other_ends]), "gx", up_pairs)
     blocks[5], far_keep = lax.optimization_barrier((blocks[5], far_keep))
     first = first_image(blocks)
-    token = in_order(left, right, first)
+    token = in_order(right, first)
     blocks = [keep, near_keep, far_keep, other, near_other, far_other, own, left, right]
     return jnp.transpose(image(token, first, blocks), (3, 0, 1, 2))
 

time: 100 us -> 102 us (1.020)
  the two profiles are of different devices: /device:TPU:0 before, /device:TPU:9 now
where the time goes in v11:
time: 102 us
  starting transfers between devices  44.9 us (44%)
  Pallas kernels  30.5 us (30%)
  waiting for transfers between devices  26.1 us (26%)
    ppermute x23, starting transfers between devices, exchange(): return lax.ppermute(array, axis, pairs)  44.9 us
    ppermute x23, waiting for transfers between devices, exchange(): return lax.ppermute(array, axis, pairs)  26.1 us
    pallas_call x1, Pallas kernels, steps(): pl.pallas_call(steps_kernel, out_shape=(jax.ShapeDtypeStruct((2, rows, li...  13 us
    pallas_call x1, Pallas kernels, image(): pl.pallas_call(image_kernel, grid=(samples,), out_shape=jax.ShapeDtypeStr...  8.05 us
    pallas_call x1, Pallas kernels, pack(): pl.pallas_call(pack_kernel, out_shape=(apart, apart, jax.ShapeDtypeStruct...  3.79 us
    pallas_call x1, Pallas kernels, first_image(): pl.pallas_call(first_image_kernel, grid=(samples,), out_shape=jax.ShapeDt...  2.53 us
  transfers between devices with their start and end apart: 23, of which 9 were waited for; matrix products, arithmetic and copies ran while one was open for 0% of the time, Pallas kernels for 18%

profile of v11, /device:TPU:9, one launch (start us, length us, event | category | flops | bytes accessed | tf_op | source)
XLA Modules:
  0.0 101.9 jit_solution(10599367782048343290)
XLA Ops:
  0.0 3.8 %pack.1 = (f32[2,4,96,128]{3,2,1,0:T(8,128)}, f32[2,4,96,128]{3,2,1,0:T(8,128)}, f32[2,8,32,128]{3,2,1,0:T(8,128)}, f32[2,24,16,128]{3,2,1,0:T(8,128)}, f32[2,8,...) custom-call(f32[1,32,128,128]{3,2,1,0:T(8,128)} %source.3, ...), custom_call_target="tpu_custom_call" | custom-call | flops 10000000000 | bytes 7340032 | tf_op jit(solution)/shard_map/pack/pallas_call | solution.py:113
  7.0 2.1 %collective-permute-start.2 = (f32[2,4,96,128]{3,2,1,0:T(8,128)}, f32[2,4,96,128]{3,2,1,0:T(8,128)S(1)}, u32[]{:S(2)}, u32[]{:S(2)}) collective-permute-start(f32[2,4,96,128]{3,2,1,0:T(8,128)} %get-tuple-element.55), channel_id=1, source_target_pairs={{0,2},{2,4},{4,6},{6,8},{8,10},{10,12},{12,14},{1,3},{3,5},{5,7},{... | collective-permute-start | bytes 1179656 | tf_op jit(solution)/shard_map/ppermute | solution.py:687
  9.1 4.0 %collective-permute-start.3 = (f32[2,4,96,128]{3,2,1,0:T(8,128)}, f32[2,4,96,128]{3,2,1,0:T(8,128)S(1)}, u32[]{:S(2)}, u32[]{:S(2)}) collective-permute-start(f32[2,4,96,128]{3,2,1,0:T(8,128)} %get-tuple-element.56), channel_id=1, source_target_pairs={{2,0},{4,2},{6,4},{8,6},{10,8},{12,10},{14,12},{3,1},{5,3},{7,5},{... | collective-permute-start | bytes 1179656 | tf_op jit(solution)/shard_map/ppermute | solution.py:687
  13.2 13.0 %steps.1 = (f32[2,32,32,128]{3,2,1,0:T(8,128)S(1)}, f32[32,32,128]{2,1,0:T(8,128)S(1)}, f32[2,4,128,128]{3,2,1,0:T(8,128)S(1)}, f32[2,2,4,32,128]{4,3,2,1,0:T(8,128)S(1)}, f32[2,32,128]{2,1,0:T(8,128)S(1)}) custom-call(f32[1,32,128,128]{3,2,1,0:T(8,128)} %source.3, f32[1,32,128,128]{3,2,1,0:T(8,128)} %receiver.3, f32[1,32,128,128]{3,2,1,0:T(8,128)} %source_before.1, ...), custom_call_target="tpu_custom_call" | custom-call | flops 20000000000 | bytes 1048576 | tf_op jit(solution)/shard_map/steps/pallas_call | solution.py:330
  26.3 3.3 %collective-permute-start.5 = (f32[2,8,32,128]{3,2,1,0:T(8,128)S(1)}, f32[2,8,32,128]{3,2,1,0:T(8,128)S(1)}, u32[]{:S(2)}, u32[]{:S(2)}) collective-permute-start(f32[2,8,32,128]{3,2,1,0:T(8,128)S(1)} %collective-permute-done.4.near), channel_id=1, source_target_pairs={{0,4},{4,8},{8,12},{6,2},{10,6},{14,10},{1,5},{5,9},{9,13},{7,3},{... | collective-permute-start | bytes 786440 | tf_op jit(solution)/shard_map/ppermute | solution.py:687
  30.4 4.5 %collective-permute-done.5.far = f32[2,8,32,128]{3,2,1,0:T(8,128)S(1)} collective-permute-done((f32[2,8,32,128]{3,2,1,0:T(8,128)S(1)}, f32[2,8,32,128]{3,2,1,0:T(8,128)S(1)}, u32[]{:S(2)}, u32[]{:S(2)}) %collective-permute-start.5) | collective-permute-done | bytes 262176 | tf_op jit(solution)/shard_map/ppermute | solution.py:687
  35.9 2.2 %collective-permute-start.9 = (f32[2,2,8,16,128]{4,3,2,1,0:T(8,128)S(1)}, f32[2,2,8,16,128]{4,3,2,1,0:T(8,128)S(1)}, u32[]{:S(2)}, u32[]{:S(2)}) collective-permute-start(f32[2,2,8,16,128]{4,3,2,1,0:T(8,128)S(1)} %get-tuple-element.68), channel_id=1, source_target_pairs={{0,16},{16,0},{1,17},{17,1},{2,18},{18,2},{3,19},{19,3},{4,20},{20... | collective-permute-start | bytes 786440 | tf_op jit(solution)/shard_map/ppermute | solution.py:687
  39.5 1.5 %collective-permute-done.6.side = f32[2,32,128]{2,1,0:T(8,128)S(1)} collective-permute-done((f32[2,32,128]{2,1,0:T(8,128)S(1)}, f32[2,32,128]{2,1,0:T(8,128)S(1)}, u32[]{:S(2)}, u32[]{:S(2)}) %collective-permute-start.6) | collective-permute-done | bytes 32800 | tf_op jit(solution)/shard_map/ppermute | solution.py:687
  41.0 3.2 %collective-permute-start.13 = (f32[2,24,16,128]{3,2,1,0:T(8,128)S(1)}, f32[2,24,16,128]{3,2,1,0:T(8,128)S(1)}, u32[]{:S(2)}, u32[]{:S(2)}) collective-permute-start(f32[2,24,16,128]{3,2,1,0:T(8,128)S(1)} %collective-permute-done.7.refs_1_), channel_id=1, source_target_pairs={{0,4},{4,8},{8,12},{6,2},{10,6},{14,10},{1,5},{5,9},{9,13},{7,3},{... | collective-permute-start | bytes 1179656 | tf_op jit(solution)/shard_map/ppermute | solution.py:687
  44.2 1.9 %collective-permute-start.11 = (f32[2,4,32,128]{3,2,1,0:T(8,128)S(1)}, f32[2,4,32,128]{3,2,1,0:T(8,128)S(1)}, u32[]{:S(2)}, u32[]{:S(2)}) collective-permute-start(f32[2,4,32,128]{3,2,1,0:T(8,128)S(1)} %get-tuple-element.71), channel_id=1, source_target_pairs={{0,2},{2,4},{4,6},{6,8},{8,10},{10,12},{12,14},{1,3},{3,5},{5,7},{... | collective-permute-start | bytes 393224 | tf_op jit(solution)/shard_map/ppermute | solution.py:687
  46.1 4.3 %collective-permute-start.12 = (f32[2,4,32,128]{3,2,1,0:T(8,128)S(1)}, f32[2,4,32,128]{3,2,1,0:T(8,128)S(1)}, u32[]{:S(2)}, u32[]{:S(2)}) collective-permute-start(f32[2,4,32,128]{3,2,1,0:T(8,128)S(1)} %get-tuple-element.72), channel_id=1, source_target_pairs={{2,0},{4,2},{6,4},{8,6},{10,8},{12,10},{14,12},{3,1},{5,3},{7,5},{... | collective-permute-start | bytes 393224 | tf_op jit(solution)/shard_map/ppermute | solution.py:687
  50.4 1.5 %finish_middle.1 = (f32[2,24,16,128]{3,2,1,0:T(8,128)S(1)}, f32[2,24,16,128]{3,2,1,0:T(8,128)S(1)}) custom-call(f32[2,32,32,128]{3,2,1,0:T(8,128)S(1)} %get-tuple-element.54.partial, f32[2,2,8,32,128]{4,3,2,1,0:T(8,128)S(1)} %get-tuple-element.64.ends, f32[32,32,128]{2,1,0:T(8,128)S(1)} %get-tuple-element.60.kept_courant, ...), custom_call_target="tpu_custom_call" | custom-call | flops 1 | bytes 1 | tf_op jit(solution)/shard_map/finish_middle/pallas_call | solution.py:473
  51.8 2.5 %collective-permute-start.10 = (f32[2,24,16,128]{3,2,1,0:T(8,128)S(1)}, f32[2,24,16,128]{3,2,1,0:T(8,128)S(1)}, u32[]{:S(2)}, u32[]{:S(2)}) collective-permute-start(f32[2,24,16,128]{3,2,1,0:T(8,128)S(1)} %get-tuple-element.70), channel_id=1, source_target_pairs={{0,16},{16,0},{1,17},{17,1},{2,18},{18,2},{3,19},{19,3},{4,20},{20... | collective-permute-start | bytes 1179656 | tf_op jit(solution)/shard_map/ppermute | solution.py:687
  56.6 2.3 %collective-permute-start.20 = (f32[2,24,16,128]{3,2,1,0:T(8,128)S(1)}, f32[2,24,16,128]{3,2,1,0:T(8,128)S(1)}, u32[]{:S(2)}, u32[]{:S(2)}) collective-permute-start(f32[2,24,16,128]{3,2,1,0:T(8,128)S(1)} %collective-permute-done.10.refs_3_), channel_id=1, source_target_pairs={{0,2},{2,0},{4,6},{6,4},{8,10},{10,8},{12,14},{14,12},{1,3},{3,1},... | collective-permute-start | bytes 1179656 | tf_op jit(solution)/shard_map/ppermute | solution.py:687
  58.8 1.9 %collective-permute-start.18 = (f32[2,24,16,128]{3,2,1,0:T(8,128)S(1)}, f32[2,24,16,128]{3,2,1,0:T(8,128)S(1)}, u32[]{:S(2)}, u32[]{:S(2)}) collective-permute-start(f32[2,24,16,128]{3,2,1,0:T(8,128)S(1)} %collective-permute-done.14.refs_4_), channel_id=1, source_target_pairs={{0,4},{4,8},{8,12},{6,2},{10,6},{14,10},{1,5},{5,9},{9,13},{7,3},{... | collective-permute-start | bytes 1179656 | tf_op jit(solution)/shard_map/ppermute | solution.py:687
  60.7 4.3 %collective-permute-done.16.refs_1_ = f32[2,24,16,128]{3,2,1,0:T(8,128)S(1)} collective-permute-done((f32[2,24,16,128]{3,2,1,0:T(8,128)S(1)}, f32[2,24,16,128]{3,2,1,0:T(8,128)S(1)}, u32[]{:S(2)}, u32[]{:S(2)}) %collective-permute-start.16) | collective-permute-done | bytes 393248 | tf_op jit(solution)/shard_map/ppermute | solution.py:687
  65.0 3.2 %collective-permute-start.19 = (f32[2,24,16,128]{3,2,1,0:T(8,128)S(1)}, f32[2,24,16,128]{3,2,1,0:T(8,128)S(1)}, u32[]{:S(2)}, u32[]{:S(2)}) collective-permute-start(f32[2,24,16,128]{3,2,1,0:T(8,128)S(1)} %collective-permute-done.16.refs_1_), channel_id=1, source_target_pairs={{0,4},{4,8},{8,12},{6,2},{10,6},{14,10},{1,5},{5,9},{9,13},{7,3},{... | collective-permute-start | bytes 1179656 | tf_op jit(solution)/shard_map/ppermute | solution.py:687
  68.2 5.2 %collective-permute-done.20.refs_4_ = f32[2,24,16,128]{3,2,1,0:T(8,128)S(1)} collective-permute-done((f32[2,24,16,128]{3,2,1,0:T(8,128)S(1)}, f32[2,24,16,128]{3,2,1,0:T(8,128)S(1)}, u32[]{:S(2)}, u32[]{:S(2)}) %collective-permute-start.20) | collective-permute-done | bytes 393248 | tf_op jit(solution)/shard_map/ppermute | solution.py:687
  73.4 3.2 %collective-permute-start.21 = (f32[2,24,16,128]{3,2,1,0:T(8,128)S(1)}, f32[2,24,16,128]{3,2,1,0:T(8,128)S(1)}, u32[]{:S(2)}, u32[]{:S(2)}) collective-permute-start(f32[2,24,16,128]{3,2,1,0:T(8,128)S(1)} %collective-permute-done.20.refs_4_), channel_id=1, source_target_pairs={{0,4},{4,8},{8,12},{6,2},{10,6},{14,10},{1,5},{5,9},{9,13},{7,3},{... | collective-permute-start | bytes 1179656 | tf_op jit(solution)/shard_map/ppermute | solution.py:687
  76.7 2.2 %collective-permute-start.22 = (f32[2,2,8,16,128]{4,3,2,1,0:T(8,128)S(1)}, f32[2,2,8,16,128]{4,3,2,1,0:T(8,128)S(1)}, u32[]{:S(2)}, u32[]{:S(2)}) collective-permute-start(f32[2,2,8,16,128]{4,3,2,1,0:T(8,128)S(1)} %get-tuple-element.95), channel_id=1, source_target_pairs={{0,2},{2,4},{4,6},{6,8},{8,10},{10,12},{12,14},{1,3},{3,5},{5,7},{... | collective-permute-start | bytes 786440 | tf_op jit(solution)/shard_map/ppermute | solution.py:687
  78.9 3.9 %collective-permute-start.17 = (f32[2,2,8,16,128]{4,3,2,1,0:T(8,128)S(1)}, f32[2,2,8,16,128]{4,3,2,1,0:T(8,128)S(1)}, u32[]{:S(2)}, u32[]{:S(2)}) collective-permute-start(f32[2,2,8,16,128]{4,3,2,1,0:T(8,128)S(1)} %get-tuple-element.96.refs_6_), channel_id=1, source_target_pairs={{2,0},{4,2},{6,4},{8,6},{10,8},{12,10},{14,12},{3,1},{5,3},{7,5},{... | collective-permute-start | bytes 786440 | tf_op jit(solution)/shard_map/ppermute | solution.py:687
  82.9 2.5 %first_image.1.refs_1_.first = f32[8,65,16,128]{3,2,1,0:T(8,128)S(1)} custom-call(f32[2,24,16,128]{3,2,1,0:T(8,128)S(1)} %copy-done, f32[2,24,16,128]{3,2,1,0:T(8,128)S(1)} %collective-permute-done.7.refs_1_, f32[2,24,16,128]{3,2,1,0:T(8,128)S(1)} %collective-permute-done.13.refs_2_, f32[2,24,16,128]{3,2,1,0:T(8,128)S(1)} %collective-permute-done.1.refs_3_, ...), custom_call_target="tpu_custom_call" | custom-call | flops 10000000000 | bytes 8388608 | tf_op jit(solution)/shard_map/first_image/pallas_call | solution.py:573
  85.4 7.9 %collective-permute-done.17.refs_0_.refs_8_ = f32[2,2,8,16,128]{4,3,2,1,0:T(8,128)S(1)} collective-permute-done((f32[2,2,8,16,128]{4,3,2,1,0:T(8,128)S(1)}, f32[2,2,8,16,128]{4,3,2,1,0:T(8,128)S(1)}, u32[]{:S(2)}, u32[]{:S(2)}) %collective-permute-start.17) | collective-permute-done | bytes 262176 | tf_op jit(solution)/shard_map/ppermute | solution.py:687
  93.8 8.1 %image.1 = f32[8,32,64,65]{3,2,1,0:T(8,128)} custom-call(s32[1]{0:T(128)} %in_order.1.token, f32[8,65,16,128]{3,2,1,0:T(8,128)S(1)} %first_image.1.refs_1_.first, f32[2,24,16,128]{3,2,1,0:T(8,128)S(1)} %get-tuple-element.81.refs_0_, f32[2,24,16,128]{3,2,1,0:T(8,128)S(1)} %collective-permute-done.16.refs_1_, ...), custom_call_target="tpu_custom_call" | custom-call | flops 10000000000 | bytes 16777216 | tf_op jit(solution)/shard_map/image/pallas_call | solution.py:643
  (39 shorter events, 9.1 us)
Async XLA Ops:
  3.8 9.4 %collective-permute-start.1 = (f32[2,24,16,128]{3,2,1,0:T(8,128)}, f32[2,24,16,128]{3,2,1,0:T(8,128)S(1)}, u32[]{:S(2)}, u32[]{:S(2)}) collective-permute-start(f32[2,24,16,128]{3,2,1,0:T(8,128)} %get-tuple-element.52), channel_id=1, source_target_pairs={{0,16},{16,0},{1,17},{17,1},{2,18},{18,2},{3,19},{19,3},{4,20},{20... | collective-permute-start | bytes 1179656 | tf_op jit(solution)/shard_map/ppermute | solution.py:687
  4.5 8.7 %collective-permute-start = (f32[32,8,128]{2,1,0:T(8,128)}, f32[32,8,128]{2,1,0:T(8,128)S(1)}, u32[]{:S(2)}, u32[]{:S(2)}) collective-permute-start(f32[32,8,128]{2,1,0:T(8,128)} %get-tuple-element.50), channel_id=1, source_target_pairs={{0,1},{1,0},{2,3},{3,2},{4,5},{5,4},{6,7},{7,6},{8,9},{9,8},{10,11... | collective-permute-start | bytes 393224 | tf_op jit(solution)/shard_map/ppermute | solution.py:687
  5.8 20.5 %collective-permute-start.4 = (f32[2,8,32,128]{3,2,1,0:T(8,128)}, f32[2,8,32,128]{3,2,1,0:T(8,128)S(1)}, u32[]{:S(2)}, u32[]{:S(2)}) collective-permute-start(f32[2,8,32,128]{3,2,1,0:T(8,128)} %get-tuple-element.57), channel_id=1, source_target_pairs={{0,2},{2,0},{4,6},{6,4},{8,10},{10,8},{12,14},{14,12},{1,3},{3,1},... | collective-permute-start | bytes 786440 | tf_op jit(solution)/shard_map/ppermute | solution.py:687
  7.0 22.7 %collective-permute-start.2 = (f32[2,4,96,128]{3,2,1,0:T(8,128)}, f32[2,4,96,128]{3,2,1,0:T(8,128)S(1)}, u32[]{:S(2)}, u32[]{:S(2)}) collective-permute-start(f32[2,4,96,128]{3,2,1,0:T(8,128)} %get-tuple-element.55), channel_id=1, source_target_pairs={{0,2},{2,4},{4,6},{6,8},{8,10},{10,12},{12,14},{1,3},{3,5},{5,7},{... | collective-permute-start | bytes 1179656 | tf_op jit(solution)/shard_map/ppermute | solution.py:687
  9.1 21.2 %collective-permute-start.3 = (f32[2,4,96,128]{3,2,1,0:T(8,128)}, f32[2,4,96,128]{3,2,1,0:T(8,128)S(1)}, u32[]{:S(2)}, u32[]{:S(2)}) collective-permute-start(f32[2,4,96,128]{3,2,1,0:T(8,128)} %get-tuple-element.56), channel_id=1, source_target_pairs={{2,0},{4,2},{6,4},{8,6},{10,8},{12,10},{14,12},{3,1},{5,3},{7,5},{... | collective-permute-start | bytes 1179656 | tf_op jit(solution)/shard_map/ppermute | solution.py:687
  26.3 8.6 %collective-permute-start.5 = (f32[2,8,32,128]{3,2,1,0:T(8,128)S(1)}, f32[2,8,32,128]{3,2,1,0:T(8,128)S(1)}, u32[]{:S(2)}, u32[]{:S(2)}) collective-permute-start(f32[2,8,32,128]{3,2,1,0:T(8,128)S(1)} %collective-permute-done.4.near), channel_id=1, source_target_pairs={{0,4},{4,8},{8,12},{6,2},{10,6},{14,10},{1,5},{5,9},{9,13},{7,3},{... | collective-permute-start | bytes 786440 | tf_op jit(solution)/shard_map/ppermute | solution.py:687
  29.6 11.3 %collective-permute-start.7 = (f32[2,24,16,128]{3,2,1,0:T(8,128)S(1)}, f32[2,24,16,128]{3,2,1,0:T(8,128)S(1)}, u32[]{:S(2)}, u32[]{:S(2)}) collective-permute-start(f32[2,24,16,128]{3,2,1,0:T(8,128)S(1)} %copy-done), channel_id=1, source_target_pairs={{0,2},{2,0},{4,6},{6,4},{8,10},{10,8},{12,14},{14,12},{1,3},{3,1},... | collective-permute-start | bytes 1179656 | tf_op jit(solution)/shard_map/ppermute | solution.py:687
  35.9 5.0 %collective-permute-start.9 = (f32[2,2,8,16,128]{4,3,2,1,0:T(8,128)S(1)}, f32[2,2,8,16,128]{4,3,2,1,0:T(8,128)S(1)}, u32[]{:S(2)}, u32[]{:S(2)}) collective-permute-start(f32[2,2,8,16,128]{4,3,2,1,0:T(8,128)S(1)} %get-tuple-element.68), channel_id=1, source_target_pairs={{0,16},{16,0},{1,17},{17,1},{2,18},{18,2},{3,19},{19,3},{4,20},{20... | collective-permute-start | bytes 786440 | tf_op jit(solution)/shard_map/ppermute | solution.py:687
  38.1 1.3 %collective-permute-start.8 = (f32[2,8,16,128]{3,2,1,0:T(8,128)S(1)}, f32[2,8,16,128]{3,2,1,0:T(8,128)S(1)}, u32[]{:S(2)}, u32[]{:S(2)}) collective-permute-start(f32[2,8,16,128]{3,2,1,0:T(8,128)S(1)} %copy-done.3), channel_id=1, source_target_pairs={{0,16},{16,0},{1,17},{17,1},{2,18},{18,2},{3,19},{19,3},{4,20},{20... | collective-permute-start | bytes 393224 | tf_op jit(solution)/shard_map/ppermute | solution.py:687
  38.2 2.8 %collective-permute-start.6 = (f32[2,32,128]{2,1,0:T(8,128)S(1)}, f32[2,32,128]{2,1,0:T(8,128)S(1)}, u32[]{:S(2)}, u32[]{:S(2)}) collective-permute-start(f32[2,32,128]{2,1,0:T(8,128)S(1)} %get-tuple-element.65), channel_id=1, source_target_pairs={{0,1},{1,0},{2,3},{3,2},{4,5},{5,4},{6,7},{7,6},{8,9},{9,8},{10,11... | collective-permute-start | bytes 98312 | tf_op jit(solution)/shard_map/ppermute | solution.py:687
  38.5 15.9 %collective-permute-start.14 = (f32[2,24,16,128]{3,2,1,0:T(8,128)S(1)}, f32[2,24,16,128]{3,2,1,0:T(8,128)S(1)}, u32[]{:S(2)}, u32[]{:S(2)}) collective-permute-start(f32[2,24,16,128]{3,2,1,0:T(8,128)S(1)} %collective-permute-done.1.refs_3_), channel_id=1, source_target_pairs={{0,2},{2,0},{4,6},{6,4},{8,10},{10,8},{12,14},{14,12},{1,3},{3,1},... | collective-permute-start | bytes 1179656 | tf_op jit(solution)/shard_map/ppermute | solution.py:687
  41.0 14.0 %collective-permute-start.13 = (f32[2,24,16,128]{3,2,1,0:T(8,128)S(1)}, f32[2,24,16,128]{3,2,1,0:T(8,128)S(1)}, u32[]{:S(2)}, u32[]{:S(2)}) collective-permute-start(f32[2,24,16,128]{3,2,1,0:T(8,128)S(1)} %collective-permute-done.7.refs_1_), channel_id=1, source_target_pairs={{0,4},{4,8},{8,12},{6,2},{10,6},{14,10},{1,5},{5,9},{9,13},{7,3},{... | collective-permute-start | bytes 1179656 | tf_op jit(solution)/shard_map/ppermute | solution.py:687
  44.2 10.2 %collective-permute-start.11 = (f32[2,4,32,128]{3,2,1,0:T(8,128)S(1)}, f32[2,4,32,128]{3,2,1,0:T(8,128)S(1)}, u32[]{:S(2)}, u32[]{:S(2)}) collective-permute-start(f32[2,4,32,128]{3,2,1,0:T(8,128)S(1)} %get-tuple-element.71), channel_id=1, source_target_pairs={{0,2},{2,4},{4,6},{6,8},{8,10},{10,12},{12,14},{1,3},{3,5},{5,7},{... | collective-permute-start | bytes 393224 | tf_op jit(solution)/shard_map/ppermute | solution.py:687
  46.1 8.9 %collective-permute-start.12 = (f32[2,4,32,128]{3,2,1,0:T(8,128)S(1)}, f32[2,4,32,128]{3,2,1,0:T(8,128)S(1)}, u32[]{:S(2)}, u32[]{:S(2)}) collective-permute-start(f32[2,4,32,128]{3,2,1,0:T(8,128)S(1)} %get-tuple-element.72), channel_id=1, source_target_pairs={{2,0},{4,2},{6,4},{8,6},{10,8},{12,10},{14,12},{3,1},{5,3},{7,5},{... | collective-permute-start | bytes 393224 | tf_op jit(solution)/shard_map/ppermute | solution.py:687
  51.8 3.8 %collective-permute-start.10 = (f32[2,24,16,128]{3,2,1,0:T(8,128)S(1)}, f32[2,24,16,128]{3,2,1,0:T(8,128)S(1)}, u32[]{:S(2)}, u32[]{:S(2)}) collective-permute-start(f32[2,24,16,128]{3,2,1,0:T(8,128)S(1)} %get-tuple-element.70), channel_id=1, source_target_pairs={{0,16},{16,0},{1,17},{17,1},{2,18},{18,2},{3,19},{19,3},{4,20},{20... | collective-permute-start | bytes 1179656 | tf_op jit(solution)/shard_map/ppermute | solution.py:687
  54.3 28.6 %copy-start.2 = (f32[2,8,16,128]{3,2,1,0:T(8,128)S(1)}, f32[2,8,16,128]{3,2,1,0:T(8,128)}, u32[]{:S(2)}) copy-start(f32[2,8,16,128]{3,2,1,0:T(8,128)} %get-tuple-element.87.refs_6_) | copy-start | bytes 393220
  54.3 10.7 %collective-permute-start.16 = (f32[2,24,16,128]{3,2,1,0:T(8,128)S(1)}, f32[2,24,16,128]{3,2,1,0:T(8,128)S(1)}, u32[]{:S(2)}, u32[]{:S(2)}) collective-permute-start(f32[2,24,16,128]{3,2,1,0:T(8,128)S(1)} %get-tuple-element.81.refs_0_), channel_id=1, source_target_pairs={{0,2},{2,0},{4,6},{6,4},{8,10},{10,8},{12,14},{14,12},{1,3},{3,1},... | collective-permute-start | bytes 1179656 | tf_op jit(solution)/shard_map/ppermute | solution.py:687
  55.7 9.3 %collective-permute-start.15 = (f32[2,8,16,128]{3,2,1,0:T(8,128)S(1)}, f32[2,8,16,128]{3,2,1,0:T(8,128)S(1)}, u32[]{:S(2)}, u32[]{:S(2)}) collective-permute-start(f32[2,8,16,128]{3,2,1,0:T(8,128)S(1)} %get-tuple-element.80), channel_id=1, source_target_pairs={{0,16},{16,0},{1,17},{17,1},{2,18},{18,2},{3,19},{19,3},{4,20},{20... | collective-permute-start | bytes 393224 | tf_op jit(solution)/shard_map/ppermute | solution.py:687
  56.6 16.9 %collective-permute-start.20 = (f32[2,24,16,128]{3,2,1,0:T(8,128)S(1)}, f32[2,24,16,128]{3,2,1,0:T(8,128)S(1)}, u32[]{:S(2)}, u32[]{:S(2)}) collective-permute-start(f32[2,24,16,128]{3,2,1,0:T(8,128)S(1)} %collective-permute-done.10.refs_3_), channel_id=1, source_target_pairs={{0,2},{2,0},{4,6},{6,4},{8,10},{10,8},{12,14},{14,12},{1,3},{3,1},... | collective-permute-start | bytes 1179656 | tf_op jit(solution)/shard_map/ppermute | solution.py:687
  58.8 24.0 %collective-permute-start.18 = (f32[2,24,16,128]{3,2,1,0:T(8,128)S(1)}, f32[2,24,16,128]{3,2,1,0:T(8,128)S(1)}, u32[]{:S(2)}, u32[]{:S(2)}) collective-permute-start(f32[2,24,16,128]{3,2,1,0:T(8,128)S(1)} %collective-permute-done.14.refs_4_), channel_id=1, source_target_pairs={{0,4},{4,8},{8,12},{6,2},{10,6},{14,10},{1,5},{5,9},{9,13},{7,3},{... | collective-permute-start | bytes 1179656 | tf_op jit(solution)/shard_map/ppermute | solution.py:687
  65.0 17.9 %collective-permute-start.19 = (f32[2,24,16,128]{3,2,1,0:T(8,128)S(1)}, f32[2,24,16,128]{3,2,1,0:T(8,128)S(1)}, u32[]{:S(2)}, u32[]{:S(2)}) collective-permute-start(f32[2,24,16,128]{3,2,1,0:T(8,128)S(1)} %collective-permute-done.16.refs_1_), channel_id=1, source_target_pairs={{0,4},{4,8},{8,12},{6,2},{10,6},{14,10},{1,5},{5,9},{9,13},{7,3},{... | collective-permute-start | bytes 1179656 | tf_op jit(solution)/shard_map/ppermute | solution.py:687
  73.4 20.4 %collective-permute-start.21 = (f32[2,24,16,128]{3,2,1,0:T(8,128)S(1)}, f32[2,24,16,128]{3,2,1,0:T(8,128)S(1)}, u32[]{:S(2)}, u32[]{:S(2)}) collective-permute-start(f32[2,24,16,128]{3,2,1,0:T(8,128)S(1)} %collective-permute-done.20.refs_4_), channel_id=1, source_target_pairs={{0,4},{4,8},{8,12},{6,2},{10,6},{14,10},{1,5},{5,9},{9,13},{7,3},{... | collective-permute-start | bytes 1179656 | tf_op jit(solution)/shard_map/ppermute | solution.py:687
  76.7 17.2 %collective-permute-start.22 = (f32[2,2,8,16,128]{4,3,2,1,0:T(8,128)S(1)}, f32[2,2,8,16,128]{4,3,2,1,0:T(8,128)S(1)}, u32[]{:S(2)}, u32[]{:S(2)}) collective-permute-start(f32[2,2,8,16,128]{4,3,2,1,0:T(8,128)S(1)} %get-tuple-element.95), channel_id=1, source_target_pairs={{0,2},{2,4},{4,6},{6,8},{8,10},{10,12},{12,14},{1,3},{3,5},{5,7},{... | collective-permute-start | bytes 786440 | tf_op jit(solution)/shard_map/ppermute | solution.py:687
  78.9 14.4 %collective-permute-start.17 = (f32[2,2,8,16,128]{4,3,2,1,0:T(8,128)S(1)}, f32[2,2,8,16,128]{4,3,2,1,0:T(8,128)S(1)}, u32[]{:S(2)}, u32[]{:S(2)}) collective-permute-start(f32[2,2,8,16,128]{4,3,2,1,0:T(8,128)S(1)} %get-tuple-element.96.refs_6_), channel_id=1, source_target_pairs={{2,0},{4,2},{6,4},{8,6},{10,8},{12,10},{14,12},{3,1},{5,3},{7,5},{... | collective-permute-start | bytes 786440 | tf_op jit(solution)/shard_map/ppermute | solution.py:687
  (3 other events, 41.5 us)

commit v12 on v10

--- a/solution.py
+++ b/solution.py
@@ -724,12 +724,13 @@
     other_ends, near_keep = barrier((other_ends, near_keep))
     own = jnp.stack([keep_ends, other_ends])
     far_keep = exchange(near_keep, "gx", onward)
-    left = exchange(own, "gx", up_pairs)
     right = exchange(own, "gx", down_pairs)
+    late, near_other = barrier((own, near_other))
+    left = exchange(late, "gx", up_pairs)
     far_other = exchange(near_other, "gx", onward)
     blocks[5], far_keep = lax.optimization_barrier((blocks[5], far_keep))
     first = first_image(blocks)
-    token = in_order(left, right, first)
+    token = in_order(right, first)
     blocks = [keep, near_keep, far_keep, other, near_other, far_other, own, left, right]
     return jnp.transpose(image(token, first, blocks), (3, 0, 1, 2))
 

time: 100 us -> 104 us (1.040)
  waiting for transfers between devices: 21.1 us -> 23.3 us
  starting transfers between devices: 47.5 us -> 49.6 us
    ppermute x23, waiting for transfers between devices: 21.1 us -> 23.3 us  [exchange(): return lax.ppermute(array, axis, pairs)]
    ppermute x23, starting transfers between devices: 47.5 us -> 49.6 us  [exchange(): return lax.ppermute(array, axis, pairs)]
  transfers between devices with their start and end apart: 23 -> 23, of which waited for: 7 -> 7; matrix products, arithmetic and copies ran while one was open for 0% -> 0% of each run, Pallas kernels for 19% -> 18%
where the time goes in v12:
time: 104 us; the launch traced here: 103 us
  starting transfers between devices  49.6 us (48%)
  Pallas kernels  30.2 us (29%)
  waiting for transfers between devices  23.3 us (22%)
    ppermute x23, starting transfers between devices, exchange(): return lax.ppermute(array, axis, pairs)  49.6 us
    ppermute x23, waiting for transfers between devices, exchange(): return lax.ppermute(array, axis, pairs)  23.3 us
    pallas_call x1, Pallas kernels, steps(): pl.pallas_call(steps_kernel, out_shape=(jax.ShapeDtypeStruct((2, rows, li...  13 us
    pallas_call x1, Pallas kernels, image(): pl.pallas_call(image_kernel, grid=(samples,), out_shape=jax.ShapeDtypeStr...  7.71 us
    pallas_call x1, Pallas kernels, pack(): pl.pallas_call(pack_kernel, out_shape=(apart, apart, jax.ShapeDtypeStruct...  3.78 us
    pallas_call x1, Pallas kernels, first_image(): pl.pallas_call(first_image_kernel, grid=(samples,), out_shape=jax.ShapeDt...  2.53 us
  transfers between devices with their start and end apart: 23, of which 7 were waited for; matrix products, arithmetic and copies ran while one was open for 0% of the time, Pallas kernels for 18%

profile of v12, /device:TPU:0, one launch (start us, length us, event | category | flops | bytes accessed | tf_op | source)
XLA Modules:
  0.0 103.4 jit_solution(9029816573166929708)
XLA Ops:
  0.0 3.8 %pack.1 = (f32[2,4,96,128]{3,2,1,0:T(8,128)}, f32[2,4,96,128]{3,2,1,0:T(8,128)}, f32[2,8,32,128]{3,2,1,0:T(8,128)}, f32[2,24,16,128]{3,2,1,0:T(8,128)}, f32[2,8,...) custom-call(f32[1,32,128,128]{3,2,1,0:T(8,128)} %source.3, ...), custom_call_target="tpu_custom_call" | custom-call | flops 10000000000 | bytes 7340032 | tf_op jit(solution)/shard_map/pack/pallas_call | solution.py:113
  4.3 2.6 %collective-permute-start = (f32[32,8,128]{2,1,0:T(8,128)}, f32[32,8,128]{2,1,0:T(8,128)S(1)}, u32[]{:S(2)}, u32[]{:S(2)}) collective-permute-start(f32[32,8,128]{2,1,0:T(8,128)} %get-tuple-element.50), channel_id=1, source_target_pairs={{0,1},{1,0},{2,3},{3,2},{4,5},{5,4},{6,7},{7,6},{8,9},{9,8},{10,11... | collective-permute-start | bytes 393224 | tf_op jit(solution)/shard_map/ppermute | solution.py:685
  6.9 1.5 %collective-permute-start.4 = (f32[2,8,32,128]{3,2,1,0:T(8,128)}, f32[2,8,32,128]{3,2,1,0:T(8,128)S(1)}, u32[]{:S(2)}, u32[]{:S(2)}) collective-permute-start(f32[2,8,32,128]{3,2,1,0:T(8,128)} %get-tuple-element.57), channel_id=1, source_target_pairs={{0,2},{2,0},{4,6},{6,4},{8,10},{10,8},{12,14},{14,12},{1,3},{3,1},... | collective-permute-start | bytes 786440 | tf_op jit(solution)/shard_map/ppermute | solution.py:685
  8.4 2.4 %collective-permute-start.2 = (f32[2,4,96,128]{3,2,1,0:T(8,128)}, f32[2,4,96,128]{3,2,1,0:T(8,128)S(1)}, u32[]{:S(2)}, u32[]{:S(2)}) collective-permute-start(f32[2,4,96,128]{3,2,1,0:T(8,128)} %get-tuple-element.55), channel_id=1, source_target_pairs={{0,2},{2,4},{4,6},{6,8},{8,10},{10,12},{12,14},{1,3},{3,5},{5,7},{... | collective-permute-start | bytes 1179656 | tf_op jit(solution)/shard_map/ppermute | solution.py:685
  10.8 1.3 %collective-permute-start.3 = (f32[2,4,96,128]{3,2,1,0:T(8,128)}, f32[2,4,96,128]{3,2,1,0:T(8,128)S(1)}, u32[]{:S(2)}, u32[]{:S(2)}) collective-permute-start(f32[2,4,96,128]{3,2,1,0:T(8,128)} %get-tuple-element.56), channel_id=1, source_target_pairs={{2,0},{4,2},{6,4},{8,6},{10,8},{12,10},{14,12},{3,1},{5,3},{7,5},{... | collective-permute-start | bytes 1179656 | tf_op jit(solution)/shard_map/ppermute | solution.py:685
  12.2 13.0 %steps.1 = (f32[2,32,32,128]{3,2,1,0:T(8,128)S(1)}, f32[32,32,128]{2,1,0:T(8,128)S(1)}, f32[2,4,128,128]{3,2,1,0:T(8,128)S(1)}, f32[2,2,4,32,128]{4,3,2,1,0:T(8,128)S(1)}, f32[2,32,128]{2,1,0:T(8,128)S(1)}) custom-call(f32[1,32,128,128]{3,2,1,0:T(8,128)} %source.3, f32[1,32,128,128]{3,2,1,0:T(8,128)} %receiver.3, f32[1,32,128,128]{3,2,1,0:T(8,128)} %source_before.1, ...), custom_call_target="tpu_custom_call" | custom-call | flops 20000000000 | bytes 1048576 | tf_op jit(solution)/shard_map/steps/pallas_call | solution.py:330
  25.2 6.6 %collective-permute-start.5 = (f32[2,8,32,128]{3,2,1,0:T(8,128)S(1)}, f32[2,8,32,128]{3,2,1,0:T(8,128)S(1)}, u32[]{:S(2)}, u32[]{:S(2)}) collective-permute-start(f32[2,8,32,128]{3,2,1,0:T(8,128)S(1)} %collective-permute-done.4.near), channel_id=1, source_target_pairs={{0,4},{4,8},{8,12},{6,2},{10,6},{14,10},{1,5},{5,9},{9,13},{7,3},{... | collective-permute-start | bytes 786440 | tf_op jit(solution)/shard_map/ppermute | solution.py:685
  32.0 4.9 %collective-permute-done.5.far = f32[2,8,32,128]{3,2,1,0:T(8,128)S(1)} collective-permute-done((f32[2,8,32,128]{3,2,1,0:T(8,128)S(1)}, f32[2,8,32,128]{3,2,1,0:T(8,128)S(1)}, u32[]{:S(2)}, u32[]{:S(2)}) %collective-permute-start.5) | collective-permute-done | bytes 262176 | tf_op jit(solution)/shard_map/ppermute | solution.py:685
  39.0 1.3 %collective-permute-start.14 = (f32[2,24,16,128]{3,2,1,0:T(8,128)S(1)}, f32[2,24,16,128]{3,2,1,0:T(8,128)S(1)}, u32[]{:S(2)}, u32[]{:S(2)}) collective-permute-start(f32[2,24,16,128]{3,2,1,0:T(8,128)S(1)} %collective-permute-done.1.refs_3_), channel_id=1, source_target_pairs={{0,2},{2,0},{4,6},{6,4},{8,10},{10,8},{12,14},{14,12},{1,3},{3,1},... | collective-permute-start | bytes 1179656 | tf_op jit(solution)/shard_map/ppermute | solution.py:685
  40.3 2.1 %collective-permute-done.6.side = f32[2,32,128]{2,1,0:T(8,128)S(1)} collective-permute-done((f32[2,32,128]{2,1,0:T(8,128)S(1)}, f32[2,32,128]{2,1,0:T(8,128)S(1)}, u32[]{:S(2)}, u32[]{:S(2)}) %collective-permute-start.6) | collective-permute-done | bytes 32800 | tf_op jit(solution)/shard_map/ppermute | solution.py:685
  42.6 4.2 %collective-permute-start.13 = (f32[2,24,16,128]{3,2,1,0:T(8,128)S(1)}, f32[2,24,16,128]{3,2,1,0:T(8,128)S(1)}, u32[]{:S(2)}, u32[]{:S(2)}) collective-permute-start(f32[2,24,16,128]{3,2,1,0:T(8,128)S(1)} %collective-permute-done.7.refs_1_), channel_id=1, source_target_pairs={{0,4},{4,8},{8,12},{6,2},{10,6},{14,10},{1,5},{5,9},{9,13},{7,3},{... | collective-permute-start | bytes 1179656 | tf_op jit(solution)/shard_map/ppermute | solution.py:685
  46.8 1.3 %collective-permute-start.11 = (f32[2,4,32,128]{3,2,1,0:T(8,128)S(1)}, f32[2,4,32,128]{3,2,1,0:T(8,128)S(1)}, u32[]{:S(2)}, u32[]{:S(2)}) collective-permute-start(f32[2,4,32,128]{3,2,1,0:T(8,128)S(1)} %get-tuple-element.71), channel_id=1, source_target_pairs={{0,2},{2,4},{4,6},{6,8},{8,10},{10,12},{12,14},{1,3},{3,5},{5,7},{... | collective-permute-start | bytes 393224 | tf_op jit(solution)/shard_map/ppermute | solution.py:685
  49.4 1.5 %finish_middle.1 = (f32[2,24,16,128]{3,2,1,0:T(8,128)S(1)}, f32[2,24,16,128]{3,2,1,0:T(8,128)S(1)}) custom-call(f32[2,32,32,128]{3,2,1,0:T(8,128)S(1)} %get-tuple-element.54.partial, f32[2,2,8,32,128]{4,3,2,1,0:T(8,128)S(1)} %get-tuple-element.64.ends, f32[32,32,128]{2,1,0:T(8,128)S(1)} %get-tuple-element.60.kept_courant, ...), custom_call_target="tpu_custom_call" | custom-call | flops 1 | bytes 1 | tf_op jit(solution)/shard_map/finish_middle/pallas_call | solution.py:473
  51.0 4.3 %collective-permute-start.16 = (f32[2,24,16,128]{3,2,1,0:T(8,128)S(1)}, f32[2,24,16,128]{3,2,1,0:T(8,128)S(1)}, u32[]{:S(2)}, u32[]{:S(2)}) collective-permute-start(f32[2,24,16,128]{3,2,1,0:T(8,128)S(1)} %get-tuple-element.81.refs_0_), channel_id=1, source_target_pairs={{0,2},{2,0},{4,6},{6,4},{8,10},{10,8},{12,14},{14,12},{1,3},{3,1},... | collective-permute-start | bytes 1179656 | tf_op jit(solution)/shard_map/ppermute | solution.py:685
  56.8 3.1 %collective-permute-start.20 = (f32[2,24,16,128]{3,2,1,0:T(8,128)S(1)}, f32[2,24,16,128]{3,2,1,0:T(8,128)S(1)}, u32[]{:S(2)}, u32[]{:S(2)}) collective-permute-start(f32[2,24,16,128]{3,2,1,0:T(8,128)S(1)} %collective-permute-done.10.refs_3_), channel_id=1, source_target_pairs={{0,2},{2,0},{4,6},{6,4},{8,10},{10,8},{12,14},{14,12},{1,3},{3,1},... | collective-permute-start | bytes 1179656 | tf_op jit(solution)/shard_map/ppermute | solution.py:685
  59.9 3.5 %collective-permute-start.18 = (f32[2,24,16,128]{3,2,1,0:T(8,128)S(1)}, f32[2,24,16,128]{3,2,1,0:T(8,128)S(1)}, u32[]{:S(2)}, u32[]{:S(2)}) collective-permute-start(f32[2,24,16,128]{3,2,1,0:T(8,128)S(1)} %collective-permute-done.14.refs_4_), channel_id=1, source_target_pairs={{0,4},{4,8},{8,12},{6,2},{10,6},{14,10},{1,5},{5,9},{9,13},{7,3},{... | collective-permute-start | bytes 1179656 | tf_op jit(solution)/shard_map/ppermute | solution.py:685
  63.4 2.1 %collective-permute-done.16.refs_1_ = f32[2,24,16,128]{3,2,1,0:T(8,128)S(1)} collective-permute-done((f32[2,24,16,128]{3,2,1,0:T(8,128)S(1)}, f32[2,24,16,128]{3,2,1,0:T(8,128)S(1)}, u32[]{:S(2)}, u32[]{:S(2)}) %collective-permute-start.16) | collective-permute-done | bytes 393248 | tf_op jit(solution)/shard_map/ppermute | solution.py:685
  65.5 5.1 %collective-permute-start.19 = (f32[2,24,16,128]{3,2,1,0:T(8,128)S(1)}, f32[2,24,16,128]{3,2,1,0:T(8,128)S(1)}, u32[]{:S(2)}, u32[]{:S(2)}) collective-permute-start(f32[2,24,16,128]{3,2,1,0:T(8,128)S(1)} %collective-permute-done.16.refs_1_), channel_id=1, source_target_pairs={{0,4},{4,8},{8,12},{6,2},{10,6},{14,10},{1,5},{5,9},{9,13},{7,3},{... | collective-permute-start | bytes 1179656 | tf_op jit(solution)/shard_map/ppermute | solution.py:685
  71.9 7.6 %collective-permute-done.20.refs_4_ = f32[2,24,16,128]{3,2,1,0:T(8,128)S(1)} collective-permute-done((f32[2,24,16,128]{3,2,1,0:T(8,128)S(1)}, f32[2,24,16,128]{3,2,1,0:T(8,128)S(1)}, u32[]{:S(2)}, u32[]{:S(2)}) %collective-permute-start.20) | collective-permute-done | bytes 393248 | tf_op jit(solution)/shard_map/ppermute | solution.py:685
  79.5 4.4 %collective-permute-start.22 = (f32[2,2,8,16,128]{4,3,2,1,0:T(8,128)S(1)}, f32[2,2,8,16,128]{4,3,2,1,0:T(8,128)S(1)}, u32[]{:S(2)}, u32[]{:S(2)}) collective-permute-start(f32[2,2,8,16,128]{4,3,2,1,0:T(8,128)S(1)} %pad_maximum_fusion.refs_6_), channel_id=1, source_target_pairs={{0,2},{2,4},{4,6},{6,8},{8,10},{10,12},{12,14},{1,3},{3,5},{5,7},{... | collective-permute-start | bytes 786440 | tf_op jit(solution)/shard_map/ppermute | solution.py:685
  83.9 3.5 %collective-permute-start.21 = (f32[2,24,16,128]{3,2,1,0:T(8,128)S(1)}, f32[2,24,16,128]{3,2,1,0:T(8,128)S(1)}, u32[]{:S(2)}, u32[]{:S(2)}) collective-permute-start(f32[2,24,16,128]{3,2,1,0:T(8,128)S(1)} %collective-permute-done.20.refs_4_), channel_id=1, source_target_pairs={{0,4},{4,8},{8,12},{6,2},{10,6},{14,10},{1,5},{5,9},{9,13},{7,3},{... | collective-permute-start | bytes 1179656 | tf_op jit(solution)/shard_map/ppermute | solution.py:685
  87.4 2.5 %first_image.1.refs_1_.first = f32[8,65,16,128]{3,2,1,0:T(8,128)S(1)} custom-call(f32[2,24,16,128]{3,2,1,0:T(8,128)S(1)} %copy-done, f32[2,24,16,128]{3,2,1,0:T(8,128)S(1)} %collective-permute-done.7.refs_1_, f32[2,24,16,128]{3,2,1,0:T(8,128)S(1)} %collective-permute-done.13.refs_2_, f32[2,24,16,128]{3,2,1,0:T(8,128)S(1)} %collective-permute-done.1.refs_3_, ...), custom_call_target="tpu_custom_call" | custom-call | flops 10000000000 | bytes 8388608 | tf_op jit(solution)/shard_map/first_image/pallas_call | solution.py:573
  90.5 5.2 %collective-permute-done.21.refs_5_ = f32[2,24,16,128]{3,2,1,0:T(8,128)S(1)} collective-permute-done((f32[2,24,16,128]{3,2,1,0:T(8,128)S(1)}, f32[2,24,16,128]{3,2,1,0:T(8,128)S(1)}, u32[]{:S(2)}, u32[]{:S(2)}) %collective-permute-start.21) | collective-permute-done | bytes 393248 | tf_op jit(solution)/shard_map/ppermute | solution.py:685
  95.7 7.7 %image.1 = f32[8,32,64,65]{3,2,1,0:T(8,128)} custom-call(s32[1]{0:T(128)} %in_order.1.token, f32[8,65,16,128]{3,2,1,0:T(8,128)S(1)} %first_image.1.refs_1_.first, f32[2,24,16,128]{3,2,1,0:T(8,128)S(1)} %get-tuple-element.81.refs_0_, f32[2,24,16,128]{3,2,1,0:T(8,128)S(1)} %collective-permute-done.16.refs_1_, ...), custom_call_target="tpu_custom_call" | custom-call | flops 10000000000 | bytes 16777216 | tf_op jit(solution)/shard_map/image/pallas_call | solution.py:641
  (39 shorter events, 7.6 us)
Async XLA Ops:
  3.8 8.3 %collective-permute-start.1 = (f32[2,24,16,128]{3,2,1,0:T(8,128)}, f32[2,24,16,128]{3,2,1,0:T(8,128)S(1)}, u32[]{:S(2)}, u32[]{:S(2)}) collective-permute-start(f32[2,24,16,128]{3,2,1,0:T(8,128)} %get-tuple-element.52), channel_id=1, source_target_pairs={{0,16},{16,0},{1,17},{17,1},{2,18},{18,2},{3,19},{19,3},{4,20},{20... | collective-permute-start | bytes 1179656 | tf_op jit(solution)/shard_map/ppermute | solution.py:685
  4.3 7.8 %collective-permute-start = (f32[32,8,128]{2,1,0:T(8,128)}, f32[32,8,128]{2,1,0:T(8,128)S(1)}, u32[]{:S(2)}, u32[]{:S(2)}) collective-permute-start(f32[32,8,128]{2,1,0:T(8,128)} %get-tuple-element.50), channel_id=1, source_target_pairs={{0,1},{1,0},{2,3},{3,2},{4,5},{5,4},{6,7},{7,6},{8,9},{9,8},{10,11... | collective-permute-start | bytes 393224 | tf_op jit(solution)/shard_map/ppermute | solution.py:685
  6.9 18.3 %collective-permute-start.4 = (f32[2,8,32,128]{3,2,1,0:T(8,128)}, f32[2,8,32,128]{3,2,1,0:T(8,128)S(1)}, u32[]{:S(2)}, u32[]{:S(2)}) collective-permute-start(f32[2,8,32,128]{3,2,1,0:T(8,128)} %get-tuple-element.57), channel_id=1, source_target_pairs={{0,2},{2,0},{4,6},{6,4},{8,10},{10,8},{12,14},{14,12},{1,3},{3,1},... | collective-permute-start | bytes 786440 | tf_op jit(solution)/shard_map/ppermute | solution.py:685
  8.4 23.6 %collective-permute-start.2 = (f32[2,4,96,128]{3,2,1,0:T(8,128)}, f32[2,4,96,128]{3,2,1,0:T(8,128)S(1)}, u32[]{:S(2)}, u32[]{:S(2)}) collective-permute-start(f32[2,4,96,128]{3,2,1,0:T(8,128)} %get-tuple-element.55), channel_id=1, source_target_pairs={{0,2},{2,4},{4,6},{6,8},{8,10},{10,12},{12,14},{1,3},{3,5},{5,7},{... | collective-permute-start | bytes 1179656 | tf_op jit(solution)/shard_map/ppermute | solution.py:685
  10.8 21.1 %collective-permute-start.3 = (f32[2,4,96,128]{3,2,1,0:T(8,128)}, f32[2,4,96,128]{3,2,1,0:T(8,128)S(1)}, u32[]{:S(2)}, u32[]{:S(2)}) collective-permute-start(f32[2,4,96,128]{3,2,1,0:T(8,128)} %get-tuple-element.56), channel_id=1, source_target_pairs={{2,0},{4,2},{6,4},{8,6},{10,8},{12,10},{14,12},{3,1},{5,3},{7,5},{... | collective-permute-start | bytes 1179656 | tf_op jit(solution)/shard_map/ppermute | solution.py:685
  25.2 11.7 %collective-permute-start.5 = (f32[2,8,32,128]{3,2,1,0:T(8,128)S(1)}, f32[2,8,32,128]{3,2,1,0:T(8,128)S(1)}, u32[]{:S(2)}, u32[]{:S(2)}) collective-permute-start(f32[2,8,32,128]{3,2,1,0:T(8,128)S(1)} %collective-permute-done.4.near), channel_id=1, source_target_pairs={{0,4},{4,8},{8,12},{6,2},{10,6},{14,10},{1,5},{5,9},{9,13},{7,3},{... | collective-permute-start | bytes 786440 | tf_op jit(solution)/shard_map/ppermute | solution.py:685
  31.9 10.7 %collective-permute-start.7 = (f32[2,24,16,128]{3,2,1,0:T(8,128)S(1)}, f32[2,24,16,128]{3,2,1,0:T(8,128)S(1)}, u32[]{:S(2)}, u32[]{:S(2)}) collective-permute-start(f32[2,24,16,128]{3,2,1,0:T(8,128)S(1)} %copy-done), channel_id=1, source_target_pairs={{0,2},{2,0},{4,6},{6,4},{8,10},{10,8},{12,14},{14,12},{1,3},{3,1},... | collective-permute-start | bytes 1179656 | tf_op jit(solution)/shard_map/ppermute | solution.py:685
  37.9 4.7 %collective-permute-start.9 = (f32[2,2,8,16,128]{4,3,2,1,0:T(8,128)S(1)}, f32[2,2,8,16,128]{4,3,2,1,0:T(8,128)S(1)}, u32[]{:S(2)}, u32[]{:S(2)}) collective-permute-start(f32[2,2,8,16,128]{4,3,2,1,0:T(8,128)S(1)} %get-tuple-element.68), channel_id=1, source_target_pairs={{0,16},{16,0},{1,17},{17,1},{2,18},{18,2},{3,19},{19,3},{4,20},{20... | collective-permute-start | bytes 786440 | tf_op jit(solution)/shard_map/ppermute | solution.py:685
  38.0 2.3 %collective-permute-start.8 = (f32[2,8,16,128]{3,2,1,0:T(8,128)S(1)}, f32[2,8,16,128]{3,2,1,0:T(8,128)S(1)}, u32[]{:S(2)}, u32[]{:S(2)}) collective-permute-start(f32[2,8,16,128]{3,2,1,0:T(8,128)S(1)} %copy-done.3), channel_id=1, source_target_pairs={{0,16},{16,0},{1,17},{17,1},{2,18},{18,2},{3,19},{19,3},{4,20},{20... | collective-permute-start | bytes 393224 | tf_op jit(solution)/shard_map/ppermute | solution.py:685
  38.5 3.9 %collective-permute-start.6 = (f32[2,32,128]{2,1,0:T(8,128)S(1)}, f32[2,32,128]{2,1,0:T(8,128)S(1)}, u32[]{:S(2)}, u32[]{:S(2)}) collective-permute-start(f32[2,32,128]{2,1,0:T(8,128)S(1)} %get-tuple-element.65), channel_id=1, source_target_pairs={{0,1},{1,0},{2,3},{3,2},{4,5},{5,4},{6,7},{7,6},{8,9},{9,8},{10,11... | collective-permute-start | bytes 98312 | tf_op jit(solution)/shard_map/ppermute | solution.py:685
  39.0 11.9 %collective-permute-start.14 = (f32[2,24,16,128]{3,2,1,0:T(8,128)S(1)}, f32[2,24,16,128]{3,2,1,0:T(8,128)S(1)}, u32[]{:S(2)}, u32[]{:S(2)}) collective-permute-start(f32[2,24,16,128]{3,2,1,0:T(8,128)S(1)} %collective-permute-done.1.refs_3_), channel_id=1, source_target_pairs={{0,2},{2,0},{4,6},{6,4},{8,10},{10,8},{12,14},{14,12},{1,3},{3,1},... | collective-permute-start | bytes 1179656 | tf_op jit(solution)/shard_map/ppermute | solution.py:685
  42.6 14.0 %collective-permute-start.13 = (f32[2,24,16,128]{3,2,1,0:T(8,128)S(1)}, f32[2,24,16,128]{3,2,1,0:T(8,128)S(1)}, u32[]{:S(2)}, u32[]{:S(2)}) collective-permute-start(f32[2,24,16,128]{3,2,1,0:T(8,128)S(1)} %collective-permute-done.7.refs_1_), channel_id=1, source_target_pairs={{0,4},{4,8},{8,12},{6,2},{10,6},{14,10},{1,5},{5,9},{9,13},{7,3},{... | collective-permute-start | bytes 1179656 | tf_op jit(solution)/shard_map/ppermute | solution.py:685
  46.8 8.5 %collective-permute-start.11 = (f32[2,4,32,128]{3,2,1,0:T(8,128)S(1)}, f32[2,4,32,128]{3,2,1,0:T(8,128)S(1)}, u32[]{:S(2)}, u32[]{:S(2)}) collective-permute-start(f32[2,4,32,128]{3,2,1,0:T(8,128)S(1)} %get-tuple-element.71), channel_id=1, source_target_pairs={{0,2},{2,4},{4,6},{6,8},{8,10},{10,12},{12,14},{1,3},{3,5},{5,7},{... | collective-permute-start | bytes 393224 | tf_op jit(solution)/shard_map/ppermute | solution.py:685
  48.1 8.5 %collective-permute-start.12 = (f32[2,4,32,128]{3,2,1,0:T(8,128)S(1)}, f32[2,4,32,128]{3,2,1,0:T(8,128)S(1)}, u32[]{:S(2)}, u32[]{:S(2)}) collective-permute-start(f32[2,4,32,128]{3,2,1,0:T(8,128)S(1)} %get-tuple-element.72), channel_id=1, source_target_pairs={{2,0},{4,2},{6,4},{8,6},{10,8},{12,10},{14,12},{3,1},{5,3},{7,5},{... | collective-permute-start | bytes 393224 | tf_op jit(solution)/shard_map/ppermute | solution.py:685
  50.9 5.9 %collective-permute-start.10 = (f32[2,24,16,128]{3,2,1,0:T(8,128)S(1)}, f32[2,24,16,128]{3,2,1,0:T(8,128)S(1)}, u32[]{:S(2)}, u32[]{:S(2)}) collective-permute-start(f32[2,24,16,128]{3,2,1,0:T(8,128)S(1)} %get-tuple-element.70), channel_id=1, source_target_pairs={{0,16},{16,0},{1,17},{17,1},{2,18},{18,2},{3,19},{19,3},{4,20},{20... | collective-permute-start | bytes 1179656 | tf_op jit(solution)/shard_map/ppermute | solution.py:685
  51.0 36.5 %copy-start.2 = (f32[2,8,16,128]{3,2,1,0:T(8,128)S(1)}, f32[2,8,16,128]{3,2,1,0:T(8,128)}, u32[]{:S(2)}) copy-start(f32[2,8,16,128]{3,2,1,0:T(8,128)} %get-tuple-element.87.refs_6_) | copy-start | bytes 393220
  51.0 14.5 %collective-permute-start.16 = (f32[2,24,16,128]{3,2,1,0:T(8,128)S(1)}, f32[2,24,16,128]{3,2,1,0:T(8,128)S(1)}, u32[]{:S(2)}, u32[]{:S(2)}) collective-permute-start(f32[2,24,16,128]{3,2,1,0:T(8,128)S(1)} %get-tuple-element.81.refs_0_), channel_id=1, source_target_pairs={{0,2},{2,0},{4,6},{6,4},{8,10},{10,8},{12,14},{14,12},{1,3},{3,1},... | collective-permute-start | bytes 1179656 | tf_op jit(solution)/shard_map/ppermute | solution.py:685
  56.8 8.7 %collective-permute-start.15 = (f32[2,8,16,128]{3,2,1,0:T(8,128)S(1)}, f32[2,8,16,128]{3,2,1,0:T(8,128)S(1)}, u32[]{:S(2)}, u32[]{:S(2)}) collective-permute-start(f32[2,8,16,128]{3,2,1,0:T(8,128)S(1)} %get-tuple-element.80), channel_id=1, source_target_pairs={{0,16},{16,0},{1,17},{17,1},{2,18},{18,2},{3,19},{19,3},{4,20},{20... | collective-permute-start | bytes 393224 | tf_op jit(solution)/shard_map/ppermute | solution.py:685
  56.8 22.7 %collective-permute-start.20 = (f32[2,24,16,128]{3,2,1,0:T(8,128)S(1)}, f32[2,24,16,128]{3,2,1,0:T(8,128)S(1)}, u32[]{:S(2)}, u32[]{:S(2)}) collective-permute-start(f32[2,24,16,128]{3,2,1,0:T(8,128)S(1)} %collective-permute-done.10.refs_3_), channel_id=1, source_target_pairs={{0,2},{2,0},{4,6},{6,4},{8,10},{10,8},{12,14},{14,12},{1,3},{3,1},... | collective-permute-start | bytes 1179656 | tf_op jit(solution)/shard_map/ppermute | solution.py:685
  59.9 27.5 %collective-permute-start.18 = (f32[2,24,16,128]{3,2,1,0:T(8,128)S(1)}, f32[2,24,16,128]{3,2,1,0:T(8,128)S(1)}, u32[]{:S(2)}, u32[]{:S(2)}) collective-permute-start(f32[2,24,16,128]{3,2,1,0:T(8,128)S(1)} %collective-permute-done.14.refs_4_), channel_id=1, source_target_pairs={{0,4},{4,8},{8,12},{6,2},{10,6},{14,10},{1,5},{5,9},{9,13},{7,3},{... | collective-permute-start | bytes 1179656 | tf_op jit(solution)/shard_map/ppermute | solution.py:685
  65.5 21.9 %collective-permute-start.19 = (f32[2,24,16,128]{3,2,1,0:T(8,128)S(1)}, f32[2,24,16,128]{3,2,1,0:T(8,128)S(1)}, u32[]{:S(2)}, u32[]{:S(2)}) collective-permute-start(f32[2,24,16,128]{3,2,1,0:T(8,128)S(1)} %collective-permute-done.16.refs_1_), channel_id=1, source_target_pairs={{0,4},{4,8},{8,12},{6,2},{10,6},{14,10},{1,5},{5,9},{9,13},{7,3},{... | collective-permute-start | bytes 1179656 | tf_op jit(solution)/shard_map/ppermute | solution.py:685
  70.6 19.3 %collective-permute-start.17 = (f32[2,2,8,16,128]{4,3,2,1,0:T(8,128)S(1)}, f32[2,2,8,16,128]{4,3,2,1,0:T(8,128)S(1)}, u32[]{:S(2)}, u32[]{:S(2)}) collective-permute-start(f32[2,2,8,16,128]{4,3,2,1,0:T(8,128)S(1)} %pad_maximum_fusion.refs_6_), channel_id=1, source_target_pairs={{2,0},{4,2},{6,4},{8,6},{10,8},{12,10},{14,12},{3,1},{5,3},{7,5},{... | collective-permute-start | bytes 786440 | tf_op jit(solution)/shard_map/ppermute | solution.py:685
  79.5 11.0 %collective-permute-start.22 = (f32[2,2,8,16,128]{4,3,2,1,0:T(8,128)S(1)}, f32[2,2,8,16,128]{4,3,2,1,0:T(8,128)S(1)}, u32[]{:S(2)}, u32[]{:S(2)}) collective-permute-start(f32[2,2,8,16,128]{4,3,2,1,0:T(8,128)S(1)} %pad_maximum_fusion.refs_6_), channel_id=1, source_target_pairs={{0,2},{2,4},{4,6},{6,8},{8,10},{10,12},{12,14},{1,3},{3,5},{5,7},{... | collective-permute-start | bytes 786440 | tf_op jit(solution)/shard_map/ppermute | solution.py:685
  83.9 11.8 %collective-permute-start.21 = (f32[2,24,16,128]{3,2,1,0:T(8,128)S(1)}, f32[2,24,16,128]{3,2,1,0:T(8,128)S(1)}, u32[]{:S(2)}, u32[]{:S(2)}) collective-permute-start(f32[2,24,16,128]{3,2,1,0:T(8,128)S(1)} %collective-permute-done.20.refs_4_), channel_id=1, source_target_pairs={{0,4},{4,8},{8,12},{6,2},{10,6},{14,10},{1,5},{5,9},{9,13},{7,3},{... | collective-permute-start | bytes 1179656 | tf_op jit(solution)/shard_map/ppermute | solution.py:685
  (3 other events, 44.6 us)

commit v13 on v10

--- a/solution.py
+++ b/solution.py
@@ -101,7 +101,8 @@
         if index == pieces - 1:
             end_rows(up, rows - REACH, REACH)
             high -= REACH
-        lax.fori_loop(low, high, middle_row, 0, unroll=4)
+        if low < high:
+            lax.fori_loop(low, high, middle_row, 0, unroll=4)
 
 
 def pack(source, receiver):
@@ -126,7 +127,7 @@
         out_specs=(VMEM,) * 8,
         scratch_shapes=[
             pltpu.VMEM((2, rows, size_y, size_z), F32),
-            pltpu.SemaphoreType.DMA((4, 2)),
+            pltpu.SemaphoreType.DMA((8, 2)),
         ],
         compiler_params=params(56),
         cost_estimate=cost(10**10, 7 * 2**20),

time: 100 us -> 100 us (level)
  no operation moved by 1% of the time
where the time goes in v13:
time: 100 us; the launch traced here: 99 us
  starting transfers between devices  47.5 us (48%)
  Pallas kernels  30 us (30%)
  waiting for transfers between devices  21.1 us (21%)
    ppermute x23, starting transfers between devices, exchange(): return lax.ppermute(array, axis, pairs)  47.5 us
    ppermute x23, waiting for transfers between devices, exchange(): return lax.ppermute(array, axis, pairs)  21.1 us
    pallas_call x1, Pallas kernels, steps(): pl.pallas_call(steps_kernel, out_shape=(jax.ShapeDtypeStruct((2, rows, li...  13 us
    pallas_call x1, Pallas kernels, image(): pl.pallas_call(image_kernel, grid=(samples,), out_shape=jax.ShapeDtypeStr...  7.71 us
    pallas_call x1, Pallas kernels, pack(): pl.pallas_call(pack_kernel, out_shape=(apart, apart, jax.ShapeDtypeStruct...  3.65 us
    pallas_call x1, Pallas kernels, first_image(): pl.pallas_call(first_image_kernel, grid=(samples,), out_shape=jax.ShapeDt...  2.53 us
  transfers between devices with their start and end apart: 23, of which 7 were waited for; matrix products, arithmetic and copies ran while one was open for 0% of the time, Pallas kernels for 19%

profile of v13, /device:TPU:0, one launch (start us, length us, event | category | flops | bytes accessed | tf_op | source)
XLA Modules:
  0.0 99.0 jit_solution(743563595540807479)
XLA Ops:
  0.0 3.6 %pack.1 = (f32[2,4,96,128]{3,2,1,0:T(8,128)}, f32[2,4,96,128]{3,2,1,0:T(8,128)}, f32[2,8,32,128]{3,2,1,0:T(8,128)}, f32[2,24,16,128]{3,2,1,0:T(8,128)}, f32[2,8,...) custom-call(f32[1,32,128,128]{3,2,1,0:T(8,128)} %source.3, ...), custom_call_target="tpu_custom_call" | custom-call | flops 10000000000 | bytes 7340032 | tf_op jit(solution)/shard_map/pack/pallas_call | solution.py:114
  4.2 2.6 %collective-permute-start = (f32[32,8,128]{2,1,0:T(8,128)}, f32[32,8,128]{2,1,0:T(8,128)S(1)}, u32[]{:S(2)}, u32[]{:S(2)}) collective-permute-start(f32[32,8,128]{2,1,0:T(8,128)} %get-tuple-element.48), channel_id=1, source_target_pairs={{0,1},{1,0},{2,3},{3,2},{4,5},{5,4},{6,7},{7,6},{8,9},{9,8},{10,11... | collective-permute-start | bytes 393224 | tf_op jit(solution)/shard_map/ppermute | solution.py:686
  6.7 1.5 %collective-permute-start.4 = (f32[2,8,32,128]{3,2,1,0:T(8,128)}, f32[2,8,32,128]{3,2,1,0:T(8,128)S(1)}, u32[]{:S(2)}, u32[]{:S(2)}) collective-permute-start(f32[2,8,32,128]{3,2,1,0:T(8,128)} %get-tuple-element.55), channel_id=1, source_target_pairs={{0,2},{2,0},{4,6},{6,4},{8,10},{10,8},{12,14},{14,12},{1,3},{3,1},... | collective-permute-start | bytes 786440 | tf_op jit(solution)/shard_map/ppermute | solution.py:686
  8.3 2.4 %collective-permute-start.2 = (f32[2,4,96,128]{3,2,1,0:T(8,128)}, f32[2,4,96,128]{3,2,1,0:T(8,128)S(1)}, u32[]{:S(2)}, u32[]{:S(2)}) collective-permute-start(f32[2,4,96,128]{3,2,1,0:T(8,128)} %get-tuple-element.53), channel_id=1, source_target_pairs={{0,2},{2,4},{4,6},{6,8},{8,10},{10,12},{12,14},{1,3},{3,5},{5,7},{... | collective-permute-start | bytes 1179656 | tf_op jit(solution)/shard_map/ppermute | solution.py:686
  10.7 1.3 %collective-permute-start.3 = (f32[2,4,96,128]{3,2,1,0:T(8,128)}, f32[2,4,96,128]{3,2,1,0:T(8,128)S(1)}, u32[]{:S(2)}, u32[]{:S(2)}) collective-permute-start(f32[2,4,96,128]{3,2,1,0:T(8,128)} %get-tuple-element.54), channel_id=1, source_target_pairs={{2,0},{4,2},{6,4},{8,6},{10,8},{12,10},{14,12},{3,1},{5,3},{7,5},{... | collective-permute-start | bytes 1179656 | tf_op jit(solution)/shard_map/ppermute | solution.py:686
  12.0 13.0 %steps.1 = (f32[2,32,32,128]{3,2,1,0:T(8,128)S(1)}, f32[32,32,128]{2,1,0:T(8,128)S(1)}, f32[2,4,128,128]{3,2,1,0:T(8,128)S(1)}, f32[2,2,4,32,128]{4,3,2,1,0:T(8,128)S(1)}, f32[2,32,128]{2,1,0:T(8,128)S(1)}) custom-call(f32[1,32,128,128]{3,2,1,0:T(8,128)} %source.3, f32[1,32,128,128]{3,2,1,0:T(8,128)} %receiver.3, f32[1,32,128,128]{3,2,1,0:T(8,128)} %source_before.1, ...), custom_call_target="tpu_custom_call" | custom-call | flops 20000000000 | bytes 1048576 | tf_op jit(solution)/shard_map/steps/pallas_call | solution.py:331
  25.1 6.6 %collective-permute-start.5 = (f32[2,8,32,128]{3,2,1,0:T(8,128)S(1)}, f32[2,8,32,128]{3,2,1,0:T(8,128)S(1)}, u32[]{:S(2)}, u32[]{:S(2)}) collective-permute-start(f32[2,8,32,128]{3,2,1,0:T(8,128)S(1)} %collective-permute-done.4.near), channel_id=1, source_target_pairs={{0,4},{4,8},{8,12},{6,2},{10,6},{14,10},{1,5},{5,9},{9,13},{7,3},{... | collective-permute-start | bytes 786440 | tf_op jit(solution)/shard_map/ppermute | solution.py:686
  31.9 4.9 %collective-permute-done.5.far = f32[2,8,32,128]{3,2,1,0:T(8,128)S(1)} collective-permute-done((f32[2,8,32,128]{3,2,1,0:T(8,128)S(1)}, f32[2,8,32,128]{3,2,1,0:T(8,128)S(1)}, u32[]{:S(2)}, u32[]{:S(2)}) %collective-permute-start.5) | collective-permute-done | bytes 262176 | tf_op jit(solution)/shard_map/ppermute | solution.py:686
  38.9 1.3 %collective-permute-start.14 = (f32[2,24,16,128]{3,2,1,0:T(8,128)S(1)}, f32[2,24,16,128]{3,2,1,0:T(8,128)S(1)}, u32[]{:S(2)}, u32[]{:S(2)}) collective-permute-start(f32[2,24,16,128]{3,2,1,0:T(8,128)S(1)} %collective-permute-done.1.refs_3_), channel_id=1, source_target_pairs={{0,2},{2,0},{4,6},{6,4},{8,10},{10,8},{12,14},{14,12},{1,3},{3,1},... | collective-permute-start | bytes 1179656 | tf_op jit(solution)/shard_map/ppermute | solution.py:686
  40.2 2.1 %collective-permute-done.6.side = f32[2,32,128]{2,1,0:T(8,128)S(1)} collective-permute-done((f32[2,32,128]{2,1,0:T(8,128)S(1)}, f32[2,32,128]{2,1,0:T(8,128)S(1)}, u32[]{:S(2)}, u32[]{:S(2)}) %collective-permute-start.6) | collective-permute-done | bytes 32800 | tf_op jit(solution)/shard_map/ppermute | solution.py:686
  42.4 4.2 %collective-permute-start.13 = (f32[2,24,16,128]{3,2,1,0:T(8,128)S(1)}, f32[2,24,16,128]{3,2,1,0:T(8,128)S(1)}, u32[]{:S(2)}, u32[]{:S(2)}) collective-permute-start(f32[2,24,16,128]{3,2,1,0:T(8,128)S(1)} %collective-permute-done.7.refs_1_), channel_id=1, source_target_pairs={{0,4},{4,8},{8,12},{6,2},{10,6},{14,10},{1,5},{5,9},{9,13},{7,3},{... | collective-permute-start | bytes 1179656 | tf_op jit(solution)/shard_map/ppermute | solution.py:686
  46.7 1.3 %collective-permute-start.11 = (f32[2,4,32,128]{3,2,1,0:T(8,128)S(1)}, f32[2,4,32,128]{3,2,1,0:T(8,128)S(1)}, u32[]{:S(2)}, u32[]{:S(2)}) collective-permute-start(f32[2,4,32,128]{3,2,1,0:T(8,128)S(1)} %get-tuple-element.69), channel_id=1, source_target_pairs={{0,2},{2,4},{4,6},{6,8},{8,10},{10,12},{12,14},{1,3},{3,5},{5,7},{... | collective-permute-start | bytes 393224 | tf_op jit(solution)/shard_map/ppermute | solution.py:686
  48.0 1.3 %collective-permute-start.12 = (f32[2,4,32,128]{3,2,1,0:T(8,128)S(1)}, f32[2,4,32,128]{3,2,1,0:T(8,128)S(1)}, u32[]{:S(2)}, u32[]{:S(2)}) collective-permute-start(f32[2,4,32,128]{3,2,1,0:T(8,128)S(1)} %get-tuple-element.70), channel_id=1, source_target_pairs={{2,0},{4,2},{6,4},{8,6},{10,8},{12,10},{14,12},{3,1},{5,3},{7,5},{... | collective-permute-start | bytes 393224 | tf_op jit(solution)/shard_map/ppermute | solution.py:686
  49.3 1.5 %finish_middle.1 = (f32[2,24,16,128]{3,2,1,0:T(8,128)S(1)}, f32[2,24,16,128]{3,2,1,0:T(8,128)S(1)}) custom-call(f32[2,32,32,128]{3,2,1,0:T(8,128)S(1)} %get-tuple-element.52.partial, f32[2,2,8,32,128]{4,3,2,1,0:T(8,128)S(1)} %get-tuple-element.62.ends, f32[32,32,128]{2,1,0:T(8,128)S(1)} %get-tuple-element.58.kept_courant, ...), custom_call_target="tpu_custom_call" | custom-call | flops 1 | bytes 1 | tf_op jit(solution)/shard_map/finish_middle/pallas_call | solution.py:474
  50.8 4.3 %collective-permute-start.16 = (f32[2,24,16,128]{3,2,1,0:T(8,128)S(1)}, f32[2,24,16,128]{3,2,1,0:T(8,128)S(1)}, u32[]{:S(2)}, u32[]{:S(2)}) collective-permute-start(f32[2,24,16,128]{3,2,1,0:T(8,128)S(1)} %get-tuple-element.79.refs_0_), channel_id=1, source_target_pairs={{0,2},{2,0},{4,6},{6,4},{8,10},{10,8},{12,14},{14,12},{1,3},{3,1},... | collective-permute-start | bytes 1179656 | tf_op jit(solution)/shard_map/ppermute | solution.py:686
  56.7 4.0 %collective-permute-start.19 = (f32[2,24,16,128]{3,2,1,0:T(8,128)S(1)}, f32[2,24,16,128]{3,2,1,0:T(8,128)S(1)}, u32[]{:S(2)}, u32[]{:S(2)}) collective-permute-start(f32[2,24,16,128]{3,2,1,0:T(8,128)S(1)} %collective-permute-done.14.refs_4_), channel_id=1, source_target_pairs={{0,4},{4,8},{8,12},{6,2},{10,6},{14,10},{1,5},{5,9},{9,13},{7,3},{... | collective-permute-start | bytes 1179656 | tf_op jit(solution)/shard_map/ppermute | solution.py:686
  61.1 4.3 %collective-permute-done.16.refs_1_ = f32[2,24,16,128]{3,2,1,0:T(8,128)S(1)} collective-permute-done((f32[2,24,16,128]{3,2,1,0:T(8,128)S(1)}, f32[2,24,16,128]{3,2,1,0:T(8,128)S(1)}, u32[]{:S(2)}, u32[]{:S(2)}) %collective-permute-start.16) | collective-permute-done | bytes 393248 | tf_op jit(solution)/shard_map/ppermute | solution.py:686
  65.4 5.1 %collective-permute-start.20 = (f32[2,24,16,128]{3,2,1,0:T(8,128)S(1)}, f32[2,24,16,128]{3,2,1,0:T(8,128)S(1)}, u32[]{:S(2)}, u32[]{:S(2)}) collective-permute-start(f32[2,24,16,128]{3,2,1,0:T(8,128)S(1)} %collective-permute-done.16.refs_1_), channel_id=1, source_target_pairs={{0,4},{4,8},{8,12},{6,2},{10,6},{14,10},{1,5},{5,9},{9,13},{7,3},{... | collective-permute-start | bytes 1179656 | tf_op jit(solution)/shard_map/ppermute | solution.py:686
  71.8 4.6 %collective-permute-start.17 = (f32[2,2,8,16,128]{4,3,2,1,0:T(8,128)S(1)}, f32[2,2,8,16,128]{4,3,2,1,0:T(8,128)S(1)}, u32[]{:S(2)}, u32[]{:S(2)}) collective-permute-start(f32[2,2,8,16,128]{4,3,2,1,0:T(8,128)S(1)} %pad_maximum_fusion.refs_6_), channel_id=1, source_target_pairs={{0,2},{2,4},{4,6},{6,8},{8,10},{10,12},{12,14},{1,3},{3,5},{5,7},{... | collective-permute-start | bytes 786440 | tf_op jit(solution)/shard_map/ppermute | solution.py:686
  76.4 3.0 %collective-permute-done.21.refs_4_ = f32[2,24,16,128]{3,2,1,0:T(8,128)S(1)} collective-permute-done((f32[2,24,16,128]{3,2,1,0:T(8,128)S(1)}, f32[2,24,16,128]{3,2,1,0:T(8,128)S(1)}, u32[]{:S(2)}, u32[]{:S(2)}) %collective-permute-start.21) | collective-permute-done | bytes 393248 | tf_op jit(solution)/shard_map/ppermute | solution.py:686
  79.4 3.5 %collective-permute-start.22 = (f32[2,24,16,128]{3,2,1,0:T(8,128)S(1)}, f32[2,24,16,128]{3,2,1,0:T(8,128)S(1)}, u32[]{:S(2)}, u32[]{:S(2)}) collective-permute-start(f32[2,24,16,128]{3,2,1,0:T(8,128)S(1)} %collective-permute-done.21.refs_4_), channel_id=1, source_target_pairs={{0,4},{4,8},{8,12},{6,2},{10,6},{14,10},{1,5},{5,9},{9,13},{7,3},{... | collective-permute-start | bytes 1179656 | tf_op jit(solution)/shard_map/ppermute | solution.py:686
  82.9 2.5 %first_image.1.refs_2_.first = f32[8,65,16,128]{3,2,1,0:T(8,128)S(1)} custom-call(f32[2,24,16,128]{3,2,1,0:T(8,128)S(1)} %copy-done, f32[2,24,16,128]{3,2,1,0:T(8,128)S(1)} %collective-permute-done.7.refs_1_, f32[2,24,16,128]{3,2,1,0:T(8,128)S(1)} %collective-permute-done.13.refs_2_, f32[2,24,16,128]{3,2,1,0:T(8,128)S(1)} %collective-permute-done.1.refs_3_, ...), custom_call_target="tpu_custom_call" | custom-call | flops 10000000000 | bytes 8388608 | tf_op jit(solution)/shard_map/first_image/pallas_call | solution.py:574
  86.0 5.3 %collective-permute-done.22.refs_5_ = f32[2,24,16,128]{3,2,1,0:T(8,128)S(1)} collective-permute-done((f32[2,24,16,128]{3,2,1,0:T(8,128)S(1)}, f32[2,24,16,128]{3,2,1,0:T(8,128)S(1)}, u32[]{:S(2)}, u32[]{:S(2)}) %collective-permute-start.22) | collective-permute-done | bytes 393248 | tf_op jit(solution)/shard_map/ppermute | solution.py:686
  91.3 7.7 %image.1 = f32[8,32,64,65]{3,2,1,0:T(8,128)} custom-call(s32[1]{0:T(128)} %in_order.1.token, f32[8,65,16,128]{3,2,1,0:T(8,128)S(1)} %first_image.1.refs_2_.first, f32[2,24,16,128]{3,2,1,0:T(8,128)S(1)} %get-tuple-element.79.refs_0_, f32[2,24,16,128]{3,2,1,0:T(8,128)S(1)} %collective-permute-done.16.refs_1_, ...), custom_call_target="tpu_custom_call" | custom-call | flops 10000000000 | bytes 16777216 | tf_op jit(solution)/shard_map/image/pallas_call | solution.py:642
  (39 shorter events, 6.7 us)
Async XLA Ops:
  3.7 8.3 %collective-permute-start.1 = (f32[2,24,16,128]{3,2,1,0:T(8,128)}, f32[2,24,16,128]{3,2,1,0:T(8,128)S(1)}, u32[]{:S(2)}, u32[]{:S(2)}) collective-permute-start(f32[2,24,16,128]{3,2,1,0:T(8,128)} %get-tuple-element.50), channel_id=1, source_target_pairs={{0,16},{16,0},{1,17},{17,1},{2,18},{18,2},{3,19},{19,3},{4,20},{20... | collective-permute-start | bytes 1179656 | tf_op jit(solution)/shard_map/ppermute | solution.py:686
  4.2 7.8 %collective-permute-start = (f32[32,8,128]{2,1,0:T(8,128)}, f32[32,8,128]{2,1,0:T(8,128)S(1)}, u32[]{:S(2)}, u32[]{:S(2)}) collective-permute-start(f32[32,8,128]{2,1,0:T(8,128)} %get-tuple-element.48), channel_id=1, source_target_pairs={{0,1},{1,0},{2,3},{3,2},{4,5},{5,4},{6,7},{7,6},{8,9},{9,8},{10,11... | collective-permute-start | bytes 393224 | tf_op jit(solution)/shard_map/ppermute | solution.py:686
  6.7 18.3 %collective-permute-start.4 = (f32[2,8,32,128]{3,2,1,0:T(8,128)}, f32[2,8,32,128]{3,2,1,0:T(8,128)S(1)}, u32[]{:S(2)}, u32[]{:S(2)}) collective-permute-start(f32[2,8,32,128]{3,2,1,0:T(8,128)} %get-tuple-element.55), channel_id=1, source_target_pairs={{0,2},{2,0},{4,6},{6,4},{8,10},{10,8},{12,14},{14,12},{1,3},{3,1},... | collective-permute-start | bytes 786440 | tf_op jit(solution)/shard_map/ppermute | solution.py:686
  8.3 23.6 %collective-permute-start.2 = (f32[2,4,96,128]{3,2,1,0:T(8,128)}, f32[2,4,96,128]{3,2,1,0:T(8,128)S(1)}, u32[]{:S(2)}, u32[]{:S(2)}) collective-permute-start(f32[2,4,96,128]{3,2,1,0:T(8,128)} %get-tuple-element.53), channel_id=1, source_target_pairs={{0,2},{2,4},{4,6},{6,8},{8,10},{10,12},{12,14},{1,3},{3,5},{5,7},{... | collective-permute-start | bytes 1179656 | tf_op jit(solution)/shard_map/ppermute | solution.py:686
  10.7 21.1 %collective-permute-start.3 = (f32[2,4,96,128]{3,2,1,0:T(8,128)}, f32[2,4,96,128]{3,2,1,0:T(8,128)S(1)}, u32[]{:S(2)}, u32[]{:S(2)}) collective-permute-start(f32[2,4,96,128]{3,2,1,0:T(8,128)} %get-tuple-element.54), channel_id=1, source_target_pairs={{2,0},{4,2},{6,4},{8,6},{10,8},{12,10},{14,12},{3,1},{5,3},{7,5},{... | collective-permute-start | bytes 1179656 | tf_op jit(solution)/shard_map/ppermute | solution.py:686
  25.1 11.7 %collective-permute-start.5 = (f32[2,8,32,128]{3,2,1,0:T(8,128)S(1)}, f32[2,8,32,128]{3,2,1,0:T(8,128)S(1)}, u32[]{:S(2)}, u32[]{:S(2)}) collective-permute-start(f32[2,8,32,128]{3,2,1,0:T(8,128)S(1)} %collective-permute-done.4.near), channel_id=1, source_target_pairs={{0,4},{4,8},{8,12},{6,2},{10,6},{14,10},{1,5},{5,9},{9,13},{7,3},{... | collective-permute-start | bytes 786440 | tf_op jit(solution)/shard_map/ppermute | solution.py:686
  31.8 10.7 %collective-permute-start.7 = (f32[2,24,16,128]{3,2,1,0:T(8,128)S(1)}, f32[2,24,16,128]{3,2,1,0:T(8,128)S(1)}, u32[]{:S(2)}, u32[]{:S(2)}) collective-permute-start(f32[2,24,16,128]{3,2,1,0:T(8,128)S(1)} %copy-done), channel_id=1, source_target_pairs={{0,2},{2,0},{4,6},{6,4},{8,10},{10,8},{12,14},{14,12},{1,3},{3,1},... | collective-permute-start | bytes 1179656 | tf_op jit(solution)/shard_map/ppermute | solution.py:686
  37.8 4.7 %collective-permute-start.9 = (f32[2,2,8,16,128]{4,3,2,1,0:T(8,128)S(1)}, f32[2,2,8,16,128]{4,3,2,1,0:T(8,128)S(1)}, u32[]{:S(2)}, u32[]{:S(2)}) collective-permute-start(f32[2,2,8,16,128]{4,3,2,1,0:T(8,128)S(1)} %get-tuple-element.66), channel_id=1, source_target_pairs={{0,16},{16,0},{1,17},{17,1},{2,18},{18,2},{3,19},{19,3},{4,20},{20... | collective-permute-start | bytes 786440 | tf_op jit(solution)/shard_map/ppermute | solution.py:686
  37.9 2.3 %collective-permute-start.8 = (f32[2,8,16,128]{3,2,1,0:T(8,128)S(1)}, f32[2,8,16,128]{3,2,1,0:T(8,128)S(1)}, u32[]{:S(2)}, u32[]{:S(2)}) collective-permute-start(f32[2,8,16,128]{3,2,1,0:T(8,128)S(1)} %copy-done.3), channel_id=1, source_target_pairs={{0,16},{16,0},{1,17},{17,1},{2,18},{18,2},{3,19},{19,3},{4,20},{20... | collective-permute-start | bytes 393224 | tf_op jit(solution)/shard_map/ppermute | solution.py:686
  38.3 3.9 %collective-permute-start.6 = (f32[2,32,128]{2,1,0:T(8,128)S(1)}, f32[2,32,128]{2,1,0:T(8,128)S(1)}, u32[]{:S(2)}, u32[]{:S(2)}) collective-permute-start(f32[2,32,128]{2,1,0:T(8,128)S(1)} %get-tuple-element.63), channel_id=1, source_target_pairs={{0,1},{1,0},{2,3},{3,2},{4,5},{5,4},{6,7},{7,6},{8,9},{9,8},{10,11... | collective-permute-start | bytes 98312 | tf_op jit(solution)/shard_map/ppermute | solution.py:686
  38.9 11.9 %collective-permute-start.14 = (f32[2,24,16,128]{3,2,1,0:T(8,128)S(1)}, f32[2,24,16,128]{3,2,1,0:T(8,128)S(1)}, u32[]{:S(2)}, u32[]{:S(2)}) collective-permute-start(f32[2,24,16,128]{3,2,1,0:T(8,128)S(1)} %collective-permute-done.1.refs_3_), channel_id=1, source_target_pairs={{0,2},{2,0},{4,6},{6,4},{8,10},{10,8},{12,14},{14,12},{1,3},{3,1},... | collective-permute-start | bytes 1179656 | tf_op jit(solution)/shard_map/ppermute | solution.py:686
  42.4 14.0 %collective-permute-start.13 = (f32[2,24,16,128]{3,2,1,0:T(8,128)S(1)}, f32[2,24,16,128]{3,2,1,0:T(8,128)S(1)}, u32[]{:S(2)}, u32[]{:S(2)}) collective-permute-start(f32[2,24,16,128]{3,2,1,0:T(8,128)S(1)} %collective-permute-done.7.refs_1_), channel_id=1, source_target_pairs={{0,4},{4,8},{8,12},{6,2},{10,6},{14,10},{1,5},{5,9},{9,13},{7,3},{... | collective-permute-start | bytes 1179656 | tf_op jit(solution)/shard_map/ppermute | solution.py:686
  46.7 8.5 %collective-permute-start.11 = (f32[2,4,32,128]{3,2,1,0:T(8,128)S(1)}, f32[2,4,32,128]{3,2,1,0:T(8,128)S(1)}, u32[]{:S(2)}, u32[]{:S(2)}) collective-permute-start(f32[2,4,32,128]{3,2,1,0:T(8,128)S(1)} %get-tuple-element.69), channel_id=1, source_target_pairs={{0,2},{2,4},{4,6},{6,8},{8,10},{10,12},{12,14},{1,3},{3,5},{5,7},{... | collective-permute-start | bytes 393224 | tf_op jit(solution)/shard_map/ppermute | solution.py:686
  48.0 8.5 %collective-permute-start.12 = (f32[2,4,32,128]{3,2,1,0:T(8,128)S(1)}, f32[2,4,32,128]{3,2,1,0:T(8,128)S(1)}, u32[]{:S(2)}, u32[]{:S(2)}) collective-permute-start(f32[2,4,32,128]{3,2,1,0:T(8,128)S(1)} %get-tuple-element.70), channel_id=1, source_target_pairs={{2,0},{4,2},{6,4},{8,6},{10,8},{12,10},{14,12},{3,1},{5,3},{7,5},{... | collective-permute-start | bytes 393224 | tf_op jit(solution)/shard_map/ppermute | solution.py:686
  50.7 5.9 %collective-permute-start.10 = (f32[2,24,16,128]{3,2,1,0:T(8,128)S(1)}, f32[2,24,16,128]{3,2,1,0:T(8,128)S(1)}, u32[]{:S(2)}, u32[]{:S(2)}) collective-permute-start(f32[2,24,16,128]{3,2,1,0:T(8,128)S(1)} %get-tuple-element.68), channel_id=1, source_target_pairs={{0,16},{16,0},{1,17},{17,1},{2,18},{18,2},{3,19},{19,3},{4,20},{20... | collective-permute-start | bytes 1179656 | tf_op jit(solution)/shard_map/ppermute | solution.py:686
  50.8 32.1 %copy-start.2 = (f32[2,8,16,128]{3,2,1,0:T(8,128)S(1)}, f32[2,8,16,128]{3,2,1,0:T(8,128)}, u32[]{:S(2)}) copy-start(f32[2,8,16,128]{3,2,1,0:T(8,128)} %get-tuple-element.85.refs_6_) | copy-start | bytes 393220
  50.8 14.5 %collective-permute-start.16 = (f32[2,24,16,128]{3,2,1,0:T(8,128)S(1)}, f32[2,24,16,128]{3,2,1,0:T(8,128)S(1)}, u32[]{:S(2)}, u32[]{:S(2)}) collective-permute-start(f32[2,24,16,128]{3,2,1,0:T(8,128)S(1)} %get-tuple-element.79.refs_0_), channel_id=1, source_target_pairs={{0,2},{2,0},{4,6},{6,4},{8,10},{10,8},{12,14},{14,12},{1,3},{3,1},... | collective-permute-start | bytes 1179656 | tf_op jit(solution)/shard_map/ppermute | solution.py:686
  56.6 8.7 %collective-permute-start.15 = (f32[2,8,16,128]{3,2,1,0:T(8,128)S(1)}, f32[2,8,16,128]{3,2,1,0:T(8,128)S(1)}, u32[]{:S(2)}, u32[]{:S(2)}) collective-permute-start(f32[2,8,16,128]{3,2,1,0:T(8,128)S(1)} %get-tuple-element.78), channel_id=1, source_target_pairs={{0,16},{16,0},{1,17},{17,1},{2,18},{18,2},{3,19},{19,3},{4,20},{20... | collective-permute-start | bytes 393224 | tf_op jit(solution)/shard_map/ppermute | solution.py:686
  56.7 26.2 %collective-permute-start.19 = (f32[2,24,16,128]{3,2,1,0:T(8,128)S(1)}, f32[2,24,16,128]{3,2,1,0:T(8,128)S(1)}, u32[]{:S(2)}, u32[]{:S(2)}) collective-permute-start(f32[2,24,16,128]{3,2,1,0:T(8,128)S(1)} %collective-permute-done.14.refs_4_), channel_id=1, source_target_pairs={{0,4},{4,8},{8,12},{6,2},{10,6},{14,10},{1,5},{5,9},{9,13},{7,3},{... | collective-permute-start | bytes 1179656 | tf_op jit(solution)/shard_map/ppermute | solution.py:686
  60.7 18.7 %collective-permute-start.21 = (f32[2,24,16,128]{3,2,1,0:T(8,128)S(1)}, f32[2,24,16,128]{3,2,1,0:T(8,128)S(1)}, u32[]{:S(2)}, u32[]{:S(2)}) collective-permute-start(f32[2,24,16,128]{3,2,1,0:T(8,128)S(1)} %collective-permute-done.10.refs_3_), channel_id=1, source_target_pairs={{0,2},{2,0},{4,6},{6,4},{8,10},{10,8},{12,14},{14,12},{1,3},{3,1},... | collective-permute-start | bytes 1179656 | tf_op jit(solution)/shard_map/ppermute | solution.py:686
  65.4 17.5 %collective-permute-start.20 = (f32[2,24,16,128]{3,2,1,0:T(8,128)S(1)}, f32[2,24,16,128]{3,2,1,0:T(8,128)S(1)}, u32[]{:S(2)}, u32[]{:S(2)}) collective-permute-start(f32[2,24,16,128]{3,2,1,0:T(8,128)S(1)} %collective-permute-done.16.refs_1_), channel_id=1, source_target_pairs={{0,4},{4,8},{8,12},{6,2},{10,6},{14,10},{1,5},{5,9},{9,13},{7,3},{... | collective-permute-start | bytes 1179656 | tf_op jit(solution)/shard_map/ppermute | solution.py:686
  70.5 15.0 %collective-permute-start.18 = (f32[2,2,8,16,128]{4,3,2,1,0:T(8,128)S(1)}, f32[2,2,8,16,128]{4,3,2,1,0:T(8,128)S(1)}, u32[]{:S(2)}, u32[]{:S(2)}) collective-permute-start(f32[2,2,8,16,128]{4,3,2,1,0:T(8,128)S(1)} %pad_maximum_fusion.refs_6_), channel_id=1, source_target_pairs={{2,0},{4,2},{6,4},{8,6},{10,8},{12,10},{14,12},{3,1},{5,3},{7,5},{... | collective-permute-start | bytes 786440 | tf_op jit(solution)/shard_map/ppermute | solution.py:686
  71.8 13.7 %collective-permute-start.17 = (f32[2,2,8,16,128]{4,3,2,1,0:T(8,128)S(1)}, f32[2,2,8,16,128]{4,3,2,1,0:T(8,128)S(1)}, u32[]{:S(2)}, u32[]{:S(2)}) collective-permute-start(f32[2,2,8,16,128]{4,3,2,1,0:T(8,128)S(1)} %pad_maximum_fusion.refs_6_), channel_id=1, source_target_pairs={{0,2},{2,4},{4,6},{6,8},{8,10},{10,12},{12,14},{1,3},{3,5},{5,7},{... | collective-permute-start | bytes 786440 | tf_op jit(solution)/shard_map/ppermute | solution.py:686
  79.4 11.9 %collective-permute-start.22 = (f32[2,24,16,128]{3,2,1,0:T(8,128)S(1)}, f32[2,24,16,128]{3,2,1,0:T(8,128)S(1)}, u32[]{:S(2)}, u32[]{:S(2)}) collective-permute-start(f32[2,24,16,128]{3,2,1,0:T(8,128)S(1)} %collective-permute-done.21.refs_4_), channel_id=1, source_target_pairs={{0,4},{4,8},{8,12},{6,2},{10,6},{14,10},{1,5},{5,9},{9,13},{7,3},{... | collective-permute-start | bytes 1179656 | tf_op jit(solution)/shard_map/ppermute | solution.py:686
  (3 other events, 44.5 us)

commit v14 on v13

--- a/solution.py
+++ b/solution.py
@@ -605,7 +605,7 @@
 
     def leave(at_step, chunk, half):
         slot = at_step % 2
-        here = pl.ds(half * lines + 8 * chunk, 8)
+        here = pl.ds(half * lines + 4 * chunk, 4)
         return pltpu.make_async_copy(staged.at[slot, here], out.at[at_step, here], out_sems.at[slot, chunk, half])
 
     sample = 4 * step
@@ -617,23 +617,25 @@
 
         @pl.when(step >= 2)
         def _():
-            for half in range(2):
-                leave(step - 2, chunk, half).wait()
+            for part in range(2 * chunk, 2 * chunk + 2):
+                for half in range(2):
+                    leave(step - 2, part, half).wait()
 
         for line in range(8):
             values = turned[chunk, line * OFFSET_ROWS : (line + 1) * OFFSET_ROWS, :].T
             at = 8 * chunk + line
             staged[step % 2, at] = values[: size_z // 2, :OFFSETS]
             staged[step % 2, lines + at] = values[size_z // 2 :, :OFFSETS]
-        for half in range(2):
-            leave(step, chunk, half).start()
+            if line % 4 == 3:
+                for half in range(2):
+                    leave(step, at // 4, half).start()
 
     @pl.when(step == steps_in_all - 1)
     def _():
         for back in (1, 0):
-            for chunk in range(chunks):
+            for part in range(2 * chunks):
                 for half in range(2):
-                    leave(step - back, chunk, half).wait()
+                    leave(step - back, part, half).wait()
 
 
 def image(token, first, blocks):
@@ -650,7 +652,7 @@
             pltpu.VMEM((lines // 8, 8 * OFFSET_ROWS, size_z), F32),
             pltpu.VMEM((2, 2 * lines, size_z // 2, OFFSETS), F32),
             pltpu.SemaphoreType.DMA((18,)),
-            pltpu.SemaphoreType.DMA((2, lines // 8, 2)),
+            pltpu.SemaphoreType.DMA((2, lines // 4, 2)),
         ],
         compiler_params=params(20),
         cost_estimate=cost(10**10, 16 * 2**20),

time: 100 us -> 100 us (level)
  no operation moved by 1% of the time
where the time goes in v14:
time: 100 us; the launch traced here: 99.1 us
  starting transfers between devices  47.5 us (48%)
  Pallas kernels  30.1 us (30%)
  waiting for transfers between devices  21.1 us (21%)
    ppermute x23, starting transfers between devices, exchange(): return lax.ppermute(array, axis, pairs)  47.5 us
    ppermute x23, waiting for transfers between devices, exchange(): return lax.ppermute(array, axis, pairs)  21.1 us
    pallas_call x1, Pallas kernels, steps(): pl.pallas_call(steps_kernel, out_shape=(jax.ShapeDtypeStruct((2, rows, li...  13 us
    pallas_call x1, Pallas kernels, image(): pl.pallas_call(image_kernel, grid=(samples,), out_shape=jax.ShapeDtypeStr...  7.8 us
    pallas_call x1, Pallas kernels, pack(): pl.pallas_call(pack_kernel, out_shape=(apart, apart, jax.ShapeDtypeStruct...  3.65 us
    pallas_call x1, Pallas kernels, first_image(): pl.pallas_call(first_image_kernel, grid=(samples,), out_shape=jax.ShapeDt...  2.53 us
  transfers between devices with their start and end apart: 23, of which 7 were waited for; matrix products, arithmetic and copies ran while one was open for 0% of the time, Pallas kernels for 19%

profile of v14, /device:TPU:0, one launch (start us, length us, event | category | flops | bytes accessed | tf_op | source)
XLA Modules:
  0.0 99.1 jit_solution(5465326752847829106)
XLA Ops:
  0.0 3.6 %pack.1 = (f32[2,4,96,128]{3,2,1,0:T(8,128)}, f32[2,4,96,128]{3,2,1,0:T(8,128)}, f32[2,8,32,128]{3,2,1,0:T(8,128)}, f32[2,24,16,128]{3,2,1,0:T(8,128)}, f32[2,8,...) custom-call(f32[1,32,128,128]{3,2,1,0:T(8,128)} %source.3, ...), custom_call_target="tpu_custom_call" | custom-call | flops 10000000000 | bytes 7340032 | tf_op jit(solution)/shard_map/pack/pallas_call | solution.py:114
  4.2 2.6 %collective-permute-start = (f32[32,8,128]{2,1,0:T(8,128)}, f32[32,8,128]{2,1,0:T(8,128)S(1)}, u32[]{:S(2)}, u32[]{:S(2)}) collective-permute-start(f32[32,8,128]{2,1,0:T(8,128)} %get-tuple-element.48), channel_id=1, source_target_pairs={{0,1},{1,0},{2,3},{3,2},{4,5},{5,4},{6,7},{7,6},{8,9},{9,8},{10,11... | collective-permute-start | bytes 393224 | tf_op jit(solution)/shard_map/ppermute | solution.py:688
  6.7 1.5 %collective-permute-start.4 = (f32[2,8,32,128]{3,2,1,0:T(8,128)}, f32[2,8,32,128]{3,2,1,0:T(8,128)S(1)}, u32[]{:S(2)}, u32[]{:S(2)}) collective-permute-start(f32[2,8,32,128]{3,2,1,0:T(8,128)} %get-tuple-element.55), channel_id=1, source_target_pairs={{0,2},{2,0},{4,6},{6,4},{8,10},{10,8},{12,14},{14,12},{1,3},{3,1},... | collective-permute-start | bytes 786440 | tf_op jit(solution)/shard_map/ppermute | solution.py:688
  8.3 2.4 %collective-permute-start.2 = (f32[2,4,96,128]{3,2,1,0:T(8,128)}, f32[2,4,96,128]{3,2,1,0:T(8,128)S(1)}, u32[]{:S(2)}, u32[]{:S(2)}) collective-permute-start(f32[2,4,96,128]{3,2,1,0:T(8,128)} %get-tuple-element.53), channel_id=1, source_target_pairs={{0,2},{2,4},{4,6},{6,8},{8,10},{10,12},{12,14},{1,3},{3,5},{5,7},{... | collective-permute-start | bytes 1179656 | tf_op jit(solution)/shard_map/ppermute | solution.py:688
  10.7 1.3 %collective-permute-start.3 = (f32[2,4,96,128]{3,2,1,0:T(8,128)}, f32[2,4,96,128]{3,2,1,0:T(8,128)S(1)}, u32[]{:S(2)}, u32[]{:S(2)}) collective-permute-start(f32[2,4,96,128]{3,2,1,0:T(8,128)} %get-tuple-element.54), channel_id=1, source_target_pairs={{2,0},{4,2},{6,4},{8,6},{10,8},{12,10},{14,12},{3,1},{5,3},{7,5},{... | collective-permute-start | bytes 1179656 | tf_op jit(solution)/shard_map/ppermute | solution.py:688
  12.0 13.0 %steps.1 = (f32[2,32,32,128]{3,2,1,0:T(8,128)S(1)}, f32[32,32,128]{2,1,0:T(8,128)S(1)}, f32[2,4,128,128]{3,2,1,0:T(8,128)S(1)}, f32[2,2,4,32,128]{4,3,2,1,0:T(8,128)S(1)}, f32[2,32,128]{2,1,0:T(8,128)S(1)}) custom-call(f32[1,32,128,128]{3,2,1,0:T(8,128)} %source.3, f32[1,32,128,128]{3,2,1,0:T(8,128)} %receiver.3, f32[1,32,128,128]{3,2,1,0:T(8,128)} %source_before.1, ...), custom_call_target="tpu_custom_call" | custom-call | flops 20000000000 | bytes 1048576 | tf_op jit(solution)/shard_map/steps/pallas_call | solution.py:331
  25.1 6.6 %collective-permute-start.5 = (f32[2,8,32,128]{3,2,1,0:T(8,128)S(1)}, f32[2,8,32,128]{3,2,1,0:T(8,128)S(1)}, u32[]{:S(2)}, u32[]{:S(2)}) collective-permute-start(f32[2,8,32,128]{3,2,1,0:T(8,128)S(1)} %collective-permute-done.4.near), channel_id=1, source_target_pairs={{0,4},{4,8},{8,12},{6,2},{10,6},{14,10},{1,5},{5,9},{9,13},{7,3},{... | collective-permute-start | bytes 786440 | tf_op jit(solution)/shard_map/ppermute | solution.py:688
  31.9 4.9 %collective-permute-done.5.far = f32[2,8,32,128]{3,2,1,0:T(8,128)S(1)} collective-permute-done((f32[2,8,32,128]{3,2,1,0:T(8,128)S(1)}, f32[2,8,32,128]{3,2,1,0:T(8,128)S(1)}, u32[]{:S(2)}, u32[]{:S(2)}) %collective-permute-start.5) | collective-permute-done | bytes 262176 | tf_op jit(solution)/shard_map/ppermute | solution.py:688
  38.9 1.3 %collective-permute-start.14 = (f32[2,24,16,128]{3,2,1,0:T(8,128)S(1)}, f32[2,24,16,128]{3,2,1,0:T(8,128)S(1)}, u32[]{:S(2)}, u32[]{:S(2)}) collective-permute-start(f32[2,24,16,128]{3,2,1,0:T(8,128)S(1)} %collective-permute-done.1.refs_3_), channel_id=1, source_target_pairs={{0,2},{2,0},{4,6},{6,4},{8,10},{10,8},{12,14},{14,12},{1,3},{3,1},... | collective-permute-start | bytes 1179656 | tf_op jit(solution)/shard_map/ppermute | solution.py:688
  40.2 2.1 %collective-permute-done.6.side = f32[2,32,128]{2,1,0:T(8,128)S(1)} collective-permute-done((f32[2,32,128]{2,1,0:T(8,128)S(1)}, f32[2,32,128]{2,1,0:T(8,128)S(1)}, u32[]{:S(2)}, u32[]{:S(2)}) %collective-permute-start.6) | collective-permute-done | bytes 32800 | tf_op jit(solution)/shard_map/ppermute | solution.py:688
  42.4 4.2 %collective-permute-start.13 = (f32[2,24,16,128]{3,2,1,0:T(8,128)S(1)}, f32[2,24,16,128]{3,2,1,0:T(8,128)S(1)}, u32[]{:S(2)}, u32[]{:S(2)}) collective-permute-start(f32[2,24,16,128]{3,2,1,0:T(8,128)S(1)} %collective-permute-done.7.refs_1_), channel_id=1, source_target_pairs={{0,4},{4,8},{8,12},{6,2},{10,6},{14,10},{1,5},{5,9},{9,13},{7,3},{... | collective-permute-start | bytes 1179656 | tf_op jit(solution)/shard_map/ppermute | solution.py:688
  46.7 1.3 %collective-permute-start.11 = (f32[2,4,32,128]{3,2,1,0:T(8,128)S(1)}, f32[2,4,32,128]{3,2,1,0:T(8,128)S(1)}, u32[]{:S(2)}, u32[]{:S(2)}) collective-permute-start(f32[2,4,32,128]{3,2,1,0:T(8,128)S(1)} %get-tuple-element.69), channel_id=1, source_target_pairs={{0,2},{2,4},{4,6},{6,8},{8,10},{10,12},{12,14},{1,3},{3,5},{5,7},{... | collective-permute-start | bytes 393224 | tf_op jit(solution)/shard_map/ppermute | solution.py:688
  48.0 1.3 %collective-permute-start.12 = (f32[2,4,32,128]{3,2,1,0:T(8,128)S(1)}, f32[2,4,32,128]{3,2,1,0:T(8,128)S(1)}, u32[]{:S(2)}, u32[]{:S(2)}) collective-permute-start(f32[2,4,32,128]{3,2,1,0:T(8,128)S(1)} %get-tuple-element.70), channel_id=1, source_target_pairs={{2,0},{4,2},{6,4},{8,6},{10,8},{12,10},{14,12},{3,1},{5,3},{7,5},{... | collective-permute-start | bytes 393224 | tf_op jit(solution)/shard_map/ppermute | solution.py:688
  49.3 1.5 %finish_middle.1 = (f32[2,24,16,128]{3,2,1,0:T(8,128)S(1)}, f32[2,24,16,128]{3,2,1,0:T(8,128)S(1)}) custom-call(f32[2,32,32,128]{3,2,1,0:T(8,128)S(1)} %get-tuple-element.52.partial, f32[2,2,8,32,128]{4,3,2,1,0:T(8,128)S(1)} %get-tuple-element.62.ends, f32[32,32,128]{2,1,0:T(8,128)S(1)} %get-tuple-element.58.kept_courant, ...), custom_call_target="tpu_custom_call" | custom-call | flops 1 | bytes 1 | tf_op jit(solution)/shard_map/finish_middle/pallas_call | solution.py:474
  50.8 4.3 %collective-permute-start.16 = (f32[2,24,16,128]{3,2,1,0:T(8,128)S(1)}, f32[2,24,16,128]{3,2,1,0:T(8,128)S(1)}, u32[]{:S(2)}, u32[]{:S(2)}) collective-permute-start(f32[2,24,16,128]{3,2,1,0:T(8,128)S(1)} %get-tuple-element.79.refs_0_), channel_id=1, source_target_pairs={{0,2},{2,0},{4,6},{6,4},{8,10},{10,8},{12,14},{14,12},{1,3},{3,1},... | collective-permute-start | bytes 1179656 | tf_op jit(solution)/shard_map/ppermute | solution.py:688
  56.7 4.0 %collective-permute-start.19 = (f32[2,24,16,128]{3,2,1,0:T(8,128)S(1)}, f32[2,24,16,128]{3,2,1,0:T(8,128)S(1)}, u32[]{:S(2)}, u32[]{:S(2)}) collective-permute-start(f32[2,24,16,128]{3,2,1,0:T(8,128)S(1)} %collective-permute-done.14.refs_4_), channel_id=1, source_target_pairs={{0,4},{4,8},{8,12},{6,2},{10,6},{14,10},{1,5},{5,9},{9,13},{7,3},{... | collective-permute-start | bytes 1179656 | tf_op jit(solution)/shard_map/ppermute | solution.py:688
  61.1 4.3 %collective-permute-done.16.refs_1_ = f32[2,24,16,128]{3,2,1,0:T(8,128)S(1)} collective-permute-done((f32[2,24,16,128]{3,2,1,0:T(8,128)S(1)}, f32[2,24,16,128]{3,2,1,0:T(8,128)S(1)}, u32[]{:S(2)}, u32[]{:S(2)}) %collective-permute-start.16) | collective-permute-done | bytes 393248 | tf_op jit(solution)/shard_map/ppermute | solution.py:688
  65.4 5.1 %collective-permute-start.20 = (f32[2,24,16,128]{3,2,1,0:T(8,128)S(1)}, f32[2,24,16,128]{3,2,1,0:T(8,128)S(1)}, u32[]{:S(2)}, u32[]{:S(2)}) collective-permute-start(f32[2,24,16,128]{3,2,1,0:T(8,128)S(1)} %collective-permute-done.16.refs_1_), channel_id=1, source_target_pairs={{0,4},{4,8},{8,12},{6,2},{10,6},{14,10},{1,5},{5,9},{9,13},{7,3},{... | collective-permute-start | bytes 1179656 | tf_op jit(solution)/shard_map/ppermute | solution.py:688
  71.8 4.6 %collective-permute-start.17 = (f32[2,2,8,16,128]{4,3,2,1,0:T(8,128)S(1)}, f32[2,2,8,16,128]{4,3,2,1,0:T(8,128)S(1)}, u32[]{:S(2)}, u32[]{:S(2)}) collective-permute-start(f32[2,2,8,16,128]{4,3,2,1,0:T(8,128)S(1)} %pad_maximum_fusion.refs_6_), channel_id=1, source_target_pairs={{0,2},{2,4},{4,6},{6,8},{8,10},{10,12},{12,14},{1,3},{3,5},{5,7},{... | collective-permute-start | bytes 786440 | tf_op jit(solution)/shard_map/ppermute | solution.py:688
  76.4 3.0 %collective-permute-done.21.refs_4_ = f32[2,24,16,128]{3,2,1,0:T(8,128)S(1)} collective-permute-done((f32[2,24,16,128]{3,2,1,0:T(8,128)S(1)}, f32[2,24,16,128]{3,2,1,0:T(8,128)S(1)}, u32[]{:S(2)}, u32[]{:S(2)}) %collective-permute-start.21) | collective-permute-done | bytes 393248 | tf_op jit(solution)/shard_map/ppermute | solution.py:688
  79.4 3.5 %collective-permute-start.22 = (f32[2,24,16,128]{3,2,1,0:T(8,128)S(1)}, f32[2,24,16,128]{3,2,1,0:T(8,128)S(1)}, u32[]{:S(2)}, u32[]{:S(2)}) collective-permute-start(f32[2,24,16,128]{3,2,1,0:T(8,128)S(1)} %collective-permute-done.21.refs_4_), channel_id=1, source_target_pairs={{0,4},{4,8},{8,12},{6,2},{10,6},{14,10},{1,5},{5,9},{9,13},{7,3},{... | collective-permute-start | bytes 1179656 | tf_op jit(solution)/shard_map/ppermute | solution.py:688
  82.9 2.5 %first_image.1.refs_2_.first = f32[8,65,16,128]{3,2,1,0:T(8,128)S(1)} custom-call(f32[2,24,16,128]{3,2,1,0:T(8,128)S(1)} %copy-done, f32[2,24,16,128]{3,2,1,0:T(8,128)S(1)} %collective-permute-done.7.refs_1_, f32[2,24,16,128]{3,2,1,0:T(8,128)S(1)} %collective-permute-done.13.refs_2_, f32[2,24,16,128]{3,2,1,0:T(8,128)S(1)} %collective-permute-done.1.refs_3_, ...), custom_call_target="tpu_custom_call" | custom-call | flops 10000000000 | bytes 8388608 | tf_op jit(solution)/shard_map/first_image/pallas_call | solution.py:574
  86.0 5.3 %collective-permute-done.22.refs_5_ = f32[2,24,16,128]{3,2,1,0:T(8,128)S(1)} collective-permute-done((f32[2,24,16,128]{3,2,1,0:T(8,128)S(1)}, f32[2,24,16,128]{3,2,1,0:T(8,128)S(1)}, u32[]{:S(2)}, u32[]{:S(2)}) %collective-permute-start.22) | collective-permute-done | bytes 393248 | tf_op jit(solution)/shard_map/ppermute | solution.py:688
  91.3 7.8 %image.1 = f32[8,32,64,65]{3,2,1,0:T(8,128)} custom-call(s32[1]{0:T(128)} %in_order.1.token, f32[8,65,16,128]{3,2,1,0:T(8,128)S(1)} %first_image.1.refs_2_.first, f32[2,24,16,128]{3,2,1,0:T(8,128)S(1)} %get-tuple-element.79.refs_0_, f32[2,24,16,128]{3,2,1,0:T(8,128)S(1)} %collective-permute-done.16.refs_1_, ...), custom_call_target="tpu_custom_call" | custom-call | flops 10000000000 | bytes 16777216 | tf_op jit(solution)/shard_map/image/pallas_call | solution.py:644
  (39 shorter events, 6.7 us)
Async XLA Ops:
  3.7 8.3 %collective-permute-start.1 = (f32[2,24,16,128]{3,2,1,0:T(8,128)}, f32[2,24,16,128]{3,2,1,0:T(8,128)S(1)}, u32[]{:S(2)}, u32[]{:S(2)}) collective-permute-start(f32[2,24,16,128]{3,2,1,0:T(8,128)} %get-tuple-element.50), channel_id=1, source_target_pairs={{0,16},{16,0},{1,17},{17,1},{2,18},{18,2},{3,19},{19,3},{4,20},{20... | collective-permute-start | bytes 1179656 | tf_op jit(solution)/shard_map/ppermute | solution.py:688
  4.2 7.8 %collective-permute-start = (f32[32,8,128]{2,1,0:T(8,128)}, f32[32,8,128]{2,1,0:T(8,128)S(1)}, u32[]{:S(2)}, u32[]{:S(2)}) collective-permute-start(f32[32,8,128]{2,1,0:T(8,128)} %get-tuple-element.48), channel_id=1, source_target_pairs={{0,1},{1,0},{2,3},{3,2},{4,5},{5,4},{6,7},{7,6},{8,9},{9,8},{10,11... | collective-permute-start | bytes 393224 | tf_op jit(solution)/shard_map/ppermute | solution.py:688
  6.7 18.3 %collective-permute-start.4 = (f32[2,8,32,128]{3,2,1,0:T(8,128)}, f32[2,8,32,128]{3,2,1,0:T(8,128)S(1)}, u32[]{:S(2)}, u32[]{:S(2)}) collective-permute-start(f32[2,8,32,128]{3,2,1,0:T(8,128)} %get-tuple-element.55), channel_id=1, source_target_pairs={{0,2},{2,0},{4,6},{6,4},{8,10},{10,8},{12,14},{14,12},{1,3},{3,1},... | collective-permute-start | bytes 786440 | tf_op jit(solution)/shard_map/ppermute | solution.py:688
  8.3 23.6 %collective-permute-start.2 = (f32[2,4,96,128]{3,2,1,0:T(8,128)}, f32[2,4,96,128]{3,2,1,0:T(8,128)S(1)}, u32[]{:S(2)}, u32[]{:S(2)}) collective-permute-start(f32[2,4,96,128]{3,2,1,0:T(8,128)} %get-tuple-element.53), channel_id=1, source_target_pairs={{0,2},{2,4},{4,6},{6,8},{8,10},{10,12},{12,14},{1,3},{3,5},{5,7},{... | collective-permute-start | bytes 1179656 | tf_op jit(solution)/shard_map/ppermute | solution.py:688
  10.7 21.1 %collective-permute-start.3 = (f32[2,4,96,128]{3,2,1,0:T(8,128)}, f32[2,4,96,128]{3,2,1,0:T(8,128)S(1)}, u32[]{:S(2)}, u32[]{:S(2)}) collective-permute-start(f32[2,4,96,128]{3,2,1,0:T(8,128)} %get-tuple-element.54), channel_id=1, source_target_pairs={{2,0},{4,2},{6,4},{8,6},{10,8},{12,10},{14,12},{3,1},{5,3},{7,5},{... | collective-permute-start | bytes 1179656 | tf_op jit(solution)/shard_map/ppermute | solution.py:688
  25.1 11.7 %collective-permute-start.5 = (f32[2,8,32,128]{3,2,1,0:T(8,128)S(1)}, f32[2,8,32,128]{3,2,1,0:T(8,128)S(1)}, u32[]{:S(2)}, u32[]{:S(2)}) collective-permute-start(f32[2,8,32,128]{3,2,1,0:T(8,128)S(1)} %collective-permute-done.4.near), channel_id=1, source_target_pairs={{0,4},{4,8},{8,12},{6,2},{10,6},{14,10},{1,5},{5,9},{9,13},{7,3},{... | collective-permute-start | bytes 786440 | tf_op jit(solution)/shard_map/ppermute | solution.py:688
  31.8 10.7 %collective-permute-start.7 = (f32[2,24,16,128]{3,2,1,0:T(8,128)S(1)}, f32[2,24,16,128]{3,2,1,0:T(8,128)S(1)}, u32[]{:S(2)}, u32[]{:S(2)}) collective-permute-start(f32[2,24,16,128]{3,2,1,0:T(8,128)S(1)} %copy-done), channel_id=1, source_target_pairs={{0,2},{2,0},{4,6},{6,4},{8,10},{10,8},{12,14},{14,12},{1,3},{3,1},... | collective-permute-start | bytes 1179656 | tf_op jit(solution)/shard_map/ppermute | solution.py:688
  37.8 4.7 %collective-permute-start.9 = (f32[2,2,8,16,128]{4,3,2,1,0:T(8,128)S(1)}, f32[2,2,8,16,128]{4,3,2,1,0:T(8,128)S(1)}, u32[]{:S(2)}, u32[]{:S(2)}) collective-permute-start(f32[2,2,8,16,128]{4,3,2,1,0:T(8,128)S(1)} %get-tuple-element.66), channel_id=1, source_target_pairs={{0,16},{16,0},{1,17},{17,1},{2,18},{18,2},{3,19},{19,3},{4,20},{20... | collective-permute-start | bytes 786440 | tf_op jit(solution)/shard_map/ppermute | solution.py:688
  37.9 2.3 %collective-permute-start.8 = (f32[2,8,16,128]{3,2,1,0:T(8,128)S(1)}, f32[2,8,16,128]{3,2,1,0:T(8,128)S(1)}, u32[]{:S(2)}, u32[]{:S(2)}) collective-permute-start(f32[2,8,16,128]{3,2,1,0:T(8,128)S(1)} %copy-done.3), channel_id=1, source_target_pairs={{0,16},{16,0},{1,17},{17,1},{2,18},{18,2},{3,19},{19,3},{4,20},{20... | collective-permute-start | bytes 393224 | tf_op jit(solution)/shard_map/ppermute | solution.py:688
  38.3 3.9 %collective-permute-start.6 = (f32[2,32,128]{2,1,0:T(8,128)S(1)}, f32[2,32,128]{2,1,0:T(8,128)S(1)}, u32[]{:S(2)}, u32[]{:S(2)}) collective-permute-start(f32[2,32,128]{2,1,0:T(8,128)S(1)} %get-tuple-element.63), channel_id=1, source_target_pairs={{0,1},{1,0},{2,3},{3,2},{4,5},{5,4},{6,7},{7,6},{8,9},{9,8},{10,11... | collective-permute-start | bytes 98312 | tf_op jit(solution)/shard_map/ppermute | solution.py:688
  38.9 11.9 %collective-permute-start.14 = (f32[2,24,16,128]{3,2,1,0:T(8,128)S(1)}, f32[2,24,16,128]{3,2,1,0:T(8,128)S(1)}, u32[]{:S(2)}, u32[]{:S(2)}) collective-permute-start(f32[2,24,16,128]{3,2,1,0:T(8,128)S(1)} %collective-permute-done.1.refs_3_), channel_id=1, source_target_pairs={{0,2},{2,0},{4,6},{6,4},{8,10},{10,8},{12,14},{14,12},{1,3},{3,1},... | collective-permute-start | bytes 1179656 | tf_op jit(solution)/shard_map/ppermute | solution.py:688
  42.4 14.0 %collective-permute-start.13 = (f32[2,24,16,128]{3,2,1,0:T(8,128)S(1)}, f32[2,24,16,128]{3,2,1,0:T(8,128)S(1)}, u32[]{:S(2)}, u32[]{:S(2)}) collective-permute-start(f32[2,24,16,128]{3,2,1,0:T(8,128)S(1)} %collective-permute-done.7.refs_1_), channel_id=1, source_target_pairs={{0,4},{4,8},{8,12},{6,2},{10,6},{14,10},{1,5},{5,9},{9,13},{7,3},{... | collective-permute-start | bytes 1179656 | tf_op jit(solution)/shard_map/ppermute | solution.py:688
  46.7 8.5 %collective-permute-start.11 = (f32[2,4,32,128]{3,2,1,0:T(8,128)S(1)}, f32[2,4,32,128]{3,2,1,0:T(8,128)S(1)}, u32[]{:S(2)}, u32[]{:S(2)}) collective-permute-start(f32[2,4,32,128]{3,2,1,0:T(8,128)S(1)} %get-tuple-element.69), channel_id=1, source_target_pairs={{0,2},{2,4},{4,6},{6,8},{8,10},{10,12},{12,14},{1,3},{3,5},{5,7},{... | collective-permute-start | bytes 393224 | tf_op jit(solution)/shard_map/ppermute | solution.py:688
  48.0 8.5 %collective-permute-start.12 = (f32[2,4,32,128]{3,2,1,0:T(8,128)S(1)}, f32[2,4,32,128]{3,2,1,0:T(8,128)S(1)}, u32[]{:S(2)}, u32[]{:S(2)}) collective-permute-start(f32[2,4,32,128]{3,2,1,0:T(8,128)S(1)} %get-tuple-element.70), channel_id=1, source_target_pairs={{2,0},{4,2},{6,4},{8,6},{10,8},{12,10},{14,12},{3,1},{5,3},{7,5},{... | collective-permute-start | bytes 393224 | tf_op jit(solution)/shard_map/ppermute | solution.py:688
  50.7 5.9 %collective-permute-start.10 = (f32[2,24,16,128]{3,2,1,0:T(8,128)S(1)}, f32[2,24,16,128]{3,2,1,0:T(8,128)S(1)}, u32[]{:S(2)}, u32[]{:S(2)}) collective-permute-start(f32[2,24,16,128]{3,2,1,0:T(8,128)S(1)} %get-tuple-element.68), channel_id=1, source_target_pairs={{0,16},{16,0},{1,17},{17,1},{2,18},{18,2},{3,19},{19,3},{4,20},{20... | collective-permute-start | bytes 1179656 | tf_op jit(solution)/shard_map/ppermute | solution.py:688
  50.8 32.1 %copy-start.2 = (f32[2,8,16,128]{3,2,1,0:T(8,128)S(1)}, f32[2,8,16,128]{3,2,1,0:T(8,128)}, u32[]{:S(2)}) copy-start(f32[2,8,16,128]{3,2,1,0:T(8,128)} %get-tuple-element.85.refs_6_) | copy-start | bytes 393220
  50.8 14.5 %collective-permute-start.16 = (f32[2,24,16,128]{3,2,1,0:T(8,128)S(1)}, f32[2,24,16,128]{3,2,1,0:T(8,128)S(1)}, u32[]{:S(2)}, u32[]{:S(2)}) collective-permute-start(f32[2,24,16,128]{3,2,1,0:T(8,128)S(1)} %get-tuple-element.79.refs_0_), channel_id=1, source_target_pairs={{0,2},{2,0},{4,6},{6,4},{8,10},{10,8},{12,14},{14,12},{1,3},{3,1},... | collective-permute-start | bytes 1179656 | tf_op jit(solution)/shard_map/ppermute | solution.py:688
  56.6 8.7 %collective-permute-start.15 = (f32[2,8,16,128]{3,2,1,0:T(8,128)S(1)}, f32[2,8,16,128]{3,2,1,0:T(8,128)S(1)}, u32[]{:S(2)}, u32[]{:S(2)}) collective-permute-start(f32[2,8,16,128]{3,2,1,0:T(8,128)S(1)} %get-tuple-element.78), channel_id=1, source_target_pairs={{0,16},{16,0},{1,17},{17,1},{2,18},{18,2},{3,19},{19,3},{4,20},{20... | collective-permute-start | bytes 393224 | tf_op jit(solution)/shard_map/ppermute | solution.py:688
  56.7 26.2 %collective-permute-start.19 = (f32[2,24,16,128]{3,2,1,0:T(8,128)S(1)}, f32[2,24,16,128]{3,2,1,0:T(8,128)S(1)}, u32[]{:S(2)}, u32[]{:S(2)}) collective-permute-start(f32[2,24,16,128]{3,2,1,0:T(8,128)S(1)} %collective-permute-done.14.refs_4_), channel_id=1, source_target_pairs={{0,4},{4,8},{8,12},{6,2},{10,6},{14,10},{1,5},{5,9},{9,13},{7,3},{... | collective-permute-start | bytes 1179656 | tf_op jit(solution)/shard_map/ppermute | solution.py:688
  60.7 18.7 %collective-permute-start.21 = (f32[2,24,16,128]{3,2,1,0:T(8,128)S(1)}, f32[2,24,16,128]{3,2,1,0:T(8,128)S(1)}, u32[]{:S(2)}, u32[]{:S(2)}) collective-permute-start(f32[2,24,16,128]{3,2,1,0:T(8,128)S(1)} %collective-permute-done.10.refs_3_), channel_id=1, source_target_pairs={{0,2},{2,0},{4,6},{6,4},{8,10},{10,8},{12,14},{14,12},{1,3},{3,1},... | collective-permute-start | bytes 1179656 | tf_op jit(solution)/shard_map/ppermute | solution.py:688
  65.4 17.5 %collective-permute-start.20 = (f32[2,24,16,128]{3,2,1,0:T(8,128)S(1)}, f32[2,24,16,128]{3,2,1,0:T(8,128)S(1)}, u32[]{:S(2)}, u32[]{:S(2)}) collective-permute-start(f32[2,24,16,128]{3,2,1,0:T(8,128)S(1)} %collective-permute-done.16.refs_1_), channel_id=1, source_target_pairs={{0,4},{4,8},{8,12},{6,2},{10,6},{14,10},{1,5},{5,9},{9,13},{7,3},{... | collective-permute-start | bytes 1179656 | tf_op jit(solution)/shard_map/ppermute | solution.py:688
  70.5 15.0 %collective-permute-start.18 = (f32[2,2,8,16,128]{4,3,2,1,0:T(8,128)S(1)}, f32[2,2,8,16,128]{4,3,2,1,0:T(8,128)S(1)}, u32[]{:S(2)}, u32[]{:S(2)}) collective-permute-start(f32[2,2,8,16,128]{4,3,2,1,0:T(8,128)S(1)} %pad_maximum_fusion.refs_6_), channel_id=1, source_target_pairs={{2,0},{4,2},{6,4},{8,6},{10,8},{12,10},{14,12},{3,1},{5,3},{7,5},{... | collective-permute-start | bytes 786440 | tf_op jit(solution)/shard_map/ppermute | solution.py:688
  71.8 13.7 %collective-permute-start.17 = (f32[2,2,8,16,128]{4,3,2,1,0:T(8,128)S(1)}, f32[2,2,8,16,128]{4,3,2,1,0:T(8,128)S(1)}, u32[]{:S(2)}, u32[]{:S(2)}) collective-permute-start(f32[2,2,8,16,128]{4,3,2,1,0:T(8,128)S(1)} %pad_maximum_fusion.refs_6_), channel_id=1, source_target_pairs={{0,2},{2,4},{4,6},{6,8},{8,10},{10,12},{12,14},{1,3},{3,5},{5,7},{... | collective-permute-start | bytes 786440 | tf_op jit(solution)/shard_map/ppermute | solution.py:688
  79.4 11.9 %collective-permute-start.22 = (f32[2,24,16,128]{3,2,1,0:T(8,128)S(1)}, f32[2,24,16,128]{3,2,1,0:T(8,128)S(1)}, u32[]{:S(2)}, u32[]{:S(2)}) collective-permute-start(f32[2,24,16,128]{3,2,1,0:T(8,128)S(1)} %collective-permute-done.21.refs_4_), channel_id=1, source_target_pairs={{0,4},{4,8},{8,12},{6,2},{10,6},{14,10},{1,5},{5,9},{9,13},{7,3},{... | collective-permute-start | bytes 1179656 | tf_op jit(solution)/shard_map/ppermute | solution.py:688
  (3 other events, 44.5 us)
